TPU v7x, 32 devices: a whole 2x2x4 slice. The times are simulated.
32 devices in a mesh: seq: 16 (over z, y, core), head: 2 (over x).
Axes of the slice: x: 2, y: 2, z: 4, core: 2. Of those that a mesh axis runs over, the one named last changes fastest.
Arguments:
- query_input: bfloat16 [4096, 2048], P('seq', 'head'), may hold values from -6 to 6
- key_input: bfloat16 [4096, 2048], P('seq', 'head'), may hold values from -6 to 6
- value_input: bfloat16 [4096, 4096], P('seq', 'head'), may hold values from -6 to 6
- kernel_taps: float32 [2, 4, 2048], P(None, None, 'head'), may hold values from -3 to 3
- input_gate: float32 [8, 4096], P('head', 'seq'), may hold values from -6 to 300
- forget_gate: float32 [8, 4096], P('head', 'seq'), may hold values from -0.5 to 16
- request_lengths: int32 [4], replicated, may hold values from 1 to 2048, as said below
- output_weight: bfloat16 [4096, 2048], P('head'), may hold values from -0.09375 to 0.09375
Outputs:
- mixed_out: bfloat16 [4096, 2048], P('seq', 'head')
Inputs may be any that keep to these rules, and one draw needn't show every extreme that they name: `request_lengths`: the lengths sum to 4096; the longest request has exactly 2048 tokens.
All inputs are finite; a program needn't handle non-finite values.
Results may differ from a plain program's by a relative error of at most 0.012.
Values may be sent and summed in bfloat16 or wider, within the bound.
No kernel may reach another device: no remote copies, remote signals or barrier semaphores. Data moves between devices by JAX's collectives and lax.ppermute only.
A program may use at most 128 MiB of HBM per device.

v0:
```python
import math

import jax
import jax.numpy as jnp
from jax import lax
from jax.sharding import PartitionSpec as P

very_negative = -1e30


def entering(part, axis, combine, identity):
    place = lax.axis_index(axis)
    gathered = jax.tree.map(lambda a: lax.all_gather(a, axis), part)
    state = jax.tree.map(lambda a, e: jnp.zeros_like(a) + jnp.asarray(e, a.dtype), part, identity)

    def one(turn, state):
        return combine(
            state, jax.tree.map(lambda a: lax.dynamic_index_in_dim(a, turn, 0, False), gathered)
        )

    return lax.fori_loop(0, place, one, state)


def shifted_2(value, axis, steps):
    count = lax.axis_size(axis)
    initial, last = (max(0, -steps), min(count, count - steps))
    return lax.ppermute(value, axis, [(source, source + steps) for source in range(initial, last)])


def conv_silu(extended, wide_segment, kernel_part, segments):
    length = segments.shape[0]
    taps = kernel_part.shape[0]
    running = jnp.zeros((length, extended.shape[1]), jnp.float32)
    for shift_by in range(taps):
        piece_rows = extended[taps - 1 - shift_by : taps - 1 - shift_by + length].astype(
            jnp.float32
        )
        same_req = (wide_segment[taps - 1 - shift_by : taps - 1 - shift_by + length] == segments)[
            :, None
        ]
        running = running + jnp.where(same_req, kernel_part[shift_by][None, :] * piece_rows, 0.0)
    return jax.nn.silu(running).astype(jnp.bfloat16)


def block_pass(state, block):
    memory, normal, stabilizer, segment_prev = state
    query_block, key_block, value_block, forget_block, input_block, segment_block = block
    block_len = query_block.shape[0]
    key_scale = 1.0 / math.sqrt(query_block.shape[2])
    cumulative = jnp.cumsum(forget_block, axis=1)
    positions = jnp.arange(block_len, dtype=jnp.int32)
    allowed = (positions[None, :] <= positions[:, None]) & (
        segment_block[None, :] == segment_block[:, None]
    )
    log_weight = jnp.where(
        allowed[None],
        input_block[:, None, :] + cumulative[:, :, None] - cumulative[:, None, :],
        very_negative,
    )
    linked = segment_block == segment_prev
    carried = jnp.where(linked[None, :], stabilizer[:, None] + cumulative, very_negative)
    row_max = jnp.maximum(jnp.max(log_weight, axis=2), carried)
    scores = (
        jnp.einsum("thd,shd->hts", query_block, key_block, preferred_element_type=jnp.float32)
        * key_scale
    )
    weights = scores * jnp.exp(log_weight - row_max[:, :, None])
    reach_share = jnp.exp(carried - row_max)
    scaled_query = query_block.astype(jnp.float32) * key_scale
    from_memory = jnp.einsum("thd,hdv->thv", scaled_query, memory, precision=lax.Precision.HIGHEST)
    from_normal = jnp.einsum("thd,hd->ht", scaled_query, normal, precision=lax.Precision.HIGHEST)
    numerator = jnp.einsum(
        "hts,shv->thv",
        weights.astype(jnp.bfloat16),
        value_block,
        preferred_element_type=jnp.float32,
    )
    numerator = numerator + reach_share.T[:, :, None] * from_memory
    denominator = jnp.sum(weights, axis=2) + reach_share * from_normal
    segment_last = segment_block[block_len - 1]
    tail_weight = jnp.where(
        (segment_block == segment_last)[None, :],
        input_block + cumulative[:, -1:] - cumulative,
        very_negative,
    )
    tail_carry = jnp.where(
        segment_prev == segment_last, stabilizer + cumulative[:, -1], very_negative
    )
    stabilizer_new = jnp.maximum(jnp.max(tail_weight, axis=1), tail_carry)
    factor = jnp.exp(tail_weight - stabilizer_new[:, None])
    weighted_keys = key_block.astype(jnp.float32) * factor.T[:, :, None]
    decay_share = jnp.exp(tail_carry - stabilizer_new)
    memory_new = decay_share[:, None, None] * memory + jnp.einsum(
        "shd,shv->hdv",
        weighted_keys.astype(jnp.bfloat16),
        value_block,
        preferred_element_type=jnp.float32,
    )
    normal_new = decay_share[:, None] * normal + jnp.sum(weighted_keys, axis=0)
    return (
        (memory_new, normal_new, stabilizer_new, segment_last),
        (numerator, denominator, row_max),
    )


def combine_states(before_part, after_part):
    memory_one, normal_one, stab_one, decay_one = before_part
    memory_two, normal_two, stab_two, decay_two = after_part
    shifted = stab_one + decay_two
    stab_both = jnp.maximum(shifted, stab_two)
    share_one = jnp.exp(shifted - stab_both)
    share_two = jnp.exp(stab_two - stab_both)
    memory_both = share_one[:, None, None] * memory_one + share_two[:, None, None] * memory_two
    normal_both = share_one[:, None] * normal_one + share_two[:, None] * normal_two
    return (memory_both, normal_both, stab_both, decay_one + decay_two)


def incoming_state(memory_part, normal_part, stab_part, through_part):
    identity_state = (
        jnp.zeros_like(memory_part),
        jnp.zeros_like(normal_part),
        jnp.full(stab_part.shape, very_negative, jnp.float32),
        jnp.zeros_like(through_part),
    )
    return entering(
        (memory_part, normal_part, stab_part, through_part), "seq", combine_states, identity_state
    )


def unstack_rows(outputs, tok_rows):
    numerator, denominator, row_max = outputs
    heads_here = numerator.shape[2]
    numerator = numerator.reshape(tok_rows, heads_here, numerator.shape[3])
    denominator = denominator.transpose(1, 0, 2).reshape(heads_here, tok_rows)
    row_max = row_max.transpose(1, 0, 2).reshape(heads_here, tok_rows)
    return (numerator, denominator, row_max)


def on_device(
    query_input,
    key_input,
    value_input,
    kernel_taps,
    input_gate,
    forget_gate,
    request_lengths,
    output_weight,
):
    tok_rows = query_input.shape[0]
    heads_here = input_gate.shape[0]
    key_width = query_input.shape[1] // heads_here
    value_width = value_input.shape[1] // heads_here
    kernel_len = kernel_taps.shape[1]
    offset = lax.axis_index("seq") * tok_rows
    starts = jnp.cumsum(request_lengths) - request_lengths

    def segment_of(position):
        return jnp.sum((starts[None, :] <= position[:, None]).astype(jnp.int32), axis=1) - 1

    segments = segment_of(offset + jnp.arange(tok_rows, dtype=jnp.int32))
    wide_segment = segment_of(
        offset - (kernel_len - 1) + jnp.arange(tok_rows + kernel_len - 1, dtype=jnp.int32)
    )
    segment_before = segment_of(jnp.reshape(offset - 1, (1,)))[0]
    tail_query, tail_key = shifted_2(
        (query_input[tok_rows - (kernel_len - 1) :], key_input[tok_rows - (kernel_len - 1) :]),
        "seq",
        1,
    )
    query_conv = conv_silu(
        jnp.concatenate([tail_query, query_input]), wide_segment, kernel_taps[0], segments
    )
    key_conv = conv_silu(
        jnp.concatenate([tail_key, key_input]), wide_segment, kernel_taps[1], segments
    )
    query_heads = query_conv.reshape(tok_rows, heads_here, key_width)
    key_heads = key_conv.reshape(tok_rows, heads_here, key_width)
    value_heads = value_input.reshape(tok_rows, heads_here, value_width)
    log_forget = jax.nn.log_sigmoid(forget_gate)
    cumulative = jnp.cumsum(log_forget, axis=1)
    block_len = min(512, tok_rows)
    block_count = tok_rows // block_len
    blocks = (
        query_heads.reshape(block_count, block_len, heads_here, key_width),
        key_heads.reshape(block_count, block_len, heads_here, key_width),
        value_heads.reshape(block_count, block_len, heads_here, value_width),
        log_forget.reshape(heads_here, block_count, block_len).transpose(1, 0, 2),
        input_gate.reshape(heads_here, block_count, block_len).transpose(1, 0, 2),
        segments.reshape(block_count, block_len),
    )
    segment_last = segments[tok_rows - 1]
    through = jnp.where(segment_before == segment_last, cumulative[:, -1], very_negative)
    tail_weight = jnp.where(
        (segments == segment_last)[None, :],
        input_gate + cumulative[:, -1:] - cumulative,
        very_negative,
    )
    stab_local = jnp.max(tail_weight, axis=1)
    factor = jnp.exp(tail_weight - stab_local[:, None])
    weighted_keys = key_heads.astype(jnp.float32) * factor.T[:, :, None]
    memory_local = jnp.einsum(
        "shd,shv->hdv",
        weighted_keys.astype(jnp.bfloat16),
        value_heads,
        preferred_element_type=jnp.float32,
    )
    normal_local = jnp.sum(weighted_keys, axis=0)
    memory_in, normal_in, stab_in, _ = incoming_state(
        memory_local, normal_local, stab_local, through
    )
    _, outputs = lax.scan(block_pass, (memory_in, normal_in, stab_in, segment_before), blocks)
    numerator, denominator, row_max = unstack_rows(outputs, tok_rows)
    floor_value = jnp.maximum(jnp.abs(denominator), 1.0).T
    head_out = (
        (numerator / floor_value[:, :, None])
        .reshape(tok_rows, heads_here * value_width)
        .astype(jnp.bfloat16)
    )
    partial_value = jnp.dot(head_out, output_weight, preferred_element_type=jnp.float32)
    mixed_out = lax.psum_scatter(partial_value, "head", scatter_dimension=1, tiled=True)
    return mixed_out.astype(jnp.bfloat16)


def solution(mesh):
    placed = (
        P("seq", "head"),
        P("seq", "head"),
        P("seq", "head"),
        P(None, None, "head"),
        P("head", "seq"),
        P("head", "seq"),
        P(),
        P("head", None),
    )
    return jax.shard_map(
        on_device, mesh=mesh, in_specs=placed, out_specs=P("seq", "head"), check_vma=False
    )
```

profile of v0, /device:TPU:0, one launch (start us, length us, event | category | flops | bytes accessed | tf_op | source)
XLA Modules:
  0.0 289.1 jit_solution(6152678437494579850)
XLA Ops:
  6.5 0.8 slice.116
  7.3 2.3 collective-permute-start.1
  9.7 0.8 reduce-window.21
  10.5 1.3 fusion.40
  11.9 0.7 slice.124
  14.0 0.8 slice_compare_fusion.3
  14.8 0.7 fusion.33
  15.5 1.2 reduce-window.22
  17.1 0.9 fusion.46
  18.3 0.9 fusion.43
  19.1 0.8 exponential_bitcast_fusion
  20.4 1.3 multiply_reduce_fusion
  21.9 1.8 fusion.11
  23.8 4.5 %collective-permute-start = (bf16[3,1024]{1,0:T(4,128)(2,1)S(1)}, bf16[3,1024]{1,0:T(4,128)(2,1)S(1)}, u32[]{:S(2)}, u32[]{:S(2)}) collective-permute-start(bf16[3,1024]{1,0:T(4,128)(2,1)S(1)} %slice.106), channel_id=1, source_target_pairs={{0,2},{2,4},{4,6},{6,8},{8,10},{10,12},{12,14},{14,16},{16,18},{18... | collective-permute-start | bytes 18440 | tf_op jit(solution)/shard_map/ppermute | solution.py:27
  28.3 0.7 dynamic-slice.3
  30.1 31.5 %all-reduce.2 = (f32[64]{0:T(128)S(1)}, f32[64]{0:T(128)S(1)}) all-reduce(f32[64]{0:T(128)S(1)} %dynamic-update-slice, f32[64]{0:T(128)S(1)} %dynamic-update-slice.1), channel_id=2, replica_groups=mesh['seq'=16,'head'=2] {'seq'}, use_global_device_ids=true, to_apply=%add | all-reduce | flops 128 | bytes 1024
  62.3 17.7 %all_gather.28 = f32[16,4,256]{2,1,0:T(4,128)S(1)} all-gather(f32[1,4,256]{2,1,0:T(4,128)S(1)} %all_gather.27), channel_id=1, replica_groups=mesh['seq'=16,'head'=2] {'seq'}, dimensions={0}, use_global_device_ids=true | all-gather | bytes 69632 | tf_op jit(solution)/shard_map/all_gather | solution.py:13
  80.0 1.3 multiply_convert_fusion.2
  81.3 114.1 %all-gather.5.cloned.1.call-done = f32[64,256,512]{2,1,0:T(8,128)} async-done(((f32[4,256,512]{2,1,0:T(8,128)}), f32[64,256,512]{2,1,0:T(8,128)}) %all-gather.5.cloned.1.call-update) | async-done | bytes 33554448 | tf_op jit(solution)/shard_map/all_gather | solution.py:13
  196.4 1.0 fusion.13
  197.4 2.1 fusion.14
  200.8 7.1 %fusion.48 = f32[256,2048]{1,0:T(8,128)} fusion(bf16[256,2048]{0,1:T(8,128)(2,1)S(1)} %bitcast.126, bf16[2048,2048]{1,0:T(8,128)(2,1)} %param.17), kind=kOutput, calls=%fused_computation.92 | convolution fusion | flops 2147483648 | bytes 11534336 | tf_op jit(solution)/shard_map/dot_general | solution.py:219
  207.9 72.3 %reduce-scatter.2.cloned.1.call-done = f32[256,1024]{1,0:T(8,128)} async-done(((f32[256,2048]{1,0:T(8,128)}), f32[256,1024]{1,0:T(8,128)}) %reduce-scatter.2.cloned.1.call-update) | async-done | bytes 1048592 | tf_op jit(solution)/shard_map/reduce_scatter | solution.py:220
  280.2 2.1 convert_element_type.90
  (55 shorter events, 4.8 us)
Async XLA Ops:
  6.5 13.8 %copy-start.2 = (bf16[256,1024]{1,0:T(8,128)(2,1)S(1)}, bf16[256,1024]{1,0:T(8,128)(2,1)}, u32[]{:S(2)}) copy-start(bf16[256,1024]{1,0:T(8,128)(2,1)} %param.11) | copy-start | bytes 1572868
  6.5 188.8 %all-gather.5.cloned.1.call-start = ((), (), s32[]{:S(2)}) async-start(), calls=%async_computation.2 | async-start | bytes 35651584 | tf_op jit(solution)/shard_map/all_gather | solution.py:13
  7.3 13.0 %collective-permute-start.1 = (bf16[3,1024]{1,0:T(4,128)(2,1)S(1)}, bf16[3,1024]{1,0:T(4,128)(2,1)S(1)}, u32[]{:S(2)}, u32[]{:S(2)}) collective-permute-start(bf16[3,1024]{1,0:T(4,128)(2,1)S(1)} %slice.116), channel_id=1, source_target_pairs={{0,2},{2,4},{4,6},{6,8},{8,10},{10,12},{12,14},{14,16},{16,18},{18... | collective-permute-start | bytes 18440 | tf_op jit(solution)/shard_map/ppermute | solution.py:27
  20.3 1.5 copy-start
  21.9 1.9 copy-start.3
  21.9 6.4 %copy-start.5 = (u32[32]{0:T(128)S(1)}, u32[32]{0:T(128)}, u32[]{:S(2)}) copy-start(u32[32]{0:T(128)} %constant.101) | copy-start | bytes 388
  21.9 40.0 %copy-start.4 = (f32[4,256]{1,0:T(4,128)S(1)}, f32[4,256]{1,0:T(4,128)}, u32[]{:S(2)}) copy-start(f32[4,256]{1,0:T(4,128)} %param.14) | copy-start | bytes 12292
  23.7 256.5 %reduce-scatter.2.cloned.1.call-start = ((), (), s32[]{:S(2)}) async-start(), calls=%async_computation.1 | async-start | bytes 3145728 | tf_op jit(solution)/shard_map/reduce_scatter | solution.py:220
  23.8 56.2 %collective-permute-start = (bf16[3,1024]{1,0:T(4,128)(2,1)S(1)}, bf16[3,1024]{1,0:T(4,128)(2,1)S(1)}, u32[]{:S(2)}, u32[]{:S(2)}) collective-permute-start(bf16[3,1024]{1,0:T(4,128)(2,1)S(1)} %slice.106), channel_id=1, source_target_pairs={{0,2},{2,4},{4,6},{6,8},{8,10},{10,12},{12,14},{14,16},{16,18},{18... | collective-permute-start | bytes 18440 | tf_op jit(solution)/shard_map/ppermute | solution.py:27
  197.4 2.2 copy-start.1
Sparse Core Ops, SparseCore 0:
  23.8 171.5 all-gather.4
  208.0 72.1 reduce-scatter.1
where the time goes:
time: 290 us; the launch traced here: 289 us
  waiting for transfers between devices  186 us (64%)
  blocking collectives  49.1 us (17%)
  between operations  15.7 us (5%)
  matrix products  13.3 us (5%)
  other arithmetic  12.3 us (4%)
  starting transfers between devices  6.93 us (2%)
  local copies, waits for them, and re-layouts  5.41 us (2%)
    all_gather x1, waiting for transfers between devices, entering(): gathered = jax.tree.map(lambda a: lax.all_gather(a, axis), part)  114 us
    reduce_scatter x1, waiting for transfers between devices, on_device(): lax.psum_scatter(partial_value, 'head', scatter_dimension=1, tiled=True)  72.3 us
    unnamed x1, blocking collectives  31.5 us
    all_gather x1, blocking collectives, entering(): gathered = jax.tree.map(lambda a: lax.all_gather(a, axis), part)  17.7 us
    dot_general x1, matrix products, on_device(): jnp.dot(head_out, output_weight, preferred_element_type=jnp.float32)  7.08 us
    ppermute x2, starting transfers between devices, shifted_2(): lax.ppermute(value, axis, [(source, source + steps) for source in range(i...  6.88 us
  transfers between devices with their start and end apart: 4, of which 2 were waited for; matrix products, arithmetic and copies ran while one was open for 4% of the time, Pallas kernels for 0%

commit v1 on v0

v1 whole, which is shorter than its diff:
```python
import functools
import math

import jax
import jax.numpy as jnp
from jax import lax
from jax.experimental import pallas as pl
from jax.experimental.pallas import tpu as pltpu
from jax.sharding import PartitionSpec as P

very_negative = -1e30
INFO = 16
TAIL = 16
BF16 = jnp.bfloat16
F32 = jnp.float32


def iota(shape, dim):
    return lax.broadcasted_iota(jnp.int32, shape, dim)


def dot(a, b, contract=((1,), (0,))):
    return lax.dot_general(a, b, (contract, ((), ())), preferred_element_type=F32)


def split3(x):
    high = x.astype(BF16).astype(F32)
    rest = x - high
    mid = rest.astype(BF16).astype(F32)
    return high, mid, (rest - mid).astype(BF16).astype(F32)


def segment_of(lengths_ref, position):
    start = jnp.int32(0)
    count = jnp.zeros_like(position)
    for r in range(lengths_ref.shape[0]):
        count = count + (start <= position).astype(jnp.int32)
        start = start + lengths_ref[r]
    return count - 1


def gate_rows(forget_ref, input_ref, padded):
    heads, length = forget_ref.shape
    padded[...] = jnp.zeros_like(padded)
    padded[0, 0:heads, :] = forget_ref[...]
    padded[1, 0:heads, :] = input_ref[...]
    forget = padded[0]
    log_forget = -(jnp.maximum(-forget, 0.0) + jnp.log1p(jnp.exp(-jnp.abs(forget))))
    upto = jnp.where(iota((length, length), 0) <= iota((length, length), 1), 1.0, 0.0).astype(BF16)
    cumulative = sum(dot(part.astype(BF16), upto) for part in split3(log_forget))
    return padded[1], cumulative


def conv_silu(x_ref, columns, tail, taps_ref, which, same, wide):
    length = x_ref.shape[0]
    taps = taps_ref.shape[1]
    wide[0:8, :] = tail[TAIL - 8 : TAIL]
    wide[8 : 8 + length, :] = x_ref[:, columns].astype(F32)
    total = taps_ref[which, 0:1, columns] * wide[8 : 8 + length, :]
    for lag in range(1, taps):
        total = total + taps_ref[which, lag : lag + 1, columns] * (
            wide[8 - lag : 8 - lag + length, :] * same[lag]
        )
    return (total / (1.0 + jnp.exp(-total))).astype(BF16)


def same_request(lengths_ref, offset, length, taps):
    position = offset + iota((length, 1), 0)
    here = segment_of(lengths_ref, position)
    return here, [
        None if lag == 0 else (segment_of(lengths_ref, position - lag) == here).astype(F32)
        for lag in range(taps)
    ]


def write_info(ref, index, normal, stab, decay):
    n0, n1, n2 = split3(normal)
    s0, s1, s2 = (jnp.broadcast_to(a, (1, 128)) for a in split3(stab))
    d0, d1, d2 = (jnp.broadcast_to(a, (1, 128)) for a in split3(decay))
    row = iota((INFO, 512), 0)
    block = jnp.where(row == 0, jnp.concatenate([n0, n1], axis=1), 0.0)
    block = jnp.where(row == 1, jnp.concatenate([n2, s0, s1], axis=1), block)
    block = jnp.where(row == 2, jnp.concatenate([s2, d0, d1, d2], axis=1), block)
    rows = ref.shape[-2] - INFO
    ref[index + (pl.ds(rows, INFO), slice(None))] = block.astype(BF16)


def read_info(block):
    b = block.astype(F32)
    normal = b[0:1, 0:256] + b[0:1, 256:512] + b[1:2, 0:256]
    stab = b[1:2, 256:257] + b[1:2, 384:385] + b[2:3, 0:1]
    decay = b[2:3, 128:129] + b[2:3, 256:257] + b[2:3, 384:385]
    return normal, stab, decay


def local_kernel(
    lengths_ref, key_ref, tail_ref, taps_ref, value_ref, input_ref, forget_ref,
    conv_ref, keep_ref, send_ref, padded, wide,
):
    length = key_ref.shape[0]
    heads = input_ref.shape[0]
    key_width = key_ref.shape[1] // heads
    value_width = value_ref.shape[1] // heads
    rows = keep_ref.shape[1] - INFO
    place = lax.axis_index("seq")
    core = lax.rem(place, 2)
    offset = place * length
    _, same = same_request(lengths_ref, offset, length, taps_ref.shape[1])
    gate, cumulative = gate_rows(forget_ref, input_ref, padded)
    segment = segment_of(lengths_ref, offset + iota((1, length), 1))
    last = segment_of(lengths_ref, jnp.full((1, 1), offset + length - 1, jnp.int32))
    before = segment_of(lengths_ref, jnp.full((1, 1), offset - 1, jnp.int32))
    total = cumulative[:, length - 1 : length]
    tail_weight = jnp.where(segment == last, gate + total - cumulative, very_negative)
    stab = jnp.max(tail_weight, axis=1, keepdims=True)
    factor = jnp.exp(tail_weight - stab).T
    through = jnp.where(before == last, total, very_negative)
    for h in range(heads):
        columns = slice(h * key_width, (h + 1) * key_width)
        tail = tail_ref[1, :, columns].astype(F32)
        conv = conv_silu(key_ref, columns, tail, taps_ref, 1, same, wide)
        conv_ref[:, columns] = conv
        weighted = conv.astype(F32) * factor[:, h : h + 1]
        normal = jnp.sum(weighted, axis=0, keepdims=True)
        value = value_ref[:, h * value_width : (h + 1) * value_width]
        memory = dot(weighted.astype(BF16), value, ((0,), (0,))).astype(BF16)
        for part in range(key_width // rows):
            piece = h * (key_width // rows) + part
            owner, slot = piece // 4, piece % 4
            content = memory[part * rows : (part + 1) * rows]

            def write(ref, slot=slot, content=content, normal=normal, h=h):
                ref[slot, 0:rows, :] = content
                write_info(ref, (slot,), normal, stab[h : h + 1], through[h : h + 1])

            pl.when(core == owner)(functools.partial(write, keep_ref))
            pl.when(core != owner)(functools.partial(write, send_ref))


def chip_kernel(keep_ref, got_ref, *outs):
    place = lax.axis_index("seq")
    first = lax.rem(place, 2) == 0
    mine = lax.rem(place // 2, 4)
    rows = keep_ref.shape[1] - INFO
    for off, out in enumerate(outs):
        slot = lax.bitwise_xor(mine, off)
        n_a, m_a, d_a = read_info(keep_ref[slot, rows:, :])
        n_b, m_b, d_b = read_info(got_ref[slot, rows:, :])
        m_a = m_a + jnp.where(first, d_b, 0.0)
        m_b = m_b + jnp.where(first, 0.0, d_a)
        m = jnp.maximum(m_a, m_b)
        w_a, w_b = jnp.exp(m_a - m), jnp.exp(m_b - m)
        out[0:rows, :] = (
            w_a * keep_ref[slot, 0:rows, :].astype(F32) + w_b * got_ref[slot, 0:rows, :].astype(F32)
        ).astype(BF16)
        write_info(out, (), w_a * n_a + w_b * n_b, m, d_a + d_b)


def shifted_stab(infos, ranks, upto):
    out = []
    for i, (_, stab, _) in enumerate(infos):
        for j, (_, _, decay) in enumerate(infos):
            if i != j:
                inside = (ranks[j] > ranks[i]) & (ranks[j] < upto)
                stab = stab + jnp.where(inside, decay, 0.0)
        out.append(stab)
    return out


def total_kernel(*refs):
    *states, out = refs
    rows = out.shape[0] - INFO
    mine = lax.rem(lax.axis_index("seq") // 2, 4)
    ranks = [lax.bitwise_xor(mine, off) for off in range(4)]
    infos = [read_info(s[rows:, :]) for s in states]
    stabs = shifted_stab(infos, ranks, 4)
    m = functools.reduce(jnp.maximum, stabs)
    weights = [jnp.exp(s - m) for s in stabs]
    out[0:rows, :] = sum(w * s[0:rows, :].astype(F32) for w, s in zip(weights, states)).astype(BF16)
    write_info(
        out, (), sum(w * i[0] for w, i in zip(weights, infos)), m, sum(i[2] for i in infos)
    )


def round_kernel(bit, first, *refs):
    if first:
        total_ref, got_ref, prefix_out, total_out = refs
    else:
        prefix_ref, total_ref, got_ref, prefix_out, total_out = refs
    rows = total_ref.shape[0] - INFO
    later = lax.rem(lax.shift_right_logical(lax.axis_index("seq"), bit), 2) == 1
    n_t, m_t, d_t = read_info(total_ref[rows:, :])
    n_g, m_g, d_g = read_info(got_ref[rows:, :])
    here, got = total_ref[0:rows, :].astype(F32), got_ref[0:rows, :].astype(F32)
    a_t = m_t + jnp.where(later, 0.0, d_g)
    a_g = m_g + jnp.where(later, d_t, 0.0)
    m = jnp.maximum(a_t, a_g)
    w_t, w_g = jnp.exp(a_t - m), jnp.exp(a_g - m)
    total_out[0:rows, :] = (w_t * here + w_g * got).astype(BF16)
    write_info(total_out, (), w_t * n_t + w_g * n_g, m, d_t + d_g)
    if first:
        n_p, m_p, d_p = jnp.zeros_like(n_g), jnp.full_like(m_g, very_negative), jnp.zeros_like(d_g)
        prefix = jnp.zeros_like(got)
    else:
        n_p, m_p, d_p = read_info(prefix_ref[rows:, :])
        prefix = prefix_ref[0:rows, :].astype(F32)
    a_g = jnp.where(later, m_g + d_p, 2 * very_negative)
    m = jnp.maximum(m_p, a_g)
    w_p = jnp.exp(m_p - m)
    w_g = jnp.where(later, jnp.exp(a_g - m), 0.0)
    prefix_out[0:rows, :] = (w_p * prefix + w_g * got).astype(BF16)
    write_info(prefix_out, (), w_p * n_p + w_g * n_g, m, d_p + jnp.where(later, d_g, 0.0))


def enter_kernel(bit, prefix_ref, *refs):
    states, outs = refs[:4], refs[4:]
    rows = outs[0].shape[0] - INFO
    place = lax.axis_index("seq")
    mine = lax.rem(place // 2, 4)
    ranks = [lax.bitwise_xor(mine, off) for off in range(4)]
    infos = [read_info(s[rows:, :]) for s in states]
    n_p, m_p, _ = read_info(prefix_ref[rows:, :])
    valid = True if bit is None else lax.rem(lax.shift_right_logical(place, bit), 2) == 1
    for off, out in enumerate(outs):
        stabs = shifted_stab(infos, ranks, ranks[off])
        m_in = m_p
        for info, rank in zip(infos, ranks):
            m_in = m_in + jnp.where(rank < ranks[off], info[2], 0.0)
        m_in = jnp.where(valid, m_in, very_negative)
        stabs = [
            jnp.where(rank < ranks[off], s, 2 * very_negative) for s, rank in zip(stabs, ranks)
        ]
        m = functools.reduce(jnp.maximum, stabs, m_in)
        w_in = jnp.where(valid, jnp.exp(m_in - m), 0.0)
        total = w_in * prefix_ref[0:rows, :].astype(F32)
        normal = w_in * n_p
        for i in range(4):
            if i != off:
                w = jnp.where(ranks[i] < ranks[off], jnp.exp(stabs[i] - m), 0.0)
                total = total + w * states[i][0:rows, :].astype(F32)
                normal = normal + w * infos[i][0]
        out[0:rows, :] = total.astype(BF16)
        write_info(out, (), normal, m, jnp.zeros_like(m))


def deliver_kernel(keep_ref, got_ref, *refs):
    enter, (own_ref, other_ref) = refs[:4], refs[4:]
    place = lax.axis_index("seq")
    first = lax.rem(place, 2) == 0
    mine = lax.rem(place // 2, 4)
    rows = keep_ref.shape[1] - INFO

    def fill(same_ref, next_ref, local_ref):
        for off in range(4):
            slot = lax.bitwise_xor(mine, off)
            n_e, m_e, _ = read_info(enter[off][rows:, :])
            n_l, m_l, d_l = read_info(local_ref[slot, rows:, :])
            a_e = m_e + d_l
            m = jnp.maximum(a_e, m_l)
            w_e, w_l = jnp.exp(a_e - m), jnp.exp(m_l - m)
            same_ref[slot] = enter[off][...]
            next_ref[slot, 0:rows, :] = (
                w_e * enter[off][0:rows, :].astype(F32)
                + w_l * local_ref[slot, 0:rows, :].astype(F32)
            ).astype(BF16)
            write_info(next_ref, (slot,), w_e * n_e + w_l * n_l, m, jnp.zeros_like(m))

    pl.when(first)(lambda: fill(own_ref, other_ref, keep_ref))
    pl.when(jnp.logical_not(first))(lambda: fill(other_ref, own_ref, got_ref))


def intra_kernel(
    lengths_ref, query_ref, tail_ref, taps_ref, key_ref, value_ref, input_ref, forget_ref,
    conv_ref, numerator_ref, stats_ref, padded, wide,
):
    length = query_ref.shape[0]
    heads = input_ref.shape[0]
    key_width = query_ref.shape[1] // heads
    value_width = value_ref.shape[1] // heads
    key_scale = 1.0 / math.sqrt(key_width)
    offset = lax.axis_index("seq") * length
    segment, same = same_request(lengths_ref, offset, length, taps_ref.shape[1])
    gate, cumulative = gate_rows(forget_ref, input_ref, padded)
    by_token = cumulative.T
    segment_row = segment_of(lengths_ref, offset + iota((1, length), 1))
    before = segment_of(lengths_ref, jnp.full((1, 1), offset - 1, jnp.int32))
    allowed = (iota((length, length), 1) <= iota((length, length), 0)) & (segment_row == segment)
    lane = iota((length, 128), 1)
    denominators = jnp.ones((length, 128), F32)
    maxima = jnp.zeros((length, 128), F32)
    links = jnp.zeros((length, 128), F32)
    for h in range(heads):
        columns = slice(h * key_width, (h + 1) * key_width)
        tail = tail_ref[0, :, columns].astype(F32)
        conv = conv_silu(query_ref, columns, tail, taps_ref, 0, same, wide)
        conv_ref[:, columns] = conv
        here = by_token[:, h : h + 1]
        log_weight = jnp.where(
            allowed, gate[h : h + 1] - cumulative[h : h + 1] + here, very_negative
        )
        row_max = jnp.max(log_weight, axis=1, keepdims=True)
        scores = dot(conv, key_ref[:, columns], ((1,), (1,))) * key_scale
        weights = scores * jnp.exp(log_weight - row_max)
        value = value_ref[:, h * value_width : (h + 1) * value_width]
        numerator_ref[:, h * value_width : (h + 1) * value_width] = dot(
            weights.astype(BF16), value
        )
        denominators = jnp.where(lane == h, jnp.sum(weights, axis=1, keepdims=True), denominators)
        maxima = jnp.where(lane == h, row_max, maxima)
        links = jnp.where(lane == h, jnp.where(segment == before, here, very_negative), links)
    stats_ref[0] = denominators
    stats_ref[1] = maxima
    stats_ref[2] = links


def weight_copy(weight_ref, held, sem, block, width, chunk):
    start = pl.multiple_of(block * width + chunk * held.shape[1], 128)
    return pltpu.make_async_copy(weight_ref.at[:, pl.ds(start, held.shape[1])], held, sem)


def head_kernel(
    off, chunk, width,
    own_ref, got_ref, query_ref, numerator_ref, stats_ref, weight_ref,
    head_ref, part_ref, memory, info, held, sem,
):
    heads = query_ref.shape[1] // 256
    value_width = numerator_ref.shape[1] // heads
    key_width = query_ref.shape[1] // heads
    key_scale = 1.0 / math.sqrt(key_width)
    rows = own_ref.shape[1] - INFO
    block = lax.bitwise_xor(lax.axis_index("head"), off)
    copy = weight_copy(weight_ref, held, sem, block, width, chunk)
    copy.start()
    core = lax.rem(lax.axis_index("seq"), 2)
    for ref, half in ((own_ref, core), (got_ref, 1 - core)):
        for slot in range(4):
            start = pl.multiple_of((half * 4 + slot) * rows, rows)
            memory[pl.ds(start, rows), :] = ref[slot, 0:rows, :]
            info[half * 4 + slot] = ref[slot, rows:, :]
    for h in range(heads):
        normal, stab, _ = read_info(info[h * key_width // rows])
        query = query_ref[:, h * key_width : (h + 1) * key_width]
        parts = jnp.concatenate([*split3(normal), jnp.zeros((5, key_width), F32)], axis=0)
        from_normal = dot(query, parts.astype(BF16), ((1,), (1,)))
        from_normal = from_normal[:, 0:1] + from_normal[:, 1:2] + from_normal[:, 2:3]
        from_memory = dot(query, memory[h * key_width : (h + 1) * key_width, :])
        denominator = stats_ref[0, :, h : h + 1]
        row_max = stats_ref[1, :, h : h + 1]
        carried = stab + stats_ref[2, :, h : h + 1]
        m = jnp.maximum(row_max, carried)
        w_here = jnp.exp(row_max - m)
        w_in = jnp.exp(carried - m) * key_scale
        denominator = w_here * denominator + w_in * from_normal
        scale = 1.0 / jnp.maximum(jnp.abs(denominator), 1.0)
        columns = slice(h * value_width, (h + 1) * value_width)
        head_ref[:, columns] = (
            (w_here * scale) * numerator_ref[:, columns] + (w_in * scale) * from_memory
        ).astype(BF16)
    copy.wait()
    part_ref[...] = dot(head_ref[...], held[...]).astype(part_ref.dtype)


def project_kernel(off, chunk, width, head_ref, weight_ref, part_ref, held, sem):
    block = lax.bitwise_xor(lax.axis_index("head"), off)
    copy = weight_copy(weight_ref, held, sem, block, width, chunk)
    copy.start()
    copy.wait()
    part_ref[...] = dot(head_ref[...], held[...]).astype(part_ref.dtype)


def call(kernel, out_shape, spaces, scratch, name, flops=0, nbytes=0, limit=24):
    place = {"v": pltpu.VMEM, "s": pltpu.SMEM, "a": pl.ANY}
    outs = jax.tree.map(lambda _: pl.BlockSpec(memory_space=pltpu.VMEM), out_shape)
    return pl.pallas_call(
        kernel,
        out_shape=out_shape,
        in_specs=[pl.BlockSpec(memory_space=place[s]) for s in spaces],
        out_specs=outs,
        scratch_shapes=scratch,
        compiler_params=pltpu.CompilerParams(vmem_limit_bytes=limit << 20),
        cost_estimate=pl.CostEstimate(flops=flops, bytes_accessed=nbytes, transcendentals=0),
        name=name,
    )


def on_device(
    query_input, key_input, value_input, kernel_taps, input_gate, forget_gate, request_lengths,
    output_weight,
):
    seq_count, head_count = lax.axis_size("seq"), lax.axis_size("head")
    length, key_cols = query_input.shape
    heads = input_gate.shape[0]
    value_cols = value_input.shape[1]
    key_width, value_width = key_cols // heads, value_cols // heads
    rows = key_cols // 8
    out_cols = output_weight.shape[1] // head_count
    shape = jax.ShapeDtypeStruct

    def swap(x, off):
        return lax.ppermute(x, "seq", [(i, i ^ off) for i in range(seq_count)])

    tails = jnp.stack([query_input[length - TAIL :], key_input[length - TAIL :]])
    tails = lax.ppermute(tails, "seq", [(i, i + 1) for i in range(seq_count - 1)])

    one = shape((rows + INFO, value_width), BF16)
    four = shape((4, rows + INFO, value_width), BF16)
    gates = [pltpu.VMEM((2, 8, length), F32), pltpu.VMEM((length + 8, key_width), F32)]
    key_conv, keep, send = call(
        local_kernel, (shape(key_input.shape, BF16), four, four), "svvvvvv", gates, "local_state"
    )(request_lengths, key_input, tails, kernel_taps, value_input, input_gate, forget_gate)
    got = swap(send, 1)
    query_conv, numerator, stats = call(
        intra_kernel,
        (
            shape(query_input.shape, BF16),
            shape(value_input.shape, F32),
            shape((3, length, 128), F32),
        ),
        "svvvvvvv", gates, "intra",
    )(
        request_lengths, query_input, tails, kernel_taps, key_conv, value_input, input_gate,
        forget_gate,
    )
    pieces = call(chip_kernel, (one,) * 4, "vv", [], "chip_state")(keep, got)
    states = [pieces[0]] + [swap(pieces[off], 2 * off) for off in (1, 2, 3)]
    total = call(total_kernel, one, "vvvv", [], "group_total")(*states)
    bits = seq_count.bit_length() - 1
    flag = 3
    prefix = swap(total, 8)
    if bits > 4:
        flag = None
        prefix, total = call(
            functools.partial(round_kernel, 3, True), (one, one), "vv", [], "round_state"
        )(total, prefix)
        for bit in range(4, bits):
            prefix, total = call(
                functools.partial(round_kernel, bit, False), (one, one), "vvv", [], "round_state"
            )(prefix, total, swap(total, 1 << bit))
    enter = call(functools.partial(enter_kernel, flag), (one,) * 4, "vvvvv", [], "enter_state")(
        prefix, *states
    )
    enter = [enter[0]] + [swap(enter[off], 2 * off) for off in (1, 2, 3)]
    own, other = call(deliver_kernel, (four, four), "vvvvvv", [], "deliver_state")(
        keep, got, *enter
    )
    other = swap(other, 1)

    chunks = 2 if out_cols % 256 == 0 and head_count == 2 else 1
    piece = out_cols // chunks
    weight_scratch = [
        pltpu.VMEM((value_cols, piece), BF16), pltpu.SemaphoreType.DMA(()),
    ]
    head_out = None
    arrived = []
    for off in range(1, head_count):
        columns = []
        for chunk in range(chunks):
            out = shape((length, piece), BF16)
            if head_out is None:
                head_out, part = call(
                    functools.partial(head_kernel, off, chunk, out_cols),
                    (shape((length, value_cols), BF16), out),
                    "vvvvva",
                    [
                        pltpu.VMEM((key_cols, value_width), BF16),
                        pltpu.VMEM((8, INFO, value_width), BF16),
                    ]
                    + weight_scratch,
                    "head_out",
                )(own, other, query_conv, numerator, stats, output_weight)
            else:
                part = call(
                    functools.partial(project_kernel, off, chunk, out_cols), out, "va",
                    weight_scratch, "project_other",
                )(head_out, output_weight)
            columns.append(
                lax.ppermute(part, "head", [(i, i ^ off) for i in range(head_count)])
            )
        arrived.append(columns)
    mixed = call(
        functools.partial(project_kernel, 0, 0, out_cols), shape((length, out_cols), F32), "va",
        [pltpu.VMEM((value_cols, out_cols), BF16), pltpu.SemaphoreType.DMA(())], "project_own",
    )(head_out, output_weight)
    for columns in arrived:
        mixed = mixed + jnp.concatenate(columns, axis=1).astype(F32)
    return mixed.astype(BF16)


def solution(mesh):
    placed = (
        P("seq", "head"),
        P("seq", "head"),
        P("seq", "head"),
        P(None, None, "head"),
        P("head", "seq"),
        P("head", "seq"),
        P(),
        P("head", None),
    )
    return jax.shard_map(
        on_device, mesh=mesh, in_specs=placed, out_specs=P("seq", "head"), check_vma=False
    )
```

time: 290 us -> 78.6 us (0.27)
  waiting for transfers between devices: 186 us -> 31.8 us
  blocking collectives: 49.1 us -> 0 us
  between operations: 15.7 us -> 0.12 us
  Pallas kernels: 0 us -> 14.8 us
  matrix products: 13.3 us -> 0 us
  starting transfers between devices: 6.93 us -> 19.3 us
  other arithmetic: 12.3 us -> 0.94 us
  local copies, waits for them, and re-layouts: 5.41 us -> 11 us
    all_gather x1 -> x0, waiting for transfers between devices: 114 us -> none  [entering(): gathered = jax.tree.map(lambda a: lax.all_gather(a, axis), part)]
    reduce_scatter x1 -> x0, waiting for transfers between devices: 72.3 us -> none  [on_device(): lax.psum_scatter(partial_value, 'head', scatter_dimension=1, tiled=True)]
    ppermute x2 -> x12, waiting for transfers between devices: 0.01 us -> 31.8 us  [the longest x9 20.7 us: swap(): return lax.ppermute(x, 'seq', [(i, i ^ off) for i in range(seq_count)])]
    unnamed x1 -> x0, blocking collectives: 31.5 us -> none
    all_gather x1 -> x0, blocking collectives: 17.7 us -> none  [entering(): gathered = jax.tree.map(lambda a: lax.all_gather(a, axis), part)]
    pallas_call x0 -> x9, Pallas kernels: none -> 14.8 us  [the longest x1 3.94 us: on_device(): call(local_kernel, (shape(key_input.shape, BF16), four, four), 'svvvvvv',...]
    dot_general x6 -> x0, matrix products: 13.3 us -> none  [the longest x1 7.08 us: on_device(): jnp.dot(head_out, output_weight, preferred_element_type=jnp.float32)]
    ppermute x2 -> x12, starting transfers between devices: 6.88 us -> 19.3 us  [the longest x9 14.6 us: swap(): return lax.ppermute(x, 'seq', [(i, i ^ off) for i in range(seq_count)])]
  transfers between devices with their start and end apart: 4 -> 12, of which waited for: 2 -> 11; matrix products, arithmetic and copies ran while one was open for 4% -> 0% of each run, Pallas kernels for 0% -> 7%
where the time goes in v1:
time: 78.6 us; the launch traced here: 78 us
  waiting for transfers between devices  31.8 us (40%)
  starting transfers between devices  19.3 us (25%)
  Pallas kernels  14.8 us (19%)
  local copies, waits for them, and re-layouts  11 us (14%)
  other arithmetic  0.94 us (1%)
    ppermute x9, waiting for transfers between devices, swap(): return lax.ppermute(x, 'seq', [(i, i ^ off) for i in range(seq_count)])  20.7 us
    ppermute x9, starting transfers between devices, swap(): return lax.ppermute(x, 'seq', [(i, i ^ off) for i in range(seq_count)])  14.6 us
    ppermute x2, waiting for transfers between devices, on_device(): lax.ppermute(part, 'head', [(i, i ^ off) for i in range(head_count)])  10.2 us
    unnamed x26, local copies, waits for them, and re-layouts  10.1 us
    pallas_call x1, Pallas kernels, on_device(): call(local_kernel, (shape(key_input.shape, BF16), four, four), 'svvvvvv',...  3.94 us
    pallas_call x1, Pallas kernels, on_device(): call(intra_kernel, (shape(query_input.shape, BF16), shape(value_input.sha...  3.09 us
    pallas_call x1, Pallas kernels, on_device(): call(functools.partial(head_kernel, off, chunk, out_cols), (shape((length...  3.03 us
    ppermute x1, starting transfers between devices, on_device(): lax.ppermute(tails, 'seq', [(i, i + 1) for i in range(seq_count - 1)])  2.62 us
  transfers between devices with their start and end apart: 12, of which 11 were waited for; matrix products, arithmetic and copies ran while one was open for 0% of the time, Pallas kernels for 7%

profile of v1, /device:TPU:0, one launch (start us, length us, event | category | flops | bytes accessed | tf_op | source)
XLA Modules:
  0.0 78.0 jit_solution(779873805819703187)
XLA Ops:
  0.9 2.6 %collective-permute-start = (bf16[2,16,1024]{2,1,0:T(8,128)(2,1)S(1)}, bf16[2,16,1024]{2,1,0:T(8,128)(2,1)S(1)}, u32[]{:S(2)}, u32[]{:S(2)}) collective-permute-start(bf16[2,16,1024]{2,1,0:T(8,128)(2,1)S(1)} %pad_maximum_fusion), channel_id=1, source_target_pairs={{0,2},{2,4},{4,6},{6,8},{8,10},{10,12},{12,14},{14,16},{16,18},{18... | collective-permute-start | bytes 196616 | tf_op jit(solution)/shard_map/ppermute | solution.py:403
  4.5 1.2 %copy-done.1 = bf16[256,2048]{1,0:T(8,128)(2,1)S(1)} copy-done((bf16[256,2048]{1,0:T(8,128)(2,1)S(1)}, bf16[256,2048]{1,0:T(8,128)(2,1)}, u32[]{:S(2)}) %copy-start.1) | copy-done | bytes 1048600
  5.7 1.0 %copy-done.4 = bf16[256,1024]{1,0:T(8,128)(2,1)S(1)} copy-done((bf16[256,1024]{1,0:T(8,128)(2,1)S(1)}, bf16[256,1024]{1,0:T(8,128)(2,1)}, u32[]{:S(2)}) %copy-start.4) | copy-done | bytes 524312
  9.5 3.9 %local_state.1 = (bf16[256,1024]{1,0:T(8,128)(2,1)S(1)}, bf16[4,144,512]{2,1,0:T(8,128)(2,1)S(1)}, bf16[4,144,512]{2,1,0:T(8,128)(2,1)S(1)}) custom-call(s32[4]{0:T(128)S(1)} %copy-done.11, bf16[256,1024]{1,0:T(8,128)(2,1)S(1)} %copy-done.4, bf16[2,16,1024]{2,1,0:T(8,128)(2,1)S(1)} %collective-permute-done.tail_ref, f32[2,4,1024]{2,1,0:T(4,128)S(1)} %copy-done.5, ...), custom_call_target="tpu_custom_call" | custom-call | tf_op jit(solution)/shard_map/local_state/pallas_call | solution.py:408
  13.5 3.0 %collective-permute-start.1 = (bf16[4,144,512]{2,1,0:T(8,128)(2,1)S(1)}, bf16[4,144,512]{2,1,0:T(8,128)(2,1)S(1)}, u32[]{:S(2)}, u32[]{:S(2)}) collective-permute-start(bf16[4,144,512]{2,1,0:T(8,128)(2,1)S(1)} %get-tuple-element.24), channel_id=1, source_target_pairs={{0,2},{2,0},{4,6},{6,4},{8,10},{10,8},{12,14},{14,12},{16,18},{18,... | collective-permute-start | bytes 1769480 | tf_op jit(solution)/shard_map/ppermute | solution.py:400
  16.5 1.6 %collective-permute-done.1.got_ref = bf16[4,144,512]{2,1,0:T(8,128)(2,1)S(1)} collective-permute-done((bf16[4,144,512]{2,1,0:T(8,128)(2,1)S(1)}, bf16[4,144,512]{2,1,0:T(8,128)(2,1)S(1)}, u32[]{:S(2)}, u32[]{:S(2)}) %collective-permute-start.1) | collective-permute-done | bytes 589856 | tf_op jit(solution)/shard_map/ppermute | solution.py:400
  18.5 2.7 %collective-permute-start.2 = (bf16[144,512]{1,0:T(8,128)(2,1)S(1)}, bf16[144,512]{1,0:T(8,128)(2,1)S(1)}, u32[]{:S(2)}, u32[]{:S(2)}) collective-permute-start(bf16[144,512]{1,0:T(8,128)(2,1)S(1)} %get-tuple-element.26), channel_id=1, source_target_pairs={{0,4},{2,6},{4,0},{6,2},{8,12},{10,14},{12,8},{14,10},{16,20},{18,... | collective-permute-start | bytes 442376 | tf_op jit(solution)/shard_map/ppermute | solution.py:400
  21.2 1.6 %collective-permute-start.3 = (bf16[144,512]{1,0:T(8,128)(2,1)S(1)}, bf16[144,512]{1,0:T(8,128)(2,1)S(1)}, u32[]{:S(2)}, u32[]{:S(2)}) collective-permute-start(bf16[144,512]{1,0:T(8,128)(2,1)S(1)} %get-tuple-element.27), channel_id=1, source_target_pairs={{0,8},{2,10},{4,12},{6,14},{8,0},{10,2},{12,4},{14,6},{16,24},{18,... | collective-permute-start | bytes 442376 | tf_op jit(solution)/shard_map/ppermute | solution.py:400
  23.6 1.7 %collective-permute-done.2.refs_1_ = bf16[144,512]{1,0:T(8,128)(2,1)S(1)} collective-permute-done((bf16[144,512]{1,0:T(8,128)(2,1)S(1)}, bf16[144,512]{1,0:T(8,128)(2,1)S(1)}, u32[]{:S(2)}, u32[]{:S(2)}) %collective-permute-start.2) | collective-permute-done | bytes 147488 | tf_op jit(solution)/shard_map/ppermute | solution.py:400
  25.4 2.5 %collective-permute-done.3.refs_2_ = bf16[144,512]{1,0:T(8,128)(2,1)S(1)} collective-permute-done((bf16[144,512]{1,0:T(8,128)(2,1)S(1)}, bf16[144,512]{1,0:T(8,128)(2,1)S(1)}, u32[]{:S(2)}, u32[]{:S(2)}) %collective-permute-start.3) | collective-permute-done | bytes 147488 | tf_op jit(solution)/shard_map/ppermute | solution.py:400
  27.9 2.8 %collective-permute-done.4.refs_3_ = bf16[144,512]{1,0:T(8,128)(2,1)S(1)} collective-permute-done((bf16[144,512]{1,0:T(8,128)(2,1)S(1)}, bf16[144,512]{1,0:T(8,128)(2,1)S(1)}, u32[]{:S(2)}, u32[]{:S(2)}) %collective-permute-start.4) | collective-permute-done | bytes 147488 | tf_op jit(solution)/shard_map/ppermute | solution.py:400
  30.9 2.8 %collective-permute-start.5 = (bf16[144,512]{1,0:T(8,128)(2,1)S(1)}, bf16[144,512]{1,0:T(8,128)(2,1)S(1)}, u32[]{:S(2)}, u32[]{:S(2)}) collective-permute-start(bf16[144,512]{1,0:T(8,128)(2,1)S(1)} %group_total.1), channel_id=1, source_target_pairs={{0,16},{2,18},{4,20},{6,22},{8,24},{10,26},{12,28},{14,30},{16,0},... | collective-permute-start | bytes 442376 | tf_op jit(solution)/shard_map/ppermute | solution.py:400
  33.7 6.4 %collective-permute-done.5.prefix_ref = bf16[144,512]{1,0:T(8,128)(2,1)S(1)} collective-permute-done((bf16[144,512]{1,0:T(8,128)(2,1)S(1)}, bf16[144,512]{1,0:T(8,128)(2,1)S(1)}, u32[]{:S(2)}, u32[]{:S(2)}) %collective-permute-start.5) | collective-permute-done | bytes 147488 | tf_op jit(solution)/shard_map/ppermute | solution.py:400
  42.0 2.2 %collective-permute-start.8 = (bf16[144,512]{1,0:T(8,128)(2,1)S(1)}, bf16[144,512]{1,0:T(8,128)(2,1)S(1)}, u32[]{:S(2)}, u32[]{:S(2)}) collective-permute-start(bf16[144,512]{1,0:T(8,128)(2,1)S(1)} %get-tuple-element.32), channel_id=1, source_target_pairs={{0,12},{2,14},{4,8},{6,10},{8,4},{10,6},{12,0},{14,2},{16,28},{18,... | collective-permute-start | bytes 442376 | tf_op jit(solution)/shard_map/ppermute | solution.py:400
  44.2 3.0 %collective-permute-done.6.refs_1_ = bf16[144,512]{1,0:T(8,128)(2,1)S(1)} collective-permute-done((bf16[144,512]{1,0:T(8,128)(2,1)S(1)}, bf16[144,512]{1,0:T(8,128)(2,1)S(1)}, u32[]{:S(2)}, u32[]{:S(2)}) %collective-permute-start.6) | collective-permute-done | bytes 147488 | tf_op jit(solution)/shard_map/ppermute | solution.py:400
  47.6 2.4 %collective-permute-done.8.refs_3_ = bf16[144,512]{1,0:T(8,128)(2,1)S(1)} collective-permute-done((bf16[144,512]{1,0:T(8,128)(2,1)S(1)}, bf16[144,512]{1,0:T(8,128)(2,1)S(1)}, u32[]{:S(2)}, u32[]{:S(2)}) %collective-permute-start.8) | collective-permute-done | bytes 147488 | tf_op jit(solution)/shard_map/ppermute | solution.py:400
  50.4 1.2 %copy-done.2 = bf16[256,2048]{1,0:T(8,128)(2,1)S(1)} copy-done((bf16[256,2048]{1,0:T(8,128)(2,1)S(1)}, bf16[256,2048]{1,0:T(8,128)(2,1)}, u32[]{:S(2)}) %copy-start.2) | copy-done | bytes 1048600
  55.5 3.1 %intra.1 = (bf16[256,1024]{1,0:T(8,128)(2,1)S(1)}, f32[256,2048]{1,0:T(8,128)S(1)}, f32[3,256,128]{2,1,0:T(8,128)S(1)}) custom-call(s32[4]{0:T(128)S(1)} %copy-done.12, bf16[256,1024]{1,0:T(8,128)(2,1)S(1)} %copy-done.3, bf16[2,16,1024]{2,1,0:T(8,128)(2,1)S(1)} %collective-permute-done.tail_ref, f32[2,4,1024]{2,1,0:T(4,128)S(1)} %copy-done.6, ...), custom_call_target="tpu_custom_call" | custom-call | tf_op jit(solution)/shard_map/intra/pallas_call | solution.py:412
  58.6 3.0 %head_out.1 = (bf16[256,2048]{1,0:T(8,128)(2,1)S(1)}, bf16[256,512]{1,0:T(8,128)(2,1)S(1)}) custom-call(bf16[4,144,512]{2,1,0:T(8,128)(2,1)S(1)} %get-tuple-element.33.own_ref, bf16[4,144,512]{2,1,0:T(8,128)(2,1)S(1)} %collective-permute-done.9.got_ref, bf16[256,1024]{1,0:T(8,128)(2,1)S(1)} %get-tuple-element.36.query_ref, ...), custom_call_target="tpu_custom_call" | custom-call | tf_op jit(solution)/shard_map/head_out/pallas_call | solution.py:460
  61.6 1.1 %project_other.1 = bf16[256,512]{1,0:T(8,128)(2,1)S(1)} custom-call(bf16[256,2048]{1,0:T(8,128)(2,1)S(1)} %get-tuple-element.39.head_ref, bf16[2048,2048]{1,0:T(8,128)(2,1)S(1)} %copy-done), custom_call_target="tpu_custom_call" | custom-call | tf_op jit(solution)/shard_map/project_other/pallas_call | solution.py:472
  62.7 1.6 %collective-permute-start.11 = (bf16[256,512]{1,0:T(8,128)(2,1)S(1)}, bf16[256,512]{1,0:T(8,128)(2,1)S(1)}, u32[]{:S(2)}, u32[]{:S(2)}) collective-permute-start(bf16[256,512]{1,0:T(8,128)(2,1)S(1)} %project_other.1), channel_id=1, source_target_pairs={{0,1},{1,0},{2,3},{3,2},{4,5},{5,4},{6,7},{7,6},{8,9},{9,8},{10,11... | collective-permute-start | bytes 786440 | tf_op jit(solution)/shard_map/ppermute | solution.py:477
  64.8 2.1 %project_own.1 = f32[256,1024]{1,0:T(8,128)S(1)} custom-call(bf16[256,2048]{1,0:T(8,128)(2,1)S(1)} %get-tuple-element.39.head_ref, bf16[2048,2048]{1,0:T(8,128)(2,1)S(1)} %copy-done), custom_call_target="tpu_custom_call" | custom-call | tf_op jit(solution)/shard_map/project_own/pallas_call | solution.py:480
  66.9 5.0 %collective-permute-done.11 = bf16[256,512]{1,0:T(8,128)(2,1)S(1)} collective-permute-done((bf16[256,512]{1,0:T(8,128)(2,1)S(1)}, bf16[256,512]{1,0:T(8,128)(2,1)S(1)}, u32[]{:S(2)}, u32[]{:S(2)}) %collective-permute-start.11) | collective-permute-done | bytes 262176 | tf_op jit(solution)/shard_map/ppermute | solution.py:477
  71.9 5.2 %collective-permute-done.10 = bf16[256,512]{1,0:T(8,128)(2,1)S(1)} collective-permute-done((bf16[256,512]{1,0:T(8,128)(2,1)S(1)}, bf16[256,512]{1,0:T(8,128)(2,1)S(1)}, u32[]{:S(2)}, u32[]{:S(2)}) %collective-permute-start.10) | collective-permute-done | bytes 262176 | tf_op jit(solution)/shard_map/ppermute | solution.py:477
  (38 shorter events, 14.0 us)
Async XLA Ops:
  0.0 58.6 %copy-start = (bf16[2048,2048]{1,0:T(8,128)(2,1)S(1)}, bf16[2048,2048]{1,0:T(8,128)(2,1)}, u32[]{:S(2)}) copy-start(bf16[2048,2048]{1,0:T(8,128)(2,1)} %weight_ref.5) | copy-start | bytes 25165828
  0.9 3.5 %collective-permute-start = (bf16[2,16,1024]{2,1,0:T(8,128)(2,1)S(1)}, bf16[2,16,1024]{2,1,0:T(8,128)(2,1)S(1)}, u32[]{:S(2)}, u32[]{:S(2)}) collective-permute-start(bf16[2,16,1024]{2,1,0:T(8,128)(2,1)S(1)} %pad_maximum_fusion), channel_id=1, source_target_pairs={{0,2},{2,4},{4,6},{6,8},{8,10},{10,12},{12,14},{14,16},{16,18},{18... | collective-permute-start | bytes 196616 | tf_op jit(solution)/shard_map/ppermute | solution.py:403
  4.5 1.2 %copy-start.1 = (bf16[256,2048]{1,0:T(8,128)(2,1)S(1)}, bf16[256,2048]{1,0:T(8,128)(2,1)}, u32[]{:S(2)}) copy-start(bf16[256,2048]{1,0:T(8,128)(2,1)} %value_ref.3) | copy-start | bytes 3145732
  5.7 1.0 %copy-start.4 = (bf16[256,1024]{1,0:T(8,128)(2,1)S(1)}, bf16[256,1024]{1,0:T(8,128)(2,1)}, u32[]{:S(2)}) copy-start(bf16[256,1024]{1,0:T(8,128)(2,1)} %key_ref.1) | copy-start | bytes 1572868
  6.7 0.8 copy-start.5
  7.5 0.7 copy-start.7
  8.2 0.7 copy-start.9
  8.9 0.7 copy-start.11
  13.5 4.7 %collective-permute-start.1 = (bf16[4,144,512]{2,1,0:T(8,128)(2,1)S(1)}, bf16[4,144,512]{2,1,0:T(8,128)(2,1)S(1)}, u32[]{:S(2)}, u32[]{:S(2)}) collective-permute-start(bf16[4,144,512]{2,1,0:T(8,128)(2,1)S(1)} %get-tuple-element.24), channel_id=1, source_target_pairs={{0,2},{2,0},{4,6},{6,4},{8,10},{10,8},{12,14},{14,12},{16,18},{18,... | collective-permute-start | bytes 1769480 | tf_op jit(solution)/shard_map/ppermute | solution.py:400
  18.5 6.9 %collective-permute-start.2 = (bf16[144,512]{1,0:T(8,128)(2,1)S(1)}, bf16[144,512]{1,0:T(8,128)(2,1)S(1)}, u32[]{:S(2)}, u32[]{:S(2)}) collective-permute-start(bf16[144,512]{1,0:T(8,128)(2,1)S(1)} %get-tuple-element.26), channel_id=1, source_target_pairs={{0,4},{2,6},{4,0},{6,2},{8,12},{10,14},{12,8},{14,10},{16,20},{18,... | collective-permute-start | bytes 442376 | tf_op jit(solution)/shard_map/ppermute | solution.py:400
  21.2 6.6 %collective-permute-start.3 = (bf16[144,512]{1,0:T(8,128)(2,1)S(1)}, bf16[144,512]{1,0:T(8,128)(2,1)S(1)}, u32[]{:S(2)}, u32[]{:S(2)}) collective-permute-start(bf16[144,512]{1,0:T(8,128)(2,1)S(1)} %get-tuple-element.27), channel_id=1, source_target_pairs={{0,8},{2,10},{4,12},{6,14},{8,0},{10,2},{12,4},{14,6},{16,24},{18,... | collective-permute-start | bytes 442376 | tf_op jit(solution)/shard_map/ppermute | solution.py:400
  22.8 7.9 %collective-permute-start.4 = (bf16[144,512]{1,0:T(8,128)(2,1)S(1)}, bf16[144,512]{1,0:T(8,128)(2,1)S(1)}, u32[]{:S(2)}, u32[]{:S(2)}) collective-permute-start(bf16[144,512]{1,0:T(8,128)(2,1)S(1)} %get-tuple-element.28), channel_id=1, source_target_pairs={{0,12},{2,14},{4,8},{6,10},{8,4},{10,6},{12,0},{14,2},{16,28},{18,... | collective-permute-start | bytes 442376 | tf_op jit(solution)/shard_map/ppermute | solution.py:400
  30.9 9.2 %collective-permute-start.5 = (bf16[144,512]{1,0:T(8,128)(2,1)S(1)}, bf16[144,512]{1,0:T(8,128)(2,1)S(1)}, u32[]{:S(2)}, u32[]{:S(2)}) collective-permute-start(bf16[144,512]{1,0:T(8,128)(2,1)S(1)} %group_total.1), channel_id=1, source_target_pairs={{0,16},{2,18},{4,20},{6,22},{8,24},{10,26},{12,28},{14,30},{16,0},... | collective-permute-start | bytes 442376 | tf_op jit(solution)/shard_map/ppermute | solution.py:400
  40.7 6.5 %collective-permute-start.6 = (bf16[144,512]{1,0:T(8,128)(2,1)S(1)}, bf16[144,512]{1,0:T(8,128)(2,1)S(1)}, u32[]{:S(2)}, u32[]{:S(2)}) collective-permute-start(bf16[144,512]{1,0:T(8,128)(2,1)S(1)} %get-tuple-element.30), channel_id=1, source_target_pairs={{0,4},{2,6},{4,0},{6,2},{8,12},{10,14},{12,8},{14,10},{16,20},{18,... | collective-permute-start | bytes 442376 | tf_op jit(solution)/shard_map/ppermute | solution.py:400
  41.3 6.2 %collective-permute-start.7 = (bf16[144,512]{1,0:T(8,128)(2,1)S(1)}, bf16[144,512]{1,0:T(8,128)(2,1)S(1)}, u32[]{:S(2)}, u32[]{:S(2)}) collective-permute-start(bf16[144,512]{1,0:T(8,128)(2,1)S(1)} %get-tuple-element.31), channel_id=1, source_target_pairs={{0,8},{2,10},{4,12},{6,14},{8,0},{10,2},{12,4},{14,6},{16,24},{18,... | collective-permute-start | bytes 442376 | tf_op jit(solution)/shard_map/ppermute | solution.py:400
  42.0 7.9 %collective-permute-start.8 = (bf16[144,512]{1,0:T(8,128)(2,1)S(1)}, bf16[144,512]{1,0:T(8,128)(2,1)S(1)}, u32[]{:S(2)}, u32[]{:S(2)}) collective-permute-start(bf16[144,512]{1,0:T(8,128)(2,1)S(1)} %get-tuple-element.32), channel_id=1, source_target_pairs={{0,12},{2,14},{4,8},{6,10},{8,4},{10,6},{12,0},{14,2},{16,28},{18,... | collective-permute-start | bytes 442376 | tf_op jit(solution)/shard_map/ppermute | solution.py:400
  50.3 8.2 %collective-permute-start.9 = (bf16[4,144,512]{2,1,0:T(8,128)(2,1)S(1)}, bf16[4,144,512]{2,1,0:T(8,128)(2,1)S(1)}, u32[]{:S(2)}, u32[]{:S(2)}) collective-permute-start(bf16[4,144,512]{2,1,0:T(8,128)(2,1)S(1)} %get-tuple-element.34), channel_id=1, source_target_pairs={{0,2},{2,0},{4,6},{6,4},{8,10},{10,8},{12,14},{14,12},{16,18},{18,... | collective-permute-start | bytes 1769480 | tf_op jit(solution)/shard_map/ppermute | solution.py:400
  50.4 1.2 %copy-start.2 = (bf16[256,2048]{1,0:T(8,128)(2,1)S(1)}, bf16[256,2048]{1,0:T(8,128)(2,1)}, u32[]{:S(2)}) copy-start(bf16[256,2048]{1,0:T(8,128)(2,1)} %value_ref.3) | copy-start | bytes 3145732
  51.6 1.0 %copy-start.3 = (bf16[256,1024]{1,0:T(8,128)(2,1)S(1)}, bf16[256,1024]{1,0:T(8,128)(2,1)}, u32[]{:S(2)}) copy-start(bf16[256,1024]{1,0:T(8,128)(2,1)} %query_ref.1) | copy-start | bytes 1572868
  52.7 0.8 copy-start.6
  53.4 0.7 copy-start.8
  54.1 0.7 copy-start.10
  62.7 9.2 %collective-permute-start.11 = (bf16[256,512]{1,0:T(8,128)(2,1)S(1)}, bf16[256,512]{1,0:T(8,128)(2,1)S(1)}, u32[]{:S(2)}, u32[]{:S(2)}) collective-permute-start(bf16[256,512]{1,0:T(8,128)(2,1)S(1)} %project_other.1), channel_id=1, source_target_pairs={{0,1},{1,0},{2,3},{3,2},{4,5},{5,4},{6,7},{7,6},{8,9},{9,8},{10,11... | collective-permute-start | bytes 786440 | tf_op jit(solution)/shard_map/ppermute | solution.py:477
  64.3 12.8 %collective-permute-start.10 = (bf16[256,512]{1,0:T(8,128)(2,1)S(1)}, bf16[256,512]{1,0:T(8,128)(2,1)S(1)}, u32[]{:S(2)}, u32[]{:S(2)}) collective-permute-start(bf16[256,512]{1,0:T(8,128)(2,1)S(1)} %get-tuple-element.40), channel_id=1, source_target_pairs={{0,1},{1,0},{2,3},{3,2},{4,5},{5,4},{6,7},{7,6},{8,9},{9,8},{10,11... | collective-permute-start | bytes 786440 | tf_op jit(solution)/shard_map/ppermute | solution.py:477
  (1 other events, 0.7 us)

commit v2 on v1

v2 whole, which is shorter than its diff:
```python
import functools
import math

import jax
import jax.numpy as jnp
from jax import lax
from jax.experimental import pallas as pl
from jax.experimental.pallas import tpu as pltpu
from jax.sharding import PartitionSpec as P

very_negative = -1e30
INFO = 16
TAIL = 16
BF16 = jnp.bfloat16
F32 = jnp.float32


def iota(shape, dim):
    return lax.broadcasted_iota(jnp.int32, shape, dim)


def dot(a, b, contract=((1,), (0,))):
    return lax.dot_general(a, b, (contract, ((), ())), preferred_element_type=F32)


def split3(x):
    high = x.astype(BF16).astype(F32)
    rest = x - high
    mid = rest.astype(BF16).astype(F32)
    return high, mid, (rest - mid).astype(BF16).astype(F32)


def segment_of(lengths_ref, position):
    start = jnp.int32(0)
    count = jnp.zeros_like(position)
    for r in range(lengths_ref.shape[0]):
        count = count + (start <= position).astype(jnp.int32)
        start = start + lengths_ref[r]
    return count - 1


def core_place():
    place = lax.axis_index("seq")
    return lax.rem(place, 2), lax.rem(place // 2, 4)


def start_copies(sems, pairs):
    copies = [pltpu.make_async_copy(a, b, sems.at[i]) for i, (a, b) in enumerate(pairs)]
    for copy in copies:
        copy.start()
    return copies


def by_core(core, own_ref, other_ref, columns, held):
    rows = own_ref.shape[0]
    return [
        (ref.at[:, columns], held.at[pl.ds(pl.multiple_of(half * rows, rows), rows), :])
        for ref, half in ((own_ref, core), (other_ref, 1 - core))
    ]


def gate_rows(core, per_core, gates, raw, picked):
    _, heads, length = gates[0].shape
    for ref, half in ((gates[0], core), (gates[1], 1 - core)):
        for g in range(2):
            raw[g, 0:heads, pl.ds(pl.multiple_of(half * length, length), length)] = ref[g]
    first = core * per_core if heads > 1 else 0
    picked[...] = jnp.zeros_like(picked)
    for g in range(2):
        for i in range(per_core):
            picked[g, i : i + 1, :] = raw[g, pl.ds(first + i, 1), :]
    forget = picked[1]
    log_forget = -(jnp.maximum(-forget, 0.0) + jnp.log1p(jnp.exp(-jnp.abs(forget))))
    upto = jnp.where(iota((length, length), 0) <= iota((length, length), 1), 1.0, 0.0).astype(BF16)
    parts = split3(log_forget)
    sums = [
        sum(dot(part[:, b * length : (b + 1) * length].astype(BF16), upto) for part in parts)
        for b in range(2)
    ]
    cumulative = jnp.concatenate([sums[0], sums[1] + sums[0][:, length - 1 :]], axis=1)
    return picked[0], cumulative


def conv_rows(lengths_ref, offset, start, stop, taps, columns, wide):
    position = offset + start + iota((stop - start, 1), 0)
    here = segment_of(lengths_ref, position)
    total = taps[0:1, columns] * wide[8 + start : 8 + stop, :]
    for lag in range(1, taps.shape[0]):
        same = (segment_of(lengths_ref, position - lag) == here).astype(F32)
        total = total + taps[lag : lag + 1, columns] * (
            wide[8 + start - lag : 8 + stop - lag, :] * same
        )
    return (total / (1.0 + jnp.exp(-total))).astype(BF16)


def write_info(ref, normal, stab, decay):
    lines = [p[:, c : c + 128] for p in split3(normal) for c in range(0, normal.shape[1], 128)]
    lines += [jnp.broadcast_to(p, (1, 128)) for x in (stab, decay) for p in split3(x)]
    row = iota((INFO, 128), 0)
    block = jnp.zeros((INFO, 128), F32)
    for i, line in enumerate(lines):
        block = jnp.where(row == i, line, block)
    ref[ref.shape[0] - INFO :, :] = block.astype(BF16)


def read_info(ref, key_width=256):
    b = ref[ref.shape[0] - INFO :, :].astype(F32)
    k = key_width // 128
    normal = jnp.concatenate(
        [b[i : i + 1] + b[i + k : i + k + 1] + b[i + 2 * k : i + 2 * k + 1] for i in range(k)],
        axis=1,
    )
    sums = [b[i : i + 1] + b[i + 1 : i + 2] + b[i + 2 : i + 3] for i in (3 * k, 3 * k + 3)]
    return normal, sums[0][:, 0:1], sums[1][:, 0:1]


def tail_kernel(query_ref, key_ref, input_ref, forget_ref, out_ref, gate_ref, sems):
    last = query_ref.shape[0] - TAIL
    copies = start_copies(
        sems,
        [
            (ref.at[pl.ds(last, TAIL), :], out_ref.at[i])
            for i, ref in enumerate((query_ref, key_ref))
        ]
        + [(ref, gate_ref.at[i]) for i, ref in enumerate((input_ref, forget_ref))],
    )
    for copy in copies:
        copy.wait()


def local_kernel(
    per_core, lengths_ref, key_ref, key_other, value_ref, value_other,
    gates_ref, gates_other, taps_ref,
    conv_ref, values, gate_ref, taps, key_first, factor_first,
    memory_ref, normal_ref, stab_ref, through_ref,
    keys, raw, picked, wide, sems,
):
    core, _ = core_place()
    length = keys.shape[0]
    key_width = keys.shape[1] // per_core
    value_width = values.shape[1] // per_core
    split = gates_ref.shape[1] > 1
    key_columns = pl.ds(
        pl.multiple_of(core * keys.shape[1], 128) if split else 0, keys.shape[1]
    )
    value_columns = pl.ds(pl.multiple_of(core * values.shape[1], 128), values.shape[1])
    copies = start_copies(
        sems,
        [(taps_ref.at[1, :, key_columns], taps)]
        + by_core(core, key_ref, key_other, key_columns, keys)
        + by_core(core, value_ref, value_other, value_columns, values),
    )
    offset = lax.axis_index("seq") // 2 * length
    for copy in copies[:3]:
        copy.wait()
    gate, cumulative = gate_rows(core, per_core, (gates_ref, gates_other), raw, picked)
    gate_ref[0] = gate
    gate_ref[1] = cumulative
    segment = segment_of(lengths_ref, offset + iota((1, length), 1))
    last = segment_of(lengths_ref, jnp.full((1, 1), offset + length - 1, jnp.int32))
    before = segment_of(lengths_ref, jnp.full((1, 1), offset - 1, jnp.int32))
    total = cumulative[:, length - 1 : length]
    tail_weight = jnp.where(segment == last, gate + total - cumulative, very_negative)
    stab = jnp.max(tail_weight, axis=1, keepdims=True)
    factor = jnp.exp(tail_weight - stab).T
    stab_ref[...] = jnp.broadcast_to(stab, stab_ref.shape)
    through = jnp.where(before == last, total, very_negative)
    through_ref[...] = jnp.broadcast_to(through, through_ref.shape)
    factor_first[...] = factor[0:16]
    key_first[...] = keys[0:16, :]
    normal_ref[...] = jnp.zeros_like(normal_ref)
    weighted_all = []
    step = 128
    for i in range(per_core):
        columns = slice(i * key_width, (i + 1) * key_width)
        wide[0:8, :] = jnp.zeros((8, key_width), F32)
        wide[8:, :] = keys[:, columns].astype(F32)
        normal = jnp.zeros((1, key_width), F32)
        weighted_rows = []
        for start in range(0, length, step):
            conv = conv_rows(lengths_ref, offset, start, start + step, taps, columns, wide)
            conv_ref[start : start + step, columns] = conv
            weight = factor[start : start + step, i : i + 1]
            if start == 0:
                weight = jnp.where(iota((step, 1), 0) >= 8, weight, 0.0)
            weighted = conv.astype(F32) * weight
            normal = normal + jnp.sum(weighted, axis=0, keepdims=True)
            weighted_rows.append(weighted.astype(BF16))
        weighted_all.append(jnp.concatenate(weighted_rows, axis=0))
        normal_ref[i : i + 1, :] = normal
    for copy in copies[3:]:
        copy.wait()
    for i in range(per_core):
        memory_ref[i * key_width : (i + 1) * key_width, :] = dot(
            weighted_all[i], values[:, i * value_width : (i + 1) * value_width], ((0,), (0,))
        )


def pick_tail(core, which, tail_ref, tail_other, columns):
    rows = [ref[which, :, columns].astype(F32) for ref in (tail_ref, tail_other)]
    return jnp.where(core == 0, rows[0], rows[1])[TAIL - 8 :]


def first_kernel(
    per_core, length, lengths_ref, tail_ref, tail_other, taps, key_first, values, factor_first,
    memory_ref, normal_ref, stab_ref, through_ref,
    conv_ref, out0, out1, out2, out3, whole, normals, wide,
):
    core, mine = core_place()
    width = key_first.shape[1]
    key_width = width // per_core
    value_width = values.shape[1] // per_core
    split = tail_ref.shape[2] > width
    tail_columns = pl.ds(pl.multiple_of(core * width, 128) if split else 0, width)
    tail = pick_tail(core, 1, tail_ref, tail_other, tail_columns)
    offset = lax.axis_index("seq") // 2 * length
    normals[...] = jnp.zeros_like(normals)
    for i in range(per_core):
        columns = slice(i * key_width, (i + 1) * key_width)
        wide[0:8, :] = tail[:, columns]
        wide[8:, :] = key_first[:, columns].astype(F32)
        conv = conv_rows(lengths_ref, offset, 0, 16, taps, columns, wide)
        conv_ref[:, columns] = conv
        weight = jnp.where(iota((16, 1), 0) < 8, factor_first[:, i : i + 1], 0.0)
        weighted = conv.astype(F32) * weight
        normals[i : i + 1, :] = normal_ref[i : i + 1, :] + jnp.sum(weighted, axis=0, keepdims=True)
        whole[i * key_width : (i + 1) * key_width, :] = (
            memory_ref[i * key_width : (i + 1) * key_width, :]
            + dot(
                weighted.astype(BF16),
                values[0:16, i * value_width : (i + 1) * value_width],
                ((0,), (0,)),
            )
        ).astype(BF16)
    outs = (out0, out1, out2, out3)
    rows = width // 4
    for off, out in enumerate(outs):
        piece = lax.bitwise_xor(mine, off)
        content = whole[pl.ds(pl.multiple_of(piece * rows, rows), rows), :]
        for j in range(value_width // 128):
            out[j * rows : (j + 1) * rows, :] = content[:, j * 128 : (j + 1) * 128]
        head = piece // (key_width // rows)
        write_info(
            out,
            normals[pl.ds(head, 1), :],
            stab_ref[pl.ds(head, 1), :][:, 0:1],
            through_ref[pl.ds(head, 1), :][:, 0:1],
        )


def shifted_stab(infos, ranks, upto):
    out = []
    for i, (_, stab, _) in enumerate(infos):
        for j, (_, _, decay) in enumerate(infos):
            if i != j:
                inside = (ranks[j] > ranks[i]) & (ranks[j] < upto)
                stab = stab + jnp.where(inside, decay, 0.0)
        out.append(stab)
    return out


def total_kernel(*refs):
    *states, out = refs
    rows = out.shape[0] - INFO
    _, mine = core_place()
    ranks = [lax.bitwise_xor(mine, off) for off in range(4)]
    infos = [read_info(s) for s in states]
    stabs = shifted_stab(infos, ranks, 4)
    m = functools.reduce(jnp.maximum, stabs)
    weights = [jnp.exp(s - m) for s in stabs]
    out[0:rows, :] = sum(w * s[0:rows, :].astype(F32) for w, s in zip(weights, states)).astype(BF16)
    write_info(out, sum(w * i[0] for w, i in zip(weights, infos)), m, sum(i[2] for i in infos))


def is_later(bit):
    return lax.rem(lax.shift_right_logical(lax.axis_index("seq"), bit), 2) == 1


def round_kernel(bit, first, *refs):
    if first:
        total_ref, got_ref, prefix_out, total_out = refs
    else:
        prefix_ref, total_ref, got_ref, prefix_out, total_out = refs
    rows = total_ref.shape[0] - INFO
    later = is_later(bit)
    n_t, m_t, d_t = read_info(total_ref)
    n_g, m_g, d_g = read_info(got_ref)
    here, got = total_ref[0:rows, :].astype(F32), got_ref[0:rows, :].astype(F32)
    a_t = m_t + jnp.where(later, 0.0, d_g)
    a_g = m_g + jnp.where(later, d_t, 0.0)
    m = jnp.maximum(a_t, a_g)
    w_t, w_g = jnp.exp(a_t - m), jnp.exp(a_g - m)
    total_out[0:rows, :] = (w_t * here + w_g * got).astype(BF16)
    write_info(total_out, w_t * n_t + w_g * n_g, m, d_t + d_g)
    if first:
        n_p, m_p, d_p = jnp.zeros_like(n_g), jnp.full_like(m_g, very_negative), jnp.zeros_like(d_g)
        prefix = jnp.zeros_like(got)
    else:
        n_p, m_p, d_p = read_info(prefix_ref)
        prefix = prefix_ref[0:rows, :].astype(F32)
    a_g = jnp.where(later, m_g + d_p, 2 * very_negative)
    m = jnp.maximum(m_p, a_g)
    w_p = jnp.exp(m_p - m)
    w_g = jnp.where(later, jnp.exp(a_g - m), 0.0)
    prefix_out[0:rows, :] = (w_p * prefix + w_g * got).astype(BF16)
    write_info(prefix_out, w_p * n_p + w_g * n_g, m, d_p + jnp.where(later, d_g, 0.0))


def enter_kernel(bit, prefix_ref, *refs):
    states, outs = refs[:4], refs[4:]
    rows = outs[0].shape[0] - INFO
    _, mine = core_place()
    ranks = [lax.bitwise_xor(mine, off) for off in range(4)]
    infos = [read_info(s) for s in states]
    n_p, m_p, _ = read_info(prefix_ref)
    valid = True if bit is None else is_later(bit)
    for off in (1, 2, 3, 0):
        out = outs[off]
        stabs = shifted_stab(infos, ranks, ranks[off])
        m_in = m_p
        for info, rank in zip(infos, ranks):
            m_in = m_in + jnp.where(rank < ranks[off], info[2], 0.0)
        m_in = jnp.where(valid, m_in, very_negative)
        stabs = [
            jnp.where(rank < ranks[off], s, 2 * very_negative) for s, rank in zip(stabs, ranks)
        ]
        m = functools.reduce(jnp.maximum, stabs, m_in)
        w_in = jnp.where(valid, jnp.exp(m_in - m), 0.0)
        total = w_in * prefix_ref[0:rows, :].astype(F32)
        normal = w_in * n_p
        for i in range(4):
            if i != off:
                w = jnp.where(ranks[i] < ranks[off], jnp.exp(stabs[i] - m), 0.0)
                total = total + w * states[i][0:rows, :].astype(F32)
                normal = normal + w * infos[i][0]
        out[0:rows, :] = total.astype(BF16)
        write_info(out, normal, m, jnp.zeros_like(m))


def intra_kernel(
    per_core, lengths_ref, query_ref, query_other, tail_ref, tail_other, taps_ref,
    key_ref, key_first, values, gate_ref,
    conv_ref, numerator_ref, stats_ref, queries, taps, keys, wide, sems,
):
    core, _ = core_place()
    length, width = queries.shape
    key_width = width // per_core
    value_width = values.shape[1] // per_core
    key_scale = 1.0 / math.sqrt(key_width)
    split = tail_ref.shape[2] > width
    columns = pl.ds(pl.multiple_of(core * width, 128) if split else 0, width)
    copies = start_copies(
        sems,
        [(taps_ref.at[0, :, columns], taps)]
        + by_core(core, query_ref, query_other, columns, queries),
    )
    offset = lax.axis_index("seq") // 2 * length
    tail = pick_tail(core, 0, tail_ref, tail_other, columns)
    keys[...] = key_ref[...]
    keys[0:16, :] = key_first[...]
    gate, cumulative = gate_ref[0], gate_ref[1]
    by_token = cumulative.T
    segment = segment_of(lengths_ref, offset + iota((length, 1), 0))
    segment_row = segment_of(lengths_ref, offset + iota((1, length), 1))
    before = segment_of(lengths_ref, jnp.full((1, 1), offset - 1, jnp.int32))
    step = length // 2
    lane = iota((step, 128), 1)
    for copy in copies:
        copy.wait()
    stats = [[jnp.zeros((step, 128), F32)] * 3 for _ in range(2)]
    for i in range(per_core):
        here = slice(i * key_width, (i + 1) * key_width)
        value_columns = slice(i * value_width, (i + 1) * value_width)
        wide[0:8, :] = tail[:, here]
        wide[8:, :] = queries[:, here].astype(F32)
        for start in range(0, length, 128):
            conv_ref[start : start + 128, here] = conv_rows(
                lengths_ref, offset, start, start + 128, taps, here, wide
            )
        for b in range(2):
            rows, stop = slice(b * step, (b + 1) * step), (b + 1) * step
            allowed = segment_row[:, 0:stop] == segment[rows]
            allowed &= iota((step, stop), 1) <= iota((step, stop), 0) + b * step
            total = by_token[rows, i : i + 1]
            log_weight = jnp.where(
                allowed,
                gate[i : i + 1, 0:stop] - cumulative[i : i + 1, 0:stop] + total,
                very_negative,
            )
            row_max = jnp.max(log_weight, axis=1, keepdims=True)
            scores = dot(conv_ref[rows, here], keys[0:stop, here], ((1,), (1,))) * key_scale
            weights = scores * jnp.exp(log_weight - row_max)
            numerator_ref[rows, value_columns] = dot(
                weights.astype(BF16), values[0:stop, value_columns]
            )
            linked = jnp.where(segment[rows] == before, total, very_negative)
            found = (jnp.sum(weights, axis=1, keepdims=True), row_max, linked)
            stats[b] = [jnp.where(lane == i, new, old) for new, old in zip(found, stats[b])]
    for b in range(2):
        for k in range(3):
            stats_ref[k, b * step : (b + 1) * step, :] = stats[b][k]


def head_kernel(
    per_core, own_ref, got1, got2, got3, query_ref, numerator_ref, stats_ref,
    keep_ref, send_ref, memory, info,
):
    core, mine = core_place()
    key_width = query_ref.shape[1] // per_core
    value_width = numerator_ref.shape[1] // per_core
    key_scale = 1.0 / math.sqrt(key_width)
    rows = query_ref.shape[1] // 4
    step = keep_ref.shape[0]
    for off, ref in enumerate((own_ref, got1, got2, got3)):
        piece = lax.bitwise_xor(mine, off)
        start = pl.multiple_of(piece * rows, rows)
        for j in range(value_width // 128):
            memory[pl.ds(start, rows), j * 128 : (j + 1) * 128] = ref[j * rows : (j + 1) * rows, :]
        info[piece] = ref[ref.shape[0] - INFO :, :]
    row, lane = iota((128, key_width), 0), iota((1, 128), 1)
    stabs = jnp.full((1, 128), very_negative, F32)
    parts = []
    for i in range(per_core):
        normal, stab, _ = read_info(info.at[i * key_width // rows], key_width)
        stabs = jnp.where(lane == i, stab, stabs)
        block = jnp.zeros((128, key_width), F32)
        for k, part in enumerate(split3(normal)):
            block = jnp.where(row == 8 * k + i, part, block)
        parts.append(block.astype(BF16))
    for b in range(2):
        span = slice(b * step, (b + 1) * step)
        queries = [
            query_ref[span, i * key_width : (i + 1) * key_width] for i in range(per_core)
        ]
        from_normal = sum(dot(q, p, ((1,), (1,))) for q, p in zip(queries, parts))
        from_normal = (
            from_normal
            + pltpu.roll(from_normal, 128 - 8, 1)
            + pltpu.roll(from_normal, 128 - 16, 1)
        )
        row_max = stats_ref[1, span, :]
        carried = stabs + stats_ref[2, span, :]
        m = jnp.maximum(row_max, carried)
        w_here = jnp.exp(row_max - m)
        w_in = jnp.exp(carried - m) * key_scale
        denominator = w_here * stats_ref[0, span, :] + w_in * from_normal
        scale = 1.0 / jnp.maximum(jnp.abs(denominator), 1.0)
        w_here, w_in = w_here * scale, w_in * scale
        for i in range(per_core):
            columns = slice(i * value_width, (i + 1) * value_width)
            from_memory = dot(queries[i], memory[i * key_width : (i + 1) * key_width, :])
            head_out = (
                w_here[:, i : i + 1] * numerator_ref[span, columns]
                + w_in[:, i : i + 1] * from_memory
            ).astype(BF16)

            def write(ref, columns=columns, head_out=head_out):
                ref[:, columns] = head_out

            pl.when(core == b)(functools.partial(write, keep_ref))
            pl.when(core != b)(functools.partial(write, send_ref))


def weight_part(weight_ref, half, rows, start, width):
    return weight_ref[
        pl.ds(pl.multiple_of(half * rows, 128), rows), pl.ds(pl.multiple_of(start, 128), width)
    ]


def keep_kernel(off, head_ref, weight_ref, part_ref):
    core, _ = core_place()
    rows, width = head_ref.shape[1], part_ref.shape[1]
    start = lax.bitwise_xor(lax.axis_index("head"), off) * width
    part_ref[...] = dot(head_ref[...], weight_part(weight_ref, core, rows, start, width))


def send_kernel(off, chunk, head_ref, weight_ref, kept_ref, part_ref):
    core, _ = core_place()
    rows, piece, width = head_ref.shape[1], part_ref.shape[1], kept_ref.shape[1]
    start = lax.bitwise_xor(lax.axis_index("head"), off) * width + chunk * piece
    part_ref[...] = (
        dot(head_ref[...], weight_part(weight_ref, 1 - core, rows, start, piece))
        + kept_ref[:, chunk * piece : (chunk + 1) * piece]
    ).astype(part_ref.dtype)


def own_kernel(keep_ref, got_ref, weight_ref, part_ref):
    core, _ = core_place()
    rows, width = keep_ref.shape[1], part_ref.shape[1]
    start = lax.axis_index("head") * width
    part_ref[...] = dot(
        keep_ref[...], weight_part(weight_ref, core, rows, start, width)
    ) + dot(got_ref[...], weight_part(weight_ref, 1 - core, rows, start, width))


def sum_kernel(chunks, own_ref, *refs):
    *arrived, out_ref = refs
    width = out_ref.shape[1] // chunks
    for c in range(chunks):
        columns = slice(c * width, (c + 1) * width)
        total = own_ref[:, columns]
        for ref in arrived[c::chunks]:
            total = total + ref[...].astype(F32)
        out_ref[:, columns] = total.astype(out_ref.dtype)


def call(kernel, out_shape, spaces, scratch, name, flops=0, nbytes=0, limit=24):
    place = {"v": pltpu.VMEM, "s": pltpu.SMEM, "a": pl.ANY, "h": pl.ANY}
    outs = jax.tree.map(lambda _: pl.BlockSpec(memory_space=pltpu.VMEM), out_shape)
    inner = pl.pallas_call(
        kernel,
        out_shape=out_shape,
        in_specs=[pl.BlockSpec(memory_space=place[s]) for s in spaces],
        out_specs=outs,
        scratch_shapes=scratch,
        compiler_params=pltpu.CompilerParams(vmem_limit_bytes=limit << 20),
        cost_estimate=pl.CostEstimate(flops=flops, bytes_accessed=nbytes, transcendentals=0),
        name=name,
    )

    def run(*args):
        return inner(
            *(
                pltpu.with_memory_space_constraint(x, pltpu.HBM) if s in "hs" else x
                for s, x in zip(spaces, args, strict=True)
            )
        )

    return run


def on_device(
    query_input, key_input, value_input, kernel_taps, input_gate, forget_gate, request_lengths,
    output_weight,
):
    seq_count, head_count = lax.axis_size("seq"), lax.axis_size("head")
    length, key_cols = query_input.shape
    heads = input_gate.shape[0]
    value_cols = value_input.shape[1]
    out_cols = output_weight.shape[1] // head_count
    chip_length = 2 * length
    key_width = key_cols // heads
    per_core = max(1, heads // 2)
    part_keys, part_values = per_core * key_width, value_cols // 2
    value_width = part_values // per_core
    lags = kernel_taps.shape[1]
    rows = part_keys // 4

    def shape(dims, dtype=F32):
        return jax.ShapeDtypeStruct(dims, dtype)

    def swap(x, off):
        return lax.ppermute(x, "seq", [(i, i ^ off) for i in range(seq_count)])

    key_other, value_other = swap(key_input, 1), swap(value_input, 1)
    tails, gates = call(
        tail_kernel, (shape((2, TAIL, key_cols), BF16), shape((2, heads, length))), "hhhh",
        [pltpu.SemaphoreType.DMA((4,))], "tails",
    )(query_input, key_input, input_gate, forget_gate)
    gates_other = swap(gates, 1)
    tails = lax.ppermute(tails, "seq", [(i, i + 1) for i in range(seq_count - 1)])
    tails_other = swap(tails, 1)
    query_other = swap(lax.optimization_barrier((query_input, tails))[0], 1)

    one = shape((rows * value_width // 128 + INFO, 128), BF16)
    key_conv, values, gate_sums, taps, key_first, factor, memory, normal, stab, through = call(
        functools.partial(local_kernel, per_core),
        (
            shape((chip_length, part_keys), BF16),
            shape((chip_length, part_values), BF16),
            shape((2, 8, chip_length)),
            shape((lags, part_keys)),
            shape((16, part_keys), BF16),
            shape((16, 8)),
            shape((part_keys, value_width)),
            shape((8, key_width)),
            shape((8, 128)),
            shape((8, 128)),
        ),
        "shahavvh",
        [pltpu.VMEM((chip_length, part_keys), BF16)]
        + [
            pltpu.VMEM((2, max(8, heads), chip_length), F32),
            pltpu.VMEM((2, 8, chip_length), F32),
            pltpu.VMEM((chip_length + 8, key_width), F32),
            pltpu.SemaphoreType.DMA((5,)),
        ],
        "local_state",
        flops=1 << 30,
    )(
        request_lengths, key_input, key_other, value_input, value_other, gates, gates_other,
        kernel_taps,
    )
    conv_first, *pieces = call(
        functools.partial(first_kernel, per_core, chip_length),
        (shape((16, part_keys), BF16),) + (one,) * 4,
        "s" + "v" * 10,
        [
            pltpu.VMEM((part_keys, value_width), BF16),
            pltpu.VMEM((8, key_width), F32),
            pltpu.VMEM((24, key_width), F32),
        ],
        "first_tokens",
    )(
        request_lengths, tails, tails_other, taps, key_first, values, factor, memory, normal, stab,
        through,
    )
    states = [pieces[0]] + [swap(pieces[off], 2 * off) for off in (1, 2, 3)]
    inside = call(
        functools.partial(intra_kernel, per_core),
        (
            shape((chip_length, part_keys), BF16),
            shape((chip_length, part_values)),
            shape((3, chip_length, 128)),
        ),
        "shavvhvvvv",
        [
            pltpu.VMEM((chip_length, part_keys), BF16),
            pltpu.VMEM((lags, part_keys), F32),
            pltpu.VMEM((chip_length, part_keys), BF16),
            pltpu.VMEM((chip_length + 8, key_width), F32),
            pltpu.SemaphoreType.DMA((3,)),
        ],
        "intra",
        flops=4 << 30,
    )(
        request_lengths, query_input, query_other, tails, tails_other, kernel_taps, key_conv,
        conv_first, values, gate_sums,
    )
    states, inside = lax.optimization_barrier((states, inside))
    total = call(total_kernel, one, "vvvv", [], "group_total")(*states)
    bits = seq_count.bit_length() - 1
    flag = 3
    prefix = swap(total, 8)
    if bits > 4:
        flag = None
        prefix, total = call(
            functools.partial(round_kernel, 3, True), (one, one), "vv", [], "round_state"
        )(total, prefix)
        for bit in range(4, bits):
            prefix, total = call(
                functools.partial(round_kernel, bit, False), (one, one), "vvv", [], "round_state"
            )(prefix, total, swap(total, 1 << bit))
    enter = call(functools.partial(enter_kernel, flag), (one,) * 4, "vvvvv", [], "enter_state")(
        prefix, *states
    )
    enter = [enter[0]] + [swap(enter[off], 2 * off) for off in (1, 2, 3)]
    half = shape((length, part_values), BF16)
    keep, send = call(
        functools.partial(head_kernel, per_core), (half, half), "v" * 7,
        [
            pltpu.VMEM((part_keys, value_width), BF16),
            pltpu.VMEM((4, INFO, 128), BF16),
        ],
        "head_out",
    )(*enter, *inside)
    got = swap(send, 1)

    chunks = 2 if head_count == 2 and out_cols % 256 == 0 else 1
    piece = out_cols // chunks
    arrived = []
    for off in range(1, head_count):
        kept = call(
            functools.partial(keep_kernel, off), shape((length, out_cols)), "vv", [],
            "project_kept", flops=2 << 30,
        )(keep, output_weight)
        columns = [
            call(
                functools.partial(send_kernel, off, chunk), shape((length, piece), BF16), "vvv",
                [], "project_other",
            )(got, output_weight, kept)
            for chunk in range(chunks)
        ]
        arrived.append(
            [lax.ppermute(c, "head", [(i, i ^ off) for i in range(head_count)]) for c in columns]
        )
    mixed = call(
        own_kernel, shape((length, out_cols)), "vvv", [], "project_own", flops=4 << 30
    )(keep, got, output_weight)
    return call(
        functools.partial(sum_kernel, chunks), shape((length, out_cols), BF16),
        "v" * (1 + chunks * len(arrived)), [], "mixed_out",
    )(mixed, *(c for columns in arrived for c in columns))


def solution(mesh):
    placed = (
        P("seq", "head"),
        P("seq", "head"),
        P("seq", "head"),
        P(None, None, "head"),
        P("head", "seq"),
        P("head", "seq"),
        P(),
        P("head", None),
    )
    return jax.shard_map(
        on_device, mesh=mesh, in_specs=placed, out_specs=P("seq", "head"), check_vma=False
    )
```

time: 78.6 us -> 64.3 us (0.82)
  local copies, waits for them, and re-layouts: 11 us -> 0.01 us
  waiting for transfers between devices: 31.8 us -> 25.6 us
  Pallas kernels: 14.8 us -> 18.3 us
  other arithmetic: 0.94 us -> 0.01 us
    unnamed x26 -> x4, local copies, waits for them, and re-layouts: 10.1 us -> 0.01 us
    ppermute x9 -> x13, waiting for transfers between devices: 20.7 us -> 14.5 us  [swap(): return lax.ppermute(x, 'seq', [(i, i ^ off) for i in range(seq_count)])]
    pallas_call x9 -> x12, Pallas kernels: 14.8 us -> 18.3 us  [run(): inner(*(pltpu.with_memory_space_constraint(x, pltpu.HBM) if s in 'hs' els...]
    convert_element_type x1 -> x0, other arithmetic: 0.93 us -> none  [on_device(): return mixed.astype(BF16)]
    another operation x1 -> x0, local copies, waits for them, and re-layouts: 0.93 us -> none  [on_device(): tails = jnp.stack([query_input[length - TAIL:], key_input[length - TAIL:]])]
    ppermute x9 -> x13, starting transfers between devices: 14.6 us -> 15.4 us  [swap(): return lax.ppermute(x, 'seq', [(i, i ^ off) for i in range(seq_count)])]
  transfers between devices with their start and end apart: 12 -> 16, of which waited for: 11 -> 10; matrix products, arithmetic and copies ran while one was open for 0% -> 0% of each run, Pallas kernels for 7% -> 23%
where the time goes in v2:
time: 64.3 us; the launch traced here: 63.9 us
  waiting for transfers between devices  25.6 us (40%)
  starting transfers between devices  19.9 us (31%)
  Pallas kernels  18.3 us (28%)
    pallas_call x12, Pallas kernels, run(): inner(*(pltpu.with_memory_space_constraint(x, pltpu.HBM) if s in 'hs' els...  18.3 us
    ppermute x13, starting transfers between devices, swap(): return lax.ppermute(x, 'seq', [(i, i ^ off) for i in range(seq_count)])  15.4 us
    ppermute x13, waiting for transfers between devices, swap(): return lax.ppermute(x, 'seq', [(i, i ^ off) for i in range(seq_count)])  14.5 us
    ppermute x2, waiting for transfers between devices, on_device(): lax.ppermute(c, 'head', [(i, i ^ off) for i in range(head_count)])  10.2 us
    ppermute x1, starting transfers between devices, on_device(): lax.ppermute(tails, 'seq', [(i, i + 1) for i in range(seq_count - 1)])  2.36 us
    ppermute x2, starting transfers between devices, on_device(): lax.ppermute(c, 'head', [(i, i ^ off) for i in range(head_count)])  2.16 us
  transfers between devices with their start and end apart: 16, of which 10 were waited for; matrix products, arithmetic and copies ran while one was open for 0% of the time, Pallas kernels for 23%

profile of v2, /device:TPU:0, one launch (start us, length us, event | category | flops | bytes accessed | tf_op | source)
XLA Modules:
  0.0 63.9 jit_solution(9397192360015329105)
XLA Ops:
  0.5 0.8 %tails.1 = (bf16[2,16,1024]{2,1,0:T(8,128)(2,1)S(1)}, f32[2,4,256]{2,1,0:T(4,128)S(1)}) custom-call(bf16[256,1024]{1,0:T(8,128)(2,1)} %query_ref.3, bf16[256,1024]{1,0:T(8,128)(2,1)} %key_ref.3, f32[4,256]{1,0:T(4,128)} %input_ref.1, f32[4,256]{1,0:T(4,128)} %forget_ref.1), custom_call_target="tpu_custom_call" | custom-call | tf_op jit(solution)/shard_map/tails/pallas_call | solution.py:522
  1.3 2.4 %collective-permute-start = (bf16[2,16,1024]{2,1,0:T(8,128)(2,1)S(1)}, bf16[2,16,1024]{2,1,0:T(8,128)(2,1)S(1)}, u32[]{:S(2)}, u32[]{:S(2)}) collective-permute-start(bf16[2,16,1024]{2,1,0:T(8,128)(2,1)S(1)} %get-tuple-element.39), channel_id=1, source_target_pairs={{0,2},{2,4},{4,6},{6,8},{8,10},{10,12},{12,14},{14,16},{16,18},{18... | collective-permute-start | bytes 196616 | tf_op jit(solution)/shard_map/ppermute | solution.py:561
  3.7 0.9 %collective-permute-done.tail_ref = bf16[2,16,1024]{2,1,0:T(8,128)(2,1)S(1)} collective-permute-done((bf16[2,16,1024]{2,1,0:T(8,128)(2,1)S(1)}, bf16[2,16,1024]{2,1,0:T(8,128)(2,1)S(1)}, u32[]{:S(2)}, u32[]{:S(2)}) %collective-permute-start) | collective-permute-done | bytes 65568 | tf_op jit(solution)/shard_map/ppermute | solution.py:561
  4.6 3.1 %collective-permute-start.8 = (bf16[256,1024]{1,0:T(8,128)(2,1)}, bf16[256,1024]{1,0:T(8,128)(2,1)S(1)}, u32[]{:S(2)}, u32[]{:S(2)}) collective-permute-start(bf16[256,1024]{1,0:T(8,128)(2,1)} %query_ref.3), channel_id=1, source_target_pairs={{0,2},{2,0},{4,6},{6,4},{8,10},{10,8},{12,14},{14,12},{16,18},{18,... | collective-permute-start | bytes 1572872 | tf_op jit(solution)/shard_map/ppermute | solution.py:553
  8.2 0.9 %collective-permute-done.4.gates_other = f32[2,4,256]{2,1,0:T(4,128)S(1)} collective-permute-done((f32[2,4,256]{2,1,0:T(4,128)S(1)}, f32[2,4,256]{2,1,0:T(4,128)S(1)}, u32[]{:S(2)}, u32[]{:S(2)}) %collective-permute-start.4) | collective-permute-done | bytes 8224 | tf_op jit(solution)/shard_map/ppermute | solution.py:553
  9.1 4.7 %local_state.1 = (bf16[512,512]{1,0:T(8,128)(2,1)S(1)}, bf16[512,1024]{1,0:T(8,128)(2,1)S(1)}, f32[2,8,512]{2,1,0:T(8,128)S(1)}, f32[4,512]{1,0:T(4,128)S(1)}, b...) custom-call(s32[4]{0:T(128)} %lengths_ref.5, ...), custom_call_target="tpu_custom_call" | custom-call | flops 1073741824 | tf_op jit(solution)/shard_map/local_state/pallas_call | solution.py:522
  13.7 1.3 %first_tokens.1 = (bf16[16,512]{1,0:T(8,128)(2,1)S(1)}, bf16[528,128]{1,0:T(8,128)(2,1)S(1)}, bf16[528,128]{1,0:T(8,128)(2,1)S(1)}, bf16[528,128]{1,0:T(8,128)(2,1)S(1)}, bf16[528,128]{1,0:T(8,128)(2,1)S(1)}) custom-call(s32[4]{0:T(128)} %lengths_ref.5, bf16[2,16,1024]{2,1,0:T(8,128)(2,1)S(1)} %collective-permute-done.tail_ref, ...), custom_call_target="tpu_custom_call" | custom-call | tf_op jit(solution)/shard_map/first_tokens/pallas_call | solution.py:522
  15.1 2.5 %collective-permute-start.5 = (bf16[528,128]{1,0:T(8,128)(2,1)S(1)}, bf16[528,128]{1,0:T(8,128)(2,1)S(1)}, u32[]{:S(2)}, u32[]{:S(2)}) collective-permute-start(bf16[528,128]{1,0:T(8,128)(2,1)S(1)} %get-tuple-element.50), channel_id=1, source_target_pairs={{0,4},{2,6},{4,0},{6,2},{8,12},{10,14},{12,8},{14,10},{16,20},{18,... | collective-permute-start | bytes 405512 | tf_op jit(solution)/shard_map/ppermute | solution.py:553
  17.5 1.6 %collective-permute-start.6 = (bf16[528,128]{1,0:T(8,128)(2,1)S(1)}, bf16[528,128]{1,0:T(8,128)(2,1)S(1)}, u32[]{:S(2)}, u32[]{:S(2)}) collective-permute-start(bf16[528,128]{1,0:T(8,128)(2,1)S(1)} %get-tuple-element.51), channel_id=1, source_target_pairs={{0,8},{2,10},{4,12},{6,14},{8,0},{10,2},{12,4},{14,6},{16,24},{18,... | collective-permute-start | bytes 405512 | tf_op jit(solution)/shard_map/ppermute | solution.py:553
  19.1 0.8 %collective-permute-start.7 = (bf16[528,128]{1,0:T(8,128)(2,1)S(1)}, bf16[528,128]{1,0:T(8,128)(2,1)S(1)}, u32[]{:S(2)}, u32[]{:S(2)}) collective-permute-start(bf16[528,128]{1,0:T(8,128)(2,1)S(1)} %get-tuple-element.52), channel_id=1, source_target_pairs={{0,12},{2,14},{4,8},{6,10},{8,4},{10,6},{12,0},{14,2},{16,28},{18,... | collective-permute-start | bytes 405512 | tf_op jit(solution)/shard_map/ppermute | solution.py:553
  19.9 5.5 %intra.1 = (bf16[512,512]{1,0:T(8,128)(2,1)S(1)}, f32[512,1024]{1,0:T(8,128)S(1)}, f32[3,512,128]{2,1,0:T(8,128)S(1)}) custom-call(s32[4]{0:T(128)} %lengths_ref.5, bf16[256,1024]{1,0:T(8,128)(2,1)} %query_ref.3, bf16[256,1024]{1,0:T(8,128)(2,1)S(1)} %collective-permute-done.8.query_other, bf16[2,16,1024]{2,1,0:T(8,128)(2,1)S(1)} %collective-permute-done.tail_ref, ...), custom_call_target="tpu_custom_call" | custom-call | flops 4294967296 | tf_op jit(solution)/shard_map/intra/pallas_call | solution.py:522
  25.4 1.2 %collective-permute-done.7.refs_3_ = bf16[528,128]{1,0:T(8,128)(2,1)S(1)} collective-permute-done((bf16[528,128]{1,0:T(8,128)(2,1)S(1)}, bf16[528,128]{1,0:T(8,128)(2,1)S(1)}, u32[]{:S(2)}, u32[]{:S(2)}) %collective-permute-start.7) | collective-permute-done | bytes 135200 | tf_op jit(solution)/shard_map/ppermute | solution.py:553
  26.9 2.8 %collective-permute-start.9 = (bf16[528,128]{1,0:T(8,128)(2,1)S(1)}, bf16[528,128]{1,0:T(8,128)(2,1)S(1)}, u32[]{:S(2)}, u32[]{:S(2)}) collective-permute-start(bf16[528,128]{1,0:T(8,128)(2,1)S(1)} %group_total.1), channel_id=1, source_target_pairs={{0,16},{2,18},{4,20},{6,22},{8,24},{10,26},{12,28},{14,30},{16,0},... | collective-permute-start | bytes 405512 | tf_op jit(solution)/shard_map/ppermute | solution.py:553
  29.7 6.1 %collective-permute-done.9.prefix_ref = bf16[528,128]{1,0:T(8,128)(2,1)S(1)} collective-permute-done((bf16[528,128]{1,0:T(8,128)(2,1)S(1)}, bf16[528,128]{1,0:T(8,128)(2,1)S(1)}, u32[]{:S(2)}, u32[]{:S(2)}) %collective-permute-start.9) | collective-permute-done | bytes 135200 | tf_op jit(solution)/shard_map/ppermute | solution.py:553
  37.8 2.2 %collective-permute-start.12 = (bf16[528,128]{1,0:T(8,128)(2,1)S(1)}, bf16[528,128]{1,0:T(8,128)(2,1)S(1)}, u32[]{:S(2)}, u32[]{:S(2)}) collective-permute-start(bf16[528,128]{1,0:T(8,128)(2,1)S(1)} %get-tuple-element.67), channel_id=1, source_target_pairs={{0,12},{2,14},{4,8},{6,10},{8,4},{10,6},{12,0},{14,2},{16,28},{18,... | collective-permute-start | bytes 405512 | tf_op jit(solution)/shard_map/ppermute | solution.py:553
  40.0 3.0 %collective-permute-done.10.got1 = bf16[528,128]{1,0:T(8,128)(2,1)S(1)} collective-permute-done((bf16[528,128]{1,0:T(8,128)(2,1)S(1)}, bf16[528,128]{1,0:T(8,128)(2,1)S(1)}, u32[]{:S(2)}, u32[]{:S(2)}) %collective-permute-start.10) | collective-permute-done | bytes 135200 | tf_op jit(solution)/shard_map/ppermute | solution.py:553
  43.2 1.9 %collective-permute-done.12.got3 = bf16[528,128]{1,0:T(8,128)(2,1)S(1)} collective-permute-done((bf16[528,128]{1,0:T(8,128)(2,1)S(1)}, bf16[528,128]{1,0:T(8,128)(2,1)S(1)}, u32[]{:S(2)}, u32[]{:S(2)}) %collective-permute-start.12) | collective-permute-done | bytes 135200 | tf_op jit(solution)/shard_map/ppermute | solution.py:553
  45.2 1.5 %head_out.1 = (bf16[256,1024]{1,0:T(8,128)(2,1)S(1)}, bf16[256,1024]{1,0:T(8,128)(2,1)S(1)}) custom-call(bf16[528,128]{1,0:T(8,128)(2,1)S(1)} %get-tuple-element.64.own_ref, bf16[528,128]{1,0:T(8,128)(2,1)S(1)} %collective-permute-done.10.got1, bf16[528,128]{1,0:T(8,128)(2,1)S(1)} %collective-permute-done.11.got2, ...), custom_call_target="tpu_custom_call" | custom-call | tf_op jit(solution)/shard_map/head_out/pallas_call | solution.py:522
  47.4 1.1 %collective-permute-done.13.got_ref.head_ref = bf16[256,1024]{1,0:T(8,128)(2,1)S(1)} collective-permute-done((bf16[256,1024]{1,0:T(8,128)(2,1)S(1)}, bf16[256,1024]{1,0:T(8,128)(2,1)S(1)}, u32[]{:S(2)}, u32[]{:S(2)}) %collective-permute-start.13) | collective-permute-done | bytes 524320 | tf_op jit(solution)/shard_map/ppermute | solution.py:553
  49.0 1.6 %collective-permute-start.14 = (bf16[256,512]{1,0:T(8,128)(2,1)S(1)}, bf16[256,512]{1,0:T(8,128)(2,1)S(1)}, u32[]{:S(2)}, u32[]{:S(2)}) collective-permute-start(bf16[256,512]{1,0:T(8,128)(2,1)S(1)} %project_other.2), channel_id=1, source_target_pairs={{0,1},{1,0},{2,3},{3,2},{4,5},{5,4},{6,7},{7,6},{8,9},{9,8},{10,11... | collective-permute-start | bytes 786440 | tf_op jit(solution)/shard_map/ppermute | solution.py:675
  51.6 1.2 %project_own.1.own_ref = f32[256,1024]{1,0:T(8,128)S(1)} custom-call(bf16[256,1024]{1,0:T(8,128)(2,1)S(1)} %get-tuple-element.71.keep_ref.head_ref, bf16[256,1024]{1,0:T(8,128)(2,1)S(1)} %collective-permute-done.13.got_ref.head_ref, bf16[2048,2048]{1,0:T(8,128)(2,1)S(1)} %bitcast.1), custom_call_target="tpu_custom_call" | custom-call | flops 4294967296 | tf_op jit(solution)/shard_map/project_own/pallas_call | solution.py:522
  52.9 5.4 %collective-permute-done.14.refs_0_ = bf16[256,512]{1,0:T(8,128)(2,1)S(1)} collective-permute-done((bf16[256,512]{1,0:T(8,128)(2,1)S(1)}, bf16[256,512]{1,0:T(8,128)(2,1)S(1)}, u32[]{:S(2)}, u32[]{:S(2)}) %collective-permute-start.14) | collective-permute-done | bytes 262176 | tf_op jit(solution)/shard_map/ppermute | solution.py:675
  58.2 4.8 %collective-permute-done.15.refs_1_ = bf16[256,512]{1,0:T(8,128)(2,1)S(1)} collective-permute-done((bf16[256,512]{1,0:T(8,128)(2,1)S(1)}, bf16[256,512]{1,0:T(8,128)(2,1)S(1)}, u32[]{:S(2)}, u32[]{:S(2)}) %collective-permute-start.15) | collective-permute-done | bytes 262176 | tf_op jit(solution)/shard_map/ppermute | solution.py:675
  63.1 0.9 %mixed_out.1 = bf16[256,1024]{1,0:T(8,128)(2,1)} custom-call(f32[256,1024]{1,0:T(8,128)S(1)} %project_own.1.own_ref, bf16[256,512]{1,0:T(8,128)(2,1)S(1)} %collective-permute-done.14.refs_0_, bf16[256,512]{1,0:T(8,128)(2,1)S(1)} %collective-permute-done.15.refs_1_), custom_call_target="tpu_custom_call" | custom-call | tf_op jit(solution)/shard_map/mixed_out/pallas_call | solution.py:522
  (25 shorter events, 5.8 us)
Async XLA Ops:
  0.0 9.1 %collective-permute-start.3 = (bf16[256,2048]{1,0:T(8,128)(2,1)}, bf16[256,2048]{1,0:T(8,128)(2,1)S(1)}, u32[]{:S(2)}, u32[]{:S(2)}) collective-permute-start(bf16[256,2048]{1,0:T(8,128)(2,1)} %value_ref.1), channel_id=1, source_target_pairs={{0,2},{2,0},{4,6},{6,4},{8,10},{10,8},{12,14},{14,12},{16,18},{18,... | collective-permute-start | bytes 3145736 | tf_op jit(solution)/shard_map/ppermute | solution.py:553
  0.5 8.6 %collective-permute-start.2 = (bf16[256,1024]{1,0:T(8,128)(2,1)}, bf16[256,1024]{1,0:T(8,128)(2,1)S(1)}, u32[]{:S(2)}, u32[]{:S(2)}) collective-permute-start(bf16[256,1024]{1,0:T(8,128)(2,1)} %key_ref.3), channel_id=1, source_target_pairs={{0,2},{2,0},{4,6},{6,4},{8,10},{10,8},{12,14},{14,12},{16,18},{18,... | collective-permute-start | bytes 1572872 | tf_op jit(solution)/shard_map/ppermute | solution.py:553
  1.3 3.2 %collective-permute-start = (bf16[2,16,1024]{2,1,0:T(8,128)(2,1)S(1)}, bf16[2,16,1024]{2,1,0:T(8,128)(2,1)S(1)}, u32[]{:S(2)}, u32[]{:S(2)}) collective-permute-start(bf16[2,16,1024]{2,1,0:T(8,128)(2,1)S(1)} %get-tuple-element.39), channel_id=1, source_target_pairs={{0,2},{2,4},{4,6},{6,8},{8,10},{10,12},{12,14},{14,16},{16,18},{18... | collective-permute-start | bytes 196616 | tf_op jit(solution)/shard_map/ppermute | solution.py:561
  4.6 15.4 %collective-permute-start.8 = (bf16[256,1024]{1,0:T(8,128)(2,1)}, bf16[256,1024]{1,0:T(8,128)(2,1)S(1)}, u32[]{:S(2)}, u32[]{:S(2)}) collective-permute-start(bf16[256,1024]{1,0:T(8,128)(2,1)} %query_ref.3), channel_id=1, source_target_pairs={{0,2},{2,0},{4,6},{6,4},{8,10},{10,8},{12,14},{14,12},{16,18},{18,... | collective-permute-start | bytes 1572872 | tf_op jit(solution)/shard_map/ppermute | solution.py:553
  7.6 1.4 %collective-permute-start.4 = (f32[2,4,256]{2,1,0:T(4,128)S(1)}, f32[2,4,256]{2,1,0:T(4,128)S(1)}, u32[]{:S(2)}, u32[]{:S(2)}) collective-permute-start(f32[2,4,256]{2,1,0:T(4,128)S(1)} %get-tuple-element.40.gates_ref), channel_id=1, source_target_pairs={{0,2},{2,0},{4,6},{6,4},{8,10},{10,8},{12,14},{14,12},{16,18},{18,... | collective-permute-start | bytes 24584 | tf_op jit(solution)/shard_map/ppermute | solution.py:553
  7.6 6.1 %collective-permute-start.1 = (bf16[2,16,1024]{2,1,0:T(8,128)(2,1)S(1)}, bf16[2,16,1024]{2,1,0:T(8,128)(2,1)S(1)}, u32[]{:S(2)}, u32[]{:S(2)}) collective-permute-start(bf16[2,16,1024]{2,1,0:T(8,128)(2,1)S(1)} %collective-permute-done.tail_ref), channel_id=1, source_target_pairs={{0,2},{2,0},{4,6},{6,4},{8,10},{10,8},{12,14},{14,12},{16,18},{18,... | collective-permute-start | bytes 196616 | tf_op jit(solution)/shard_map/ppermute | solution.py:553
  13.7 33.0 %slice-start = ((s8[8388608]{0:T(1024)(128)(4,1)}), s8[4194304]{0:T(1024)(128)(4,1)S(1)}, s32[]{:S(2)}) async-start(s8[8388608]{0:T(1024)(128)(4,1)} %bitcast), calls=%async_computation | async-start | bytes 8388608
  15.1 10.4 %collective-permute-start.5 = (bf16[528,128]{1,0:T(8,128)(2,1)S(1)}, bf16[528,128]{1,0:T(8,128)(2,1)S(1)}, u32[]{:S(2)}, u32[]{:S(2)}) collective-permute-start(bf16[528,128]{1,0:T(8,128)(2,1)S(1)} %get-tuple-element.50), channel_id=1, source_target_pairs={{0,4},{2,6},{4,0},{6,2},{8,12},{10,14},{12,8},{14,10},{16,20},{18,... | collective-permute-start | bytes 405512 | tf_op jit(solution)/shard_map/ppermute | solution.py:553
  17.5 7.9 %collective-permute-start.6 = (bf16[528,128]{1,0:T(8,128)(2,1)S(1)}, bf16[528,128]{1,0:T(8,128)(2,1)S(1)}, u32[]{:S(2)}, u32[]{:S(2)}) collective-permute-start(bf16[528,128]{1,0:T(8,128)(2,1)S(1)} %get-tuple-element.51), channel_id=1, source_target_pairs={{0,8},{2,10},{4,12},{6,14},{8,0},{10,2},{12,4},{14,6},{16,24},{18,... | collective-permute-start | bytes 405512 | tf_op jit(solution)/shard_map/ppermute | solution.py:553
  19.1 7.5 %collective-permute-start.7 = (bf16[528,128]{1,0:T(8,128)(2,1)S(1)}, bf16[528,128]{1,0:T(8,128)(2,1)S(1)}, u32[]{:S(2)}, u32[]{:S(2)}) collective-permute-start(bf16[528,128]{1,0:T(8,128)(2,1)S(1)} %get-tuple-element.52), channel_id=1, source_target_pairs={{0,12},{2,14},{4,8},{6,10},{8,4},{10,6},{12,0},{14,2},{16,28},{18,... | collective-permute-start | bytes 405512 | tf_op jit(solution)/shard_map/ppermute | solution.py:553
  19.9 26.8 %slice-start.1 = ((s8[8388608]{0:T(1024)(128)(4,1)}), s8[4194304]{0:T(1024)(128)(4,1)S(1)}, s32[]{:S(2)}) async-start(s8[8388608]{0:T(1024)(128)(4,1)} %bitcast), calls=%async_computation.1 | async-start | bytes 8388608
  26.9 8.9 %collective-permute-start.9 = (bf16[528,128]{1,0:T(8,128)(2,1)S(1)}, bf16[528,128]{1,0:T(8,128)(2,1)S(1)}, u32[]{:S(2)}, u32[]{:S(2)}) collective-permute-start(bf16[528,128]{1,0:T(8,128)(2,1)S(1)} %group_total.1), channel_id=1, source_target_pairs={{0,16},{2,18},{4,20},{6,22},{8,24},{10,26},{12,28},{14,30},{16,0},... | collective-permute-start | bytes 405512 | tf_op jit(solution)/shard_map/ppermute | solution.py:553
  36.4 6.5 %collective-permute-start.10 = (bf16[528,128]{1,0:T(8,128)(2,1)S(1)}, bf16[528,128]{1,0:T(8,128)(2,1)S(1)}, u32[]{:S(2)}, u32[]{:S(2)}) collective-permute-start(bf16[528,128]{1,0:T(8,128)(2,1)S(1)} %get-tuple-element.65), channel_id=1, source_target_pairs={{0,4},{2,6},{4,0},{6,2},{8,12},{10,14},{12,8},{14,10},{16,20},{18,... | collective-permute-start | bytes 405512 | tf_op jit(solution)/shard_map/ppermute | solution.py:553
  37.1 6.1 %collective-permute-start.11 = (bf16[528,128]{1,0:T(8,128)(2,1)S(1)}, bf16[528,128]{1,0:T(8,128)(2,1)S(1)}, u32[]{:S(2)}, u32[]{:S(2)}) collective-permute-start(bf16[528,128]{1,0:T(8,128)(2,1)S(1)} %get-tuple-element.66), channel_id=1, source_target_pairs={{0,8},{2,10},{4,12},{6,14},{8,0},{10,2},{12,4},{14,6},{16,24},{18,... | collective-permute-start | bytes 405512 | tf_op jit(solution)/shard_map/ppermute | solution.py:553
  37.8 7.4 %collective-permute-start.12 = (bf16[528,128]{1,0:T(8,128)(2,1)S(1)}, bf16[528,128]{1,0:T(8,128)(2,1)S(1)}, u32[]{:S(2)}, u32[]{:S(2)}) collective-permute-start(bf16[528,128]{1,0:T(8,128)(2,1)S(1)} %get-tuple-element.67), channel_id=1, source_target_pairs={{0,12},{2,14},{4,8},{6,10},{8,4},{10,6},{12,0},{14,2},{16,28},{18,... | collective-permute-start | bytes 405512 | tf_op jit(solution)/shard_map/ppermute | solution.py:553
  46.6 2.0 %collective-permute-start.13 = (bf16[256,1024]{1,0:T(8,128)(2,1)S(1)}, bf16[256,1024]{1,0:T(8,128)(2,1)S(1)}, u32[]{:S(2)}, u32[]{:S(2)}) collective-permute-start(bf16[256,1024]{1,0:T(8,128)(2,1)S(1)} %get-tuple-element.72), channel_id=1, source_target_pairs={{0,2},{2,0},{4,6},{6,4},{8,10},{10,8},{12,14},{14,12},{16,18},{18,... | collective-permute-start | bytes 1572872 | tf_op jit(solution)/shard_map/ppermute | solution.py:553
  49.0 9.2 %collective-permute-start.14 = (bf16[256,512]{1,0:T(8,128)(2,1)S(1)}, bf16[256,512]{1,0:T(8,128)(2,1)S(1)}, u32[]{:S(2)}, u32[]{:S(2)}) collective-permute-start(bf16[256,512]{1,0:T(8,128)(2,1)S(1)} %project_other.2), channel_id=1, source_target_pairs={{0,1},{1,0},{2,3},{3,2},{4,5},{5,4},{6,7},{7,6},{8,9},{9,8},{10,11... | collective-permute-start | bytes 786440 | tf_op jit(solution)/shard_map/ppermute | solution.py:675
  51.1 12.0 %collective-permute-start.15 = (bf16[256,512]{1,0:T(8,128)(2,1)S(1)}, bf16[256,512]{1,0:T(8,128)(2,1)S(1)}, u32[]{:S(2)}, u32[]{:S(2)}) collective-permute-start(bf16[256,512]{1,0:T(8,128)(2,1)S(1)} %project_other.3), channel_id=1, source_target_pairs={{0,1},{1,0},{2,3},{3,2},{4,5},{5,4},{6,7},{7,6},{8,9},{9,8},{10,11... | collective-permute-start | bytes 786440 | tf_op jit(solution)/shard_map/ppermute | solution.py:675

commit v3 on v2

--- a/solution.py
+++ b/solution.py
@@ -9,6 +9,7 @@
 from jax.sharding import PartitionSpec as P
 
 very_negative = -1e30
+FIRST = 3
 INFO = 16
 TAIL = 16
 BF16 = jnp.bfloat16
@@ -42,6 +43,13 @@
 def core_place():
     place = lax.axis_index("seq")
     return lax.rem(place, 2), lax.rem(place // 2, 4)
+
+
+def piece_of(mine, off):
+    piece = lax.bitwise_xor(mine, off)
+    if lax.axis_size("seq") == 16:
+        piece = lax.bitwise_xor(piece, lax.axis_index("seq") // 8 * 2)
+    return piece
 
 
 def start_copies(sems, pairs):
@@ -81,16 +89,20 @@
     return picked[0], cumulative
 
 
-def conv_rows(lengths_ref, offset, start, stop, taps, columns, wide):
-    position = offset + start + iota((stop - start, 1), 0)
+def same_request(lengths_ref, offset, length):
+    position = offset + iota((length, 128), 0)
+    lag = iota((length, 128), 1)
     here = segment_of(lengths_ref, position)
+    return (segment_of(lengths_ref, position - lag) == here).astype(F32)
+
+
+def conv_rows(same, start, stop, taps, columns, wide):
     total = taps[0:1, columns] * wide[8 + start : 8 + stop, :]
     for lag in range(1, taps.shape[0]):
-        same = (segment_of(lengths_ref, position - lag) == here).astype(F32)
         total = total + taps[lag : lag + 1, columns] * (
-            wide[8 + start - lag : 8 + stop - lag, :] * same
+            wide[8 + start - lag : 8 + stop - lag, :] * same[start:stop, lag : lag + 1]
         )
-    return (total / (1.0 + jnp.exp(-total))).astype(BF16)
+    return (0.5 * total * (1.0 + jnp.tanh(0.5 * total))).astype(BF16)
 
 
 def write_info(ref, normal, stab, decay):
@@ -128,21 +140,18 @@
         copy.wait()
 
 
-def local_kernel(
-    per_core, lengths_ref, key_ref, key_other, value_ref, value_other,
-    gates_ref, gates_other, taps_ref,
-    conv_ref, values, gate_ref, taps, key_first, factor_first,
-    memory_ref, normal_ref, stab_ref, through_ref,
-    keys, raw, picked, wide, sems,
+def chip_kernel(
+    per_core, lengths_ref, key_ref, key_other, value_ref, value_other, gates_ref, gates_other,
+    taps_ref,
+    conv_ref, values, gate_ref, taps, key_first, levels_first, out0, out1, out2, out3,
+    keys, raw, picked, wide, weighted_ref, whole, normals, levels, sems,
 ):
-    core, _ = core_place()
-    length = keys.shape[0]
-    key_width = keys.shape[1] // per_core
+    core, mine = core_place()
+    length, width = keys.shape
+    key_width = width // per_core
     value_width = values.shape[1] // per_core
     split = gates_ref.shape[1] > 1
-    key_columns = pl.ds(
-        pl.multiple_of(core * keys.shape[1], 128) if split else 0, keys.shape[1]
-    )
+    key_columns = pl.ds(pl.multiple_of(core * width, 128) if split else 0, width)
     value_columns = pl.ds(pl.multiple_of(core * values.shape[1], 128), values.shape[1])
     copies = start_copies(
         sems,
@@ -151,8 +160,6 @@
         + by_core(core, value_ref, value_other, value_columns, values),
     )
     offset = lax.axis_index("seq") // 2 * length
-    for copy in copies[:3]:
-        copy.wait()
     gate, cumulative = gate_rows(core, per_core, (gates_ref, gates_other), raw, picked)
     gate_ref[0] = gate
     gate_ref[1] = cumulative
@@ -163,79 +170,44 @@
     tail_weight = jnp.where(segment == last, gate + total - cumulative, very_negative)
     stab = jnp.max(tail_weight, axis=1, keepdims=True)
     factor = jnp.exp(tail_weight - stab).T
-    stab_ref[...] = jnp.broadcast_to(stab, stab_ref.shape)
+    levels[0] = jnp.broadcast_to(stab, (8, 128))
     through = jnp.where(before == last, total, very_negative)
-    through_ref[...] = jnp.broadcast_to(through, through_ref.shape)
-    factor_first[...] = factor[0:16]
+    levels[1] = jnp.broadcast_to(through, (8, 128))
+    levels_first[0] = tail_weight[:, 0:128]
+    levels_first[1] = levels[1]
+    same = same_request(lengths_ref, offset, length)
+    normals[...] = jnp.zeros_like(normals)
+    for copy in copies[:3]:
+        copy.wait()
     key_first[...] = keys[0:16, :]
-    normal_ref[...] = jnp.zeros_like(normal_ref)
-    weighted_all = []
     step = 128
     for i in range(per_core):
         columns = slice(i * key_width, (i + 1) * key_width)
         wide[0:8, :] = jnp.zeros((8, key_width), F32)
         wide[8:, :] = keys[:, columns].astype(F32)
         normal = jnp.zeros((1, key_width), F32)
-        weighted_rows = []
         for start in range(0, length, step):
-            conv = conv_rows(lengths_ref, offset, start, start + step, taps, columns, wide)
+            conv = conv_rows(same, start, start + step, taps, columns, wide)
             conv_ref[start : start + step, columns] = conv
             weight = factor[start : start + step, i : i + 1]
             if start == 0:
-                weight = jnp.where(iota((step, 1), 0) >= 8, weight, 0.0)
+                weight = jnp.where(iota((step, 1), 0) >= FIRST, weight, 0.0)
             weighted = conv.astype(F32) * weight
             normal = normal + jnp.sum(weighted, axis=0, keepdims=True)
-            weighted_rows.append(weighted.astype(BF16))
-        weighted_all.append(jnp.concatenate(weighted_rows, axis=0))
-        normal_ref[i : i + 1, :] = normal
+            weighted_ref[start : start + step, columns] = weighted.astype(BF16)
+        normals[i : i + 1, :] = normal
     for copy in copies[3:]:
         copy.wait()
     for i in range(per_core):
-        memory_ref[i * key_width : (i + 1) * key_width, :] = dot(
-            weighted_all[i], values[:, i * value_width : (i + 1) * value_width], ((0,), (0,))
-        )
-
-
-def pick_tail(core, which, tail_ref, tail_other, columns):
-    rows = [ref[which, :, columns].astype(F32) for ref in (tail_ref, tail_other)]
-    return jnp.where(core == 0, rows[0], rows[1])[TAIL - 8 :]
-
-
-def first_kernel(
-    per_core, length, lengths_ref, tail_ref, tail_other, taps, key_first, values, factor_first,
-    memory_ref, normal_ref, stab_ref, through_ref,
-    conv_ref, out0, out1, out2, out3, whole, normals, wide,
-):
-    core, mine = core_place()
-    width = key_first.shape[1]
-    key_width = width // per_core
-    value_width = values.shape[1] // per_core
-    split = tail_ref.shape[2] > width
-    tail_columns = pl.ds(pl.multiple_of(core * width, 128) if split else 0, width)
-    tail = pick_tail(core, 1, tail_ref, tail_other, tail_columns)
-    offset = lax.axis_index("seq") // 2 * length
-    normals[...] = jnp.zeros_like(normals)
-    for i in range(per_core):
         columns = slice(i * key_width, (i + 1) * key_width)
-        wide[0:8, :] = tail[:, columns]
-        wide[8:, :] = key_first[:, columns].astype(F32)
-        conv = conv_rows(lengths_ref, offset, 0, 16, taps, columns, wide)
-        conv_ref[:, columns] = conv
-        weight = jnp.where(iota((16, 1), 0) < 8, factor_first[:, i : i + 1], 0.0)
-        weighted = conv.astype(F32) * weight
-        normals[i : i + 1, :] = normal_ref[i : i + 1, :] + jnp.sum(weighted, axis=0, keepdims=True)
-        whole[i * key_width : (i + 1) * key_width, :] = (
-            memory_ref[i * key_width : (i + 1) * key_width, :]
-            + dot(
-                weighted.astype(BF16),
-                values[0:16, i * value_width : (i + 1) * value_width],
-                ((0,), (0,)),
-            )
+        whole[columns, :] = dot(
+            weighted_ref[:, columns],
+            values[:, i * value_width : (i + 1) * value_width],
+            ((0,), (0,)),
         ).astype(BF16)
-    outs = (out0, out1, out2, out3)
     rows = width // 4
-    for off, out in enumerate(outs):
-        piece = lax.bitwise_xor(mine, off)
+    for off, out in enumerate((out0, out1, out2, out3)):
+        piece = piece_of(mine, off)
         content = whole[pl.ds(pl.multiple_of(piece * rows, rows), rows), :]
         for j in range(value_width // 128):
             out[j * rows : (j + 1) * rows, :] = content[:, j * 128 : (j + 1) * 128]
@@ -243,9 +215,98 @@
         write_info(
             out,
             normals[pl.ds(head, 1), :],
-            stab_ref[pl.ds(head, 1), :][:, 0:1],
-            through_ref[pl.ds(head, 1), :][:, 0:1],
+            levels[0, pl.ds(head, 1), :][:, 0:1],
+            levels[1, pl.ds(head, 1), :][:, 0:1],
         )
+
+
+def pick_tail(core, which, tail_ref, tail_other, columns):
+    rows = [ref[which, :, columns].astype(F32) for ref in (tail_ref, tail_other)]
+    return jnp.where(core == 0, rows[0], rows[1])[TAIL - 8 :]
+
+
+def first_kernel(
+    per_core, length, lengths_ref, tail_ref, tail_other, taps, key_first, values, levels_first,
+    conv_ref, out_ref, rows_ref, wide,
+):
+    core, _ = core_place()
+    width = key_first.shape[1]
+    key_width = width // per_core
+    split = tail_ref.shape[2] > width
+    tail_columns = pl.ds(pl.multiple_of(core * width, 128) if split else 0, width)
+    tail = pick_tail(core, 1, tail_ref, tail_other, tail_columns)
+    offset = lax.axis_index("seq") // 2 * length
+    same = same_request(lengths_ref, offset, 16)
+    for i in range(per_core):
+        columns = slice(i * key_width, (i + 1) * key_width)
+        wide[0:8, :] = tail[:, columns]
+        wide[8:, :] = key_first[:, columns].astype(F32)
+        conv_ref[:, columns] = conv_rows(same, 0, 16, taps, columns, wide)
+    rows_ref[...] = jnp.zeros_like(rows_ref)
+    keys, first = conv_ref[...].astype(F32), values[0:16, :].astype(F32)
+    at = 0
+    for block in (keys, first):
+        for j in range(block.shape[1] // 128):
+            rows_ref[at : at + FIRST, :] = block[0:FIRST, j * 128 : (j + 1) * 128]
+            at += FIRST
+    for k in range(2):
+        for part in split3(levels_first[k]):
+            rows_ref[at : at + per_core, :] = part[0:per_core]
+            at += per_core
+    out_ref[0] = rows_ref[...].astype(BF16)
+
+
+def join_kernel(first_ref, second_ref, out_ref):
+    count = first_ref.shape[0]
+    out_ref[0:count] = first_ref[...]
+    out_ref[count:] = second_ref[...]
+
+
+def gathered_kernel(
+    per_core, key_width, offsets, near_ref, far_ref, keys_ref, values_ref, levels_ref,
+    key_rows, value_rows,
+):
+    half = near_ref.shape[0]
+    me = lax.axis_index("seq") // 2
+    value_width = values_ref.shape[1]
+    count = 2 * half * FIRST
+    key_blocks, value_blocks = key_width // 128, value_width // 128
+    base = FIRST * per_core * (key_blocks + value_blocks)
+    ends, decays = [], []
+    for g in range(2 * half):
+        rows = (near_ref[g] if g < half else far_ref[g - half]).astype(F32)
+        for i in range(per_core):
+            at = i * count + g * FIRST
+            for j in range(key_blocks):
+                source = FIRST * (i * key_blocks + j)
+                key_rows[at : at + FIRST, j * 128 : (j + 1) * 128] = rows[source : source + FIRST]
+            for j in range(value_blocks):
+                source = FIRST * (per_core * key_blocks + i * value_blocks + j)
+                value_rows[at : at + FIRST, j * 128 : (j + 1) * 128] = rows[source : source + FIRST]
+        levels = [
+            sum(
+                rows[base + (3 * k + p) * per_core : base + (3 * k + p + 1) * per_core]
+                for p in range(3)
+            )
+            for k in range(2)
+        ]
+        ends.append(levels[0])
+        decays.append(levels[1][:, 0:1])
+    keys_ref[...] = key_rows[...].astype(BF16)
+    values_ref[...] = value_rows[...].astype(BF16)
+    chips = [lax.bitwise_xor(me, off) for off in offsets]
+    square = iota((FIRST, 128), 0) == iota((FIRST, 128), 1)
+    for g in range(2 * half):
+        since = sum(
+            jnp.where((chips[k] > chips[g]) & (chips[k] < me), decays[k], 0.0)
+            for k in range(2 * half)
+            if k != g
+        )
+        here = jnp.where(chips[g] < me, ends[g] + since, 2 * very_negative)
+        for i in range(per_core):
+            column = jnp.sum(jnp.where(square, here[i : i + 1], 0.0), axis=1, keepdims=True)
+            at = i * count + g * FIRST
+            levels_ref[at : at + FIRST, :] = jnp.broadcast_to(column, (FIRST, 128))
 
 
 def shifted_stab(infos, ranks, upto):
@@ -337,16 +398,13 @@
         write_info(out, normal, m, jnp.zeros_like(m))
 
 
-def intra_kernel(
+def query_kernel(
     per_core, lengths_ref, query_ref, query_other, tail_ref, tail_other, taps_ref,
-    key_ref, key_first, values, gate_ref,
-    conv_ref, numerator_ref, stats_ref, queries, taps, keys, wide, sems,
+    conv_ref, queries, taps, wide, sems,
 ):
     core, _ = core_place()
     length, width = queries.shape
     key_width = width // per_core
-    value_width = values.shape[1] // per_core
-    key_scale = 1.0 / math.sqrt(key_width)
     split = tail_ref.shape[2] > width
     columns = pl.ds(pl.multiple_of(core * width, 128) if split else 0, width)
     copies = start_copies(
@@ -356,6 +414,28 @@
     )
     offset = lax.axis_index("seq") // 2 * length
     tail = pick_tail(core, 0, tail_ref, tail_other, columns)
+    same = same_request(lengths_ref, offset, length)
+    for copy in copies:
+        copy.wait()
+    for i in range(per_core):
+        here = slice(i * key_width, (i + 1) * key_width)
+        wide[0:8, :] = tail[:, here]
+        wide[8:, :] = queries[:, here].astype(F32)
+        for start in range(0, length, 128):
+            conv_ref[start : start + 128, here] = conv_rows(
+                same, start, start + 128, taps, here, wide
+            )
+
+
+def intra_kernel(
+    per_core, lengths_ref, query_ref, key_ref, key_first, values, gate_ref,
+    numerator_ref, stats_ref, keys,
+):
+    length, width = query_ref.shape
+    key_width = width // per_core
+    value_width = values.shape[1] // per_core
+    key_scale = 1.0 / math.sqrt(key_width)
+    offset = lax.axis_index("seq") // 2 * length
     keys[...] = key_ref[...]
     keys[0:16, :] = key_first[...]
     gate, cumulative = gate_ref[0], gate_ref[1]
@@ -365,18 +445,10 @@
     before = segment_of(lengths_ref, jnp.full((1, 1), offset - 1, jnp.int32))
     step = length // 2
     lane = iota((step, 128), 1)
-    for copy in copies:
-        copy.wait()
     stats = [[jnp.zeros((step, 128), F32)] * 3 for _ in range(2)]
     for i in range(per_core):
         here = slice(i * key_width, (i + 1) * key_width)
         value_columns = slice(i * value_width, (i + 1) * value_width)
-        wide[0:8, :] = tail[:, here]
-        wide[8:, :] = queries[:, here].astype(F32)
-        for start in range(0, length, 128):
-            conv_ref[start : start + 128, here] = conv_rows(
-                lengths_ref, offset, start, start + 128, taps, here, wide
-            )
         for b in range(2):
             rows, stop = slice(b * step, (b + 1) * step), (b + 1) * step
             allowed = segment_row[:, 0:stop] == segment[rows]
@@ -388,7 +460,7 @@
                 very_negative,
             )
             row_max = jnp.max(log_weight, axis=1, keepdims=True)
-            scores = dot(conv_ref[rows, here], keys[0:stop, here], ((1,), (1,))) * key_scale
+            scores = dot(query_ref[rows, here], keys[0:stop, here], ((1,), (1,))) * key_scale
             weights = scores * jnp.exp(log_weight - row_max)
             numerator_ref[rows, value_columns] = dot(
                 weights.astype(BF16), values[0:stop, value_columns]
@@ -402,8 +474,8 @@
 
 
 def head_kernel(
-    per_core, own_ref, got1, got2, got3, query_ref, numerator_ref, stats_ref,
-    keep_ref, send_ref, memory, info,
+    per_core, own_ref, got1, got2, got3, keys_ref, values_ref, levels_ref,
+    query_ref, numerator_ref, stats_ref, keep_ref, send_ref, memory, info,
 ):
     core, mine = core_place()
     key_width = query_ref.shape[1] // per_core
@@ -412,16 +484,25 @@
     rows = query_ref.shape[1] // 4
     step = keep_ref.shape[0]
     for off, ref in enumerate((own_ref, got1, got2, got3)):
-        piece = lax.bitwise_xor(mine, off)
+        piece = piece_of(mine, off)
         start = pl.multiple_of(piece * rows, rows)
         for j in range(value_width // 128):
             memory[pl.ds(start, rows), j * 128 : (j + 1) * 128] = ref[j * rows : (j + 1) * rows, :]
         info[piece] = ref[ref.shape[0] - INFO :, :]
+    count = keys_ref.shape[0] // per_core
     row, lane = iota((128, key_width), 0), iota((1, 128), 1)
     stabs = jnp.full((1, 128), very_negative, F32)
     parts = []
     for i in range(per_core):
         normal, stab, _ = read_info(info.at[i * key_width // rows], key_width)
+        here = slice(i * key_width, (i + 1) * key_width)
+        extra = slice(i * count, (i + 1) * count)
+        weighted = keys_ref[extra, :].astype(F32) * jnp.exp(levels_ref[extra, 0:1] - stab)
+        normal = normal + jnp.sum(weighted, axis=0, keepdims=True)
+        memory[here, :] = (
+            memory[here, :].astype(F32)
+            + dot(weighted.astype(BF16), values_ref[extra, :], ((0,), (0,)))
+        ).astype(BF16)
         stabs = jnp.where(lane == i, stab, stabs)
         block = jnp.zeros((128, key_width), F32)
         for k, part in enumerate(split3(normal)):
@@ -494,19 +575,34 @@
 
 
 def sum_kernel(chunks, own_ref, *refs):
-    *arrived, out_ref = refs
-    width = out_ref.shape[1] // chunks
-    for c in range(chunks):
-        columns = slice(c * width, (c + 1) * width)
-        total = own_ref[:, columns]
-        for ref in arrived[c::chunks]:
-            total = total + ref[...].astype(F32)
-        out_ref[:, columns] = total.astype(out_ref.dtype)
-
-
-def call(kernel, out_shape, spaces, scratch, name, flops=0, nbytes=0, limit=24):
+    *arrived, out_ref, held, sems = refs
+    width = own_ref.shape[1] // chunks
+    parts = sems.shape[0]
+    step = own_ref.shape[0] // parts
+    copies = []
+    for part in range(parts):
+        rows = slice(part * step, (part + 1) * step)
+        for c in range(chunks):
+            columns = slice(c * width, (c + 1) * width)
+            total = own_ref[rows, columns]
+            for ref in arrived[c::chunks]:
+                total = total + ref[rows, :].astype(F32)
+            held[rows, columns] = total.astype(held.dtype)
+        copies.append(
+            pltpu.make_async_copy(
+                held.at[pl.ds(part * step, step), :],
+                out_ref.at[pl.ds(part * step, step), :],
+                sems.at[part],
+            )
+        )
+        copies[-1].start()
+    for copy in copies:
+        copy.wait()
+
+
+def call(kernel, out_shape, spaces, scratch, name, flops=0, nbytes=0, limit=24, out=pltpu.VMEM):
     place = {"v": pltpu.VMEM, "s": pltpu.SMEM, "a": pl.ANY, "h": pl.ANY}
-    outs = jax.tree.map(lambda _: pl.BlockSpec(memory_space=pltpu.VMEM), out_shape)
+    outs = jax.tree.map(lambda _: pl.BlockSpec(memory_space=out), out_shape)
     inner = pl.pallas_call(
         kernel,
         out_shape=out_shape,
@@ -558,80 +654,80 @@
         [pltpu.SemaphoreType.DMA((4,))], "tails",
     )(query_input, key_input, input_gate, forget_gate)
     gates_other = swap(gates, 1)
+    query_after, gates = lax.optimization_barrier((query_input, gates))
+    query_other = swap(query_after, 1)
     tails = lax.ppermute(tails, "seq", [(i, i + 1) for i in range(seq_count - 1)])
-    tails_other = swap(tails, 1)
-    query_other = swap(lax.optimization_barrier((query_input, tails))[0], 1)
 
     one = shape((rows * value_width // 128 + INFO, 128), BF16)
-    key_conv, values, gate_sums, taps, key_first, factor, memory, normal, stab, through = call(
-        functools.partial(local_kernel, per_core),
+    key_conv, values, gate_sums, taps, key_first, levels, *pieces = call(
+        functools.partial(chip_kernel, per_core),
         (
             shape((chip_length, part_keys), BF16),
             shape((chip_length, part_values), BF16),
             shape((2, 8, chip_length)),
             shape((lags, part_keys)),
             shape((16, part_keys), BF16),
-            shape((16, 8)),
-            shape((part_keys, value_width)),
-            shape((8, key_width)),
-            shape((8, 128)),
-            shape((8, 128)),
-        ),
+            shape((2, 8, 128)),
+        )
+        + (one,) * 4,
         "shahavvh",
-        [pltpu.VMEM((chip_length, part_keys), BF16)]
-        + [
+        [
+            pltpu.VMEM((chip_length, part_keys), BF16),
             pltpu.VMEM((2, max(8, heads), chip_length), F32),
             pltpu.VMEM((2, 8, chip_length), F32),
             pltpu.VMEM((chip_length + 8, key_width), F32),
+            pltpu.VMEM((chip_length, part_keys), BF16),
+            pltpu.VMEM((part_keys, value_width), BF16),
+            pltpu.VMEM((8, key_width), F32),
+            pltpu.VMEM((2, 8, 128), F32),
             pltpu.SemaphoreType.DMA((5,)),
         ],
-        "local_state",
+        "chip_state",
         flops=1 << 30,
     )(
         request_lengths, key_input, key_other, value_input, value_other, gates, gates_other,
         kernel_taps,
     )
-    conv_first, *pieces = call(
+    states = [pieces[0]] + [swap(pieces[off], 2 * off) for off in (1, 2, 3)]
+
+    tails, key_first = lax.optimization_barrier((tails, key_first))
+    tails_other = swap(tails, 1)
+    count = FIRST * seq_count // 2
+    lines = per_core * (FIRST * (key_width + value_width) // 128 + 6)
+    lines = -(-lines // 16) * 16
+    conv_first, message = call(
         functools.partial(first_kernel, per_core, chip_length),
-        (shape((16, part_keys), BF16),) + (one,) * 4,
-        "s" + "v" * 10,
-        [
-            pltpu.VMEM((part_keys, value_width), BF16),
-            pltpu.VMEM((8, key_width), F32),
-            pltpu.VMEM((24, key_width), F32),
-        ],
+        (shape((16, part_keys), BF16), shape((1, lines, 128), BF16)),
+        "s" + "v" * 6,
+        [pltpu.VMEM((lines, 128), F32), pltpu.VMEM((24, key_width), F32)],
         "first_tokens",
-    )(
-        request_lengths, tails, tails_other, taps, key_first, values, factor, memory, normal, stab,
-        through,
-    )
-    states = [pieces[0]] + [swap(pieces[off], 2 * off) for off in (1, 2, 3)]
-    inside = call(
-        functools.partial(intra_kernel, per_core),
-        (
-            shape((chip_length, part_keys), BF16),
-            shape((chip_length, part_values)),
-            shape((3, chip_length, 128)),
-        ),
-        "shavvhvvvv",
+    )(request_lengths, tails, tails_other, taps, key_first, values, levels)
+    bits = seq_count.bit_length() - 1
+    steps = [4, 2, 8] if bits == 4 else [1 << b for b in range(1, bits)]
+    near, far, offsets = message, swap(message, steps[0]), [0, steps[0] // 2]
+    query_conv = call(
+        functools.partial(query_kernel, per_core), shape((chip_length, part_keys), BF16),
+        "shavvh",
         [
             pltpu.VMEM((chip_length, part_keys), BF16),
             pltpu.VMEM((lags, part_keys), F32),
-            pltpu.VMEM((chip_length, part_keys), BF16),
             pltpu.VMEM((chip_length + 8, key_width), F32),
             pltpu.SemaphoreType.DMA((3,)),
         ],
-        "intra",
-        flops=4 << 30,
-    )(
-        request_lengths, query_input, query_other, tails, tails_other, kernel_taps, key_conv,
-        conv_first, values, gate_sums,
-    )
-    states, inside = lax.optimization_barrier((states, inside))
+        "query_conv",
+        flops=1 << 30,
+    )(request_lengths, query_after, query_other, tails, tails_other, kernel_taps)
+    states, query_conv, far = lax.optimization_barrier((states, query_conv, far))
     total = call(total_kernel, one, "vvvv", [], "group_total")(*states)
-    bits = seq_count.bit_length() - 1
     flag = 3
-    prefix = swap(total, 8)
+    prefix = swap(total, 12 if bits == 4 else 8)
+    near, far, total = lax.optimization_barrier((near, far, total))
+    for step in steps[1:]:
+        near = call(
+            join_kernel, shape((2 * near.shape[0], lines, 128), BF16), "vv", [], "join"
+        )(near, far)
+        far = swap(near, step)
+        offsets = offsets + [off ^ (step // 2) for off in offsets]
     if bits > 4:
         flag = None
         prefix, total = call(
@@ -644,16 +740,39 @@
     enter = call(functools.partial(enter_kernel, flag), (one,) * 4, "vvvvv", [], "enter_state")(
         prefix, *states
     )
+    gate_sums, near, *enter = lax.optimization_barrier((gate_sums, near, *enter))
     enter = [enter[0]] + [swap(enter[off], 2 * off) for off in (1, 2, 3)]
+    extras = call(
+        functools.partial(gathered_kernel, per_core, key_width, tuple(offsets)),
+        (
+            shape((per_core * count, key_width), BF16),
+            shape((per_core * count, value_width), BF16),
+            shape((per_core * count, 128)),
+        ),
+        "vv",
+        [
+            pltpu.VMEM((per_core * count, key_width), F32),
+            pltpu.VMEM((per_core * count, value_width), F32),
+        ],
+        "gathered_first",
+    )(near, far)
+    inside = call(
+        functools.partial(intra_kernel, per_core),
+        (shape((chip_length, part_values)), shape((3, chip_length, 128))),
+        "svvvvv",
+        [pltpu.VMEM((chip_length, part_keys), BF16)],
+        "intra",
+        flops=4 << 30,
+    )(request_lengths, query_conv, key_conv, conv_first, values, gate_sums)
     half = shape((length, part_values), BF16)
     keep, send = call(
-        functools.partial(head_kernel, per_core), (half, half), "v" * 7,
+        functools.partial(head_kernel, per_core), (half, half), "v" * 10,
         [
             pltpu.VMEM((part_keys, value_width), BF16),
             pltpu.VMEM((4, INFO, 128), BF16),
         ],
         "head_out",
-    )(*enter, *inside)
+    )(*enter, *extras, query_conv, *inside)
     got = swap(send, 1)
 
     chunks = 2 if head_count == 2 and out_cols % 256 == 0 else 1
@@ -679,7 +798,9 @@
     )(keep, got, output_weight)
     return call(
         functools.partial(sum_kernel, chunks), shape((length, out_cols), BF16),
-        "v" * (1 + chunks * len(arrived)), [], "mixed_out",
+        "v" * (1 + chunks * len(arrived)),
+        [pltpu.VMEM((length, out_cols), BF16), pltpu.SemaphoreType.DMA((4,))],
+        "mixed_out", out=pl.ANY,
     )(mixed, *(c for columns in arrived for c in columns))
 
 

time: 64.3 us -> 57.7 us (0.90)
  waiting for transfers between devices: 25.6 us -> 18.7 us
  starting transfers between devices: 19.9 us -> 21.9 us
  Pallas kernels: 18.3 us -> 16.7 us
    ppermute x13 -> x16, waiting for transfers between devices: 14.5 us -> 8.51 us  [swap(): return lax.ppermute(x, 'seq', [(i, i ^ off) for i in range(seq_count)])]
    ppermute x13 -> x16, starting transfers between devices: 15.4 us -> 17.4 us  [swap(): return lax.ppermute(x, 'seq', [(i, i ^ off) for i in range(seq_count)])]
    pallas_call x12 -> x16, Pallas kernels: 18.3 us -> 16.7 us  [run(): inner(*(pltpu.with_memory_space_constraint(x, pltpu.HBM) if s in 'hs' els...]
    ppermute x1, waiting for transfers between devices: 0.88 us -> 0.01 us  [on_device(): lax.ppermute(tails, 'seq', [(i, i + 1) for i in range(seq_count - 1)])]
  transfers between devices with their start and end apart: 16 -> 19, of which waited for: 10 -> 7; matrix products, arithmetic and copies ran while one was open for 0% -> 0% of each run, Pallas kernels for 23% -> 23%
where the time goes in v3:
time: 57.7 us; the launch traced here: 57.5 us
  starting transfers between devices  21.9 us (38%)
  waiting for transfers between devices  18.7 us (32%)
  Pallas kernels  16.7 us (29%)
    ppermute x16, starting transfers between devices, swap(): return lax.ppermute(x, 'seq', [(i, i ^ off) for i in range(seq_count)])  17.4 us
    pallas_call x16, Pallas kernels, run(): inner(*(pltpu.with_memory_space_constraint(x, pltpu.HBM) if s in 'hs' els...  16.7 us
    ppermute x2, waiting for transfers between devices, on_device(): lax.ppermute(c, 'head', [(i, i ^ off) for i in range(head_count)])  10.2 us
    ppermute x16, waiting for transfers between devices, swap(): return lax.ppermute(x, 'seq', [(i, i ^ off) for i in range(seq_count)])  8.51 us
    ppermute x1, starting transfers between devices, on_device(): lax.ppermute(tails, 'seq', [(i, i + 1) for i in range(seq_count - 1)])  2.32 us
    ppermute x2, starting transfers between devices, on_device(): lax.ppermute(c, 'head', [(i, i ^ off) for i in range(head_count)])  2.16 us
  transfers between devices with their start and end apart: 19, of which 7 were waited for; matrix products, arithmetic and copies ran while one was open for 0% of the time, Pallas kernels for 23%

profile of v3, /device:TPU:0, one launch (start us, length us, event | category | flops | bytes accessed | tf_op | source)
XLA Modules:
  0.0 57.5 jit_solution(15156142171012132790)
XLA Ops:
  0.5 0.8 %tails.1 = (bf16[2,16,1024]{2,1,0:T(8,128)(2,1)S(1)}, f32[2,4,256]{2,1,0:T(4,128)S(1)}) custom-call(bf16[256,1024]{1,0:T(8,128)(2,1)} %query_ref.2, bf16[256,1024]{1,0:T(8,128)(2,1)} %key_ref.3, f32[4,256]{1,0:T(4,128)} %input_ref.1, f32[4,256]{1,0:T(4,128)} %forget_ref.1), custom_call_target="tpu_custom_call" | custom-call | tf_op jit(solution)/shard_map/tails/pallas_call | solution.py:618
  1.9 2.3 %collective-permute-start.3 = (bf16[2,16,1024]{2,1,0:T(8,128)(2,1)S(1)}, bf16[2,16,1024]{2,1,0:T(8,128)(2,1)S(1)}, u32[]{:S(2)}, u32[]{:S(2)}) collective-permute-start(bf16[2,16,1024]{2,1,0:T(8,128)(2,1)S(1)} %get-tuple-element.51), channel_id=1, source_target_pairs={{0,2},{2,4},{4,6},{6,8},{8,10},{10,12},{12,14},{14,16},{16,18},{18... | collective-permute-start | bytes 196616 | tf_op jit(solution)/shard_map/ppermute | solution.py:659
  4.3 3.4 %chip_state.1 = (bf16[512,512]{1,0:T(8,128)(2,1)S(1)}, bf16[512,1024]{1,0:T(8,128)(2,1)S(1)}, f32[2,8,512]{2,1,0:T(8,128)S(1)}, f32[4,512]{1,0:T(4,128)S(1)}, bf...) custom-call(s32[4]{0:T(128)} %lengths_ref.7, ...), custom_call_target="tpu_custom_call" | custom-call | flops 1073741824 | tf_op jit(solution)/shard_map/chip_state/pallas_call | solution.py:618
  7.7 2.7 %collective-permute-start.4 = (bf16[2,16,1024]{2,1,0:T(8,128)(2,1)S(1)}, bf16[2,16,1024]{2,1,0:T(8,128)(2,1)S(1)}, u32[]{:S(2)}, u32[]{:S(2)}) collective-permute-start(bf16[2,16,1024]{2,1,0:T(8,128)(2,1)S(1)} %collective-permute-done.3.tail_ref), channel_id=1, source_target_pairs={{0,2},{2,0},{4,6},{6,4},{8,10},{10,8},{12,14},{14,12},{16,18},{18,... | collective-permute-start | bytes 196616 | tf_op jit(solution)/shard_map/ppermute | solution.py:649
  10.4 1.5 %collective-permute-start.5 = (bf16[528,128]{1,0:T(8,128)(2,1)S(1)}, bf16[528,128]{1,0:T(8,128)(2,1)S(1)}, u32[]{:S(2)}, u32[]{:S(2)}) collective-permute-start(bf16[528,128]{1,0:T(8,128)(2,1)S(1)} %get-tuple-element.60), channel_id=1, source_target_pairs={{0,4},{2,6},{4,0},{6,2},{8,12},{10,14},{12,8},{14,10},{16,20},{18,... | collective-permute-start | bytes 405512 | tf_op jit(solution)/shard_map/ppermute | solution.py:649
  12.0 1.6 %collective-permute-start.6 = (bf16[528,128]{1,0:T(8,128)(2,1)S(1)}, bf16[528,128]{1,0:T(8,128)(2,1)S(1)}, u32[]{:S(2)}, u32[]{:S(2)}) collective-permute-start(bf16[528,128]{1,0:T(8,128)(2,1)S(1)} %get-tuple-element.61), channel_id=1, source_target_pairs={{0,8},{2,10},{4,12},{6,14},{8,0},{10,2},{12,4},{14,6},{16,24},{18,... | collective-permute-start | bytes 405512 | tf_op jit(solution)/shard_map/ppermute | solution.py:649
  13.9 0.8 %first_tokens.1 = (bf16[16,512]{1,0:T(8,128)(2,1)S(1)}, bf16[1,48,128]{2,1,0:T(8,128)(2,1)S(1)}) custom-call(s32[4]{0:T(128)} %lengths_ref.7, bf16[2,16,1024]{2,1,0:T(8,128)(2,1)S(1)} %collective-permute-done.3.tail_ref, bf16[2,16,1024]{2,1,0:T(8,128)(2,1)S(1)} %collective-permute-done.4.tail_other, f32[4,512]{1,0:T(4,128)S(1)} %get-tuple-element.54.taps, ...), custom_call_target="tpu_custom_call" | custom-call | tf_op jit(solution)/shard_map/first_tokens/pallas_call | solution.py:618
  14.7 1.6 %collective-permute-start.9 = (bf16[1,48,128]{2,1,0:T(8,128)(2,1)S(1)}, bf16[1,48,128]{2,1,0:T(8,128)(2,1)S(1)}, u32[]{:S(2)}, u32[]{:S(2)}) collective-permute-start(bf16[1,48,128]{2,1,0:T(8,128)(2,1)S(1)} %get-tuple-element.69.first_ref), channel_id=1, source_target_pairs={{0,8},{2,10},{4,12},{6,14},{8,0},{10,2},{12,4},{14,6},{16,24},{18,... | collective-permute-start | bytes 36872 | tf_op jit(solution)/shard_map/ppermute | solution.py:649
  16.4 2.6 %query_conv.1.query_ref = bf16[512,512]{1,0:T(8,128)(2,1)S(1)} custom-call(s32[4]{0:T(128)} %lengths_ref.7, bf16[256,1024]{1,0:T(8,128)(2,1)} %query_ref.2, bf16[256,1024]{1,0:T(8,128)(2,1)S(1)} %collective-permute-done.8.query_other, bf16[2,16,1024]{2,1,0:T(8,128)(2,1)S(1)} %collective-permute-done.3.tail_ref, ...), custom_call_target="tpu_custom_call" | custom-call | flops 1073741824 | tf_op jit(solution)/shard_map/query_conv/pallas_call | solution.py:618
  19.0 1.4 %collective-permute-done.9.second_ref = bf16[1,48,128]{2,1,0:T(8,128)(2,1)S(1)} collective-permute-done((bf16[1,48,128]{2,1,0:T(8,128)(2,1)S(1)}, bf16[1,48,128]{2,1,0:T(8,128)(2,1)S(1)}, u32[]{:S(2)}, u32[]{:S(2)}) %collective-permute-start.9) | collective-permute-done | bytes 12320 | tf_op jit(solution)/shard_map/ppermute | solution.py:649
  20.7 3.5 %collective-permute-start.11 = (bf16[528,128]{1,0:T(8,128)(2,1)S(1)}, bf16[528,128]{1,0:T(8,128)(2,1)S(1)}, u32[]{:S(2)}, u32[]{:S(2)}) collective-permute-start(bf16[528,128]{1,0:T(8,128)(2,1)S(1)} %group_total.1), channel_id=1, source_target_pairs={{0,24},{2,26},{4,28},{6,30},{8,16},{10,18},{12,20},{14,22},{16,8},... | collective-permute-start | bytes 405512 | tf_op jit(solution)/shard_map/ppermute | solution.py:649
  24.8 3.1 %collective-permute-done.10.second_ref = bf16[2,48,128]{2,1,0:T(8,128)(2,1)S(1)} collective-permute-done((bf16[2,48,128]{2,1,0:T(8,128)(2,1)S(1)}, bf16[2,48,128]{2,1,0:T(8,128)(2,1)S(1)}, u32[]{:S(2)}, u32[]{:S(2)}) %collective-permute-start.10) | collective-permute-done | bytes 24608 | tf_op jit(solution)/shard_map/ppermute | solution.py:649
  28.6 1.0 %collective-permute-start.12 = (bf16[528,128]{1,0:T(8,128)(2,1)S(1)}, bf16[528,128]{1,0:T(8,128)(2,1)S(1)}, u32[]{:S(2)}, u32[]{:S(2)}) collective-permute-start(bf16[528,128]{1,0:T(8,128)(2,1)S(1)} %get-tuple-element.76), channel_id=1, source_target_pairs={{0,4},{2,6},{4,0},{6,2},{8,12},{10,14},{12,8},{14,10},{16,20},{18,... | collective-permute-start | bytes 405512 | tf_op jit(solution)/shard_map/ppermute | solution.py:649
  29.7 2.9 %collective-permute-start.13 = (bf16[528,128]{1,0:T(8,128)(2,1)S(1)}, bf16[528,128]{1,0:T(8,128)(2,1)S(1)}, u32[]{:S(2)}, u32[]{:S(2)}) collective-permute-start(bf16[528,128]{1,0:T(8,128)(2,1)S(1)} %get-tuple-element.77), channel_id=1, source_target_pairs={{0,8},{2,10},{4,12},{6,14},{8,0},{10,2},{12,4},{14,6},{16,24},{18,... | collective-permute-start | bytes 405512 | tf_op jit(solution)/shard_map/ppermute | solution.py:649
  32.8 2.5 %intra.1 = (f32[512,1024]{1,0:T(8,128)S(1)}, f32[3,512,128]{2,1,0:T(8,128)S(1)}) custom-call(s32[4]{0:T(128)} %lengths_ref.7, bf16[512,512]{1,0:T(8,128)(2,1)S(1)} %query_conv.1.query_ref, bf16[512,512]{1,0:T(8,128)(2,1)S(1)} %get-tuple-element.84.key_ref, bf16[16,512]{1,0:T(8,128)(2,1)S(1)} %get-tuple-element.85.key_first, ...), custom_call_target="tpu_custom_call" | custom-call | flops 4294967296 | tf_op jit(solution)/shard_map/intra/pallas_call | solution.py:618
  36.1 2.4 %collective-permute-done.14.got3 = bf16[528,128]{1,0:T(8,128)(2,1)S(1)} collective-permute-done((bf16[528,128]{1,0:T(8,128)(2,1)S(1)}, bf16[528,128]{1,0:T(8,128)(2,1)S(1)}, u32[]{:S(2)}, u32[]{:S(2)}) %collective-permute-start.14) | collective-permute-done | bytes 135200 | tf_op jit(solution)/shard_map/ppermute | solution.py:649
  38.5 1.7 %head_out.1 = (bf16[256,1024]{1,0:T(8,128)(2,1)S(1)}, bf16[256,1024]{1,0:T(8,128)(2,1)S(1)}) custom-call(bf16[528,128]{1,0:T(8,128)(2,1)S(1)} %get-tuple-element.75.own_ref, bf16[528,128]{1,0:T(8,128)(2,1)S(1)} %collective-permute-done.12.got1, bf16[528,128]{1,0:T(8,128)(2,1)S(1)} %collective-permute-done.13.got2, ...), custom_call_target="tpu_custom_call" | custom-call | tf_op jit(solution)/shard_map/head_out/pallas_call | solution.py:618
  40.3 0.7 %project_kept.1.kept_ref = f32[256,1024]{1,0:T(8,128)S(1)} custom-call(bf16[256,1024]{1,0:T(8,128)(2,1)S(1)} %get-tuple-element.89.keep_ref.head_ref, bf16[2048,2048]{1,0:T(8,128)(2,1)S(1)} %bitcast.1), custom_call_target="tpu_custom_call" | custom-call | flops 2147483648 | tf_op jit(solution)/shard_map/project_kept/pallas_call | solution.py:618
  41.0 1.1 %collective-permute-done.16.got_ref.head_ref = bf16[256,1024]{1,0:T(8,128)(2,1)S(1)} collective-permute-done((bf16[256,1024]{1,0:T(8,128)(2,1)S(1)}, bf16[256,1024]{1,0:T(8,128)(2,1)S(1)}, u32[]{:S(2)}, u32[]{:S(2)}) %collective-permute-start.16) | collective-permute-done | bytes 524320 | tf_op jit(solution)/shard_map/ppermute | solution.py:649
  42.6 1.6 %collective-permute-start.18 = (bf16[256,512]{1,0:T(8,128)(2,1)S(1)}, bf16[256,512]{1,0:T(8,128)(2,1)S(1)}, u32[]{:S(2)}, u32[]{:S(2)}) collective-permute-start(bf16[256,512]{1,0:T(8,128)(2,1)S(1)} %project_other.3), channel_id=1, source_target_pairs={{0,1},{1,0},{2,3},{3,2},{4,5},{5,4},{6,7},{7,6},{8,9},{9,8},{10,11... | collective-permute-start | bytes 786440 | tf_op jit(solution)/shard_map/ppermute | solution.py:794
  45.2 1.2 %project_own.1.own_ref = f32[256,1024]{1,0:T(8,128)S(1)} custom-call(bf16[256,1024]{1,0:T(8,128)(2,1)S(1)} %get-tuple-element.89.keep_ref.head_ref, bf16[256,1024]{1,0:T(8,128)(2,1)S(1)} %collective-permute-done.16.got_ref.head_ref, bf16[2048,2048]{1,0:T(8,128)(2,1)S(1)} %bitcast.1), custom_call_target="tpu_custom_call" | custom-call | flops 4294967296 | tf_op jit(solution)/shard_map/project_own/pallas_call | solution.py:618
  46.5 5.4 %collective-permute-done.18.refs_1_ = bf16[256,512]{1,0:T(8,128)(2,1)S(1)} collective-permute-done((bf16[256,512]{1,0:T(8,128)(2,1)S(1)}, bf16[256,512]{1,0:T(8,128)(2,1)S(1)}, u32[]{:S(2)}, u32[]{:S(2)}) %collective-permute-start.18) | collective-permute-done | bytes 262176 | tf_op jit(solution)/shard_map/ppermute | solution.py:794
  51.8 4.8 %collective-permute-done.17.refs_0_ = bf16[256,512]{1,0:T(8,128)(2,1)S(1)} collective-permute-done((bf16[256,512]{1,0:T(8,128)(2,1)S(1)}, bf16[256,512]{1,0:T(8,128)(2,1)S(1)}, u32[]{:S(2)}, u32[]{:S(2)}) %collective-permute-start.17) | collective-permute-done | bytes 262176 | tf_op jit(solution)/shard_map/ppermute | solution.py:794
  56.6 0.8 %mixed_out.1 = bf16[256,1024]{1,0:T(8,128)(2,1)} custom-call(f32[256,1024]{1,0:T(8,128)S(1)} %project_own.1.own_ref, bf16[256,512]{1,0:T(8,128)(2,1)S(1)} %collective-permute-done.17.refs_0_, bf16[256,512]{1,0:T(8,128)(2,1)S(1)} %collective-permute-done.18.refs_1_), custom_call_target="tpu_custom_call" | custom-call | tf_op jit(solution)/shard_map/mixed_out/pallas_call | solution.py:618
  (35 shorter events, 5.7 us)
Async XLA Ops:
  0.0 4.3 %collective-permute-start.1 = (bf16[256,2048]{1,0:T(8,128)(2,1)}, bf16[256,2048]{1,0:T(8,128)(2,1)S(1)}, u32[]{:S(2)}, u32[]{:S(2)}) collective-permute-start(bf16[256,2048]{1,0:T(8,128)(2,1)} %value_ref.1), channel_id=1, source_target_pairs={{0,2},{2,0},{4,6},{6,4},{8,10},{10,8},{12,14},{14,12},{16,18},{18,... | collective-permute-start | bytes 3145736 | tf_op jit(solution)/shard_map/ppermute | solution.py:649
  0.5 3.8 %collective-permute-start = (bf16[256,1024]{1,0:T(8,128)(2,1)}, bf16[256,1024]{1,0:T(8,128)(2,1)S(1)}, u32[]{:S(2)}, u32[]{:S(2)}) collective-permute-start(bf16[256,1024]{1,0:T(8,128)(2,1)} %key_ref.3), channel_id=1, source_target_pairs={{0,2},{2,0},{4,6},{6,4},{8,10},{10,8},{12,14},{14,12},{16,18},{18,... | collective-permute-start | bytes 1572872 | tf_op jit(solution)/shard_map/ppermute | solution.py:649
  1.3 15.1 %collective-permute-start.8 = (bf16[256,1024]{1,0:T(8,128)(2,1)}, bf16[256,1024]{1,0:T(8,128)(2,1)S(1)}, u32[]{:S(2)}, u32[]{:S(2)}) collective-permute-start(bf16[256,1024]{1,0:T(8,128)(2,1)} %query_ref.2), channel_id=1, source_target_pairs={{0,2},{2,0},{4,6},{6,4},{8,10},{10,8},{12,14},{14,12},{16,18},{18,... | collective-permute-start | bytes 1572872 | tf_op jit(solution)/shard_map/ppermute | solution.py:649
  1.8 2.4 %collective-permute-start.2 = (f32[2,4,256]{2,1,0:T(4,128)S(1)}, f32[2,4,256]{2,1,0:T(4,128)S(1)}, u32[]{:S(2)}, u32[]{:S(2)}) collective-permute-start(f32[2,4,256]{2,1,0:T(4,128)S(1)} %get-tuple-element.49.gates_ref), channel_id=1, source_target_pairs={{0,2},{2,0},{4,6},{6,4},{8,10},{10,8},{12,14},{14,12},{16,18},{18,... | collective-permute-start | bytes 24584 | tf_op jit(solution)/shard_map/ppermute | solution.py:649
  1.9 5.8 %collective-permute-start.3 = (bf16[2,16,1024]{2,1,0:T(8,128)(2,1)S(1)}, bf16[2,16,1024]{2,1,0:T(8,128)(2,1)S(1)}, u32[]{:S(2)}, u32[]{:S(2)}) collective-permute-start(bf16[2,16,1024]{2,1,0:T(8,128)(2,1)S(1)} %get-tuple-element.51), channel_id=1, source_target_pairs={{0,2},{2,4},{4,6},{6,8},{8,10},{10,12},{12,14},{14,16},{16,18},{18... | collective-permute-start | bytes 196616 | tf_op jit(solution)/shard_map/ppermute | solution.py:659
  7.7 6.2 %collective-permute-start.4 = (bf16[2,16,1024]{2,1,0:T(8,128)(2,1)S(1)}, bf16[2,16,1024]{2,1,0:T(8,128)(2,1)S(1)}, u32[]{:S(2)}, u32[]{:S(2)}) collective-permute-start(bf16[2,16,1024]{2,1,0:T(8,128)(2,1)S(1)} %collective-permute-done.3.tail_ref), channel_id=1, source_target_pairs={{0,2},{2,0},{4,6},{6,4},{8,10},{10,8},{12,14},{14,12},{16,18},{18,... | collective-permute-start | bytes 196616 | tf_op jit(solution)/shard_map/ppermute | solution.py:649
  10.4 10.0 %collective-permute-start.5 = (bf16[528,128]{1,0:T(8,128)(2,1)S(1)}, bf16[528,128]{1,0:T(8,128)(2,1)S(1)}, u32[]{:S(2)}, u32[]{:S(2)}) collective-permute-start(bf16[528,128]{1,0:T(8,128)(2,1)S(1)} %get-tuple-element.60), channel_id=1, source_target_pairs={{0,4},{2,6},{4,0},{6,2},{8,12},{10,14},{12,8},{14,10},{16,20},{18,... | collective-permute-start | bytes 405512 | tf_op jit(solution)/shard_map/ppermute | solution.py:649
  12.0 8.5 %collective-permute-start.6 = (bf16[528,128]{1,0:T(8,128)(2,1)S(1)}, bf16[528,128]{1,0:T(8,128)(2,1)S(1)}, u32[]{:S(2)}, u32[]{:S(2)}) collective-permute-start(bf16[528,128]{1,0:T(8,128)(2,1)S(1)} %get-tuple-element.61), channel_id=1, source_target_pairs={{0,8},{2,10},{4,12},{6,14},{8,0},{10,2},{12,4},{14,6},{16,24},{18,... | collective-permute-start | bytes 405512 | tf_op jit(solution)/shard_map/ppermute | solution.py:649
  13.5 6.9 %collective-permute-start.7 = (bf16[528,128]{1,0:T(8,128)(2,1)S(1)}, bf16[528,128]{1,0:T(8,128)(2,1)S(1)}, u32[]{:S(2)}, u32[]{:S(2)}) collective-permute-start(bf16[528,128]{1,0:T(8,128)(2,1)S(1)} %get-tuple-element.62), channel_id=1, source_target_pairs={{0,12},{2,14},{4,8},{6,10},{8,4},{10,6},{12,0},{14,2},{16,28},{18,... | collective-permute-start | bytes 405512 | tf_op jit(solution)/shard_map/ppermute | solution.py:649
  14.7 5.7 %collective-permute-start.9 = (bf16[1,48,128]{2,1,0:T(8,128)(2,1)S(1)}, bf16[1,48,128]{2,1,0:T(8,128)(2,1)S(1)}, u32[]{:S(2)}, u32[]{:S(2)}) collective-permute-start(bf16[1,48,128]{2,1,0:T(8,128)(2,1)S(1)} %get-tuple-element.69.first_ref), channel_id=1, source_target_pairs={{0,8},{2,10},{4,12},{6,14},{8,0},{10,2},{12,4},{14,6},{16,24},{18,... | collective-permute-start | bytes 36872 | tf_op jit(solution)/shard_map/ppermute | solution.py:649
  20.7 7.3 %collective-permute-start.11 = (bf16[528,128]{1,0:T(8,128)(2,1)S(1)}, bf16[528,128]{1,0:T(8,128)(2,1)S(1)}, u32[]{:S(2)}, u32[]{:S(2)}) collective-permute-start(bf16[528,128]{1,0:T(8,128)(2,1)S(1)} %group_total.1), channel_id=1, source_target_pairs={{0,24},{2,26},{4,28},{6,30},{8,16},{10,18},{12,20},{14,22},{16,8},... | collective-permute-start | bytes 405512 | tf_op jit(solution)/shard_map/ppermute | solution.py:649
  24.1 3.8 %collective-permute-start.10 = (bf16[2,48,128]{2,1,0:T(8,128)(2,1)S(1)}, bf16[2,48,128]{2,1,0:T(8,128)(2,1)S(1)}, u32[]{:S(2)}, u32[]{:S(2)}) collective-permute-start(bf16[2,48,128]{2,1,0:T(8,128)(2,1)S(1)} %join.2.first_ref), channel_id=1, source_target_pairs={{0,4},{2,6},{4,0},{6,2},{8,12},{10,14},{12,8},{14,10},{16,20},{18,... | collective-permute-start | bytes 73736 | tf_op jit(solution)/shard_map/ppermute | solution.py:649
  27.9 7.4 %collective-permute-start.15 = (bf16[4,48,128]{2,1,0:T(8,128)(2,1)S(1)}, bf16[4,48,128]{2,1,0:T(8,128)(2,1)S(1)}, u32[]{:S(2)}, u32[]{:S(2)}) collective-permute-start(bf16[4,48,128]{2,1,0:T(8,128)(2,1)S(1)} %join.3.near_ref), channel_id=1, source_target_pairs={{0,16},{2,18},{4,20},{6,22},{8,24},{10,26},{12,28},{14,30},{16,0},... | collective-permute-start | bytes 147464 | tf_op jit(solution)/shard_map/ppermute | solution.py:649
  28.0 12.3 %slice-start = ((s8[8388608]{0:T(1024)(128)(4,1)}), s8[4194304]{0:T(1024)(128)(4,1)S(1)}, s32[]{:S(2)}) async-start(s8[8388608]{0:T(1024)(128)(4,1)} %bitcast), calls=%async_computation | async-start | bytes 8388608
  28.6 7.0 %collective-permute-start.12 = (bf16[528,128]{1,0:T(8,128)(2,1)S(1)}, bf16[528,128]{1,0:T(8,128)(2,1)S(1)}, u32[]{:S(2)}, u32[]{:S(2)}) collective-permute-start(bf16[528,128]{1,0:T(8,128)(2,1)S(1)} %get-tuple-element.76), channel_id=1, source_target_pairs={{0,4},{2,6},{4,0},{6,2},{8,12},{10,14},{12,8},{14,10},{16,20},{18,... | collective-permute-start | bytes 405512 | tf_op jit(solution)/shard_map/ppermute | solution.py:649
  29.7 6.4 %collective-permute-start.13 = (bf16[528,128]{1,0:T(8,128)(2,1)S(1)}, bf16[528,128]{1,0:T(8,128)(2,1)S(1)}, u32[]{:S(2)}, u32[]{:S(2)}) collective-permute-start(bf16[528,128]{1,0:T(8,128)(2,1)S(1)} %get-tuple-element.77), channel_id=1, source_target_pairs={{0,8},{2,10},{4,12},{6,14},{8,0},{10,2},{12,4},{14,6},{16,24},{18,... | collective-permute-start | bytes 405512 | tf_op jit(solution)/shard_map/ppermute | solution.py:649
  32.5 5.9 %collective-permute-start.14 = (bf16[528,128]{1,0:T(8,128)(2,1)S(1)}, bf16[528,128]{1,0:T(8,128)(2,1)S(1)}, u32[]{:S(2)}, u32[]{:S(2)}) collective-permute-start(bf16[528,128]{1,0:T(8,128)(2,1)S(1)} %get-tuple-element.78), channel_id=1, source_target_pairs={{0,12},{2,14},{4,8},{6,10},{8,4},{10,6},{12,0},{14,2},{16,28},{18,... | collective-permute-start | bytes 405512 | tf_op jit(solution)/shard_map/ppermute | solution.py:649
  32.8 7.4 %slice-start.1 = ((s8[8388608]{0:T(1024)(128)(4,1)}), s8[4194304]{0:T(1024)(128)(4,1)S(1)}, s32[]{:S(2)}) async-start(s8[8388608]{0:T(1024)(128)(4,1)} %bitcast), calls=%async_computation.1 | async-start | bytes 8388608
  40.2 2.0 %collective-permute-start.16 = (bf16[256,1024]{1,0:T(8,128)(2,1)S(1)}, bf16[256,1024]{1,0:T(8,128)(2,1)S(1)}, u32[]{:S(2)}, u32[]{:S(2)}) collective-permute-start(bf16[256,1024]{1,0:T(8,128)(2,1)S(1)} %get-tuple-element.90), channel_id=1, source_target_pairs={{0,2},{2,0},{4,6},{6,4},{8,10},{10,8},{12,14},{14,12},{16,18},{18,... | collective-permute-start | bytes 1572872 | tf_op jit(solution)/shard_map/ppermute | solution.py:649
  42.6 9.2 %collective-permute-start.18 = (bf16[256,512]{1,0:T(8,128)(2,1)S(1)}, bf16[256,512]{1,0:T(8,128)(2,1)S(1)}, u32[]{:S(2)}, u32[]{:S(2)}) collective-permute-start(bf16[256,512]{1,0:T(8,128)(2,1)S(1)} %project_other.3), channel_id=1, source_target_pairs={{0,1},{1,0},{2,3},{3,2},{4,5},{5,4},{6,7},{7,6},{8,9},{9,8},{10,11... | collective-permute-start | bytes 786440 | tf_op jit(solution)/shard_map/ppermute | solution.py:794
  44.6 12.0 %collective-permute-start.17 = (bf16[256,512]{1,0:T(8,128)(2,1)S(1)}, bf16[256,512]{1,0:T(8,128)(2,1)S(1)}, u32[]{:S(2)}, u32[]{:S(2)}) collective-permute-start(bf16[256,512]{1,0:T(8,128)(2,1)S(1)} %project_other.2), channel_id=1, source_target_pairs={{0,1},{1,0},{2,3},{3,2},{4,5},{5,4},{6,7},{7,6},{8,9},{9,8},{10,11... | collective-permute-start | bytes 786440 | tf_op jit(solution)/shard_map/ppermute | solution.py:794

commit v4 on v3

--- a/solution.py
+++ b/solution.py
@@ -89,9 +89,8 @@
     return picked[0], cumulative
 
 
-def same_request(lengths_ref, offset, length):
-    position = offset + iota((length, 128), 0)
-    lag = iota((length, 128), 1)
+def same_request(lengths_ref, position):
+    lag = iota((position.shape[0], 128), 1)
     here = segment_of(lengths_ref, position)
     return (segment_of(lengths_ref, position - lag) == here).astype(F32)
 
@@ -126,15 +125,9 @@
     return normal, sums[0][:, 0:1], sums[1][:, 0:1]
 
 
-def tail_kernel(query_ref, key_ref, input_ref, forget_ref, out_ref, gate_ref, sems):
-    last = query_ref.shape[0] - TAIL
+def gates_kernel(input_ref, forget_ref, gate_ref, sems):
     copies = start_copies(
-        sems,
-        [
-            (ref.at[pl.ds(last, TAIL), :], out_ref.at[i])
-            for i, ref in enumerate((query_ref, key_ref))
-        ]
-        + [(ref, gate_ref.at[i]) for i, ref in enumerate((input_ref, forget_ref))],
+        sems, [(ref, gate_ref.at[i]) for i, ref in enumerate((input_ref, forget_ref))]
     )
     for copy in copies:
         copy.wait()
@@ -143,7 +136,7 @@
 def chip_kernel(
     per_core, lengths_ref, key_ref, key_other, value_ref, value_other, gates_ref, gates_other,
     taps_ref,
-    conv_ref, values, gate_ref, taps, key_first, levels_first, out0, out1, out2, out3,
+    conv_ref, values, gate_ref, taps, key_edge, levels_first, out0, out1, out2, out3,
     keys, raw, picked, wide, weighted_ref, whole, normals, levels, sems,
 ):
     core, mine = core_place()
@@ -175,11 +168,12 @@
     levels[1] = jnp.broadcast_to(through, (8, 128))
     levels_first[0] = tail_weight[:, 0:128]
     levels_first[1] = levels[1]
-    same = same_request(lengths_ref, offset, length)
+    same = same_request(lengths_ref, offset + iota((length, 128), 0))
     normals[...] = jnp.zeros_like(normals)
     for copy in copies[:3]:
         copy.wait()
-    key_first[...] = keys[0:16, :]
+    key_edge[0] = keys[0:16, :]
+    key_edge[1] = keys[length - 16 :, :]
     step = 128
     for i in range(per_core):
         columns = slice(i * key_width, (i + 1) * key_width)
@@ -220,39 +214,43 @@
         )
 
 
-def pick_tail(core, which, tail_ref, tail_other, columns):
-    rows = [ref[which, :, columns].astype(F32) for ref in (tail_ref, tail_other)]
-    return jnp.where(core == 0, rows[0], rows[1])[TAIL - 8 :]
-
-
-def first_kernel(
-    per_core, length, lengths_ref, tail_ref, tail_other, taps, key_first, values, levels_first,
-    conv_ref, out_ref, rows_ref, wide,
+def message_kernel(
+    per_core, query_ref, query_other, key_edge, values, levels_first, out_ref, rows_ref, tail, sems
 ):
     core, _ = core_place()
-    width = key_first.shape[1]
-    key_width = width // per_core
-    split = tail_ref.shape[2] > width
-    tail_columns = pl.ds(pl.multiple_of(core * width, 128) if split else 0, width)
-    tail = pick_tail(core, 1, tail_ref, tail_other, tail_columns)
-    offset = lax.axis_index("seq") // 2 * length
-    same = same_request(lengths_ref, offset, 16)
+    width = key_edge.shape[2]
+    split = query_ref.shape[1] > width
+    columns = pl.ds(pl.multiple_of(core * width, 128) if split else 0, width)
+    last = pl.ds(query_ref.shape[0] - 16, 16)
+    for ref, here in ((query_ref, core == 1), (query_other, core == 0)):
+
+        def fetch(ref=ref):
+            copy = pltpu.make_async_copy(ref.at[last, columns], tail, sems.at[0])
+            copy.start()
+            copy.wait()
+
+        pl.when(here)(fetch)
+    rows_ref[...] = jnp.zeros_like(rows_ref)
+    at = 0
+    for block in (
+        key_edge[0].astype(F32)[0:FIRST],
+        values[0:16, :].astype(F32)[0:FIRST],
+        key_edge[1].astype(F32)[16 - FIRST :],
+        tail[...].astype(F32)[16 - FIRST :],
+    ):
+        for j in range(block.shape[1] // 128):
+            rows_ref[at : at + FIRST, :] = block[:, j * 128 : (j + 1) * 128]
+            at += FIRST
+    lane, span = iota((1, 128), 1), 64 // per_core
+    line = jnp.zeros((1, 128), F32)
     for i in range(per_core):
-        columns = slice(i * key_width, (i + 1) * key_width)
-        wide[0:8, :] = tail[:, columns]
-        wide[8:, :] = key_first[:, columns].astype(F32)
-        conv_ref[:, columns] = conv_rows(same, 0, 16, taps, columns, wide)
-    rows_ref[...] = jnp.zeros_like(rows_ref)
-    keys, first = conv_ref[...].astype(F32), values[0:16, :].astype(F32)
-    at = 0
-    for block in (keys, first):
-        for j in range(block.shape[1] // 128):
-            rows_ref[at : at + FIRST, :] = block[0:FIRST, j * 128 : (j + 1) * 128]
-            at += FIRST
-    for k in range(2):
-        for part in split3(levels_first[k]):
-            rows_ref[at : at + per_core, :] = part[0:per_core]
-            at += per_core
+        ends, decay = levels_first[0, i : i + 1, :], levels_first[1, i : i + 1, :]
+        if i > 0:
+            ends = pltpu.roll(ends, i * span, 1)
+        line = jnp.where((lane >= i * span) & (lane < (i + 1) * span), ends, line)
+        line = jnp.where((lane >= 64 + i * span) & (lane < 64 + (i + 1) * span), decay, line)
+    for p, part in enumerate(split3(line)):
+        rows_ref[at + p : at + p + 1, :] = part
     out_ref[0] = rows_ref[...].astype(BF16)
 
 
@@ -263,50 +261,80 @@
 
 
 def gathered_kernel(
-    per_core, key_width, offsets, near_ref, far_ref, keys_ref, values_ref, levels_ref,
-    key_rows, value_rows,
+    per_core, length, offsets, lengths_ref, near_ref, far_ref, taps, key_edge,
+    query_taps, query_edge,
+    keys_ref, values_ref, levels_ref, conv_ref, by_chip, wide, value_rows, level_rows, narrow,
 ):
     half = near_ref.shape[0]
+    chips = 2 * half
     me = lax.axis_index("seq") // 2
+    width = key_edge.shape[2]
+    key_width = width // per_core
     value_width = values_ref.shape[1]
-    count = 2 * half * FIRST
     key_blocks, value_blocks = key_width // 128, value_width // 128
-    base = FIRST * per_core * (key_blocks + value_blocks)
-    ends, decays = [], []
-    for g in range(2 * half):
-        rows = (near_ref[g] if g < half else far_ref[g - half]).astype(F32)
+    for k, off in enumerate(offsets):
+        message = near_ref[k] if k < half else far_ref[k - half]
+        by_chip[lax.bitwise_xor(me, off)] = message.astype(F32)
+    row = iota((16 * chips, 128), 0)
+    position = length * lax.shift_right_logical(row, 4) + lax.bitwise_and(row, 15) - 8
+    same = same_request(lengths_ref, position)
+    value_rows[...] = jnp.zeros_like(value_rows)
+    level_rows[...] = jnp.full_like(level_rows, 2 * very_negative)
+    values_at = FIRST * per_core * key_blocks
+    tails_at = values_at + FIRST * per_core * value_blocks
+    levels_at = tails_at + 2 * FIRST * per_core * key_blocks
+    span = 64 // per_core
+    lines = [
+        sum(by_chip[g, levels_at + p : levels_at + p + 1, :] for p in range(3))
+        for g in range(chips)
+    ]
+    square = iota((FIRST, 128), 0) == iota((FIRST, 128), 1)
+    for i in range(per_core):
+        wide[...] = jnp.zeros_like(wide)
+        since = jnp.zeros((1, 1), F32)
+        for g in reversed(range(chips)):
+            at = 16 * g + 8
+            for j in range(key_blocks):
+                columns = slice(j * 128, (j + 1) * 128)
+                source = FIRST * (i * key_blocks + j)
+                wide[8 + at : 8 + at + FIRST, columns] = by_chip[g, source : source + FIRST, :]
+                if g > 0:
+                    source += tails_at
+                    wide[8 + at - FIRST : 8 + at, columns] = by_chip[
+                        g - 1, source : source + FIRST, :
+                    ]
+            for j in range(value_blocks):
+                source = values_at + FIRST * (i * value_blocks + j)
+                value_rows[i * 16 * chips + at : i * 16 * chips + at + FIRST, j * 128 : (j + 1) * 128] = (
+                    by_chip[g, source : source + FIRST, :]
+                )
+            ends = lines[g]
+            if i > 0:
+                ends = pltpu.roll(ends, 128 - i * span, 1)
+            ends = jnp.where(g < me, ends + since, 2 * very_negative)
+            decay = lines[g][:, 64 + i * span : 64 + i * span + 1]
+            since = since + jnp.where(g < me, decay, 0.0)
+            column = jnp.sum(jnp.where(square, ends, 0.0), axis=1, keepdims=True)
+            level_rows[i * 16 * chips + at : i * 16 * chips + at + FIRST, :] = jnp.broadcast_to(
+                column, (FIRST, 128)
+            )
+        keys_ref[i * 16 * chips : (i + 1) * 16 * chips, :] = conv_rows(
+            same, 0, 16 * chips, taps, slice(i * key_width, (i + 1) * key_width), wide
+        )
+    values_ref[...] = value_rows[...].astype(BF16)
+    levels_ref[...] = level_rows[...]
+    same = same_request(lengths_ref, me * length + iota((16, 128), 0))
+    previous = jnp.maximum(me - 1, 0)
+    for which, (weights, edge) in enumerate(((query_taps, query_edge), (taps, key_edge))):
         for i in range(per_core):
-            at = i * count + g * FIRST
+            columns = slice(i * key_width, (i + 1) * key_width)
             for j in range(key_blocks):
-                source = FIRST * (i * key_blocks + j)
-                key_rows[at : at + FIRST, j * 128 : (j + 1) * 128] = rows[source : source + FIRST]
-            for j in range(value_blocks):
-                source = FIRST * (per_core * key_blocks + i * value_blocks + j)
-                value_rows[at : at + FIRST, j * 128 : (j + 1) * 128] = rows[source : source + FIRST]
-        levels = [
-            sum(
-                rows[base + (3 * k + p) * per_core : base + (3 * k + p + 1) * per_core]
-                for p in range(3)
-            )
-            for k in range(2)
-        ]
-        ends.append(levels[0])
-        decays.append(levels[1][:, 0:1])
-    keys_ref[...] = key_rows[...].astype(BF16)
-    values_ref[...] = value_rows[...].astype(BF16)
-    chips = [lax.bitwise_xor(me, off) for off in offsets]
-    square = iota((FIRST, 128), 0) == iota((FIRST, 128), 1)
-    for g in range(2 * half):
-        since = sum(
-            jnp.where((chips[k] > chips[g]) & (chips[k] < me), decays[k], 0.0)
-            for k in range(2 * half)
-            if k != g
-        )
-        here = jnp.where(chips[g] < me, ends[g] + since, 2 * very_negative)
-        for i in range(per_core):
-            column = jnp.sum(jnp.where(square, here[i : i + 1], 0.0), axis=1, keepdims=True)
-            at = i * count + g * FIRST
-            levels_ref[at : at + FIRST, :] = jnp.broadcast_to(column, (FIRST, 128))
+                source = tails_at + FIRST * ((1 - which) * per_core + i) * key_blocks + FIRST * j
+                narrow[8 - FIRST : 8, j * 128 : (j + 1) * 128] = by_chip[
+                    previous, source : source + FIRST, :
+                ]
+            narrow[8:, :] = edge[0, :, columns].astype(F32)
+            conv_ref[which, :, columns] = conv_rows(same, 0, 16, weights, columns, narrow)
 
 
 def shifted_stab(infos, ranks, upto):
@@ -399,13 +427,13 @@
 
 
 def query_kernel(
-    per_core, lengths_ref, query_ref, query_other, tail_ref, tail_other, taps_ref,
-    conv_ref, queries, taps, wide, sems,
+    per_core, lengths_ref, query_ref, query_other, taps_ref,
+    conv_ref, taps, edge_ref, queries, wide, sems,
 ):
     core, _ = core_place()
     length, width = queries.shape
     key_width = width // per_core
-    split = tail_ref.shape[2] > width
+    split = query_ref.shape[1] > width
     columns = pl.ds(pl.multiple_of(core * width, 128) if split else 0, width)
     copies = start_copies(
         sems,
@@ -413,13 +441,14 @@
         + by_core(core, query_ref, query_other, columns, queries),
     )
     offset = lax.axis_index("seq") // 2 * length
-    tail = pick_tail(core, 0, tail_ref, tail_other, columns)
-    same = same_request(lengths_ref, offset, length)
+    same = same_request(lengths_ref, offset + iota((length, 128), 0))
     for copy in copies:
         copy.wait()
+    edge_ref[0] = queries[0:16, :]
+    edge_ref[1] = queries[length - 16 :, :]
     for i in range(per_core):
         here = slice(i * key_width, (i + 1) * key_width)
-        wide[0:8, :] = tail[:, here]
+        wide[0:8, :] = jnp.zeros((8, key_width), F32)
         wide[8:, :] = queries[:, here].astype(F32)
         for start in range(0, length, 128):
             conv_ref[start : start + 128, here] = conv_rows(
@@ -428,16 +457,18 @@
 
 
 def intra_kernel(
-    per_core, lengths_ref, query_ref, key_ref, key_first, values, gate_ref,
-    numerator_ref, stats_ref, keys,
+    per_core, lengths_ref, query_conv, key_ref, conv_first, values, gate_ref,
+    query_ref, numerator_ref, stats_ref, keys,
 ):
     length, width = query_ref.shape
     key_width = width // per_core
     value_width = values.shape[1] // per_core
     key_scale = 1.0 / math.sqrt(key_width)
     offset = lax.axis_index("seq") // 2 * length
+    query_ref[...] = query_conv[...]
+    query_ref[0:16, :] = conv_first[0]
     keys[...] = key_ref[...]
-    keys[0:16, :] = key_first[...]
+    keys[0:16, :] = conv_first[1]
     gate, cumulative = gate_ref[0], gate_ref[1]
     by_token = cumulative.T
     segment = segment_of(lengths_ref, offset + iota((length, 1), 0))
@@ -649,24 +680,21 @@
         return lax.ppermute(x, "seq", [(i, i ^ off) for i in range(seq_count)])
 
     key_other, value_other = swap(key_input, 1), swap(value_input, 1)
-    tails, gates = call(
-        tail_kernel, (shape((2, TAIL, key_cols), BF16), shape((2, heads, length))), "hhhh",
-        [pltpu.SemaphoreType.DMA((4,))], "tails",
-    )(query_input, key_input, input_gate, forget_gate)
+    query_other = swap(query_input, 1)
+    gates = call(
+        gates_kernel, shape((2, heads, length)), "hh", [pltpu.SemaphoreType.DMA((2,))], "gates"
+    )(input_gate, forget_gate)
     gates_other = swap(gates, 1)
-    query_after, gates = lax.optimization_barrier((query_input, gates))
-    query_other = swap(query_after, 1)
-    tails = lax.ppermute(tails, "seq", [(i, i + 1) for i in range(seq_count - 1)])
 
     one = shape((rows * value_width // 128 + INFO, 128), BF16)
-    key_conv, values, gate_sums, taps, key_first, levels, *pieces = call(
+    key_conv, values, gate_sums, taps, key_edge, levels, *pieces = call(
         functools.partial(chip_kernel, per_core),
         (
             shape((chip_length, part_keys), BF16),
             shape((chip_length, part_values), BF16),
             shape((2, 8, chip_length)),
             shape((lags, part_keys)),
-            shape((16, part_keys), BF16),
+            shape((2, 16, part_keys), BF16),
             shape((2, 8, 128)),
         )
         + (one,) * 4,
@@ -690,33 +718,37 @@
     )
     states = [pieces[0]] + [swap(pieces[off], 2 * off) for off in (1, 2, 3)]
 
-    tails, key_first = lax.optimization_barrier((tails, key_first))
-    tails_other = swap(tails, 1)
-    count = FIRST * seq_count // 2
-    lines = per_core * (FIRST * (key_width + value_width) // 128 + 6)
+    count = 16 * seq_count // 2
+    lines = FIRST * per_core * (3 * key_width + value_width) // 128 + 3
     lines = -(-lines // 16) * 16
-    conv_first, message = call(
-        functools.partial(first_kernel, per_core, chip_length),
-        (shape((16, part_keys), BF16), shape((1, lines, 128), BF16)),
-        "s" + "v" * 6,
-        [pltpu.VMEM((lines, 128), F32), pltpu.VMEM((24, key_width), F32)],
-        "first_tokens",
-    )(request_lengths, tails, tails_other, taps, key_first, values, levels)
+    message = call(
+        functools.partial(message_kernel, per_core), shape((1, lines, 128), BF16), "havvv",
+        [
+            pltpu.VMEM((lines, 128), F32),
+            pltpu.VMEM((16, part_keys), BF16),
+            pltpu.SemaphoreType.DMA((1,)),
+        ],
+        "message",
+    )(query_input, query_other, key_edge, values, levels)
     bits = seq_count.bit_length() - 1
     steps = [4, 2, 8] if bits == 4 else [1 << b for b in range(1, bits)]
     near, far, offsets = message, swap(message, steps[0]), [0, steps[0] // 2]
-    query_conv = call(
-        functools.partial(query_kernel, per_core), shape((chip_length, part_keys), BF16),
-        "shavvh",
+    query_conv, query_taps, query_edge = call(
+        functools.partial(query_kernel, per_core),
+        (
+            shape((chip_length, part_keys), BF16),
+            shape((lags, part_keys)),
+            shape((2, 16, part_keys), BF16),
+        ),
+        "shah",
         [
             pltpu.VMEM((chip_length, part_keys), BF16),
-            pltpu.VMEM((lags, part_keys), F32),
             pltpu.VMEM((chip_length + 8, key_width), F32),
             pltpu.SemaphoreType.DMA((3,)),
         ],
         "query_conv",
         flops=1 << 30,
-    )(request_lengths, query_after, query_other, tails, tails_other, kernel_taps)
+    )(request_lengths, query_input, query_other, kernel_taps)
     states, query_conv, far = lax.optimization_barrier((states, query_conv, far))
     total = call(total_kernel, one, "vvvv", [], "group_total")(*states)
     flag = 3
@@ -742,23 +774,31 @@
     )
     gate_sums, near, *enter = lax.optimization_barrier((gate_sums, near, *enter))
     enter = [enter[0]] + [swap(enter[off], 2 * off) for off in (1, 2, 3)]
-    extras = call(
-        functools.partial(gathered_kernel, per_core, key_width, tuple(offsets)),
+    *extras, conv_first = call(
+        functools.partial(gathered_kernel, per_core, chip_length, tuple(offsets)),
         (
             shape((per_core * count, key_width), BF16),
             shape((per_core * count, value_width), BF16),
             shape((per_core * count, 128)),
+            shape((2, 16, part_keys), BF16),
         ),
-        "vv",
+        "svvvvvv",
         [
-            pltpu.VMEM((per_core * count, key_width), F32),
+            pltpu.VMEM((seq_count // 2, lines, 128), F32),
+            pltpu.VMEM((count + 8, key_width), F32),
             pltpu.VMEM((per_core * count, value_width), F32),
+            pltpu.VMEM((per_core * count, 128), F32),
+            pltpu.VMEM((24, key_width), F32),
         ],
         "gathered_first",
-    )(near, far)
+    )(request_lengths, near, far, taps, key_edge, query_taps, query_edge)
     inside = call(
         functools.partial(intra_kernel, per_core),
-        (shape((chip_length, part_values)), shape((3, chip_length, 128))),
+        (
+            shape((chip_length, part_keys), BF16),
+            shape((chip_length, part_values)),
+            shape((3, chip_length, 128)),
+        ),
         "svvvvv",
         [pltpu.VMEM((chip_length, part_keys), BF16)],
         "intra",
@@ -772,7 +812,7 @@
             pltpu.VMEM((4, INFO, 128), BF16),
         ],
         "head_out",
-    )(*enter, *extras, query_conv, *inside)
+    )(*enter, *extras, *inside)
     got = swap(send, 1)
 
     chunks = 2 if head_count == 2 and out_cols % 256 == 0 else 1

time: 57.7 us -> 56.1 us (0.972)
  starting transfers between devices: 21.9 us -> 18.9 us
  waiting for transfers between devices: 18.7 us -> 19.7 us
    ppermute x1 -> x0, starting transfers between devices: 2.32 us -> none  [on_device(): lax.ppermute(tails, 'seq', [(i, i + 1) for i in range(seq_count - 1)])]
    ppermute x16 -> x15, waiting for transfers between devices: 8.51 us -> 9.52 us  [swap(): return lax.ppermute(x, 'seq', [(i, i ^ off) for i in range(seq_count)])]
    ppermute x16 -> x15, starting transfers between devices: 17.4 us -> 16.7 us  [swap(): return lax.ppermute(x, 'seq', [(i, i ^ off) for i in range(seq_count)])]
  transfers between devices with their start and end apart: 19 -> 17, of which waited for: 7 -> 9; matrix products, arithmetic and copies ran while one was open for 0% -> 0% of each run, Pallas kernels for 23% -> 25%
where the time goes in v4:
time: 56.1 us; the launch traced here: 55.8 us
  waiting for transfers between devices  19.7 us (35%)
  starting transfers between devices  18.9 us (34%)
  Pallas kernels  17.1 us (30%)
    pallas_call x16, Pallas kernels, run(): inner(*(pltpu.with_memory_space_constraint(x, pltpu.HBM) if s in 'hs' els...  17.1 us
    ppermute x15, starting transfers between devices, swap(): return lax.ppermute(x, 'seq', [(i, i ^ off) for i in range(seq_count)])  16.7 us
    ppermute x2, waiting for transfers between devices, on_device(): lax.ppermute(c, 'head', [(i, i ^ off) for i in range(head_count)])  10.2 us
    ppermute x15, waiting for transfers between devices, swap(): return lax.ppermute(x, 'seq', [(i, i ^ off) for i in range(seq_count)])  9.52 us
    ppermute x2, starting transfers between devices, on_device(): lax.ppermute(c, 'head', [(i, i ^ off) for i in range(head_count)])  2.16 us
  transfers between devices with their start and end apart: 17, of which 9 were waited for; matrix products, arithmetic and copies ran while one was open for 0% of the time, Pallas kernels for 25%

profile of v4, /device:TPU:0, one launch (start us, length us, event | category | flops | bytes accessed | tf_op | source)
XLA Modules:
  0.0 55.8 jit_solution(10771767849029090148)
XLA Ops:
  1.0 0.7 %gates.1.gates_ref = f32[2,4,256]{2,1,0:T(4,128)S(1)} custom-call(f32[4,256]{1,0:T(4,128)} %input_ref.1, f32[4,256]{1,0:T(4,128)} %forget_ref.1), custom_call_target="tpu_custom_call" | custom-call | tf_op jit(solution)/shard_map/gates/pallas_call | solution.py:649
  1.8 1.6 %collective-permute-done.2.gates_other = f32[2,4,256]{2,1,0:T(4,128)S(1)} collective-permute-done((f32[2,4,256]{2,1,0:T(4,128)S(1)}, f32[2,4,256]{2,1,0:T(4,128)S(1)}, u32[]{:S(2)}, u32[]{:S(2)}) %collective-permute-start.2) | collective-permute-done | bytes 8224 | tf_op jit(solution)/shard_map/ppermute | solution.py:680
  3.7 3.4 %chip_state.1 = (bf16[512,512]{1,0:T(8,128)(2,1)S(1)}, bf16[512,1024]{1,0:T(8,128)(2,1)S(1)}, f32[2,8,512]{2,1,0:T(8,128)S(1)}, f32[4,512]{1,0:T(4,128)S(1)}, bf...) custom-call(s32[4]{0:T(128)} %lengths_ref.7, ...), custom_call_target="tpu_custom_call" | custom-call | flops 1073741824 | tf_op jit(solution)/shard_map/chip_state/pallas_call | solution.py:649
  7.1 3.0 %collective-permute-start.4 = (bf16[528,128]{1,0:T(8,128)(2,1)S(1)}, bf16[528,128]{1,0:T(8,128)(2,1)S(1)}, u32[]{:S(2)}, u32[]{:S(2)}) collective-permute-start(bf16[528,128]{1,0:T(8,128)(2,1)S(1)} %get-tuple-element.50), channel_id=1, source_target_pairs={{0,4},{2,6},{4,0},{6,2},{8,12},{10,14},{12,8},{14,10},{16,20},{18,... | collective-permute-start | bytes 405512 | tf_op jit(solution)/shard_map/ppermute | solution.py:680
  10.1 1.6 %collective-permute-start.5 = (bf16[528,128]{1,0:T(8,128)(2,1)S(1)}, bf16[528,128]{1,0:T(8,128)(2,1)S(1)}, u32[]{:S(2)}, u32[]{:S(2)}) collective-permute-start(bf16[528,128]{1,0:T(8,128)(2,1)S(1)} %get-tuple-element.51), channel_id=1, source_target_pairs={{0,8},{2,10},{4,12},{6,14},{8,0},{10,2},{12,4},{14,6},{16,24},{18,... | collective-permute-start | bytes 405512 | tf_op jit(solution)/shard_map/ppermute | solution.py:680
  11.8 2.0 %collective-permute-start.7 = (bf16[1,64,128]{2,1,0:T(8,128)(2,1)S(1)}, bf16[1,64,128]{2,1,0:T(8,128)(2,1)S(1)}, u32[]{:S(2)}, u32[]{:S(2)}) collective-permute-start(bf16[1,64,128]{2,1,0:T(8,128)(2,1)S(1)} %message.1.first_ref), channel_id=1, source_target_pairs={{0,8},{2,10},{4,12},{6,14},{8,0},{10,2},{12,4},{14,6},{16,24},{18,... | collective-permute-start | bytes 49160 | tf_op jit(solution)/shard_map/ppermute | solution.py:680
  13.8 2.6 %query_conv.1 = (bf16[512,512]{1,0:T(8,128)(2,1)S(1)}, f32[4,512]{1,0:T(4,128)S(1)}, bf16[2,16,512]{2,1,0:T(8,128)(2,1)S(1)}) custom-call(s32[4]{0:T(128)} %lengths_ref.7, bf16[256,1024]{1,0:T(8,128)(2,1)} %query_ref.3, bf16[256,1024]{1,0:T(8,128)(2,1)S(1)} %collective-permute-done.3.query_other, f32[2,4,1024]{2,1,0:T(4,128)} %taps_ref.3), custom_call_target="tpu_custom_call" | custom-call | flops 1073741824 | tf_op jit(solution)/shard_map/query_conv/pallas_call | solution.py:649
  16.5 2.2 %collective-permute-done.7.second_ref = bf16[1,64,128]{2,1,0:T(8,128)(2,1)S(1)} collective-permute-done((bf16[1,64,128]{2,1,0:T(8,128)(2,1)S(1)}, bf16[1,64,128]{2,1,0:T(8,128)(2,1)S(1)}, u32[]{:S(2)}, u32[]{:S(2)}) %collective-permute-start.7) | collective-permute-done | bytes 16416 | tf_op jit(solution)/shard_map/ppermute | solution.py:680
  18.9 3.7 %collective-permute-start.9 = (bf16[528,128]{1,0:T(8,128)(2,1)S(1)}, bf16[528,128]{1,0:T(8,128)(2,1)S(1)}, u32[]{:S(2)}, u32[]{:S(2)}) collective-permute-start(bf16[528,128]{1,0:T(8,128)(2,1)S(1)} %group_total.1), channel_id=1, source_target_pairs={{0,24},{2,26},{4,28},{6,30},{8,16},{10,18},{12,20},{14,22},{16,8},... | collective-permute-start | bytes 405512 | tf_op jit(solution)/shard_map/ppermute | solution.py:680
  22.6 1.3 %collective-permute-start.8 = (bf16[2,64,128]{2,1,0:T(8,128)(2,1)S(1)}, bf16[2,64,128]{2,1,0:T(8,128)(2,1)S(1)}, u32[]{:S(2)}, u32[]{:S(2)}) collective-permute-start(bf16[2,64,128]{2,1,0:T(8,128)(2,1)S(1)} %join.2.first_ref), channel_id=1, source_target_pairs={{0,4},{2,6},{4,0},{6,2},{8,12},{10,14},{12,8},{14,10},{16,20},{18,... | collective-permute-start | bytes 98312 | tf_op jit(solution)/shard_map/ppermute | solution.py:680
  23.9 2.6 %collective-permute-done.8.second_ref = bf16[2,64,128]{2,1,0:T(8,128)(2,1)S(1)} collective-permute-done((bf16[2,64,128]{2,1,0:T(8,128)(2,1)S(1)}, bf16[2,64,128]{2,1,0:T(8,128)(2,1)S(1)}, u32[]{:S(2)}, u32[]{:S(2)}) %collective-permute-start.8) | collective-permute-done | bytes 32800 | tf_op jit(solution)/shard_map/ppermute | solution.py:680
  27.2 1.3 %collective-permute-start.10 = (bf16[528,128]{1,0:T(8,128)(2,1)S(1)}, bf16[528,128]{1,0:T(8,128)(2,1)S(1)}, u32[]{:S(2)}, u32[]{:S(2)}) collective-permute-start(bf16[528,128]{1,0:T(8,128)(2,1)S(1)} %get-tuple-element.66), channel_id=1, source_target_pairs={{0,4},{2,6},{4,0},{6,2},{8,12},{10,14},{12,8},{14,10},{16,20},{18,... | collective-permute-start | bytes 405512 | tf_op jit(solution)/shard_map/ppermute | solution.py:680
  28.5 2.3 %collective-permute-start.11 = (bf16[528,128]{1,0:T(8,128)(2,1)S(1)}, bf16[528,128]{1,0:T(8,128)(2,1)S(1)}, u32[]{:S(2)}, u32[]{:S(2)}) collective-permute-start(bf16[528,128]{1,0:T(8,128)(2,1)S(1)} %get-tuple-element.67), channel_id=1, source_target_pairs={{0,8},{2,10},{4,12},{6,14},{8,0},{10,2},{12,4},{14,6},{16,24},{18,... | collective-permute-start | bytes 405512 | tf_op jit(solution)/shard_map/ppermute | solution.py:680
  31.8 1.4 %gathered_first.1 = (bf16[256,256]{1,0:T(8,128)(2,1)S(1)}, bf16[256,512]{1,0:T(8,128)(2,1)S(1)}, f32[256,128]{1,0:T(8,128)S(1)}, bf16[2,16,512]{2,1,0:T(8,128)(2,1)S(1)}) custom-call(s32[4]{0:T(128)} %lengths_ref.7, bf16[4,64,128]{2,1,0:T(8,128)(2,1)S(1)} %join.3.near_ref, bf16[4,64,128]{2,1,0:T(8,128)(2,1)S(1)} %collective-permute-done.13.far_ref, ...), custom_call_target="tpu_custom_call" | custom-call | tf_op jit(solution)/shard_map/gathered_first/pallas_call | solution.py:649
  33.2 2.5 %intra.1 = (bf16[512,512]{1,0:T(8,128)(2,1)S(1)}, f32[512,1024]{1,0:T(8,128)S(1)}, f32[3,512,128]{2,1,0:T(8,128)S(1)}) custom-call(s32[4]{0:T(128)} %lengths_ref.7, bf16[512,512]{1,0:T(8,128)(2,1)S(1)} %get-tuple-element.76.query_conv, bf16[512,512]{1,0:T(8,128)(2,1)S(1)} %get-tuple-element.77.key_ref, bf16[2,16,512]{2,1,0:T(8,128)(2,1)S(1)} %get-tuple-element.78.conv_first, ...), custom_call_target="tpu_custom_call" | custom-call | flops 4294967296 | tf_op jit(solution)/shard_map/intra/pallas_call | solution.py:649
  35.7 1.1 %collective-permute-done.12.got3 = bf16[528,128]{1,0:T(8,128)(2,1)S(1)} collective-permute-done((bf16[528,128]{1,0:T(8,128)(2,1)S(1)}, bf16[528,128]{1,0:T(8,128)(2,1)S(1)}, u32[]{:S(2)}, u32[]{:S(2)}) %collective-permute-start.12) | collective-permute-done | bytes 135200 | tf_op jit(solution)/shard_map/ppermute | solution.py:680
  36.8 1.7 %head_out.1 = (bf16[256,1024]{1,0:T(8,128)(2,1)S(1)}, bf16[256,1024]{1,0:T(8,128)(2,1)S(1)}) custom-call(bf16[528,128]{1,0:T(8,128)(2,1)S(1)} %get-tuple-element.65.own_ref, bf16[528,128]{1,0:T(8,128)(2,1)S(1)} %collective-permute-done.10.got1, bf16[528,128]{1,0:T(8,128)(2,1)S(1)} %collective-permute-done.11.got2, ...), custom_call_target="tpu_custom_call" | custom-call | tf_op jit(solution)/shard_map/head_out/pallas_call | solution.py:649
  38.6 0.7 %project_kept.1.kept_ref = f32[256,1024]{1,0:T(8,128)S(1)} custom-call(bf16[256,1024]{1,0:T(8,128)(2,1)S(1)} %get-tuple-element.83.keep_ref.head_ref, bf16[2048,2048]{1,0:T(8,128)(2,1)S(1)} %bitcast.1), custom_call_target="tpu_custom_call" | custom-call | flops 2147483648 | tf_op jit(solution)/shard_map/project_kept/pallas_call | solution.py:649
  39.4 1.1 %collective-permute-done.14.got_ref.head_ref = bf16[256,1024]{1,0:T(8,128)(2,1)S(1)} collective-permute-done((bf16[256,1024]{1,0:T(8,128)(2,1)S(1)}, bf16[256,1024]{1,0:T(8,128)(2,1)S(1)}, u32[]{:S(2)}, u32[]{:S(2)}) %collective-permute-start.14) | collective-permute-done | bytes 524320 | tf_op jit(solution)/shard_map/ppermute | solution.py:680
  41.0 1.6 %collective-permute-start.15 = (bf16[256,512]{1,0:T(8,128)(2,1)S(1)}, bf16[256,512]{1,0:T(8,128)(2,1)S(1)}, u32[]{:S(2)}, u32[]{:S(2)}) collective-permute-start(bf16[256,512]{1,0:T(8,128)(2,1)S(1)} %project_other.2), channel_id=1, source_target_pairs={{0,1},{1,0},{2,3},{3,2},{4,5},{5,4},{6,7},{7,6},{8,9},{9,8},{10,11... | collective-permute-start | bytes 786440 | tf_op jit(solution)/shard_map/ppermute | solution.py:834
  43.6 1.2 %project_own.1.own_ref = f32[256,1024]{1,0:T(8,128)S(1)} custom-call(bf16[256,1024]{1,0:T(8,128)(2,1)S(1)} %get-tuple-element.83.keep_ref.head_ref, bf16[256,1024]{1,0:T(8,128)(2,1)S(1)} %collective-permute-done.14.got_ref.head_ref, bf16[2048,2048]{1,0:T(8,128)(2,1)S(1)} %bitcast.1), custom_call_target="tpu_custom_call" | custom-call | flops 4294967296 | tf_op jit(solution)/shard_map/project_own/pallas_call | solution.py:649
  44.8 5.4 %collective-permute-done.15.refs_0_ = bf16[256,512]{1,0:T(8,128)(2,1)S(1)} collective-permute-done((bf16[256,512]{1,0:T(8,128)(2,1)S(1)}, bf16[256,512]{1,0:T(8,128)(2,1)S(1)}, u32[]{:S(2)}, u32[]{:S(2)}) %collective-permute-start.15) | collective-permute-done | bytes 262176 | tf_op jit(solution)/shard_map/ppermute | solution.py:834
  50.2 4.8 %collective-permute-done.16.refs_1_ = bf16[256,512]{1,0:T(8,128)(2,1)S(1)} collective-permute-done((bf16[256,512]{1,0:T(8,128)(2,1)S(1)}, bf16[256,512]{1,0:T(8,128)(2,1)S(1)}, u32[]{:S(2)}, u32[]{:S(2)}) %collective-permute-start.16) | collective-permute-done | bytes 262176 | tf_op jit(solution)/shard_map/ppermute | solution.py:834
  55.0 0.8 %mixed_out.1 = bf16[256,1024]{1,0:T(8,128)(2,1)} custom-call(f32[256,1024]{1,0:T(8,128)S(1)} %project_own.1.own_ref, bf16[256,512]{1,0:T(8,128)(2,1)S(1)} %collective-permute-done.15.refs_0_, bf16[256,512]{1,0:T(8,128)(2,1)S(1)} %collective-permute-done.16.refs_1_), custom_call_target="tpu_custom_call" | custom-call | tf_op jit(solution)/shard_map/mixed_out/pallas_call | solution.py:649
  (31 shorter events, 4.8 us)
Async XLA Ops:
  0.0 3.7 %collective-permute-start.1 = (bf16[256,2048]{1,0:T(8,128)(2,1)}, bf16[256,2048]{1,0:T(8,128)(2,1)S(1)}, u32[]{:S(2)}, u32[]{:S(2)}) collective-permute-start(bf16[256,2048]{1,0:T(8,128)(2,1)} %value_ref.1), channel_id=1, source_target_pairs={{0,2},{2,0},{4,6},{6,4},{8,10},{10,8},{12,14},{14,12},{16,18},{18,... | collective-permute-start | bytes 3145736 | tf_op jit(solution)/shard_map/ppermute | solution.py:680
  0.5 3.3 %collective-permute-start = (bf16[256,1024]{1,0:T(8,128)(2,1)}, bf16[256,1024]{1,0:T(8,128)(2,1)S(1)}, u32[]{:S(2)}, u32[]{:S(2)}) collective-permute-start(bf16[256,1024]{1,0:T(8,128)(2,1)} %key_ref.1), channel_id=1, source_target_pairs={{0,2},{2,0},{4,6},{6,4},{8,10},{10,8},{12,14},{14,12},{16,18},{18,... | collective-permute-start | bytes 1572872 | tf_op jit(solution)/shard_map/ppermute | solution.py:680
  0.5 11.2 %collective-permute-start.3 = (bf16[256,1024]{1,0:T(8,128)(2,1)}, bf16[256,1024]{1,0:T(8,128)(2,1)S(1)}, u32[]{:S(2)}, u32[]{:S(2)}) collective-permute-start(bf16[256,1024]{1,0:T(8,128)(2,1)} %query_ref.3), channel_id=1, source_target_pairs={{0,2},{2,0},{4,6},{6,4},{8,10},{10,8},{12,14},{14,12},{16,18},{18,... | collective-permute-start | bytes 1572872 | tf_op jit(solution)/shard_map/ppermute | solution.py:680
  1.7 1.7 %collective-permute-start.2 = (f32[2,4,256]{2,1,0:T(4,128)S(1)}, f32[2,4,256]{2,1,0:T(4,128)S(1)}, u32[]{:S(2)}, u32[]{:S(2)}) collective-permute-start(f32[2,4,256]{2,1,0:T(4,128)S(1)} %gates.1.gates_ref), channel_id=1, source_target_pairs={{0,2},{2,0},{4,6},{6,4},{8,10},{10,8},{12,14},{14,12},{16,18},{18,... | collective-permute-start | bytes 24584 | tf_op jit(solution)/shard_map/ppermute | solution.py:680
  7.1 11.6 %collective-permute-start.4 = (bf16[528,128]{1,0:T(8,128)(2,1)S(1)}, bf16[528,128]{1,0:T(8,128)(2,1)S(1)}, u32[]{:S(2)}, u32[]{:S(2)}) collective-permute-start(bf16[528,128]{1,0:T(8,128)(2,1)S(1)} %get-tuple-element.50), channel_id=1, source_target_pairs={{0,4},{2,6},{4,0},{6,2},{8,12},{10,14},{12,8},{14,10},{16,20},{18,... | collective-permute-start | bytes 405512 | tf_op jit(solution)/shard_map/ppermute | solution.py:680
  10.1 8.6 %collective-permute-start.5 = (bf16[528,128]{1,0:T(8,128)(2,1)S(1)}, bf16[528,128]{1,0:T(8,128)(2,1)S(1)}, u32[]{:S(2)}, u32[]{:S(2)}) collective-permute-start(bf16[528,128]{1,0:T(8,128)(2,1)S(1)} %get-tuple-element.51), channel_id=1, source_target_pairs={{0,8},{2,10},{4,12},{6,14},{8,0},{10,2},{12,4},{14,6},{16,24},{18,... | collective-permute-start | bytes 405512 | tf_op jit(solution)/shard_map/ppermute | solution.py:680
  11.7 7.0 %collective-permute-start.6 = (bf16[528,128]{1,0:T(8,128)(2,1)S(1)}, bf16[528,128]{1,0:T(8,128)(2,1)S(1)}, u32[]{:S(2)}, u32[]{:S(2)}) collective-permute-start(bf16[528,128]{1,0:T(8,128)(2,1)S(1)} %get-tuple-element.52), channel_id=1, source_target_pairs={{0,12},{2,14},{4,8},{6,10},{8,4},{10,6},{12,0},{14,2},{16,28},{18,... | collective-permute-start | bytes 405512 | tf_op jit(solution)/shard_map/ppermute | solution.py:680
  11.8 6.9 %collective-permute-start.7 = (bf16[1,64,128]{2,1,0:T(8,128)(2,1)S(1)}, bf16[1,64,128]{2,1,0:T(8,128)(2,1)S(1)}, u32[]{:S(2)}, u32[]{:S(2)}) collective-permute-start(bf16[1,64,128]{2,1,0:T(8,128)(2,1)S(1)} %message.1.first_ref), channel_id=1, source_target_pairs={{0,8},{2,10},{4,12},{6,14},{8,0},{10,2},{12,4},{14,6},{16,24},{18,... | collective-permute-start | bytes 49160 | tf_op jit(solution)/shard_map/ppermute | solution.py:680
  18.9 7.6 %collective-permute-start.9 = (bf16[528,128]{1,0:T(8,128)(2,1)S(1)}, bf16[528,128]{1,0:T(8,128)(2,1)S(1)}, u32[]{:S(2)}, u32[]{:S(2)}) collective-permute-start(bf16[528,128]{1,0:T(8,128)(2,1)S(1)} %group_total.1), channel_id=1, source_target_pairs={{0,24},{2,26},{4,28},{6,30},{8,16},{10,18},{12,20},{14,22},{16,8},... | collective-permute-start | bytes 405512 | tf_op jit(solution)/shard_map/ppermute | solution.py:680
  22.6 3.9 %collective-permute-start.8 = (bf16[2,64,128]{2,1,0:T(8,128)(2,1)S(1)}, bf16[2,64,128]{2,1,0:T(8,128)(2,1)S(1)}, u32[]{:S(2)}, u32[]{:S(2)}) collective-permute-start(bf16[2,64,128]{2,1,0:T(8,128)(2,1)S(1)} %join.2.first_ref), channel_id=1, source_target_pairs={{0,4},{2,6},{4,0},{6,2},{8,12},{10,14},{12,8},{14,10},{16,20},{18,... | collective-permute-start | bytes 98312 | tf_op jit(solution)/shard_map/ppermute | solution.py:680
  26.5 5.3 %collective-permute-start.13 = (bf16[4,64,128]{2,1,0:T(8,128)(2,1)S(1)}, bf16[4,64,128]{2,1,0:T(8,128)(2,1)S(1)}, u32[]{:S(2)}, u32[]{:S(2)}) collective-permute-start(bf16[4,64,128]{2,1,0:T(8,128)(2,1)S(1)} %join.3.near_ref), channel_id=1, source_target_pairs={{0,16},{2,18},{4,20},{6,22},{8,24},{10,26},{12,28},{14,30},{16,0},... | collective-permute-start | bytes 196616 | tf_op jit(solution)/shard_map/ppermute | solution.py:680
  26.5 12.1 %slice-start = ((s8[8388608]{0:T(1024)(128)(4,1)}), s8[4194304]{0:T(1024)(128)(4,1)S(1)}, s32[]{:S(2)}) async-start(s8[8388608]{0:T(1024)(128)(4,1)} %bitcast), calls=%async_computation | async-start | bytes 8388608
  27.2 8.5 %collective-permute-start.10 = (bf16[528,128]{1,0:T(8,128)(2,1)S(1)}, bf16[528,128]{1,0:T(8,128)(2,1)S(1)}, u32[]{:S(2)}, u32[]{:S(2)}) collective-permute-start(bf16[528,128]{1,0:T(8,128)(2,1)S(1)} %get-tuple-element.66), channel_id=1, source_target_pairs={{0,4},{2,6},{4,0},{6,2},{8,12},{10,14},{12,8},{14,10},{16,20},{18,... | collective-permute-start | bytes 405512 | tf_op jit(solution)/shard_map/ppermute | solution.py:680
  28.5 7.2 %collective-permute-start.11 = (bf16[528,128]{1,0:T(8,128)(2,1)S(1)}, bf16[528,128]{1,0:T(8,128)(2,1)S(1)}, u32[]{:S(2)}, u32[]{:S(2)}) collective-permute-start(bf16[528,128]{1,0:T(8,128)(2,1)S(1)} %get-tuple-element.67), channel_id=1, source_target_pairs={{0,8},{2,10},{4,12},{6,14},{8,0},{10,2},{12,4},{14,6},{16,24},{18,... | collective-permute-start | bytes 405512 | tf_op jit(solution)/shard_map/ppermute | solution.py:680
  30.9 5.9 %collective-permute-start.12 = (bf16[528,128]{1,0:T(8,128)(2,1)S(1)}, bf16[528,128]{1,0:T(8,128)(2,1)S(1)}, u32[]{:S(2)}, u32[]{:S(2)}) collective-permute-start(bf16[528,128]{1,0:T(8,128)(2,1)S(1)} %get-tuple-element.68), channel_id=1, source_target_pairs={{0,12},{2,14},{4,8},{6,10},{8,4},{10,6},{12,0},{14,2},{16,28},{18,... | collective-permute-start | bytes 405512 | tf_op jit(solution)/shard_map/ppermute | solution.py:680
  33.2 5.5 %slice-start.1 = ((s8[8388608]{0:T(1024)(128)(4,1)}), s8[4194304]{0:T(1024)(128)(4,1)S(1)}, s32[]{:S(2)}) async-start(s8[8388608]{0:T(1024)(128)(4,1)} %bitcast), calls=%async_computation.1 | async-start | bytes 8388608
  38.5 2.0 %collective-permute-start.14 = (bf16[256,1024]{1,0:T(8,128)(2,1)S(1)}, bf16[256,1024]{1,0:T(8,128)(2,1)S(1)}, u32[]{:S(2)}, u32[]{:S(2)}) collective-permute-start(bf16[256,1024]{1,0:T(8,128)(2,1)S(1)} %get-tuple-element.84), channel_id=1, source_target_pairs={{0,2},{2,0},{4,6},{6,4},{8,10},{10,8},{12,14},{14,12},{16,18},{18,... | collective-permute-start | bytes 1572872 | tf_op jit(solution)/shard_map/ppermute | solution.py:680
  41.0 9.2 %collective-permute-start.15 = (bf16[256,512]{1,0:T(8,128)(2,1)S(1)}, bf16[256,512]{1,0:T(8,128)(2,1)S(1)}, u32[]{:S(2)}, u32[]{:S(2)}) collective-permute-start(bf16[256,512]{1,0:T(8,128)(2,1)S(1)} %project_other.2), channel_id=1, source_target_pairs={{0,1},{1,0},{2,3},{3,2},{4,5},{5,4},{6,7},{7,6},{8,9},{9,8},{10,11... | collective-permute-start | bytes 786440 | tf_op jit(solution)/shard_map/ppermute | solution.py:834
  43.0 12.0 %collective-permute-start.16 = (bf16[256,512]{1,0:T(8,128)(2,1)S(1)}, bf16[256,512]{1,0:T(8,128)(2,1)S(1)}, u32[]{:S(2)}, u32[]{:S(2)}) collective-permute-start(bf16[256,512]{1,0:T(8,128)(2,1)S(1)} %project_other.3), channel_id=1, source_target_pairs={{0,1},{1,0},{2,3},{3,2},{4,5},{5,4},{6,7},{7,6},{8,9},{9,8},{10,11... | collective-permute-start | bytes 786440 | tf_op jit(solution)/shard_map/ppermute | solution.py:834

commit v5 on v4

--- a/solution.py
+++ b/solution.py
@@ -504,16 +504,47 @@
             stats_ref[k, b * step : (b + 1) * step, :] = stats[b][k]
 
 
-def head_kernel(
+def head_rows(
+    per_core, start, memory, parts, stabs, query_ref, numerator_ref, stats_ref, out_ref
+):
+    step = out_ref.shape[0]
+    key_width = query_ref.shape[1] // per_core
+    value_width = memory.shape[1]
+    key_scale = 1.0 / math.sqrt(key_width)
+    span = pl.ds(pl.multiple_of(start, step), step)
+    queries = [query_ref[span, i * key_width : (i + 1) * key_width] for i in range(per_core)]
+    from_normal = sum(
+        dot(q, parts[i * 128 : (i + 1) * 128, :], ((1,), (1,))) for i, q in enumerate(queries)
+    )
+    from_normal = (
+        from_normal
+        + pltpu.roll(from_normal, 128 - 8, 1)
+        + pltpu.roll(from_normal, 128 - 16, 1)
+    )
+    row_max = stats_ref[1, span, :]
+    carried = stabs[0:1, :] + stats_ref[2, span, :]
+    m = jnp.maximum(row_max, carried)
+    w_here = jnp.exp(row_max - m)
+    w_in = jnp.exp(carried - m) * key_scale
+    denominator = w_here * stats_ref[0, span, :] + w_in * from_normal
+    scale = 1.0 / jnp.maximum(jnp.abs(denominator), 1.0)
+    w_here, w_in = w_here * scale, w_in * scale
+    for i in range(per_core):
+        columns = slice(i * value_width, (i + 1) * value_width)
+        from_memory = dot(queries[i], memory[i * key_width : (i + 1) * key_width, :])
+        out_ref[:, columns] = (
+            w_here[:, i : i + 1] * numerator_ref[span, columns] + w_in[:, i : i + 1] * from_memory
+        ).astype(BF16)
+
+
+def head_send_kernel(
     per_core, own_ref, got1, got2, got3, keys_ref, values_ref, levels_ref,
-    query_ref, numerator_ref, stats_ref, keep_ref, send_ref, memory, info,
+    query_ref, numerator_ref, stats_ref, send_ref, memory, parts, stabs, info,
 ):
     core, mine = core_place()
     key_width = query_ref.shape[1] // per_core
-    value_width = numerator_ref.shape[1] // per_core
-    key_scale = 1.0 / math.sqrt(key_width)
+    value_width = memory.shape[1]
     rows = query_ref.shape[1] // 4
-    step = keep_ref.shape[0]
     for off, ref in enumerate((own_ref, got1, got2, got3)):
         piece = piece_of(mine, off)
         start = pl.multiple_of(piece * rows, rows)
@@ -522,8 +553,7 @@
         info[piece] = ref[ref.shape[0] - INFO :, :]
     count = keys_ref.shape[0] // per_core
     row, lane = iota((128, key_width), 0), iota((1, 128), 1)
-    stabs = jnp.full((1, 128), very_negative, F32)
-    parts = []
+    levels = jnp.full((1, 128), very_negative, F32)
     for i in range(per_core):
         normal, stab, _ = read_info(info.at[i * key_width // rows], key_width)
         here = slice(i * key_width, (i + 1) * key_width)
@@ -534,43 +564,26 @@
             memory[here, :].astype(F32)
             + dot(weighted.astype(BF16), values_ref[extra, :], ((0,), (0,)))
         ).astype(BF16)
-        stabs = jnp.where(lane == i, stab, stabs)
+        levels = jnp.where(lane == i, stab, levels)
         block = jnp.zeros((128, key_width), F32)
         for k, part in enumerate(split3(normal)):
             block = jnp.where(row == 8 * k + i, part, block)
-        parts.append(block.astype(BF16))
-    for b in range(2):
-        span = slice(b * step, (b + 1) * step)
-        queries = [
-            query_ref[span, i * key_width : (i + 1) * key_width] for i in range(per_core)
-        ]
-        from_normal = sum(dot(q, p, ((1,), (1,))) for q, p in zip(queries, parts))
-        from_normal = (
-            from_normal
-            + pltpu.roll(from_normal, 128 - 8, 1)
-            + pltpu.roll(from_normal, 128 - 16, 1)
-        )
-        row_max = stats_ref[1, span, :]
-        carried = stabs + stats_ref[2, span, :]
-        m = jnp.maximum(row_max, carried)
-        w_here = jnp.exp(row_max - m)
-        w_in = jnp.exp(carried - m) * key_scale
-        denominator = w_here * stats_ref[0, span, :] + w_in * from_normal
-        scale = 1.0 / jnp.maximum(jnp.abs(denominator), 1.0)
-        w_here, w_in = w_here * scale, w_in * scale
-        for i in range(per_core):
-            columns = slice(i * value_width, (i + 1) * value_width)
-            from_memory = dot(queries[i], memory[i * key_width : (i + 1) * key_width, :])
-            head_out = (
-                w_here[:, i : i + 1] * numerator_ref[span, columns]
-                + w_in[:, i : i + 1] * from_memory
-            ).astype(BF16)
-
-            def write(ref, columns=columns, head_out=head_out):
-                ref[:, columns] = head_out
-
-            pl.when(core == b)(functools.partial(write, keep_ref))
-            pl.when(core != b)(functools.partial(write, send_ref))
+        parts[i * 128 : (i + 1) * 128, :] = block.astype(BF16)
+    stabs[...] = jnp.broadcast_to(levels, stabs.shape)
+    start = (1 - core) * send_ref.shape[0]
+    head_rows(
+        per_core, start, memory, parts, stabs, query_ref, numerator_ref, stats_ref, send_ref
+    )
+
+
+def head_keep_kernel(
+    per_core, memory, parts, stabs, query_ref, numerator_ref, stats_ref, keep_ref
+):
+    core, _ = core_place()
+    start = core * keep_ref.shape[0]
+    head_rows(
+        per_core, start, memory, parts, stabs, query_ref, numerator_ref, stats_ref, keep_ref
+    )
 
 
 def weight_part(weight_ref, half, rows, start, width):
@@ -605,33 +618,30 @@
     ) + dot(got_ref[...], weight_part(weight_ref, 1 - core, rows, start, width))
 
 
-def sum_kernel(chunks, own_ref, *refs):
-    *arrived, out_ref, held, sems = refs
-    width = own_ref.shape[1] // chunks
+def sum_kernel(chunk, count, own_ref, *refs):
+    arrived, (out_ref, held, sems) = refs[:count], refs[-3:]
+    width = held.shape[1]
+    columns = pl.ds(chunk * width, width)
     parts = sems.shape[0]
     step = own_ref.shape[0] // parts
     copies = []
     for part in range(parts):
         rows = slice(part * step, (part + 1) * step)
-        for c in range(chunks):
-            columns = slice(c * width, (c + 1) * width)
-            total = own_ref[rows, columns]
-            for ref in arrived[c::chunks]:
-                total = total + ref[rows, :].astype(F32)
-            held[rows, columns] = total.astype(held.dtype)
+        total = own_ref[rows, chunk * width : (chunk + 1) * width]
+        for ref in arrived:
+            total = total + ref[rows, :].astype(F32)
+        held[rows, :] = total.astype(held.dtype)
+        span = pl.ds(part * step, step)
         copies.append(
-            pltpu.make_async_copy(
-                held.at[pl.ds(part * step, step), :],
-                out_ref.at[pl.ds(part * step, step), :],
-                sems.at[part],
-            )
+            pltpu.make_async_copy(held.at[span, :], out_ref.at[span, columns], sems.at[part])
         )
         copies[-1].start()
     for copy in copies:
         copy.wait()
 
 
-def call(kernel, out_shape, spaces, scratch, name, flops=0, nbytes=0, limit=24, out=pltpu.VMEM):
+def call(kernel, out_shape, spaces, scratch, name, flops=0, nbytes=0, limit=24, out=pltpu.VMEM,
+         aliases=None):
     place = {"v": pltpu.VMEM, "s": pltpu.SMEM, "a": pl.ANY, "h": pl.ANY}
     outs = jax.tree.map(lambda _: pl.BlockSpec(memory_space=out), out_shape)
     inner = pl.pallas_call(
@@ -643,6 +653,7 @@
         compiler_params=pltpu.CompilerParams(vmem_limit_bytes=limit << 20),
         cost_estimate=pl.CostEstimate(flops=flops, bytes_accessed=nbytes, transcendentals=0),
         name=name,
+        input_output_aliases=aliases or {},
     )
 
     def run(*args):
@@ -804,44 +815,57 @@
         "intra",
         flops=4 << 30,
     )(request_lengths, query_conv, key_conv, conv_first, values, gate_sums)
-    half = shape((length, part_values), BF16)
-    keep, send = call(
-        functools.partial(head_kernel, per_core), (half, half), "v" * 10,
-        [
-            pltpu.VMEM((part_keys, value_width), BF16),
-            pltpu.VMEM((4, INFO, 128), BF16),
-        ],
-        "head_out",
+    half_out = shape((length, part_values), BF16)
+    send, *entered = call(
+        functools.partial(head_send_kernel, per_core),
+        (
+            half_out,
+            shape((part_keys, value_width), BF16),
+            shape((128 * per_core, key_width), BF16),
+            shape((8, 128)),
+        ),
+        "v" * 10, [pltpu.VMEM((4, INFO, 128), BF16)], "head_send",
     )(*enter, *extras, *inside)
+    keep = call(
+        functools.partial(head_keep_kernel, per_core), half_out, "v" * 6, [], "head_keep",
+        flops=1 << 30,
+    )(*entered, *inside)
     got = swap(send, 1)
 
     chunks = 2 if head_count == 2 and out_cols % 256 == 0 else 1
     piece = out_cols // chunks
     arrived = []
+    mixed = call(
+        own_kernel, shape((length, out_cols)), "vvv", [], "project_own", flops=4 << 30
+    )(keep, got, output_weight)
     for off in range(1, head_count):
         kept = call(
             functools.partial(keep_kernel, off), shape((length, out_cols)), "vv", [],
             "project_kept", flops=2 << 30,
         )(keep, output_weight)
-        columns = [
-            call(
+        columns, after = [], got
+        for chunk in range(chunks):
+            part = call(
                 functools.partial(send_kernel, off, chunk), shape((length, piece), BF16), "vvv",
                 [], "project_other",
-            )(got, output_weight, kept)
-            for chunk in range(chunks)
+            )(after, output_weight, kept)
+            columns.append(
+                lax.ppermute(part, "head", [(i, i ^ off) for i in range(head_count)])
+            )
+            after, mixed = lax.optimization_barrier((got, mixed))
+        arrived.append(columns)
+    out = []
+    for chunk in range(chunks):
+        out = [
+            call(
+                functools.partial(sum_kernel, chunk, len(arrived)),
+                shape((length, out_cols), BF16),
+                "v" * (1 + len(arrived)) + "a" * len(out),
+                [pltpu.VMEM((length, piece), BF16), pltpu.SemaphoreType.DMA((4,))],
+                "mixed_out", out=pl.ANY, aliases={1 + len(arrived): 0} if out else None,
+            )(mixed, *(columns[chunk] for columns in arrived), *out)
         ]
-        arrived.append(
-            [lax.ppermute(c, "head", [(i, i ^ off) for i in range(head_count)]) for c in columns]
-        )
-    mixed = call(
-        own_kernel, shape((length, out_cols)), "vvv", [], "project_own", flops=4 << 30
-    )(keep, got, output_weight)
-    return call(
-        functools.partial(sum_kernel, chunks), shape((length, out_cols), BF16),
-        "v" * (1 + chunks * len(arrived)),
-        [pltpu.VMEM((length, out_cols), BF16), pltpu.SemaphoreType.DMA((4,))],
-        "mixed_out", out=pl.ANY,
-    )(mixed, *(c for columns in arrived for c in columns))
+    return out[0]
 
 
 def solution(mesh):

time: 56.1 us -> 55.2 us (0.984)
  waiting for transfers between devices: 19.7 us -> 18.3 us
    ppermute x2, waiting for transfers between devices: 10.2 us -> 9.41 us  [on_device(): lax.ppermute(part, 'head', [(i, i ^ off) for i in range(head_count)])]
    ppermute x15, waiting for transfers between devices: 9.52 us -> 8.93 us  [swap(): return lax.ppermute(x, 'seq', [(i, i ^ off) for i in range(seq_count)])]
    pallas_call x16 -> x18, Pallas kernels: 17.1 us -> 17.5 us  [run(): inner(*(pltpu.with_memory_space_constraint(x, pltpu.HBM) if s in 'hs' els...]
  transfers between devices with their start and end apart: 17 -> 17, of which waited for: 9 -> 9; matrix products, arithmetic and copies ran while one was open for 0% -> 0% of each run, Pallas kernels for 25% -> 28%
where the time goes in v5:
time: 55.2 us; the launch traced here: 54.9 us
  starting transfers between devices  18.9 us (34%)
  waiting for transfers between devices  18.3 us (33%)
  Pallas kernels  17.5 us (32%)
    pallas_call x18, Pallas kernels, run(): inner(*(pltpu.with_memory_space_constraint(x, pltpu.HBM) if s in 'hs' els...  17.5 us
    ppermute x15, starting transfers between devices, swap(): return lax.ppermute(x, 'seq', [(i, i ^ off) for i in range(seq_count)])  16.7 us
    ppermute x2, waiting for transfers between devices, on_device(): lax.ppermute(part, 'head', [(i, i ^ off) for i in range(head_count)])  9.41 us
    ppermute x15, waiting for transfers between devices, swap(): return lax.ppermute(x, 'seq', [(i, i ^ off) for i in range(seq_count)])  8.93 us
    ppermute x2, starting transfers between devices, on_device(): lax.ppermute(part, 'head', [(i, i ^ off) for i in range(head_count)])  2.16 us
  transfers between devices with their start and end apart: 17, of which 9 were waited for; matrix products, arithmetic and copies ran while one was open for 0% of the time, Pallas kernels for 28%

profile of v5, /device:TPU:0, one launch (start us, length us, event | category | flops | bytes accessed | tf_op | source)
XLA Modules:
  0.0 54.9 jit_solution(10438349955325545868)
XLA Ops:
  1.0 0.7 %gates.1.gates_ref = f32[2,4,256]{2,1,0:T(4,128)S(1)} custom-call(f32[4,256]{1,0:T(4,128)} %input_ref.1, f32[4,256]{1,0:T(4,128)} %forget_ref.1), custom_call_target="tpu_custom_call" | custom-call | tf_op jit(solution)/shard_map/gates/pallas_call | solution.py:660
  1.8 1.6 %collective-permute-done.2.gates_other = f32[2,4,256]{2,1,0:T(4,128)S(1)} collective-permute-done((f32[2,4,256]{2,1,0:T(4,128)S(1)}, f32[2,4,256]{2,1,0:T(4,128)S(1)}, u32[]{:S(2)}, u32[]{:S(2)}) %collective-permute-start.2) | collective-permute-done | bytes 8224 | tf_op jit(solution)/shard_map/ppermute | solution.py:691
  3.7 3.4 %chip_state.1 = (bf16[512,512]{1,0:T(8,128)(2,1)S(1)}, bf16[512,1024]{1,0:T(8,128)(2,1)S(1)}, f32[2,8,512]{2,1,0:T(8,128)S(1)}, f32[4,512]{1,0:T(4,128)S(1)}, bf...) custom-call(s32[4]{0:T(128)} %lengths_ref.7, ...), custom_call_target="tpu_custom_call" | custom-call | flops 1073741824 | tf_op jit(solution)/shard_map/chip_state/pallas_call | solution.py:660
  7.1 3.0 %collective-permute-start.4 = (bf16[528,128]{1,0:T(8,128)(2,1)S(1)}, bf16[528,128]{1,0:T(8,128)(2,1)S(1)}, u32[]{:S(2)}, u32[]{:S(2)}) collective-permute-start(bf16[528,128]{1,0:T(8,128)(2,1)S(1)} %get-tuple-element.55), channel_id=1, source_target_pairs={{0,4},{2,6},{4,0},{6,2},{8,12},{10,14},{12,8},{14,10},{16,20},{18,... | collective-permute-start | bytes 405512 | tf_op jit(solution)/shard_map/ppermute | solution.py:691
  10.1 1.6 %collective-permute-start.5 = (bf16[528,128]{1,0:T(8,128)(2,1)S(1)}, bf16[528,128]{1,0:T(8,128)(2,1)S(1)}, u32[]{:S(2)}, u32[]{:S(2)}) collective-permute-start(bf16[528,128]{1,0:T(8,128)(2,1)S(1)} %get-tuple-element.56), channel_id=1, source_target_pairs={{0,8},{2,10},{4,12},{6,14},{8,0},{10,2},{12,4},{14,6},{16,24},{18,... | collective-permute-start | bytes 405512 | tf_op jit(solution)/shard_map/ppermute | solution.py:691
  11.8 2.0 %collective-permute-start.7 = (bf16[1,64,128]{2,1,0:T(8,128)(2,1)S(1)}, bf16[1,64,128]{2,1,0:T(8,128)(2,1)S(1)}, u32[]{:S(2)}, u32[]{:S(2)}) collective-permute-start(bf16[1,64,128]{2,1,0:T(8,128)(2,1)S(1)} %message.1.first_ref), channel_id=1, source_target_pairs={{0,8},{2,10},{4,12},{6,14},{8,0},{10,2},{12,4},{14,6},{16,24},{18,... | collective-permute-start | bytes 49160 | tf_op jit(solution)/shard_map/ppermute | solution.py:691
  13.8 2.6 %query_conv.1 = (bf16[512,512]{1,0:T(8,128)(2,1)S(1)}, f32[4,512]{1,0:T(4,128)S(1)}, bf16[2,16,512]{2,1,0:T(8,128)(2,1)S(1)}) custom-call(s32[4]{0:T(128)} %lengths_ref.7, bf16[256,1024]{1,0:T(8,128)(2,1)} %query_ref.3, bf16[256,1024]{1,0:T(8,128)(2,1)S(1)} %collective-permute-done.3.query_other, f32[2,4,1024]{2,1,0:T(4,128)} %taps_ref.3), custom_call_target="tpu_custom_call" | custom-call | flops 1073741824 | tf_op jit(solution)/shard_map/query_conv/pallas_call | solution.py:660
  16.5 2.2 %collective-permute-done.7.second_ref = bf16[1,64,128]{2,1,0:T(8,128)(2,1)S(1)} collective-permute-done((bf16[1,64,128]{2,1,0:T(8,128)(2,1)S(1)}, bf16[1,64,128]{2,1,0:T(8,128)(2,1)S(1)}, u32[]{:S(2)}, u32[]{:S(2)}) %collective-permute-start.7) | collective-permute-done | bytes 16416 | tf_op jit(solution)/shard_map/ppermute | solution.py:691
  18.9 3.7 %collective-permute-start.9 = (bf16[528,128]{1,0:T(8,128)(2,1)S(1)}, bf16[528,128]{1,0:T(8,128)(2,1)S(1)}, u32[]{:S(2)}, u32[]{:S(2)}) collective-permute-start(bf16[528,128]{1,0:T(8,128)(2,1)S(1)} %group_total.1), channel_id=1, source_target_pairs={{0,24},{2,26},{4,28},{6,30},{8,16},{10,18},{12,20},{14,22},{16,8},... | collective-permute-start | bytes 405512 | tf_op jit(solution)/shard_map/ppermute | solution.py:691
  22.6 1.3 %collective-permute-start.8 = (bf16[2,64,128]{2,1,0:T(8,128)(2,1)S(1)}, bf16[2,64,128]{2,1,0:T(8,128)(2,1)S(1)}, u32[]{:S(2)}, u32[]{:S(2)}) collective-permute-start(bf16[2,64,128]{2,1,0:T(8,128)(2,1)S(1)} %join.2.first_ref), channel_id=1, source_target_pairs={{0,4},{2,6},{4,0},{6,2},{8,12},{10,14},{12,8},{14,10},{16,20},{18,... | collective-permute-start | bytes 98312 | tf_op jit(solution)/shard_map/ppermute | solution.py:691
  23.9 2.6 %collective-permute-done.8.second_ref = bf16[2,64,128]{2,1,0:T(8,128)(2,1)S(1)} collective-permute-done((bf16[2,64,128]{2,1,0:T(8,128)(2,1)S(1)}, bf16[2,64,128]{2,1,0:T(8,128)(2,1)S(1)}, u32[]{:S(2)}, u32[]{:S(2)}) %collective-permute-start.8) | collective-permute-done | bytes 32800 | tf_op jit(solution)/shard_map/ppermute | solution.py:691
  27.2 1.3 %collective-permute-start.10 = (bf16[528,128]{1,0:T(8,128)(2,1)S(1)}, bf16[528,128]{1,0:T(8,128)(2,1)S(1)}, u32[]{:S(2)}, u32[]{:S(2)}) collective-permute-start(bf16[528,128]{1,0:T(8,128)(2,1)S(1)} %get-tuple-element.71), channel_id=1, source_target_pairs={{0,4},{2,6},{4,0},{6,2},{8,12},{10,14},{12,8},{14,10},{16,20},{18,... | collective-permute-start | bytes 405512 | tf_op jit(solution)/shard_map/ppermute | solution.py:691
  28.5 2.3 %collective-permute-start.11 = (bf16[528,128]{1,0:T(8,128)(2,1)S(1)}, bf16[528,128]{1,0:T(8,128)(2,1)S(1)}, u32[]{:S(2)}, u32[]{:S(2)}) collective-permute-start(bf16[528,128]{1,0:T(8,128)(2,1)S(1)} %get-tuple-element.72), channel_id=1, source_target_pairs={{0,8},{2,10},{4,12},{6,14},{8,0},{10,2},{12,4},{14,6},{16,24},{18,... | collective-permute-start | bytes 405512 | tf_op jit(solution)/shard_map/ppermute | solution.py:691
  31.8 1.4 %gathered_first.1 = (bf16[256,256]{1,0:T(8,128)(2,1)S(1)}, bf16[256,512]{1,0:T(8,128)(2,1)S(1)}, f32[256,128]{1,0:T(8,128)S(1)}, bf16[2,16,512]{2,1,0:T(8,128)(2,1)S(1)}) custom-call(s32[4]{0:T(128)} %lengths_ref.7, bf16[4,64,128]{2,1,0:T(8,128)(2,1)S(1)} %join.3.near_ref, bf16[4,64,128]{2,1,0:T(8,128)(2,1)S(1)} %collective-permute-done.13.far_ref, ...), custom_call_target="tpu_custom_call" | custom-call | tf_op jit(solution)/shard_map/gathered_first/pallas_call | solution.py:660
  33.2 2.5 %intra.1 = (bf16[512,512]{1,0:T(8,128)(2,1)S(1)}, f32[512,1024]{1,0:T(8,128)S(1)}, f32[3,512,128]{2,1,0:T(8,128)S(1)}) custom-call(s32[4]{0:T(128)} %lengths_ref.7, bf16[512,512]{1,0:T(8,128)(2,1)S(1)} %get-tuple-element.81.query_conv, bf16[512,512]{1,0:T(8,128)(2,1)S(1)} %get-tuple-element.82.key_ref, bf16[2,16,512]{2,1,0:T(8,128)(2,1)S(1)} %get-tuple-element.83.conv_first, ...), custom_call_target="tpu_custom_call" | custom-call | flops 4294967296 | tf_op jit(solution)/shard_map/intra/pallas_call | solution.py:660
  35.7 1.1 %collective-permute-done.12.got3 = bf16[528,128]{1,0:T(8,128)(2,1)S(1)} collective-permute-done((bf16[528,128]{1,0:T(8,128)(2,1)S(1)}, bf16[528,128]{1,0:T(8,128)(2,1)S(1)}, u32[]{:S(2)}, u32[]{:S(2)}) %collective-permute-start.12) | collective-permute-done | bytes 135200 | tf_op jit(solution)/shard_map/ppermute | solution.py:691
  36.8 0.9 %head_send.1 = (bf16[256,1024]{1,0:T(8,128)(2,1)S(1)}, bf16[512,512]{1,0:T(8,128)(2,1)S(1)}, bf16[256,256]{1,0:T(8,128)(2,1)S(1)}, f32[8,128]{1,0:T(8,128)S(1)}) custom-call(bf16[528,128]{1,0:T(8,128)(2,1)S(1)} %get-tuple-element.70.own_ref, bf16[528,128]{1,0:T(8,128)(2,1)S(1)} %collective-permute-done.10.got1, ...), custom_call_target="tpu_custom_call" | custom-call | tf_op jit(solution)/shard_map/head_send/pallas_call | solution.py:660
  38.4 0.7 %project_kept.1.kept_ref = f32[256,1024]{1,0:T(8,128)S(1)} custom-call(bf16[256,1024]{1,0:T(8,128)(2,1)S(1)} %head_keep.1.keep_ref.head_ref, bf16[2048,2048]{1,0:T(8,128)(2,1)S(1)} %bitcast.1), custom_call_target="tpu_custom_call" | custom-call | flops 2147483648 | tf_op jit(solution)/shard_map/project_kept/pallas_call | solution.py:660
  40.1 1.6 %collective-permute-start.16 = (bf16[256,512]{1,0:T(8,128)(2,1)S(1)}, bf16[256,512]{1,0:T(8,128)(2,1)S(1)}, u32[]{:S(2)}, u32[]{:S(2)}) collective-permute-start(bf16[256,512]{1,0:T(8,128)(2,1)S(1)} %project_other.3), channel_id=1, source_target_pairs={{0,1},{1,0},{2,3},{3,2},{4,5},{5,4},{6,7},{7,6},{8,9},{9,8},{10,11... | collective-permute-start | bytes 786440 | tf_op jit(solution)/shard_map/ppermute | solution.py:853
  41.7 1.2 %project_own.1.own_ref = f32[256,1024]{1,0:T(8,128)S(1)} custom-call(bf16[256,1024]{1,0:T(8,128)(2,1)S(1)} %head_keep.1.keep_ref.head_ref, bf16[256,1024]{1,0:T(8,128)(2,1)S(1)} %collective-permute-done.14.got_ref.head_ref, bf16[2048,2048]{1,0:T(8,128)(2,1)S(1)} %bitcast.1), custom_call_target="tpu_custom_call" | custom-call | flops 4294967296 | tf_op jit(solution)/shard_map/project_own/pallas_call | solution.py:660
  44.0 5.3 %collective-permute-done.16.refs_0_ = bf16[256,512]{1,0:T(8,128)(2,1)S(1)} collective-permute-done((bf16[256,512]{1,0:T(8,128)(2,1)S(1)}, bf16[256,512]{1,0:T(8,128)(2,1)S(1)}, u32[]{:S(2)}, u32[]{:S(2)}) %collective-permute-start.16) | collective-permute-done | bytes 262176 | tf_op jit(solution)/shard_map/ppermute | solution.py:853
  49.3 0.7 %mixed_out.2.refs_1_ = bf16[256,1024]{1,0:T(8,128)(2,1)} custom-call(f32[256,1024]{1,0:T(8,128)S(1)} %project_own.1.own_ref, bf16[256,512]{1,0:T(8,128)(2,1)S(1)} %collective-permute-done.16.refs_0_), custom_call_target="tpu_custom_call" | custom-call | tf_op jit(solution)/shard_map/mixed_out/pallas_call | solution.py:660
  50.1 4.1 %collective-permute-done.15.refs_0_ = bf16[256,512]{1,0:T(8,128)(2,1)S(1)} collective-permute-done((bf16[256,512]{1,0:T(8,128)(2,1)S(1)}, bf16[256,512]{1,0:T(8,128)(2,1)S(1)}, u32[]{:S(2)}, u32[]{:S(2)}) %collective-permute-start.15) | collective-permute-done | bytes 262176 | tf_op jit(solution)/shard_map/ppermute | solution.py:853
  54.2 0.7 %mixed_out.3 = bf16[256,1024]{1,0:T(8,128)(2,1)} custom-call(f32[256,1024]{1,0:T(8,128)S(1)} %project_own.1.own_ref, bf16[256,512]{1,0:T(8,128)(2,1)S(1)} %collective-permute-done.15.refs_0_, bf16[256,1024]{1,0:T(8,128)(2,1)} %mixed_out.2.refs_1_), custom_call_target="tpu_custom_call", output_to_operand_aliasing={{}: (2, {})} | custom-call | tf_op jit(solution)/shard_map/mixed_out/pallas_call | solution.py:660
  (33 shorter events, 6.0 us)
Async XLA Ops:
  0.0 3.7 %collective-permute-start.1 = (bf16[256,2048]{1,0:T(8,128)(2,1)}, bf16[256,2048]{1,0:T(8,128)(2,1)S(1)}, u32[]{:S(2)}, u32[]{:S(2)}) collective-permute-start(bf16[256,2048]{1,0:T(8,128)(2,1)} %value_ref.1), channel_id=1, source_target_pairs={{0,2},{2,0},{4,6},{6,4},{8,10},{10,8},{12,14},{14,12},{16,18},{18,... | collective-permute-start | bytes 3145736 | tf_op jit(solution)/shard_map/ppermute | solution.py:691
  0.5 3.3 %collective-permute-start = (bf16[256,1024]{1,0:T(8,128)(2,1)}, bf16[256,1024]{1,0:T(8,128)(2,1)S(1)}, u32[]{:S(2)}, u32[]{:S(2)}) collective-permute-start(bf16[256,1024]{1,0:T(8,128)(2,1)} %key_ref.1), channel_id=1, source_target_pairs={{0,2},{2,0},{4,6},{6,4},{8,10},{10,8},{12,14},{14,12},{16,18},{18,... | collective-permute-start | bytes 1572872 | tf_op jit(solution)/shard_map/ppermute | solution.py:691
  0.5 11.2 %collective-permute-start.3 = (bf16[256,1024]{1,0:T(8,128)(2,1)}, bf16[256,1024]{1,0:T(8,128)(2,1)S(1)}, u32[]{:S(2)}, u32[]{:S(2)}) collective-permute-start(bf16[256,1024]{1,0:T(8,128)(2,1)} %query_ref.3), channel_id=1, source_target_pairs={{0,2},{2,0},{4,6},{6,4},{8,10},{10,8},{12,14},{14,12},{16,18},{18,... | collective-permute-start | bytes 1572872 | tf_op jit(solution)/shard_map/ppermute | solution.py:691
  1.7 1.7 %collective-permute-start.2 = (f32[2,4,256]{2,1,0:T(4,128)S(1)}, f32[2,4,256]{2,1,0:T(4,128)S(1)}, u32[]{:S(2)}, u32[]{:S(2)}) collective-permute-start(f32[2,4,256]{2,1,0:T(4,128)S(1)} %gates.1.gates_ref), channel_id=1, source_target_pairs={{0,2},{2,0},{4,6},{6,4},{8,10},{10,8},{12,14},{14,12},{16,18},{18,... | collective-permute-start | bytes 24584 | tf_op jit(solution)/shard_map/ppermute | solution.py:691
  7.1 11.6 %collective-permute-start.4 = (bf16[528,128]{1,0:T(8,128)(2,1)S(1)}, bf16[528,128]{1,0:T(8,128)(2,1)S(1)}, u32[]{:S(2)}, u32[]{:S(2)}) collective-permute-start(bf16[528,128]{1,0:T(8,128)(2,1)S(1)} %get-tuple-element.55), channel_id=1, source_target_pairs={{0,4},{2,6},{4,0},{6,2},{8,12},{10,14},{12,8},{14,10},{16,20},{18,... | collective-permute-start | bytes 405512 | tf_op jit(solution)/shard_map/ppermute | solution.py:691
  10.1 8.6 %collective-permute-start.5 = (bf16[528,128]{1,0:T(8,128)(2,1)S(1)}, bf16[528,128]{1,0:T(8,128)(2,1)S(1)}, u32[]{:S(2)}, u32[]{:S(2)}) collective-permute-start(bf16[528,128]{1,0:T(8,128)(2,1)S(1)} %get-tuple-element.56), channel_id=1, source_target_pairs={{0,8},{2,10},{4,12},{6,14},{8,0},{10,2},{12,4},{14,6},{16,24},{18,... | collective-permute-start | bytes 405512 | tf_op jit(solution)/shard_map/ppermute | solution.py:691
  11.7 7.0 %collective-permute-start.6 = (bf16[528,128]{1,0:T(8,128)(2,1)S(1)}, bf16[528,128]{1,0:T(8,128)(2,1)S(1)}, u32[]{:S(2)}, u32[]{:S(2)}) collective-permute-start(bf16[528,128]{1,0:T(8,128)(2,1)S(1)} %get-tuple-element.57), channel_id=1, source_target_pairs={{0,12},{2,14},{4,8},{6,10},{8,4},{10,6},{12,0},{14,2},{16,28},{18,... | collective-permute-start | bytes 405512 | tf_op jit(solution)/shard_map/ppermute | solution.py:691
  11.8 6.9 %collective-permute-start.7 = (bf16[1,64,128]{2,1,0:T(8,128)(2,1)S(1)}, bf16[1,64,128]{2,1,0:T(8,128)(2,1)S(1)}, u32[]{:S(2)}, u32[]{:S(2)}) collective-permute-start(bf16[1,64,128]{2,1,0:T(8,128)(2,1)S(1)} %message.1.first_ref), channel_id=1, source_target_pairs={{0,8},{2,10},{4,12},{6,14},{8,0},{10,2},{12,4},{14,6},{16,24},{18,... | collective-permute-start | bytes 49160 | tf_op jit(solution)/shard_map/ppermute | solution.py:691
  18.9 7.6 %collective-permute-start.9 = (bf16[528,128]{1,0:T(8,128)(2,1)S(1)}, bf16[528,128]{1,0:T(8,128)(2,1)S(1)}, u32[]{:S(2)}, u32[]{:S(2)}) collective-permute-start(bf16[528,128]{1,0:T(8,128)(2,1)S(1)} %group_total.1), channel_id=1, source_target_pairs={{0,24},{2,26},{4,28},{6,30},{8,16},{10,18},{12,20},{14,22},{16,8},... | collective-permute-start | bytes 405512 | tf_op jit(solution)/shard_map/ppermute | solution.py:691
  22.6 3.9 %collective-permute-start.8 = (bf16[2,64,128]{2,1,0:T(8,128)(2,1)S(1)}, bf16[2,64,128]{2,1,0:T(8,128)(2,1)S(1)}, u32[]{:S(2)}, u32[]{:S(2)}) collective-permute-start(bf16[2,64,128]{2,1,0:T(8,128)(2,1)S(1)} %join.2.first_ref), channel_id=1, source_target_pairs={{0,4},{2,6},{4,0},{6,2},{8,12},{10,14},{12,8},{14,10},{16,20},{18,... | collective-permute-start | bytes 98312 | tf_op jit(solution)/shard_map/ppermute | solution.py:691
  26.5 5.3 %collective-permute-start.13 = (bf16[4,64,128]{2,1,0:T(8,128)(2,1)S(1)}, bf16[4,64,128]{2,1,0:T(8,128)(2,1)S(1)}, u32[]{:S(2)}, u32[]{:S(2)}) collective-permute-start(bf16[4,64,128]{2,1,0:T(8,128)(2,1)S(1)} %join.3.near_ref), channel_id=1, source_target_pairs={{0,16},{2,18},{4,20},{6,22},{8,24},{10,26},{12,28},{14,30},{16,0},... | collective-permute-start | bytes 196616 | tf_op jit(solution)/shard_map/ppermute | solution.py:691
  27.2 8.5 %collective-permute-start.10 = (bf16[528,128]{1,0:T(8,128)(2,1)S(1)}, bf16[528,128]{1,0:T(8,128)(2,1)S(1)}, u32[]{:S(2)}, u32[]{:S(2)}) collective-permute-start(bf16[528,128]{1,0:T(8,128)(2,1)S(1)} %get-tuple-element.71), channel_id=1, source_target_pairs={{0,4},{2,6},{4,0},{6,2},{8,12},{10,14},{12,8},{14,10},{16,20},{18,... | collective-permute-start | bytes 405512 | tf_op jit(solution)/shard_map/ppermute | solution.py:691
  28.5 7.2 %collective-permute-start.11 = (bf16[528,128]{1,0:T(8,128)(2,1)S(1)}, bf16[528,128]{1,0:T(8,128)(2,1)S(1)}, u32[]{:S(2)}, u32[]{:S(2)}) collective-permute-start(bf16[528,128]{1,0:T(8,128)(2,1)S(1)} %get-tuple-element.72), channel_id=1, source_target_pairs={{0,8},{2,10},{4,12},{6,14},{8,0},{10,2},{12,4},{14,6},{16,24},{18,... | collective-permute-start | bytes 405512 | tf_op jit(solution)/shard_map/ppermute | solution.py:691
  30.9 5.9 %collective-permute-start.12 = (bf16[528,128]{1,0:T(8,128)(2,1)S(1)}, bf16[528,128]{1,0:T(8,128)(2,1)S(1)}, u32[]{:S(2)}, u32[]{:S(2)}) collective-permute-start(bf16[528,128]{1,0:T(8,128)(2,1)S(1)} %get-tuple-element.73), channel_id=1, source_target_pairs={{0,12},{2,14},{4,8},{6,10},{8,4},{10,6},{12,0},{14,2},{16,28},{18,... | collective-permute-start | bytes 405512 | tf_op jit(solution)/shard_map/ppermute | solution.py:691
  33.2 5.2 %slice-start = ((s8[8388608]{0:T(1024)(128)(4,1)}), s8[4194304]{0:T(1024)(128)(4,1)S(1)}, s32[]{:S(2)}) async-start(s8[8388608]{0:T(1024)(128)(4,1)} %bitcast), calls=%async_computation | async-start | bytes 8388608
  33.2 5.2 %slice-start.1 = ((s8[8388608]{0:T(1024)(128)(4,1)}), s8[4194304]{0:T(1024)(128)(4,1)S(1)}, s32[]{:S(2)}) async-start(s8[8388608]{0:T(1024)(128)(4,1)} %bitcast), calls=%async_computation.1 | async-start | bytes 8388608
  37.7 2.0 %collective-permute-start.14 = (bf16[256,1024]{1,0:T(8,128)(2,1)S(1)}, bf16[256,1024]{1,0:T(8,128)(2,1)S(1)}, u32[]{:S(2)}, u32[]{:S(2)}) collective-permute-start(bf16[256,1024]{1,0:T(8,128)(2,1)S(1)} %get-tuple-element.88), channel_id=1, source_target_pairs={{0,2},{2,0},{4,6},{6,4},{8,10},{10,8},{12,14},{14,12},{16,18},{18,... | collective-permute-start | bytes 1572872 | tf_op jit(solution)/shard_map/ppermute | solution.py:691
  40.1 9.2 %collective-permute-start.16 = (bf16[256,512]{1,0:T(8,128)(2,1)S(1)}, bf16[256,512]{1,0:T(8,128)(2,1)S(1)}, u32[]{:S(2)}, u32[]{:S(2)}) collective-permute-start(bf16[256,512]{1,0:T(8,128)(2,1)S(1)} %project_other.3), channel_id=1, source_target_pairs={{0,1},{1,0},{2,3},{3,2},{4,5},{5,4},{6,7},{7,6},{8,9},{9,8},{10,11... | collective-permute-start | bytes 786440 | tf_op jit(solution)/shard_map/ppermute | solution.py:853
  43.4 10.7 %collective-permute-start.15 = (bf16[256,512]{1,0:T(8,128)(2,1)S(1)}, bf16[256,512]{1,0:T(8,128)(2,1)S(1)}, u32[]{:S(2)}, u32[]{:S(2)}) collective-permute-start(bf16[256,512]{1,0:T(8,128)(2,1)S(1)} %project_other.2), channel_id=1, source_target_pairs={{0,1},{1,0},{2,3},{3,2},{4,5},{5,4},{6,7},{7,6},{8,9},{9,8},{10,11... | collective-permute-start | bytes 786440 | tf_op jit(solution)/shard_map/ppermute | solution.py:853

commit v6 on v5

--- a/solution.py
+++ b/solution.py
@@ -125,32 +125,60 @@
     return normal, sums[0][:, 0:1], sums[1][:, 0:1]
 
 
-def gates_kernel(input_ref, forget_ref, gate_ref, sems):
+def half_columns(core, width):
+    return pl.ds(pl.multiple_of(core * width, 128), width)
+
+
+def gates_kernel(
+    input_ref, forget_ref, key_ref, value_ref, gate_ref, key_send, send_ref, sems
+):
+    core, _ = core_place()
+    width = key_send.shape[1]
+    columns = half_columns(1 - core, width) if key_ref.shape[1] > width else pl.ds(0, width)
     copies = start_copies(
-        sems, [(ref, gate_ref.at[i]) for i, ref in enumerate((input_ref, forget_ref))]
+        sems,
+        [
+            (key_ref.at[:, columns], key_send),
+            (value_ref.at[:, half_columns(1 - core, send_ref.shape[1])], send_ref),
+            (input_ref, gate_ref.at[0]),
+            (forget_ref, gate_ref.at[1]),
+        ],
     )
     for copy in copies:
         copy.wait()
 
 
+def own_kernel_parts(key_ref, value_ref, taps_ref, keys, values, taps, sems):
+    core, _ = core_place()
+    width = keys.shape[1]
+    columns = half_columns(core, width) if key_ref.shape[1] > width else pl.ds(0, width)
+    copies = start_copies(
+        sems,
+        [
+            (key_ref.at[:, columns], keys),
+            (value_ref.at[:, half_columns(core, values.shape[1])], values),
+            (taps_ref.at[1, :, columns], taps),
+        ],
+    )
+    for copy in copies:
+        copy.wait()
+
+
 def chip_kernel(
-    per_core, lengths_ref, key_ref, key_other, value_ref, value_other, gates_ref, gates_other,
-    taps_ref,
-    conv_ref, values, gate_ref, taps, key_edge, levels_first, out0, out1, out2, out3,
-    keys, raw, picked, wide, weighted_ref, whole, normals, levels, sems,
+    per_core, lengths_ref, own_keys, own_values, key_other, value_other, gates_ref, gates_other,
+    taps,
+    conv_ref, values, gate_ref, key_edge, levels_first, out0, out1, out2, out3,
+    raw, picked, wide, weighted_ref, whole, normals, levels, sems,
 ):
     core, mine = core_place()
-    length, width = keys.shape
+    rows, width = own_keys.shape
+    length = 2 * rows
     key_width = width // per_core
     value_width = values.shape[1] // per_core
-    split = gates_ref.shape[1] > 1
-    key_columns = pl.ds(pl.multiple_of(core * width, 128) if split else 0, width)
-    value_columns = pl.ds(pl.multiple_of(core * values.shape[1], 128), values.shape[1])
+    own_rows = pl.ds(pl.multiple_of(core * rows, rows), rows)
+    other_rows = pl.ds(pl.multiple_of((1 - core) * rows, rows), rows)
     copies = start_copies(
-        sems,
-        [(taps_ref.at[1, :, key_columns], taps)]
-        + by_core(core, key_ref, key_other, key_columns, keys)
-        + by_core(core, value_ref, value_other, value_columns, values),
+        sems, [(own_values, values.at[own_rows, :]), (value_other, values.at[other_rows, :])]
     )
     offset = lax.axis_index("seq") // 2 * length
     gate, cumulative = gate_rows(core, per_core, (gates_ref, gates_other), raw, picked)
@@ -170,15 +198,15 @@
     levels_first[1] = levels[1]
     same = same_request(lengths_ref, offset + iota((length, 128), 0))
     normals[...] = jnp.zeros_like(normals)
-    for copy in copies[:3]:
-        copy.wait()
-    key_edge[0] = keys[0:16, :]
-    key_edge[1] = keys[length - 16 :, :]
     step = 128
     for i in range(per_core):
         columns = slice(i * key_width, (i + 1) * key_width)
+        own, other = own_keys[:, columns], key_other[:, columns]
+        key_edge[0, :, columns] = jnp.where(core == 0, own[0:16], other[0:16])
+        key_edge[1, :, columns] = jnp.where(core == 0, other[rows - 16 :], own[rows - 16 :])
         wide[0:8, :] = jnp.zeros((8, key_width), F32)
-        wide[8:, :] = keys[:, columns].astype(F32)
+        wide[pl.ds(pl.multiple_of(8 + core * rows, 8), rows), :] = own.astype(F32)
+        wide[pl.ds(pl.multiple_of(8 + (1 - core) * rows, 8), rows), :] = other.astype(F32)
         normal = jnp.zeros((1, key_width), F32)
         for start in range(0, length, step):
             conv = conv_rows(same, start, start + step, taps, columns, wide)
@@ -190,14 +218,12 @@
             normal = normal + jnp.sum(weighted, axis=0, keepdims=True)
             weighted_ref[start : start + step, columns] = weighted.astype(BF16)
         normals[i : i + 1, :] = normal
-    for copy in copies[3:]:
-        copy.wait()
     for i in range(per_core):
         columns = slice(i * key_width, (i + 1) * key_width)
-        whole[columns, :] = dot(
-            weighted_ref[:, columns],
-            values[:, i * value_width : (i + 1) * value_width],
-            ((0,), (0,)),
+        value_columns = slice(i * value_width, (i + 1) * value_width)
+        whole[columns, :] = sum(
+            dot(weighted_ref[part, columns], ref[:, value_columns], ((0,), (0,)))
+            for part, ref in ((own_rows, own_values), (other_rows, value_other))
         ).astype(BF16)
     rows = width // 4
     for off, out in enumerate((out0, out1, out2, out3)):
@@ -212,6 +238,8 @@
             levels[0, pl.ds(head, 1), :][:, 0:1],
             levels[1, pl.ds(head, 1), :][:, 0:1],
         )
+    for copy in copies:
+        copy.wait()
 
 
 def message_kernel(
@@ -690,28 +718,42 @@
     def swap(x, off):
         return lax.ppermute(x, "seq", [(i, i ^ off) for i in range(seq_count)])
 
-    key_other, value_other = swap(key_input, 1), swap(value_input, 1)
-    query_other = swap(query_input, 1)
-    gates = call(
-        gates_kernel, shape((2, heads, length)), "hh", [pltpu.SemaphoreType.DMA((2,))], "gates"
-    )(input_gate, forget_gate)
-    gates_other = swap(gates, 1)
+    gates, key_send, value_send = call(
+        gates_kernel,
+        (
+            shape((2, heads, length)),
+            shape((length, part_keys), BF16),
+            shape((length, part_values), BF16),
+        ),
+        "hhhh", [pltpu.SemaphoreType.DMA((4,))], "gates", flops=4 << 30,
+    )(input_gate, forget_gate, key_input, value_input)
+    gates_other, key_other, value_other = swap(gates, 1), swap(key_send, 1), swap(value_send, 1)
+    key_after, value_after, gates = lax.optimization_barrier((key_input, value_input, gates))
+    own_keys, own_values, taps = call(
+        own_kernel_parts,
+        (
+            shape((length, part_keys), BF16),
+            shape((length, part_values), BF16),
+            shape((lags, part_keys)),
+        ),
+        "hhh", [pltpu.SemaphoreType.DMA((3,))], "own_part", flops=4 << 30,
+    )(key_after, value_after, kernel_taps)
+    query_after, gates = lax.optimization_barrier((query_input, gates))
+    query_other = swap(query_after, 1)
 
     one = shape((rows * value_width // 128 + INFO, 128), BF16)
-    key_conv, values, gate_sums, taps, key_edge, levels, *pieces = call(
+    key_conv, values, gate_sums, key_edge, levels, *pieces = call(
         functools.partial(chip_kernel, per_core),
         (
             shape((chip_length, part_keys), BF16),
             shape((chip_length, part_values), BF16),
             shape((2, 8, chip_length)),
-            shape((lags, part_keys)),
             shape((2, 16, part_keys), BF16),
             shape((2, 8, 128)),
         )
         + (one,) * 4,
-        "shahavvh",
+        "s" + "v" * 7,
         [
-            pltpu.VMEM((chip_length, part_keys), BF16),
             pltpu.VMEM((2, max(8, heads), chip_length), F32),
             pltpu.VMEM((2, 8, chip_length), F32),
             pltpu.VMEM((chip_length + 8, key_width), F32),
@@ -719,13 +761,12 @@
             pltpu.VMEM((part_keys, value_width), BF16),
             pltpu.VMEM((8, key_width), F32),
             pltpu.VMEM((2, 8, 128), F32),
-            pltpu.SemaphoreType.DMA((5,)),
+            pltpu.SemaphoreType.DMA((2,)),
         ],
         "chip_state",
         flops=1 << 30,
     )(
-        request_lengths, key_input, key_other, value_input, value_other, gates, gates_other,
-        kernel_taps,
+        request_lengths, own_keys, own_values, key_other, value_other, gates, gates_other, taps
     )
     states = [pieces[0]] + [swap(pieces[off], 2 * off) for off in (1, 2, 3)]
 

time: 55.2 us -> 54.7 us (level)
  waiting for transfers between devices: 18.3 us -> 16.6 us
  Pallas kernels: 17.5 us -> 18.6 us
    ppermute x15, waiting for transfers between devices: 8.93 us -> 7.21 us  [swap(): return lax.ppermute(x, 'seq', [(i, i ^ off) for i in range(seq_count)])]
    pallas_call x18 -> x19, Pallas kernels: 17.5 us -> 18.6 us  [run(): inner(*(pltpu.with_memory_space_constraint(x, pltpu.HBM) if s in 'hs' els...]
  transfers between devices with their start and end apart: 17 -> 17, of which waited for: 9 -> 8; matrix products, arithmetic and copies ran while one was open for 0% -> 0% of each run, Pallas kernels for 28% -> 28%
where the time goes in v6:
time: 54.7 us; the launch traced here: 54.4 us
  starting transfers between devices  18.9 us (35%)
  Pallas kernels  18.6 us (34%)
  waiting for transfers between devices  16.6 us (30%)
    pallas_call x19, Pallas kernels, run(): inner(*(pltpu.with_memory_space_constraint(x, pltpu.HBM) if s in 'hs' els...  18.6 us
    ppermute x15, starting transfers between devices, swap(): return lax.ppermute(x, 'seq', [(i, i ^ off) for i in range(seq_count)])  16.8 us
    ppermute x2, waiting for transfers between devices, on_device(): lax.ppermute(part, 'head', [(i, i ^ off) for i in range(head_count)])  9.41 us
    ppermute x15, waiting for transfers between devices, swap(): return lax.ppermute(x, 'seq', [(i, i ^ off) for i in range(seq_count)])  7.21 us
    ppermute x2, starting transfers between devices, on_device(): lax.ppermute(part, 'head', [(i, i ^ off) for i in range(head_count)])  2.16 us
  transfers between devices with their start and end apart: 17, of which 8 were waited for; matrix products, arithmetic and copies ran while one was open for 0% of the time, Pallas kernels for 28%

profile of v6, /device:TPU:0, one launch (start us, length us, event | category | flops | bytes accessed | tf_op | source)
XLA Modules:
  0.0 54.4 jit_solution(9352829704024405242)
XLA Ops:
  0.0 1.2 %gates.1 = (f32[2,4,256]{2,1,0:T(4,128)S(1)}, bf16[256,512]{1,0:T(8,128)(2,1)S(1)}, bf16[256,1024]{1,0:T(8,128)(2,1)S(1)}) custom-call(f32[4,256]{1,0:T(4,128)} %input_ref.1, f32[4,256]{1,0:T(4,128)} %forget_ref.1, bf16[256,1024]{1,0:T(8,128)(2,1)} %key_ref.2, bf16[256,2048]{1,0:T(8,128)(2,1)} %value_ref.2), custom_call_target="tpu_custom_call" | custom-call | flops 4294967296 | tf_op jit(solution)/shard_map/gates/pallas_call | solution.py:688
  2.3 1.1 %own_part.1 = (bf16[256,512]{1,0:T(8,128)(2,1)S(1)}, bf16[256,1024]{1,0:T(8,128)(2,1)S(1)}, f32[4,512]{1,0:T(4,128)S(1)}) custom-call(bf16[256,1024]{1,0:T(8,128)(2,1)} %key_ref.2, bf16[256,2048]{1,0:T(8,128)(2,1)} %value_ref.2, f32[2,4,1024]{2,1,0:T(4,128)} %taps_ref.3), custom_call_target="tpu_custom_call" | custom-call | flops 4294967296 | tf_op jit(solution)/shard_map/own_part/pallas_call | solution.py:688
  3.7 2.9 %chip_state.1 = (bf16[512,512]{1,0:T(8,128)(2,1)S(1)}, bf16[512,1024]{1,0:T(8,128)(2,1)S(1)}, f32[2,8,512]{2,1,0:T(8,128)S(1)}, bf16[2,16,512]{2,1,0:T(8,128)(2,...) custom-call(s32[4]{0:T(128)} %lengths_ref.7, ...), custom_call_target="tpu_custom_call" | custom-call | flops 1073741824 | tf_op jit(solution)/shard_map/chip_state/pallas_call | solution.py:688
  6.6 3.0 %collective-permute-start.4 = (bf16[528,128]{1,0:T(8,128)(2,1)S(1)}, bf16[528,128]{1,0:T(8,128)(2,1)S(1)}, u32[]{:S(2)}, u32[]{:S(2)}) collective-permute-start(bf16[528,128]{1,0:T(8,128)(2,1)S(1)} %get-tuple-element.76), channel_id=1, source_target_pairs={{0,4},{2,6},{4,0},{6,2},{8,12},{10,14},{12,8},{14,10},{16,20},{18,... | collective-permute-start | bytes 405512 | tf_op jit(solution)/shard_map/ppermute | solution.py:719
  9.6 1.6 %collective-permute-start.5 = (bf16[528,128]{1,0:T(8,128)(2,1)S(1)}, bf16[528,128]{1,0:T(8,128)(2,1)S(1)}, u32[]{:S(2)}, u32[]{:S(2)}) collective-permute-start(bf16[528,128]{1,0:T(8,128)(2,1)S(1)} %get-tuple-element.77), channel_id=1, source_target_pairs={{0,8},{2,10},{4,12},{6,14},{8,0},{10,2},{12,4},{14,6},{16,24},{18,... | collective-permute-start | bytes 405512 | tf_op jit(solution)/shard_map/ppermute | solution.py:719
  11.3 2.0 %collective-permute-start.7 = (bf16[1,64,128]{2,1,0:T(8,128)(2,1)S(1)}, bf16[1,64,128]{2,1,0:T(8,128)(2,1)S(1)}, u32[]{:S(2)}, u32[]{:S(2)}) collective-permute-start(bf16[1,64,128]{2,1,0:T(8,128)(2,1)S(1)} %message.1.first_ref), channel_id=1, source_target_pairs={{0,8},{2,10},{4,12},{6,14},{8,0},{10,2},{12,4},{14,6},{16,24},{18,... | collective-permute-start | bytes 49160 | tf_op jit(solution)/shard_map/ppermute | solution.py:719
  13.3 2.6 %query_conv.1 = (bf16[512,512]{1,0:T(8,128)(2,1)S(1)}, f32[4,512]{1,0:T(4,128)S(1)}, bf16[2,16,512]{2,1,0:T(8,128)(2,1)S(1)}) custom-call(s32[4]{0:T(128)} %lengths_ref.7, bf16[256,1024]{1,0:T(8,128)(2,1)} %query_ref.3, bf16[256,1024]{1,0:T(8,128)(2,1)S(1)} %collective-permute-done.3.query_other, f32[2,4,1024]{2,1,0:T(4,128)} %taps_ref.3), custom_call_target="tpu_custom_call" | custom-call | flops 1073741824 | tf_op jit(solution)/shard_map/query_conv/pallas_call | solution.py:688
  15.9 2.2 %collective-permute-done.7.second_ref = bf16[1,64,128]{2,1,0:T(8,128)(2,1)S(1)} collective-permute-done((bf16[1,64,128]{2,1,0:T(8,128)(2,1)S(1)}, bf16[1,64,128]{2,1,0:T(8,128)(2,1)S(1)}, u32[]{:S(2)}, u32[]{:S(2)}) %collective-permute-start.7) | collective-permute-done | bytes 16416 | tf_op jit(solution)/shard_map/ppermute | solution.py:719
  18.4 3.7 %collective-permute-start.9 = (bf16[528,128]{1,0:T(8,128)(2,1)S(1)}, bf16[528,128]{1,0:T(8,128)(2,1)S(1)}, u32[]{:S(2)}, u32[]{:S(2)}) collective-permute-start(bf16[528,128]{1,0:T(8,128)(2,1)S(1)} %group_total.1), channel_id=1, source_target_pairs={{0,24},{2,26},{4,28},{6,30},{8,16},{10,18},{12,20},{14,22},{16,8},... | collective-permute-start | bytes 405512 | tf_op jit(solution)/shard_map/ppermute | solution.py:719
  22.1 1.3 %collective-permute-start.8 = (bf16[2,64,128]{2,1,0:T(8,128)(2,1)S(1)}, bf16[2,64,128]{2,1,0:T(8,128)(2,1)S(1)}, u32[]{:S(2)}, u32[]{:S(2)}) collective-permute-start(bf16[2,64,128]{2,1,0:T(8,128)(2,1)S(1)} %join.2.first_ref), channel_id=1, source_target_pairs={{0,4},{2,6},{4,0},{6,2},{8,12},{10,14},{12,8},{14,10},{16,20},{18,... | collective-permute-start | bytes 98312 | tf_op jit(solution)/shard_map/ppermute | solution.py:719
  23.4 2.6 %collective-permute-done.8.second_ref = bf16[2,64,128]{2,1,0:T(8,128)(2,1)S(1)} collective-permute-done((bf16[2,64,128]{2,1,0:T(8,128)(2,1)S(1)}, bf16[2,64,128]{2,1,0:T(8,128)(2,1)S(1)}, u32[]{:S(2)}, u32[]{:S(2)}) %collective-permute-start.8) | collective-permute-done | bytes 32800 | tf_op jit(solution)/shard_map/ppermute | solution.py:719
  26.7 1.3 %collective-permute-start.10 = (bf16[528,128]{1,0:T(8,128)(2,1)S(1)}, bf16[528,128]{1,0:T(8,128)(2,1)S(1)}, u32[]{:S(2)}, u32[]{:S(2)}) collective-permute-start(bf16[528,128]{1,0:T(8,128)(2,1)S(1)} %get-tuple-element.92), channel_id=1, source_target_pairs={{0,4},{2,6},{4,0},{6,2},{8,12},{10,14},{12,8},{14,10},{16,20},{18,... | collective-permute-start | bytes 405512 | tf_op jit(solution)/shard_map/ppermute | solution.py:719
  28.0 2.4 %collective-permute-start.11 = (bf16[528,128]{1,0:T(8,128)(2,1)S(1)}, bf16[528,128]{1,0:T(8,128)(2,1)S(1)}, u32[]{:S(2)}, u32[]{:S(2)}) collective-permute-start(bf16[528,128]{1,0:T(8,128)(2,1)S(1)} %get-tuple-element.93), channel_id=1, source_target_pairs={{0,8},{2,10},{4,12},{6,14},{8,0},{10,2},{12,4},{14,6},{16,24},{18,... | collective-permute-start | bytes 405512 | tf_op jit(solution)/shard_map/ppermute | solution.py:719
  31.3 1.4 %gathered_first.1 = (bf16[256,256]{1,0:T(8,128)(2,1)S(1)}, bf16[256,512]{1,0:T(8,128)(2,1)S(1)}, f32[256,128]{1,0:T(8,128)S(1)}, bf16[2,16,512]{2,1,0:T(8,128)(2,1)S(1)}) custom-call(s32[4]{0:T(128)} %lengths_ref.7, bf16[4,64,128]{2,1,0:T(8,128)(2,1)S(1)} %join.3.near_ref, bf16[4,64,128]{2,1,0:T(8,128)(2,1)S(1)} %collective-permute-done.13.far_ref, ...), custom_call_target="tpu_custom_call" | custom-call | tf_op jit(solution)/shard_map/gathered_first/pallas_call | solution.py:688
  32.7 2.5 %intra.1 = (bf16[512,512]{1,0:T(8,128)(2,1)S(1)}, f32[512,1024]{1,0:T(8,128)S(1)}, f32[3,512,128]{2,1,0:T(8,128)S(1)}) custom-call(s32[4]{0:T(128)} %lengths_ref.7, bf16[512,512]{1,0:T(8,128)(2,1)S(1)} %get-tuple-element.101.query_conv, bf16[512,512]{1,0:T(8,128)(2,1)S(1)} %get-tuple-element.102.key_ref, ...), custom_call_target="tpu_custom_call" | custom-call | flops 4294967296 | tf_op jit(solution)/shard_map/intra/pallas_call | solution.py:688
  35.2 1.1 %collective-permute-done.12.got3 = bf16[528,128]{1,0:T(8,128)(2,1)S(1)} collective-permute-done((bf16[528,128]{1,0:T(8,128)(2,1)S(1)}, bf16[528,128]{1,0:T(8,128)(2,1)S(1)}, u32[]{:S(2)}, u32[]{:S(2)}) %collective-permute-start.12) | collective-permute-done | bytes 135200 | tf_op jit(solution)/shard_map/ppermute | solution.py:719
  36.3 0.9 %head_send.1 = (bf16[256,1024]{1,0:T(8,128)(2,1)S(1)}, bf16[512,512]{1,0:T(8,128)(2,1)S(1)}, bf16[256,256]{1,0:T(8,128)(2,1)S(1)}, f32[8,128]{1,0:T(8,128)S(1)}) custom-call(bf16[528,128]{1,0:T(8,128)(2,1)S(1)} %get-tuple-element.91.own_ref, bf16[528,128]{1,0:T(8,128)(2,1)S(1)} %collective-permute-done.10.got1, ...), custom_call_target="tpu_custom_call" | custom-call | tf_op jit(solution)/shard_map/head_send/pallas_call | solution.py:688
  37.9 0.7 %project_kept.1.kept_ref = f32[256,1024]{1,0:T(8,128)S(1)} custom-call(bf16[256,1024]{1,0:T(8,128)(2,1)S(1)} %head_keep.1.keep_ref.head_ref, bf16[2048,2048]{1,0:T(8,128)(2,1)S(1)} %bitcast.1), custom_call_target="tpu_custom_call" | custom-call | flops 2147483648 | tf_op jit(solution)/shard_map/project_kept/pallas_call | solution.py:688
  39.6 1.5 %collective-permute-start.16 = (bf16[256,512]{1,0:T(8,128)(2,1)S(1)}, bf16[256,512]{1,0:T(8,128)(2,1)S(1)}, u32[]{:S(2)}, u32[]{:S(2)}) collective-permute-start(bf16[256,512]{1,0:T(8,128)(2,1)S(1)} %project_other.3), channel_id=1, source_target_pairs={{0,1},{1,0},{2,3},{3,2},{4,5},{5,4},{6,7},{7,6},{8,9},{9,8},{10,11... | collective-permute-start | bytes 786440 | tf_op jit(solution)/shard_map/ppermute | solution.py:894
  41.2 1.2 %project_own.1.own_ref = f32[256,1024]{1,0:T(8,128)S(1)} custom-call(bf16[256,1024]{1,0:T(8,128)(2,1)S(1)} %head_keep.1.keep_ref.head_ref, bf16[256,1024]{1,0:T(8,128)(2,1)S(1)} %collective-permute-done.14.got_ref.head_ref, bf16[2048,2048]{1,0:T(8,128)(2,1)S(1)} %bitcast.1), custom_call_target="tpu_custom_call" | custom-call | flops 4294967296 | tf_op jit(solution)/shard_map/project_own/pallas_call | solution.py:688
  43.5 5.3 %collective-permute-done.16.refs_0_ = bf16[256,512]{1,0:T(8,128)(2,1)S(1)} collective-permute-done((bf16[256,512]{1,0:T(8,128)(2,1)S(1)}, bf16[256,512]{1,0:T(8,128)(2,1)S(1)}, u32[]{:S(2)}, u32[]{:S(2)}) %collective-permute-start.16) | collective-permute-done | bytes 262176 | tf_op jit(solution)/shard_map/ppermute | solution.py:894
  48.9 0.7 %mixed_out.2.refs_1_ = bf16[256,1024]{1,0:T(8,128)(2,1)} custom-call(f32[256,1024]{1,0:T(8,128)S(1)} %project_own.1.own_ref, bf16[256,512]{1,0:T(8,128)(2,1)S(1)} %collective-permute-done.16.refs_0_), custom_call_target="tpu_custom_call" | custom-call | tf_op jit(solution)/shard_map/mixed_out/pallas_call | solution.py:688
  49.6 4.1 %collective-permute-done.15.refs_0_ = bf16[256,512]{1,0:T(8,128)(2,1)S(1)} collective-permute-done((bf16[256,512]{1,0:T(8,128)(2,1)S(1)}, bf16[256,512]{1,0:T(8,128)(2,1)S(1)}, u32[]{:S(2)}, u32[]{:S(2)}) %collective-permute-start.15) | collective-permute-done | bytes 262176 | tf_op jit(solution)/shard_map/ppermute | solution.py:894
  53.7 0.7 %mixed_out.3 = bf16[256,1024]{1,0:T(8,128)(2,1)} custom-call(f32[256,1024]{1,0:T(8,128)S(1)} %project_own.1.own_ref, bf16[256,512]{1,0:T(8,128)(2,1)S(1)} %collective-permute-done.15.refs_0_, bf16[256,1024]{1,0:T(8,128)(2,1)} %mixed_out.2.refs_1_), custom_call_target="tpu_custom_call", output_to_operand_aliasing={{}: (2, {})} | custom-call | tf_op jit(solution)/shard_map/mixed_out/pallas_call | solution.py:688
  (36 shorter events, 5.9 us)
Async XLA Ops:
  0.0 2.3 %copy-start = (bf16[256,1024]{1,0:T(8,128)(2,1)S(1)}, bf16[256,1024]{1,0:T(8,128)(2,1)}, u32[]{:S(2)}) copy-start(bf16[256,1024]{1,0:T(8,128)(2,1)} %query_ref.3) | copy-start | bytes 1572868
  1.2 2.4 %collective-permute-start.1 = (bf16[256,1024]{1,0:T(8,128)(2,1)S(1)}, bf16[256,1024]{1,0:T(8,128)(2,1)S(1)}, u32[]{:S(2)}, u32[]{:S(2)}) collective-permute-start(bf16[256,1024]{1,0:T(8,128)(2,1)S(1)} %get-tuple-element.66), channel_id=1, source_target_pairs={{0,2},{2,0},{4,6},{6,4},{8,10},{10,8},{12,14},{14,12},{16,18},{18,... | collective-permute-start | bytes 1572872 | tf_op jit(solution)/shard_map/ppermute | solution.py:719
  1.7 1.8 %collective-permute-start.2 = (f32[2,4,256]{2,1,0:T(4,128)S(1)}, f32[2,4,256]{2,1,0:T(4,128)S(1)}, u32[]{:S(2)}, u32[]{:S(2)}) collective-permute-start(f32[2,4,256]{2,1,0:T(4,128)S(1)} %get-tuple-element.68.gates_ref), channel_id=1, source_target_pairs={{0,2},{2,0},{4,6},{6,4},{8,10},{10,8},{12,14},{14,12},{16,18},{18,... | collective-permute-start | bytes 24584 | tf_op jit(solution)/shard_map/ppermute | solution.py:719
  1.8 1.8 %collective-permute-start = (bf16[256,512]{1,0:T(8,128)(2,1)S(1)}, bf16[256,512]{1,0:T(8,128)(2,1)S(1)}, u32[]{:S(2)}, u32[]{:S(2)}) collective-permute-start(bf16[256,512]{1,0:T(8,128)(2,1)S(1)} %get-tuple-element.65), channel_id=1, source_target_pairs={{0,2},{2,0},{4,6},{6,4},{8,10},{10,8},{12,14},{14,12},{16,18},{18,... | collective-permute-start | bytes 786440 | tf_op jit(solution)/shard_map/ppermute | solution.py:719
  2.3 8.9 %collective-permute-start.3 = (bf16[256,1024]{1,0:T(8,128)(2,1)S(1)}, bf16[256,1024]{1,0:T(8,128)(2,1)S(1)}, u32[]{:S(2)}, u32[]{:S(2)}) collective-permute-start(bf16[256,1024]{1,0:T(8,128)(2,1)S(1)} %copy-done), channel_id=1, source_target_pairs={{0,2},{2,0},{4,6},{6,4},{8,10},{10,8},{12,14},{14,12},{16,18},{18,... | collective-permute-start | bytes 1572872 | tf_op jit(solution)/shard_map/ppermute | solution.py:719
  6.6 11.6 %collective-permute-start.4 = (bf16[528,128]{1,0:T(8,128)(2,1)S(1)}, bf16[528,128]{1,0:T(8,128)(2,1)S(1)}, u32[]{:S(2)}, u32[]{:S(2)}) collective-permute-start(bf16[528,128]{1,0:T(8,128)(2,1)S(1)} %get-tuple-element.76), channel_id=1, source_target_pairs={{0,4},{2,6},{4,0},{6,2},{8,12},{10,14},{12,8},{14,10},{16,20},{18,... | collective-permute-start | bytes 405512 | tf_op jit(solution)/shard_map/ppermute | solution.py:719
  9.6 8.6 %collective-permute-start.5 = (bf16[528,128]{1,0:T(8,128)(2,1)S(1)}, bf16[528,128]{1,0:T(8,128)(2,1)S(1)}, u32[]{:S(2)}, u32[]{:S(2)}) collective-permute-start(bf16[528,128]{1,0:T(8,128)(2,1)S(1)} %get-tuple-element.77), channel_id=1, source_target_pairs={{0,8},{2,10},{4,12},{6,14},{8,0},{10,2},{12,4},{14,6},{16,24},{18,... | collective-permute-start | bytes 405512 | tf_op jit(solution)/shard_map/ppermute | solution.py:719
  11.2 7.0 %collective-permute-start.6 = (bf16[528,128]{1,0:T(8,128)(2,1)S(1)}, bf16[528,128]{1,0:T(8,128)(2,1)S(1)}, u32[]{:S(2)}, u32[]{:S(2)}) collective-permute-start(bf16[528,128]{1,0:T(8,128)(2,1)S(1)} %get-tuple-element.78), channel_id=1, source_target_pairs={{0,12},{2,14},{4,8},{6,10},{8,4},{10,6},{12,0},{14,2},{16,28},{18,... | collective-permute-start | bytes 405512 | tf_op jit(solution)/shard_map/ppermute | solution.py:719
  11.3 6.9 %collective-permute-start.7 = (bf16[1,64,128]{2,1,0:T(8,128)(2,1)S(1)}, bf16[1,64,128]{2,1,0:T(8,128)(2,1)S(1)}, u32[]{:S(2)}, u32[]{:S(2)}) collective-permute-start(bf16[1,64,128]{2,1,0:T(8,128)(2,1)S(1)} %message.1.first_ref), channel_id=1, source_target_pairs={{0,8},{2,10},{4,12},{6,14},{8,0},{10,2},{12,4},{14,6},{16,24},{18,... | collective-permute-start | bytes 49160 | tf_op jit(solution)/shard_map/ppermute | solution.py:719
  18.4 7.6 %collective-permute-start.9 = (bf16[528,128]{1,0:T(8,128)(2,1)S(1)}, bf16[528,128]{1,0:T(8,128)(2,1)S(1)}, u32[]{:S(2)}, u32[]{:S(2)}) collective-permute-start(bf16[528,128]{1,0:T(8,128)(2,1)S(1)} %group_total.1), channel_id=1, source_target_pairs={{0,24},{2,26},{4,28},{6,30},{8,16},{10,18},{12,20},{14,22},{16,8},... | collective-permute-start | bytes 405512 | tf_op jit(solution)/shard_map/ppermute | solution.py:719
  22.1 3.9 %collective-permute-start.8 = (bf16[2,64,128]{2,1,0:T(8,128)(2,1)S(1)}, bf16[2,64,128]{2,1,0:T(8,128)(2,1)S(1)}, u32[]{:S(2)}, u32[]{:S(2)}) collective-permute-start(bf16[2,64,128]{2,1,0:T(8,128)(2,1)S(1)} %join.2.first_ref), channel_id=1, source_target_pairs={{0,4},{2,6},{4,0},{6,2},{8,12},{10,14},{12,8},{14,10},{16,20},{18,... | collective-permute-start | bytes 98312 | tf_op jit(solution)/shard_map/ppermute | solution.py:719
  26.0 5.3 %collective-permute-start.13 = (bf16[4,64,128]{2,1,0:T(8,128)(2,1)S(1)}, bf16[4,64,128]{2,1,0:T(8,128)(2,1)S(1)}, u32[]{:S(2)}, u32[]{:S(2)}) collective-permute-start(bf16[4,64,128]{2,1,0:T(8,128)(2,1)S(1)} %join.3.near_ref), channel_id=1, source_target_pairs={{0,16},{2,18},{4,20},{6,22},{8,24},{10,26},{12,28},{14,30},{16,0},... | collective-permute-start | bytes 196616 | tf_op jit(solution)/shard_map/ppermute | solution.py:719
  26.7 8.5 %collective-permute-start.10 = (bf16[528,128]{1,0:T(8,128)(2,1)S(1)}, bf16[528,128]{1,0:T(8,128)(2,1)S(1)}, u32[]{:S(2)}, u32[]{:S(2)}) collective-permute-start(bf16[528,128]{1,0:T(8,128)(2,1)S(1)} %get-tuple-element.92), channel_id=1, source_target_pairs={{0,4},{2,6},{4,0},{6,2},{8,12},{10,14},{12,8},{14,10},{16,20},{18,... | collective-permute-start | bytes 405512 | tf_op jit(solution)/shard_map/ppermute | solution.py:719
  28.0 7.2 %collective-permute-start.11 = (bf16[528,128]{1,0:T(8,128)(2,1)S(1)}, bf16[528,128]{1,0:T(8,128)(2,1)S(1)}, u32[]{:S(2)}, u32[]{:S(2)}) collective-permute-start(bf16[528,128]{1,0:T(8,128)(2,1)S(1)} %get-tuple-element.93), channel_id=1, source_target_pairs={{0,8},{2,10},{4,12},{6,14},{8,0},{10,2},{12,4},{14,6},{16,24},{18,... | collective-permute-start | bytes 405512 | tf_op jit(solution)/shard_map/ppermute | solution.py:719
  30.4 5.9 %collective-permute-start.12 = (bf16[528,128]{1,0:T(8,128)(2,1)S(1)}, bf16[528,128]{1,0:T(8,128)(2,1)S(1)}, u32[]{:S(2)}, u32[]{:S(2)}) collective-permute-start(bf16[528,128]{1,0:T(8,128)(2,1)S(1)} %get-tuple-element.94), channel_id=1, source_target_pairs={{0,12},{2,14},{4,8},{6,10},{8,4},{10,6},{12,0},{14,2},{16,28},{18,... | collective-permute-start | bytes 405512 | tf_op jit(solution)/shard_map/ppermute | solution.py:719
  32.6 5.2 %slice-start = ((s8[8388608]{0:T(1024)(128)(4,1)}), s8[4194304]{0:T(1024)(128)(4,1)S(1)}, s32[]{:S(2)}) async-start(s8[8388608]{0:T(1024)(128)(4,1)} %bitcast), calls=%async_computation | async-start | bytes 8388608
  32.7 5.2 %slice-start.1 = ((s8[8388608]{0:T(1024)(128)(4,1)}), s8[4194304]{0:T(1024)(128)(4,1)S(1)}, s32[]{:S(2)}) async-start(s8[8388608]{0:T(1024)(128)(4,1)} %bitcast), calls=%async_computation.1 | async-start | bytes 8388608
  37.2 2.0 %collective-permute-start.14 = (bf16[256,1024]{1,0:T(8,128)(2,1)S(1)}, bf16[256,1024]{1,0:T(8,128)(2,1)S(1)}, u32[]{:S(2)}, u32[]{:S(2)}) collective-permute-start(bf16[256,1024]{1,0:T(8,128)(2,1)S(1)} %get-tuple-element.108), channel_id=1, source_target_pairs={{0,2},{2,0},{4,6},{6,4},{8,10},{10,8},{12,14},{14,12},{16,18},{18,... | collective-permute-start | bytes 1572872 | tf_op jit(solution)/shard_map/ppermute | solution.py:719
  39.6 9.2 %collective-permute-start.16 = (bf16[256,512]{1,0:T(8,128)(2,1)S(1)}, bf16[256,512]{1,0:T(8,128)(2,1)S(1)}, u32[]{:S(2)}, u32[]{:S(2)}) collective-permute-start(bf16[256,512]{1,0:T(8,128)(2,1)S(1)} %project_other.3), channel_id=1, source_target_pairs={{0,1},{1,0},{2,3},{3,2},{4,5},{5,4},{6,7},{7,6},{8,9},{9,8},{10,11... | collective-permute-start | bytes 786440 | tf_op jit(solution)/shard_map/ppermute | solution.py:894
  42.9 10.8 %collective-permute-start.15 = (bf16[256,512]{1,0:T(8,128)(2,1)S(1)}, bf16[256,512]{1,0:T(8,128)(2,1)S(1)}, u32[]{:S(2)}, u32[]{:S(2)}) collective-permute-start(bf16[256,512]{1,0:T(8,128)(2,1)S(1)} %project_other.2), channel_id=1, source_target_pairs={{0,1},{1,0},{2,3},{3,2},{4,5},{5,4},{6,7},{7,6},{8,9},{9,8},{10,11... | collective-permute-start | bytes 786440 | tf_op jit(solution)/shard_map/ppermute | solution.py:894

commit v7 on v6

--- a/solution.py
+++ b/solution.py
@@ -167,19 +167,16 @@
 def chip_kernel(
     per_core, lengths_ref, own_keys, own_values, key_other, value_other, gates_ref, gates_other,
     taps,
-    conv_ref, values, gate_ref, key_edge, levels_first, out0, out1, out2, out3,
-    raw, picked, wide, weighted_ref, whole, normals, levels, sems,
+    conv_ref, gate_ref, key_edge, levels_first, out0, out1, out2, out3,
+    raw, picked, wide, weighted_ref, whole, normals, levels,
 ):
     core, mine = core_place()
     rows, width = own_keys.shape
     length = 2 * rows
     key_width = width // per_core
-    value_width = values.shape[1] // per_core
+    value_width = own_values.shape[1] // per_core
     own_rows = pl.ds(pl.multiple_of(core * rows, rows), rows)
     other_rows = pl.ds(pl.multiple_of((1 - core) * rows, rows), rows)
-    copies = start_copies(
-        sems, [(own_values, values.at[own_rows, :]), (value_other, values.at[other_rows, :])]
-    )
     offset = lax.axis_index("seq") // 2 * length
     gate, cumulative = gate_rows(core, per_core, (gates_ref, gates_other), raw, picked)
     gate_ref[0] = gate
@@ -238,12 +235,11 @@
             levels[0, pl.ds(head, 1), :][:, 0:1],
             levels[1, pl.ds(head, 1), :][:, 0:1],
         )
-    for copy in copies:
-        copy.wait()
 
 
 def message_kernel(
-    per_core, query_ref, query_other, key_edge, values, levels_first, out_ref, rows_ref, tail, sems
+    per_core, query_ref, query_other, key_edge, own_values, value_other, levels_first,
+    out_ref, rows_ref, tail, sems,
 ):
     core, _ = core_place()
     width = key_edge.shape[2]
@@ -262,7 +258,7 @@
     at = 0
     for block in (
         key_edge[0].astype(F32)[0:FIRST],
-        values[0:16, :].astype(F32)[0:FIRST],
+        jnp.where(core == 0, own_values[0:16, :], value_other[0:16, :]).astype(F32)[0:FIRST],
         key_edge[1].astype(F32)[16 - FIRST :],
         tail[...].astype(F32)[16 - FIRST :],
     ):
@@ -431,8 +427,8 @@
     infos = [read_info(s) for s in states]
     n_p, m_p, _ = read_info(prefix_ref)
     valid = True if bit is None else is_later(bit)
-    for off in (1, 2, 3, 0):
-        out = outs[off]
+    weights = []
+    for off, out in enumerate(outs):
         stabs = shifted_stab(infos, ranks, ranks[off])
         m_in = m_p
         for info, rank in zip(infos, ranks):
@@ -442,21 +438,26 @@
             jnp.where(rank < ranks[off], s, 2 * very_negative) for s, rank in zip(stabs, ranks)
         ]
         m = functools.reduce(jnp.maximum, stabs, m_in)
-        w_in = jnp.where(valid, jnp.exp(m_in - m), 0.0)
-        total = w_in * prefix_ref[0:rows, :].astype(F32)
-        normal = w_in * n_p
-        for i in range(4):
-            if i != off:
-                w = jnp.where(ranks[i] < ranks[off], jnp.exp(stabs[i] - m), 0.0)
-                total = total + w * states[i][0:rows, :].astype(F32)
-                normal = normal + w * infos[i][0]
-        out[0:rows, :] = total.astype(BF16)
-        write_info(out, normal, m, jnp.zeros_like(m))
+        mine_in = [jnp.where(valid, jnp.exp(m_in - m), 0.0)] + [
+            jnp.where(rank < ranks[off], jnp.exp(s - m), 0.0) for s, rank in zip(stabs, ranks)
+        ]
+        weights.append(mine_in)
+        normals = [n_p] + [info[0] for info in infos]
+        write_info(out, sum(w * n for w, n in zip(mine_in, normals)), m, jnp.zeros_like(m))
+    step = math.gcd(rows, 64)
+    for at in range(0, rows, step):
+        parts = [r[at : at + step, :].astype(F32) for r in (prefix_ref, *states)]
+        for off, out in enumerate(outs):
+            out[at : at + step, :] = sum(
+                w * part
+                for k, (w, part) in enumerate(zip(weights[off], parts))
+                if k != off + 1
+            ).astype(BF16)
 
 
 def query_kernel(
-    per_core, lengths_ref, query_ref, query_other, taps_ref,
-    conv_ref, taps, edge_ref, queries, wide, sems,
+    per_core, lengths_ref, query_ref, query_other, taps_ref, own_values, value_other,
+    conv_ref, taps, edge_ref, values, queries, wide, sems,
 ):
     core, _ = core_place()
     length, width = queries.shape
@@ -466,7 +467,8 @@
     copies = start_copies(
         sems,
         [(taps_ref.at[0, :, columns], taps)]
-        + by_core(core, query_ref, query_other, columns, queries),
+        + by_core(core, query_ref, query_other, columns, queries)
+        + by_core(core, own_values, value_other, slice(None), values),
     )
     offset = lax.axis_index("seq") // 2 * length
     same = same_request(lengths_ref, offset + iota((length, 128), 0))
@@ -742,11 +744,10 @@
     query_other = swap(query_after, 1)
 
     one = shape((rows * value_width // 128 + INFO, 128), BF16)
-    key_conv, values, gate_sums, key_edge, levels, *pieces = call(
+    key_conv, gate_sums, key_edge, levels, *pieces = call(
         functools.partial(chip_kernel, per_core),
         (
             shape((chip_length, part_keys), BF16),
-            shape((chip_length, part_values), BF16),
             shape((2, 8, chip_length)),
             shape((2, 16, part_keys), BF16),
             shape((2, 8, 128)),
@@ -761,7 +762,6 @@
             pltpu.VMEM((part_keys, value_width), BF16),
             pltpu.VMEM((8, key_width), F32),
             pltpu.VMEM((2, 8, 128), F32),
-            pltpu.SemaphoreType.DMA((2,)),
         ],
         "chip_state",
         flops=1 << 30,
@@ -774,33 +774,34 @@
     lines = FIRST * per_core * (3 * key_width + value_width) // 128 + 3
     lines = -(-lines // 16) * 16
     message = call(
-        functools.partial(message_kernel, per_core), shape((1, lines, 128), BF16), "havvv",
+        functools.partial(message_kernel, per_core), shape((1, lines, 128), BF16), "havvvv",
         [
             pltpu.VMEM((lines, 128), F32),
             pltpu.VMEM((16, part_keys), BF16),
             pltpu.SemaphoreType.DMA((1,)),
         ],
         "message",
-    )(query_input, query_other, key_edge, values, levels)
+    )(query_input, query_other, key_edge, own_values, value_other, levels)
     bits = seq_count.bit_length() - 1
     steps = [4, 2, 8] if bits == 4 else [1 << b for b in range(1, bits)]
     near, far, offsets = message, swap(message, steps[0]), [0, steps[0] // 2]
-    query_conv, query_taps, query_edge = call(
+    query_conv, query_taps, query_edge, values = call(
         functools.partial(query_kernel, per_core),
         (
             shape((chip_length, part_keys), BF16),
             shape((lags, part_keys)),
             shape((2, 16, part_keys), BF16),
+            shape((chip_length, part_values), BF16),
         ),
-        "shah",
+        "shahvv",
         [
             pltpu.VMEM((chip_length, part_keys), BF16),
             pltpu.VMEM((chip_length + 8, key_width), F32),
-            pltpu.SemaphoreType.DMA((3,)),
+            pltpu.SemaphoreType.DMA((5,)),
         ],
         "query_conv",
         flops=1 << 30,
-    )(request_lengths, query_input, query_other, kernel_taps)
+    )(request_lengths, query_input, query_other, kernel_taps, own_values, value_other)
     states, query_conv, far = lax.optimization_barrier((states, query_conv, far))
     total = call(total_kernel, one, "vvvv", [], "group_total")(*states)
     flag = 3
@@ -902,7 +903,7 @@
                 functools.partial(sum_kernel, chunk, len(arrived)),
                 shape((length, out_cols), BF16),
                 "v" * (1 + len(arrived)) + "a" * len(out),
-                [pltpu.VMEM((length, piece), BF16), pltpu.SemaphoreType.DMA((4,))],
+                [pltpu.VMEM((length, piece), BF16), pltpu.SemaphoreType.DMA((2,))],
                 "mixed_out", out=pl.ANY, aliases={1 + len(arrived): 0} if out else None,
             )(mixed, *(columns[chunk] for columns in arrived), *out)
         ]

time: 54.7 us -> 54.4 us (level)
  transfers between devices with their start and end apart: 17 -> 17, of which waited for: 8 -> 8; matrix products, arithmetic and copies ran while one was open for 0% -> 0% of each run, Pallas kernels for 28% -> 27%
where the time goes in v7:
time: 54.4 us; the launch traced here: 54.1 us
  starting transfers between devices  18.9 us (35%)
  Pallas kernels  18.3 us (34%)
  waiting for transfers between devices  16.6 us (31%)
    pallas_call x19, Pallas kernels, run(): inner(*(pltpu.with_memory_space_constraint(x, pltpu.HBM) if s in 'hs' els...  18.3 us
    ppermute x15, starting transfers between devices, swap(): return lax.ppermute(x, 'seq', [(i, i ^ off) for i in range(seq_count)])  16.8 us
    ppermute x2, waiting for transfers between devices, on_device(): lax.ppermute(part, 'head', [(i, i ^ off) for i in range(head_count)])  9.41 us
    ppermute x15, waiting for transfers between devices, swap(): return lax.ppermute(x, 'seq', [(i, i ^ off) for i in range(seq_count)])  7.22 us
    ppermute x2, starting transfers between devices, on_device(): lax.ppermute(part, 'head', [(i, i ^ off) for i in range(head_count)])  2.16 us
  transfers between devices with their start and end apart: 17, of which 8 were waited for; matrix products, arithmetic and copies ran while one was open for 0% of the time, Pallas kernels for 27%

profile of v7, /device:TPU:0, one launch (start us, length us, event | category | flops | bytes accessed | tf_op | source)
XLA Modules:
  0.0 54.1 jit_solution(1822018028442621630)
XLA Ops:
  0.0 1.2 %gates.1 = (f32[2,4,256]{2,1,0:T(4,128)S(1)}, bf16[256,512]{1,0:T(8,128)(2,1)S(1)}, bf16[256,1024]{1,0:T(8,128)(2,1)S(1)}) custom-call(f32[4,256]{1,0:T(4,128)} %input_ref.1, f32[4,256]{1,0:T(4,128)} %forget_ref.1, bf16[256,1024]{1,0:T(8,128)(2,1)} %key_ref.2, bf16[256,2048]{1,0:T(8,128)(2,1)} %value_ref.2), custom_call_target="tpu_custom_call" | custom-call | flops 4294967296 | tf_op jit(solution)/shard_map/gates/pallas_call | solution.py:690
  2.3 1.1 %own_part.1 = (bf16[256,512]{1,0:T(8,128)(2,1)S(1)}, bf16[256,1024]{1,0:T(8,128)(2,1)S(1)}, f32[4,512]{1,0:T(4,128)S(1)}) custom-call(bf16[256,1024]{1,0:T(8,128)(2,1)} %key_ref.2, bf16[256,2048]{1,0:T(8,128)(2,1)} %value_ref.2, f32[2,4,1024]{2,1,0:T(4,128)} %taps_ref.3), custom_call_target="tpu_custom_call" | custom-call | flops 4294967296 | tf_op jit(solution)/shard_map/own_part/pallas_call | solution.py:690
  3.7 2.8 %chip_state.1 = (bf16[512,512]{1,0:T(8,128)(2,1)S(1)}, f32[2,8,512]{2,1,0:T(8,128)S(1)}, bf16[2,16,512]{2,1,0:T(8,128)(2,1)S(1)}, f32[2,8,128]{2,1,0:T(8,128)S(1...) custom-call(s32[4]{0:T(128)} %lengths_ref.7, ...), custom_call_target="tpu_custom_call" | custom-call | flops 1073741824 | tf_op jit(solution)/shard_map/chip_state/pallas_call | solution.py:690
  6.5 3.0 %collective-permute-start.4 = (bf16[528,128]{1,0:T(8,128)(2,1)S(1)}, bf16[528,128]{1,0:T(8,128)(2,1)S(1)}, u32[]{:S(2)}, u32[]{:S(2)}) collective-permute-start(bf16[528,128]{1,0:T(8,128)(2,1)S(1)} %get-tuple-element.75), channel_id=1, source_target_pairs={{0,4},{2,6},{4,0},{6,2},{8,12},{10,14},{12,8},{14,10},{16,20},{18,... | collective-permute-start | bytes 405512 | tf_op jit(solution)/shard_map/ppermute | solution.py:721
  9.5 1.6 %collective-permute-start.5 = (bf16[528,128]{1,0:T(8,128)(2,1)S(1)}, bf16[528,128]{1,0:T(8,128)(2,1)S(1)}, u32[]{:S(2)}, u32[]{:S(2)}) collective-permute-start(bf16[528,128]{1,0:T(8,128)(2,1)S(1)} %get-tuple-element.76), channel_id=1, source_target_pairs={{0,8},{2,10},{4,12},{6,14},{8,0},{10,2},{12,4},{14,6},{16,24},{18,... | collective-permute-start | bytes 405512 | tf_op jit(solution)/shard_map/ppermute | solution.py:721
  11.1 2.0 %collective-permute-start.7 = (bf16[1,64,128]{2,1,0:T(8,128)(2,1)S(1)}, bf16[1,64,128]{2,1,0:T(8,128)(2,1)S(1)}, u32[]{:S(2)}, u32[]{:S(2)}) collective-permute-start(bf16[1,64,128]{2,1,0:T(8,128)(2,1)S(1)} %message.1.first_ref), channel_id=1, source_target_pairs={{0,8},{2,10},{4,12},{6,14},{8,0},{10,2},{12,4},{14,6},{16,24},{18,... | collective-permute-start | bytes 49160 | tf_op jit(solution)/shard_map/ppermute | solution.py:721
  13.2 2.7 %query_conv.1 = (bf16[512,512]{1,0:T(8,128)(2,1)S(1)}, f32[4,512]{1,0:T(4,128)S(1)}, bf16[2,16,512]{2,1,0:T(8,128)(2,1)S(1)}, bf16[512,1024]{1,0:T(8,128)(2,1)S(1)}) custom-call(s32[4]{0:T(128)} %lengths_ref.7, bf16[256,1024]{1,0:T(8,128)(2,1)} %query_ref.3, bf16[256,1024]{1,0:T(8,128)(2,1)S(1)} %collective-permute-done.3.query_other, ...), custom_call_target="tpu_custom_call" | custom-call | flops 1073741824 | tf_op jit(solution)/shard_map/query_conv/pallas_call | solution.py:690
  15.8 2.2 %collective-permute-done.7.second_ref = bf16[1,64,128]{2,1,0:T(8,128)(2,1)S(1)} collective-permute-done((bf16[1,64,128]{2,1,0:T(8,128)(2,1)S(1)}, bf16[1,64,128]{2,1,0:T(8,128)(2,1)S(1)}, u32[]{:S(2)}, u32[]{:S(2)}) %collective-permute-start.7) | collective-permute-done | bytes 16416 | tf_op jit(solution)/shard_map/ppermute | solution.py:721
  18.3 3.7 %collective-permute-start.9 = (bf16[528,128]{1,0:T(8,128)(2,1)S(1)}, bf16[528,128]{1,0:T(8,128)(2,1)S(1)}, u32[]{:S(2)}, u32[]{:S(2)}) collective-permute-start(bf16[528,128]{1,0:T(8,128)(2,1)S(1)} %group_total.1), channel_id=1, source_target_pairs={{0,24},{2,26},{4,28},{6,30},{8,16},{10,18},{12,20},{14,22},{16,8},... | collective-permute-start | bytes 405512 | tf_op jit(solution)/shard_map/ppermute | solution.py:721
  22.0 1.3 %collective-permute-start.8 = (bf16[2,64,128]{2,1,0:T(8,128)(2,1)S(1)}, bf16[2,64,128]{2,1,0:T(8,128)(2,1)S(1)}, u32[]{:S(2)}, u32[]{:S(2)}) collective-permute-start(bf16[2,64,128]{2,1,0:T(8,128)(2,1)S(1)} %join.2.first_ref), channel_id=1, source_target_pairs={{0,4},{2,6},{4,0},{6,2},{8,12},{10,14},{12,8},{14,10},{16,20},{18,... | collective-permute-start | bytes 98312 | tf_op jit(solution)/shard_map/ppermute | solution.py:721
  23.2 2.6 %collective-permute-done.8.second_ref = bf16[2,64,128]{2,1,0:T(8,128)(2,1)S(1)} collective-permute-done((bf16[2,64,128]{2,1,0:T(8,128)(2,1)S(1)}, bf16[2,64,128]{2,1,0:T(8,128)(2,1)S(1)}, u32[]{:S(2)}, u32[]{:S(2)}) %collective-permute-start.8) | collective-permute-done | bytes 32800 | tf_op jit(solution)/shard_map/ppermute | solution.py:721
  26.4 1.3 %collective-permute-start.10 = (bf16[528,128]{1,0:T(8,128)(2,1)S(1)}, bf16[528,128]{1,0:T(8,128)(2,1)S(1)}, u32[]{:S(2)}, u32[]{:S(2)}) collective-permute-start(bf16[528,128]{1,0:T(8,128)(2,1)S(1)} %get-tuple-element.91), channel_id=1, source_target_pairs={{0,4},{2,6},{4,0},{6,2},{8,12},{10,14},{12,8},{14,10},{16,20},{18,... | collective-permute-start | bytes 405512 | tf_op jit(solution)/shard_map/ppermute | solution.py:721
  27.7 2.4 %collective-permute-start.11 = (bf16[528,128]{1,0:T(8,128)(2,1)S(1)}, bf16[528,128]{1,0:T(8,128)(2,1)S(1)}, u32[]{:S(2)}, u32[]{:S(2)}) collective-permute-start(bf16[528,128]{1,0:T(8,128)(2,1)S(1)} %get-tuple-element.92), channel_id=1, source_target_pairs={{0,8},{2,10},{4,12},{6,14},{8,0},{10,2},{12,4},{14,6},{16,24},{18,... | collective-permute-start | bytes 405512 | tf_op jit(solution)/shard_map/ppermute | solution.py:721
  30.5 0.8 %collective-permute-done.13.far_ref = bf16[4,64,128]{2,1,0:T(8,128)(2,1)S(1)} collective-permute-done((bf16[4,64,128]{2,1,0:T(8,128)(2,1)S(1)}, bf16[4,64,128]{2,1,0:T(8,128)(2,1)S(1)}, u32[]{:S(2)}, u32[]{:S(2)}) %collective-permute-start.13) | collective-permute-done | bytes 65568 | tf_op jit(solution)/shard_map/ppermute | solution.py:721
  31.3 1.4 %gathered_first.1 = (bf16[256,256]{1,0:T(8,128)(2,1)S(1)}, bf16[256,512]{1,0:T(8,128)(2,1)S(1)}, f32[256,128]{1,0:T(8,128)S(1)}, bf16[2,16,512]{2,1,0:T(8,128)(2,1)S(1)}) custom-call(s32[4]{0:T(128)} %lengths_ref.7, bf16[4,64,128]{2,1,0:T(8,128)(2,1)S(1)} %join.3.near_ref, bf16[4,64,128]{2,1,0:T(8,128)(2,1)S(1)} %collective-permute-done.13.far_ref, ...), custom_call_target="tpu_custom_call" | custom-call | tf_op jit(solution)/shard_map/gathered_first/pallas_call | solution.py:690
  32.7 2.5 %intra.1 = (bf16[512,512]{1,0:T(8,128)(2,1)S(1)}, f32[512,1024]{1,0:T(8,128)S(1)}, f32[3,512,128]{2,1,0:T(8,128)S(1)}) custom-call(s32[4]{0:T(128)} %lengths_ref.7, bf16[512,512]{1,0:T(8,128)(2,1)S(1)} %get-tuple-element.100.query_conv, bf16[512,512]{1,0:T(8,128)(2,1)S(1)} %get-tuple-element.101.key_ref, ...), custom_call_target="tpu_custom_call" | custom-call | flops 4294967296 | tf_op jit(solution)/shard_map/intra/pallas_call | solution.py:690
  35.3 0.8 %collective-permute-done.12.got3 = bf16[528,128]{1,0:T(8,128)(2,1)S(1)} collective-permute-done((bf16[528,128]{1,0:T(8,128)(2,1)S(1)}, bf16[528,128]{1,0:T(8,128)(2,1)S(1)}, u32[]{:S(2)}, u32[]{:S(2)}) %collective-permute-start.12) | collective-permute-done | bytes 135200 | tf_op jit(solution)/shard_map/ppermute | solution.py:721
  36.0 0.9 %head_send.1 = (bf16[256,1024]{1,0:T(8,128)(2,1)S(1)}, bf16[512,512]{1,0:T(8,128)(2,1)S(1)}, bf16[256,256]{1,0:T(8,128)(2,1)S(1)}, f32[8,128]{1,0:T(8,128)S(1)}) custom-call(bf16[528,128]{1,0:T(8,128)(2,1)S(1)} %get-tuple-element.90.own_ref, bf16[528,128]{1,0:T(8,128)(2,1)S(1)} %collective-permute-done.10.got1, ...), custom_call_target="tpu_custom_call" | custom-call | tf_op jit(solution)/shard_map/head_send/pallas_call | solution.py:690
  39.4 1.5 %collective-permute-start.16 = (bf16[256,512]{1,0:T(8,128)(2,1)S(1)}, bf16[256,512]{1,0:T(8,128)(2,1)S(1)}, u32[]{:S(2)}, u32[]{:S(2)}) collective-permute-start(bf16[256,512]{1,0:T(8,128)(2,1)S(1)} %project_other.3), channel_id=1, source_target_pairs={{0,1},{1,0},{2,3},{3,2},{4,5},{5,4},{6,7},{7,6},{8,9},{9,8},{10,11... | collective-permute-start | bytes 786440 | tf_op jit(solution)/shard_map/ppermute | solution.py:895
  40.9 1.2 %project_own.1.own_ref = f32[256,1024]{1,0:T(8,128)S(1)} custom-call(bf16[256,1024]{1,0:T(8,128)(2,1)S(1)} %head_keep.1.keep_ref.head_ref, bf16[256,1024]{1,0:T(8,128)(2,1)S(1)} %collective-permute-done.14.got_ref.head_ref, bf16[2048,2048]{1,0:T(8,128)(2,1)S(1)} %bitcast.1), custom_call_target="tpu_custom_call" | custom-call | flops 4294967296 | tf_op jit(solution)/shard_map/project_own/pallas_call | solution.py:690
  43.2 5.3 %collective-permute-done.16.refs_0_ = bf16[256,512]{1,0:T(8,128)(2,1)S(1)} collective-permute-done((bf16[256,512]{1,0:T(8,128)(2,1)S(1)}, bf16[256,512]{1,0:T(8,128)(2,1)S(1)}, u32[]{:S(2)}, u32[]{:S(2)}) %collective-permute-start.16) | collective-permute-done | bytes 262176 | tf_op jit(solution)/shard_map/ppermute | solution.py:895
  48.6 0.7 %mixed_out.2.refs_1_ = bf16[256,1024]{1,0:T(8,128)(2,1)} custom-call(f32[256,1024]{1,0:T(8,128)S(1)} %project_own.1.own_ref, bf16[256,512]{1,0:T(8,128)(2,1)S(1)} %collective-permute-done.16.refs_0_), custom_call_target="tpu_custom_call" | custom-call | tf_op jit(solution)/shard_map/mixed_out/pallas_call | solution.py:690
  49.3 4.1 %collective-permute-done.15.refs_0_ = bf16[256,512]{1,0:T(8,128)(2,1)S(1)} collective-permute-done((bf16[256,512]{1,0:T(8,128)(2,1)S(1)}, bf16[256,512]{1,0:T(8,128)(2,1)S(1)}, u32[]{:S(2)}, u32[]{:S(2)}) %collective-permute-start.15) | collective-permute-done | bytes 262176 | tf_op jit(solution)/shard_map/ppermute | solution.py:895
  53.4 0.7 %mixed_out.3 = bf16[256,1024]{1,0:T(8,128)(2,1)} custom-call(f32[256,1024]{1,0:T(8,128)S(1)} %project_own.1.own_ref, bf16[256,512]{1,0:T(8,128)(2,1)S(1)} %collective-permute-done.15.refs_0_, bf16[256,1024]{1,0:T(8,128)(2,1)} %mixed_out.2.refs_1_), custom_call_target="tpu_custom_call", output_to_operand_aliasing={{}: (2, {})} | custom-call | tf_op jit(solution)/shard_map/mixed_out/pallas_call | solution.py:690
  (36 shorter events, 5.9 us)
Async XLA Ops:
  0.0 2.3 %copy-start = (bf16[256,1024]{1,0:T(8,128)(2,1)S(1)}, bf16[256,1024]{1,0:T(8,128)(2,1)}, u32[]{:S(2)}) copy-start(bf16[256,1024]{1,0:T(8,128)(2,1)} %query_ref.3) | copy-start | bytes 1572868
  1.2 2.4 %collective-permute-start.1 = (bf16[256,1024]{1,0:T(8,128)(2,1)S(1)}, bf16[256,1024]{1,0:T(8,128)(2,1)S(1)}, u32[]{:S(2)}, u32[]{:S(2)}) collective-permute-start(bf16[256,1024]{1,0:T(8,128)(2,1)S(1)} %get-tuple-element.66), channel_id=1, source_target_pairs={{0,2},{2,0},{4,6},{6,4},{8,10},{10,8},{12,14},{14,12},{16,18},{18,... | collective-permute-start | bytes 1572872 | tf_op jit(solution)/shard_map/ppermute | solution.py:721
  1.7 1.8 %collective-permute-start.2 = (f32[2,4,256]{2,1,0:T(4,128)S(1)}, f32[2,4,256]{2,1,0:T(4,128)S(1)}, u32[]{:S(2)}, u32[]{:S(2)}) collective-permute-start(f32[2,4,256]{2,1,0:T(4,128)S(1)} %get-tuple-element.68.gates_ref), channel_id=1, source_target_pairs={{0,2},{2,0},{4,6},{6,4},{8,10},{10,8},{12,14},{14,12},{16,18},{18,... | collective-permute-start | bytes 24584 | tf_op jit(solution)/shard_map/ppermute | solution.py:721
  1.8 1.8 %collective-permute-start = (bf16[256,512]{1,0:T(8,128)(2,1)S(1)}, bf16[256,512]{1,0:T(8,128)(2,1)S(1)}, u32[]{:S(2)}, u32[]{:S(2)}) collective-permute-start(bf16[256,512]{1,0:T(8,128)(2,1)S(1)} %get-tuple-element.65), channel_id=1, source_target_pairs={{0,2},{2,0},{4,6},{6,4},{8,10},{10,8},{12,14},{14,12},{16,18},{18,... | collective-permute-start | bytes 786440 | tf_op jit(solution)/shard_map/ppermute | solution.py:721
  2.3 8.8 %collective-permute-start.3 = (bf16[256,1024]{1,0:T(8,128)(2,1)S(1)}, bf16[256,1024]{1,0:T(8,128)(2,1)S(1)}, u32[]{:S(2)}, u32[]{:S(2)}) collective-permute-start(bf16[256,1024]{1,0:T(8,128)(2,1)S(1)} %copy-done), channel_id=1, source_target_pairs={{0,2},{2,0},{4,6},{6,4},{8,10},{10,8},{12,14},{14,12},{16,18},{18,... | collective-permute-start | bytes 1572872 | tf_op jit(solution)/shard_map/ppermute | solution.py:721
  6.5 11.6 %collective-permute-start.4 = (bf16[528,128]{1,0:T(8,128)(2,1)S(1)}, bf16[528,128]{1,0:T(8,128)(2,1)S(1)}, u32[]{:S(2)}, u32[]{:S(2)}) collective-permute-start(bf16[528,128]{1,0:T(8,128)(2,1)S(1)} %get-tuple-element.75), channel_id=1, source_target_pairs={{0,4},{2,6},{4,0},{6,2},{8,12},{10,14},{12,8},{14,10},{16,20},{18,... | collective-permute-start | bytes 405512 | tf_op jit(solution)/shard_map/ppermute | solution.py:721
  9.5 8.6 %collective-permute-start.5 = (bf16[528,128]{1,0:T(8,128)(2,1)S(1)}, bf16[528,128]{1,0:T(8,128)(2,1)S(1)}, u32[]{:S(2)}, u32[]{:S(2)}) collective-permute-start(bf16[528,128]{1,0:T(8,128)(2,1)S(1)} %get-tuple-element.76), channel_id=1, source_target_pairs={{0,8},{2,10},{4,12},{6,14},{8,0},{10,2},{12,4},{14,6},{16,24},{18,... | collective-permute-start | bytes 405512 | tf_op jit(solution)/shard_map/ppermute | solution.py:721
  11.0 7.0 %collective-permute-start.6 = (bf16[528,128]{1,0:T(8,128)(2,1)S(1)}, bf16[528,128]{1,0:T(8,128)(2,1)S(1)}, u32[]{:S(2)}, u32[]{:S(2)}) collective-permute-start(bf16[528,128]{1,0:T(8,128)(2,1)S(1)} %get-tuple-element.77), channel_id=1, source_target_pairs={{0,12},{2,14},{4,8},{6,10},{8,4},{10,6},{12,0},{14,2},{16,28},{18,... | collective-permute-start | bytes 405512 | tf_op jit(solution)/shard_map/ppermute | solution.py:721
  11.1 6.9 %collective-permute-start.7 = (bf16[1,64,128]{2,1,0:T(8,128)(2,1)S(1)}, bf16[1,64,128]{2,1,0:T(8,128)(2,1)S(1)}, u32[]{:S(2)}, u32[]{:S(2)}) collective-permute-start(bf16[1,64,128]{2,1,0:T(8,128)(2,1)S(1)} %message.1.first_ref), channel_id=1, source_target_pairs={{0,8},{2,10},{4,12},{6,14},{8,0},{10,2},{12,4},{14,6},{16,24},{18,... | collective-permute-start | bytes 49160 | tf_op jit(solution)/shard_map/ppermute | solution.py:721
  18.3 7.6 %collective-permute-start.9 = (bf16[528,128]{1,0:T(8,128)(2,1)S(1)}, bf16[528,128]{1,0:T(8,128)(2,1)S(1)}, u32[]{:S(2)}, u32[]{:S(2)}) collective-permute-start(bf16[528,128]{1,0:T(8,128)(2,1)S(1)} %group_total.1), channel_id=1, source_target_pairs={{0,24},{2,26},{4,28},{6,30},{8,16},{10,18},{12,20},{14,22},{16,8},... | collective-permute-start | bytes 405512 | tf_op jit(solution)/shard_map/ppermute | solution.py:721
  22.0 3.9 %collective-permute-start.8 = (bf16[2,64,128]{2,1,0:T(8,128)(2,1)S(1)}, bf16[2,64,128]{2,1,0:T(8,128)(2,1)S(1)}, u32[]{:S(2)}, u32[]{:S(2)}) collective-permute-start(bf16[2,64,128]{2,1,0:T(8,128)(2,1)S(1)} %join.2.first_ref), channel_id=1, source_target_pairs={{0,4},{2,6},{4,0},{6,2},{8,12},{10,14},{12,8},{14,10},{16,20},{18,... | collective-permute-start | bytes 98312 | tf_op jit(solution)/shard_map/ppermute | solution.py:721
  25.9 5.4 %collective-permute-start.13 = (bf16[4,64,128]{2,1,0:T(8,128)(2,1)S(1)}, bf16[4,64,128]{2,1,0:T(8,128)(2,1)S(1)}, u32[]{:S(2)}, u32[]{:S(2)}) collective-permute-start(bf16[4,64,128]{2,1,0:T(8,128)(2,1)S(1)} %join.3.near_ref), channel_id=1, source_target_pairs={{0,16},{2,18},{4,20},{6,22},{8,24},{10,26},{12,28},{14,30},{16,0},... | collective-permute-start | bytes 196616 | tf_op jit(solution)/shard_map/ppermute | solution.py:721
  26.4 8.8 %collective-permute-start.10 = (bf16[528,128]{1,0:T(8,128)(2,1)S(1)}, bf16[528,128]{1,0:T(8,128)(2,1)S(1)}, u32[]{:S(2)}, u32[]{:S(2)}) collective-permute-start(bf16[528,128]{1,0:T(8,128)(2,1)S(1)} %get-tuple-element.91), channel_id=1, source_target_pairs={{0,4},{2,6},{4,0},{6,2},{8,12},{10,14},{12,8},{14,10},{16,20},{18,... | collective-permute-start | bytes 405512 | tf_op jit(solution)/shard_map/ppermute | solution.py:721
  27.7 7.5 %collective-permute-start.11 = (bf16[528,128]{1,0:T(8,128)(2,1)S(1)}, bf16[528,128]{1,0:T(8,128)(2,1)S(1)}, u32[]{:S(2)}, u32[]{:S(2)}) collective-permute-start(bf16[528,128]{1,0:T(8,128)(2,1)S(1)} %get-tuple-element.92), channel_id=1, source_target_pairs={{0,8},{2,10},{4,12},{6,14},{8,0},{10,2},{12,4},{14,6},{16,24},{18,... | collective-permute-start | bytes 405512 | tf_op jit(solution)/shard_map/ppermute | solution.py:721
  30.1 5.9 %collective-permute-start.12 = (bf16[528,128]{1,0:T(8,128)(2,1)S(1)}, bf16[528,128]{1,0:T(8,128)(2,1)S(1)}, u32[]{:S(2)}, u32[]{:S(2)}) collective-permute-start(bf16[528,128]{1,0:T(8,128)(2,1)S(1)} %get-tuple-element.93), channel_id=1, source_target_pairs={{0,12},{2,14},{4,8},{6,10},{8,4},{10,6},{12,0},{14,2},{16,28},{18,... | collective-permute-start | bytes 405512 | tf_op jit(solution)/shard_map/ppermute | solution.py:721
  32.7 4.9 %slice-start = ((s8[8388608]{0:T(1024)(128)(4,1)}), s8[4194304]{0:T(1024)(128)(4,1)S(1)}, s32[]{:S(2)}) async-start(s8[8388608]{0:T(1024)(128)(4,1)} %bitcast), calls=%async_computation | async-start | bytes 8388608
  32.7 4.9 %slice-start.1 = ((s8[8388608]{0:T(1024)(128)(4,1)}), s8[4194304]{0:T(1024)(128)(4,1)S(1)}, s32[]{:S(2)}) async-start(s8[8388608]{0:T(1024)(128)(4,1)} %bitcast), calls=%async_computation.1 | async-start | bytes 8388608
  36.9 2.0 %collective-permute-start.14 = (bf16[256,1024]{1,0:T(8,128)(2,1)S(1)}, bf16[256,1024]{1,0:T(8,128)(2,1)S(1)}, u32[]{:S(2)}, u32[]{:S(2)}) collective-permute-start(bf16[256,1024]{1,0:T(8,128)(2,1)S(1)} %get-tuple-element.108), channel_id=1, source_target_pairs={{0,2},{2,0},{4,6},{6,4},{8,10},{10,8},{12,14},{14,12},{16,18},{18,... | collective-permute-start | bytes 1572872 | tf_op jit(solution)/shard_map/ppermute | solution.py:721
  39.4 9.2 %collective-permute-start.16 = (bf16[256,512]{1,0:T(8,128)(2,1)S(1)}, bf16[256,512]{1,0:T(8,128)(2,1)S(1)}, u32[]{:S(2)}, u32[]{:S(2)}) collective-permute-start(bf16[256,512]{1,0:T(8,128)(2,1)S(1)} %project_other.3), channel_id=1, source_target_pairs={{0,1},{1,0},{2,3},{3,2},{4,5},{5,4},{6,7},{7,6},{8,9},{9,8},{10,11... | collective-permute-start | bytes 786440 | tf_op jit(solution)/shard_map/ppermute | solution.py:895
  42.6 10.8 %collective-permute-start.15 = (bf16[256,512]{1,0:T(8,128)(2,1)S(1)}, bf16[256,512]{1,0:T(8,128)(2,1)S(1)}, u32[]{:S(2)}, u32[]{:S(2)}) collective-permute-start(bf16[256,512]{1,0:T(8,128)(2,1)S(1)} %project_other.2), channel_id=1, source_target_pairs={{0,1},{1,0},{2,3},{3,2},{4,5},{5,4},{6,7},{7,6},{8,9},{9,8},{10,11... | collective-permute-start | bytes 786440 | tf_op jit(solution)/shard_map/ppermute | solution.py:895

commit v8 on v7

--- a/solution.py
+++ b/solution.py
@@ -95,11 +95,20 @@
     return (segment_of(lengths_ref, position - lag) == here).astype(F32)
 
 
-def conv_rows(same, start, stop, taps, columns, wide):
+def lag_masks(same, start, stop, lags, width):
+    return [
+        None if lag == 0 else jnp.broadcast_to(same[start:stop, lag : lag + 1], (stop - start, width))
+        for lag in range(lags)
+    ]
+
+
+def conv_rows(same, start, stop, taps, columns, wide, masks=None):
+    if masks is None:
+        masks = lag_masks(same, start, stop, taps.shape[0], wide.shape[1])
     total = taps[0:1, columns] * wide[8 + start : 8 + stop, :]
     for lag in range(1, taps.shape[0]):
         total = total + taps[lag : lag + 1, columns] * (
-            wide[8 + start - lag : 8 + stop - lag, :] * same[start:stop, lag : lag + 1]
+            wide[8 + start - lag : 8 + stop - lag, :] * masks[lag]
         )
     return (0.5 * total * (1.0 + jnp.tanh(0.5 * total))).astype(BF16)
 
@@ -196,25 +205,29 @@
     same = same_request(lengths_ref, offset + iota((length, 128), 0))
     normals[...] = jnp.zeros_like(normals)
     step = 128
+    key_edge[0] = jnp.where(core == 0, own_keys[0:16, :], key_other[0:16, :])
+    key_edge[1] = jnp.where(core == 0, key_other[rows - 16 :, :], own_keys[rows - 16 :, :])
     for i in range(per_core):
         columns = slice(i * key_width, (i + 1) * key_width)
-        own, other = own_keys[:, columns], key_other[:, columns]
-        key_edge[0, :, columns] = jnp.where(core == 0, own[0:16], other[0:16])
-        key_edge[1, :, columns] = jnp.where(core == 0, other[rows - 16 :], own[rows - 16 :])
-        wide[0:8, :] = jnp.zeros((8, key_width), F32)
-        wide[pl.ds(pl.multiple_of(8 + core * rows, 8), rows), :] = own.astype(F32)
-        wide[pl.ds(pl.multiple_of(8 + (1 - core) * rows, 8), rows), :] = other.astype(F32)
-        normal = jnp.zeros((1, key_width), F32)
-        for start in range(0, length, step):
-            conv = conv_rows(same, start, start + step, taps, columns, wide)
+        wide[i, 0:8, :] = jnp.zeros((8, key_width), F32)
+        for ref, half in ((own_keys, core), (key_other, 1 - core)):
+            span = pl.ds(pl.multiple_of(8 + half * rows, 8), rows)
+            wide[i, span, :] = ref[:, columns].astype(F32)
+    totals = [jnp.zeros((1, key_width), F32) for _ in range(per_core)]
+    for start in range(0, length, step):
+        masks = lag_masks(same, start, start + step, taps.shape[0], key_width)
+        for i in range(per_core):
+            columns = slice(i * key_width, (i + 1) * key_width)
+            conv = conv_rows(same, start, start + step, taps, columns, wide.at[i], masks)
             conv_ref[start : start + step, columns] = conv
             weight = factor[start : start + step, i : i + 1]
             if start == 0:
                 weight = jnp.where(iota((step, 1), 0) >= FIRST, weight, 0.0)
             weighted = conv.astype(F32) * weight
-            normal = normal + jnp.sum(weighted, axis=0, keepdims=True)
+            totals[i] = totals[i] + jnp.sum(weighted, axis=0, keepdims=True)
             weighted_ref[start : start + step, columns] = weighted.astype(BF16)
-        normals[i : i + 1, :] = normal
+    for i in range(per_core):
+        normals[i : i + 1, :] = totals[i]
     for i in range(per_core):
         columns = slice(i * key_width, (i + 1) * key_width)
         value_columns = slice(i * value_width, (i + 1) * value_width)
@@ -757,7 +770,7 @@
         [
             pltpu.VMEM((2, max(8, heads), chip_length), F32),
             pltpu.VMEM((2, 8, chip_length), F32),
-            pltpu.VMEM((chip_length + 8, key_width), F32),
+            pltpu.VMEM((per_core, chip_length + 8, key_width), F32),
             pltpu.VMEM((chip_length, part_keys), BF16),
             pltpu.VMEM((part_keys, value_width), BF16),
             pltpu.VMEM((8, key_width), F32),

time: 54.4 us -> 54.3 us (level)
  no operation moved by 1% of the time
where the time goes in v8:
time: 54.3 us; the launch traced here: 54.1 us
  starting transfers between devices  18.9 us (35%)
  Pallas kernels  18.3 us (34%)
  waiting for transfers between devices  16.6 us (31%)
    pallas_call x19, Pallas kernels, run(): inner(*(pltpu.with_memory_space_constraint(x, pltpu.HBM) if s in 'hs' els...  18.3 us
    ppermute x15, starting transfers between devices, swap(): return lax.ppermute(x, 'seq', [(i, i ^ off) for i in range(seq_count)])  16.8 us
    ppermute x2, waiting for transfers between devices, on_device(): lax.ppermute(part, 'head', [(i, i ^ off) for i in range(head_count)])  9.41 us
    ppermute x15, waiting for transfers between devices, swap(): return lax.ppermute(x, 'seq', [(i, i ^ off) for i in range(seq_count)])  7.21 us
    ppermute x2, starting transfers between devices, on_device(): lax.ppermute(part, 'head', [(i, i ^ off) for i in range(head_count)])  2.16 us
  transfers between devices with their start and end apart: 17, of which 8 were waited for; matrix products, arithmetic and copies ran while one was open for 0% of the time, Pallas kernels for 27%

profile of v8, /device:TPU:0, one launch (start us, length us, event | category | flops | bytes accessed | tf_op | source)
XLA Modules:
  0.0 54.1 jit_solution(17606574620779182674)
XLA Ops:
  0.0 1.2 %gates.1 = (f32[2,4,256]{2,1,0:T(4,128)S(1)}, bf16[256,512]{1,0:T(8,128)(2,1)S(1)}, bf16[256,1024]{1,0:T(8,128)(2,1)S(1)}) custom-call(f32[4,256]{1,0:T(4,128)} %input_ref.1, f32[4,256]{1,0:T(4,128)} %forget_ref.1, bf16[256,1024]{1,0:T(8,128)(2,1)} %key_ref.2, bf16[256,2048]{1,0:T(8,128)(2,1)} %value_ref.2), custom_call_target="tpu_custom_call" | custom-call | flops 4294967296 | tf_op jit(solution)/shard_map/gates/pallas_call | solution.py:703
  2.3 1.1 %own_part.1 = (bf16[256,512]{1,0:T(8,128)(2,1)S(1)}, bf16[256,1024]{1,0:T(8,128)(2,1)S(1)}, f32[4,512]{1,0:T(4,128)S(1)}) custom-call(bf16[256,1024]{1,0:T(8,128)(2,1)} %key_ref.2, bf16[256,2048]{1,0:T(8,128)(2,1)} %value_ref.2, f32[2,4,1024]{2,1,0:T(4,128)} %taps_ref.3), custom_call_target="tpu_custom_call" | custom-call | flops 4294967296 | tf_op jit(solution)/shard_map/own_part/pallas_call | solution.py:703
  3.7 2.8 %chip_state.1 = (bf16[512,512]{1,0:T(8,128)(2,1)S(1)}, f32[2,8,512]{2,1,0:T(8,128)S(1)}, bf16[2,16,512]{2,1,0:T(8,128)(2,1)S(1)}, f32[2,8,128]{2,1,0:T(8,128)S(1...) custom-call(s32[4]{0:T(128)} %lengths_ref.7, ...), custom_call_target="tpu_custom_call" | custom-call | flops 1073741824 | tf_op jit(solution)/shard_map/chip_state/pallas_call | solution.py:703
  6.4 3.0 %collective-permute-start.4 = (bf16[528,128]{1,0:T(8,128)(2,1)S(1)}, bf16[528,128]{1,0:T(8,128)(2,1)S(1)}, u32[]{:S(2)}, u32[]{:S(2)}) collective-permute-start(bf16[528,128]{1,0:T(8,128)(2,1)S(1)} %get-tuple-element.75), channel_id=1, source_target_pairs={{0,4},{2,6},{4,0},{6,2},{8,12},{10,14},{12,8},{14,10},{16,20},{18,... | collective-permute-start | bytes 405512 | tf_op jit(solution)/shard_map/ppermute | solution.py:734
  9.4 1.6 %collective-permute-start.5 = (bf16[528,128]{1,0:T(8,128)(2,1)S(1)}, bf16[528,128]{1,0:T(8,128)(2,1)S(1)}, u32[]{:S(2)}, u32[]{:S(2)}) collective-permute-start(bf16[528,128]{1,0:T(8,128)(2,1)S(1)} %get-tuple-element.76), channel_id=1, source_target_pairs={{0,8},{2,10},{4,12},{6,14},{8,0},{10,2},{12,4},{14,6},{16,24},{18,... | collective-permute-start | bytes 405512 | tf_op jit(solution)/shard_map/ppermute | solution.py:734
  11.1 2.0 %collective-permute-start.7 = (bf16[1,64,128]{2,1,0:T(8,128)(2,1)S(1)}, bf16[1,64,128]{2,1,0:T(8,128)(2,1)S(1)}, u32[]{:S(2)}, u32[]{:S(2)}) collective-permute-start(bf16[1,64,128]{2,1,0:T(8,128)(2,1)S(1)} %message.1.first_ref), channel_id=1, source_target_pairs={{0,8},{2,10},{4,12},{6,14},{8,0},{10,2},{12,4},{14,6},{16,24},{18,... | collective-permute-start | bytes 49160 | tf_op jit(solution)/shard_map/ppermute | solution.py:734
  13.1 2.7 %query_conv.1 = (bf16[512,512]{1,0:T(8,128)(2,1)S(1)}, f32[4,512]{1,0:T(4,128)S(1)}, bf16[2,16,512]{2,1,0:T(8,128)(2,1)S(1)}, bf16[512,1024]{1,0:T(8,128)(2,1)S(1)}) custom-call(s32[4]{0:T(128)} %lengths_ref.7, bf16[256,1024]{1,0:T(8,128)(2,1)} %query_ref.3, bf16[256,1024]{1,0:T(8,128)(2,1)S(1)} %collective-permute-done.3.query_other, ...), custom_call_target="tpu_custom_call" | custom-call | flops 1073741824 | tf_op jit(solution)/shard_map/query_conv/pallas_call | solution.py:703
  15.8 2.2 %collective-permute-done.7.second_ref = bf16[1,64,128]{2,1,0:T(8,128)(2,1)S(1)} collective-permute-done((bf16[1,64,128]{2,1,0:T(8,128)(2,1)S(1)}, bf16[1,64,128]{2,1,0:T(8,128)(2,1)S(1)}, u32[]{:S(2)}, u32[]{:S(2)}) %collective-permute-start.7) | collective-permute-done | bytes 16416 | tf_op jit(solution)/shard_map/ppermute | solution.py:734
  18.2 3.7 %collective-permute-start.9 = (bf16[528,128]{1,0:T(8,128)(2,1)S(1)}, bf16[528,128]{1,0:T(8,128)(2,1)S(1)}, u32[]{:S(2)}, u32[]{:S(2)}) collective-permute-start(bf16[528,128]{1,0:T(8,128)(2,1)S(1)} %group_total.1), channel_id=1, source_target_pairs={{0,24},{2,26},{4,28},{6,30},{8,16},{10,18},{12,20},{14,22},{16,8},... | collective-permute-start | bytes 405512 | tf_op jit(solution)/shard_map/ppermute | solution.py:734
  21.9 1.3 %collective-permute-start.8 = (bf16[2,64,128]{2,1,0:T(8,128)(2,1)S(1)}, bf16[2,64,128]{2,1,0:T(8,128)(2,1)S(1)}, u32[]{:S(2)}, u32[]{:S(2)}) collective-permute-start(bf16[2,64,128]{2,1,0:T(8,128)(2,1)S(1)} %join.2.first_ref), channel_id=1, source_target_pairs={{0,4},{2,6},{4,0},{6,2},{8,12},{10,14},{12,8},{14,10},{16,20},{18,... | collective-permute-start | bytes 98312 | tf_op jit(solution)/shard_map/ppermute | solution.py:734
  23.2 2.6 %collective-permute-done.8.second_ref = bf16[2,64,128]{2,1,0:T(8,128)(2,1)S(1)} collective-permute-done((bf16[2,64,128]{2,1,0:T(8,128)(2,1)S(1)}, bf16[2,64,128]{2,1,0:T(8,128)(2,1)S(1)}, u32[]{:S(2)}, u32[]{:S(2)}) %collective-permute-start.8) | collective-permute-done | bytes 32800 | tf_op jit(solution)/shard_map/ppermute | solution.py:734
  26.3 1.3 %collective-permute-start.10 = (bf16[528,128]{1,0:T(8,128)(2,1)S(1)}, bf16[528,128]{1,0:T(8,128)(2,1)S(1)}, u32[]{:S(2)}, u32[]{:S(2)}) collective-permute-start(bf16[528,128]{1,0:T(8,128)(2,1)S(1)} %get-tuple-element.91), channel_id=1, source_target_pairs={{0,4},{2,6},{4,0},{6,2},{8,12},{10,14},{12,8},{14,10},{16,20},{18,... | collective-permute-start | bytes 405512 | tf_op jit(solution)/shard_map/ppermute | solution.py:734
  27.7 2.4 %collective-permute-start.11 = (bf16[528,128]{1,0:T(8,128)(2,1)S(1)}, bf16[528,128]{1,0:T(8,128)(2,1)S(1)}, u32[]{:S(2)}, u32[]{:S(2)}) collective-permute-start(bf16[528,128]{1,0:T(8,128)(2,1)S(1)} %get-tuple-element.92), channel_id=1, source_target_pairs={{0,8},{2,10},{4,12},{6,14},{8,0},{10,2},{12,4},{14,6},{16,24},{18,... | collective-permute-start | bytes 405512 | tf_op jit(solution)/shard_map/ppermute | solution.py:734
  30.4 0.8 %collective-permute-done.13.far_ref = bf16[4,64,128]{2,1,0:T(8,128)(2,1)S(1)} collective-permute-done((bf16[4,64,128]{2,1,0:T(8,128)(2,1)S(1)}, bf16[4,64,128]{2,1,0:T(8,128)(2,1)S(1)}, u32[]{:S(2)}, u32[]{:S(2)}) %collective-permute-start.13) | collective-permute-done | bytes 65568 | tf_op jit(solution)/shard_map/ppermute | solution.py:734
  31.2 1.4 %gathered_first.1 = (bf16[256,256]{1,0:T(8,128)(2,1)S(1)}, bf16[256,512]{1,0:T(8,128)(2,1)S(1)}, f32[256,128]{1,0:T(8,128)S(1)}, bf16[2,16,512]{2,1,0:T(8,128)(2,1)S(1)}) custom-call(s32[4]{0:T(128)} %lengths_ref.7, bf16[4,64,128]{2,1,0:T(8,128)(2,1)S(1)} %join.3.near_ref, bf16[4,64,128]{2,1,0:T(8,128)(2,1)S(1)} %collective-permute-done.13.far_ref, ...), custom_call_target="tpu_custom_call" | custom-call | tf_op jit(solution)/shard_map/gathered_first/pallas_call | solution.py:703
  32.6 2.5 %intra.1 = (bf16[512,512]{1,0:T(8,128)(2,1)S(1)}, f32[512,1024]{1,0:T(8,128)S(1)}, f32[3,512,128]{2,1,0:T(8,128)S(1)}) custom-call(s32[4]{0:T(128)} %lengths_ref.7, bf16[512,512]{1,0:T(8,128)(2,1)S(1)} %get-tuple-element.100.query_conv, bf16[512,512]{1,0:T(8,128)(2,1)S(1)} %get-tuple-element.101.key_ref, ...), custom_call_target="tpu_custom_call" | custom-call | flops 4294967296 | tf_op jit(solution)/shard_map/intra/pallas_call | solution.py:703
  35.2 0.8 %collective-permute-done.12.got3 = bf16[528,128]{1,0:T(8,128)(2,1)S(1)} collective-permute-done((bf16[528,128]{1,0:T(8,128)(2,1)S(1)}, bf16[528,128]{1,0:T(8,128)(2,1)S(1)}, u32[]{:S(2)}, u32[]{:S(2)}) %collective-permute-start.12) | collective-permute-done | bytes 135200 | tf_op jit(solution)/shard_map/ppermute | solution.py:734
  36.0 0.9 %head_send.1 = (bf16[256,1024]{1,0:T(8,128)(2,1)S(1)}, bf16[512,512]{1,0:T(8,128)(2,1)S(1)}, bf16[256,256]{1,0:T(8,128)(2,1)S(1)}, f32[8,128]{1,0:T(8,128)S(1)}) custom-call(bf16[528,128]{1,0:T(8,128)(2,1)S(1)} %get-tuple-element.90.own_ref, bf16[528,128]{1,0:T(8,128)(2,1)S(1)} %collective-permute-done.10.got1, ...), custom_call_target="tpu_custom_call" | custom-call | tf_op jit(solution)/shard_map/head_send/pallas_call | solution.py:703
  39.3 1.6 %collective-permute-start.16 = (bf16[256,512]{1,0:T(8,128)(2,1)S(1)}, bf16[256,512]{1,0:T(8,128)(2,1)S(1)}, u32[]{:S(2)}, u32[]{:S(2)}) collective-permute-start(bf16[256,512]{1,0:T(8,128)(2,1)S(1)} %project_other.3), channel_id=1, source_target_pairs={{0,1},{1,0},{2,3},{3,2},{4,5},{5,4},{6,7},{7,6},{8,9},{9,8},{10,11... | collective-permute-start | bytes 786440 | tf_op jit(solution)/shard_map/ppermute | solution.py:908
  40.8 1.2 %project_own.1.own_ref = f32[256,1024]{1,0:T(8,128)S(1)} custom-call(bf16[256,1024]{1,0:T(8,128)(2,1)S(1)} %head_keep.1.keep_ref.head_ref, bf16[256,1024]{1,0:T(8,128)(2,1)S(1)} %collective-permute-done.14.got_ref.head_ref, bf16[2048,2048]{1,0:T(8,128)(2,1)S(1)} %bitcast.1), custom_call_target="tpu_custom_call" | custom-call | flops 4294967296 | tf_op jit(solution)/shard_map/project_own/pallas_call | solution.py:703
  43.2 5.3 %collective-permute-done.16.refs_0_ = bf16[256,512]{1,0:T(8,128)(2,1)S(1)} collective-permute-done((bf16[256,512]{1,0:T(8,128)(2,1)S(1)}, bf16[256,512]{1,0:T(8,128)(2,1)S(1)}, u32[]{:S(2)}, u32[]{:S(2)}) %collective-permute-start.16) | collective-permute-done | bytes 262176 | tf_op jit(solution)/shard_map/ppermute | solution.py:908
  48.5 0.7 %mixed_out.2.refs_1_ = bf16[256,1024]{1,0:T(8,128)(2,1)} custom-call(f32[256,1024]{1,0:T(8,128)S(1)} %project_own.1.own_ref, bf16[256,512]{1,0:T(8,128)(2,1)S(1)} %collective-permute-done.16.refs_0_), custom_call_target="tpu_custom_call" | custom-call | tf_op jit(solution)/shard_map/mixed_out/pallas_call | solution.py:703
  49.3 4.1 %collective-permute-done.15.refs_0_ = bf16[256,512]{1,0:T(8,128)(2,1)S(1)} collective-permute-done((bf16[256,512]{1,0:T(8,128)(2,1)S(1)}, bf16[256,512]{1,0:T(8,128)(2,1)S(1)}, u32[]{:S(2)}, u32[]{:S(2)}) %collective-permute-start.15) | collective-permute-done | bytes 262176 | tf_op jit(solution)/shard_map/ppermute | solution.py:908
  53.3 0.7 %mixed_out.3 = bf16[256,1024]{1,0:T(8,128)(2,1)} custom-call(f32[256,1024]{1,0:T(8,128)S(1)} %project_own.1.own_ref, bf16[256,512]{1,0:T(8,128)(2,1)S(1)} %collective-permute-done.15.refs_0_, bf16[256,1024]{1,0:T(8,128)(2,1)} %mixed_out.2.refs_1_), custom_call_target="tpu_custom_call", output_to_operand_aliasing={{}: (2, {})} | custom-call | tf_op jit(solution)/shard_map/mixed_out/pallas_call | solution.py:703
  (36 shorter events, 5.9 us)
Async XLA Ops:
  0.0 2.3 %copy-start = (bf16[256,1024]{1,0:T(8,128)(2,1)S(1)}, bf16[256,1024]{1,0:T(8,128)(2,1)}, u32[]{:S(2)}) copy-start(bf16[256,1024]{1,0:T(8,128)(2,1)} %query_ref.3) | copy-start | bytes 1572868
  1.2 2.4 %collective-permute-start.1 = (bf16[256,1024]{1,0:T(8,128)(2,1)S(1)}, bf16[256,1024]{1,0:T(8,128)(2,1)S(1)}, u32[]{:S(2)}, u32[]{:S(2)}) collective-permute-start(bf16[256,1024]{1,0:T(8,128)(2,1)S(1)} %get-tuple-element.66), channel_id=1, source_target_pairs={{0,2},{2,0},{4,6},{6,4},{8,10},{10,8},{12,14},{14,12},{16,18},{18,... | collective-permute-start | bytes 1572872 | tf_op jit(solution)/shard_map/ppermute | solution.py:734
  1.7 1.8 %collective-permute-start.2 = (f32[2,4,256]{2,1,0:T(4,128)S(1)}, f32[2,4,256]{2,1,0:T(4,128)S(1)}, u32[]{:S(2)}, u32[]{:S(2)}) collective-permute-start(f32[2,4,256]{2,1,0:T(4,128)S(1)} %get-tuple-element.68.gates_ref), channel_id=1, source_target_pairs={{0,2},{2,0},{4,6},{6,4},{8,10},{10,8},{12,14},{14,12},{16,18},{18,... | collective-permute-start | bytes 24584 | tf_op jit(solution)/shard_map/ppermute | solution.py:734
  1.8 1.8 %collective-permute-start = (bf16[256,512]{1,0:T(8,128)(2,1)S(1)}, bf16[256,512]{1,0:T(8,128)(2,1)S(1)}, u32[]{:S(2)}, u32[]{:S(2)}) collective-permute-start(bf16[256,512]{1,0:T(8,128)(2,1)S(1)} %get-tuple-element.65), channel_id=1, source_target_pairs={{0,2},{2,0},{4,6},{6,4},{8,10},{10,8},{12,14},{14,12},{16,18},{18,... | collective-permute-start | bytes 786440 | tf_op jit(solution)/shard_map/ppermute | solution.py:734
  2.3 8.7 %collective-permute-start.3 = (bf16[256,1024]{1,0:T(8,128)(2,1)S(1)}, bf16[256,1024]{1,0:T(8,128)(2,1)S(1)}, u32[]{:S(2)}, u32[]{:S(2)}) collective-permute-start(bf16[256,1024]{1,0:T(8,128)(2,1)S(1)} %copy-done), channel_id=1, source_target_pairs={{0,2},{2,0},{4,6},{6,4},{8,10},{10,8},{12,14},{14,12},{16,18},{18,... | collective-permute-start | bytes 1572872 | tf_op jit(solution)/shard_map/ppermute | solution.py:734
  6.4 11.6 %collective-permute-start.4 = (bf16[528,128]{1,0:T(8,128)(2,1)S(1)}, bf16[528,128]{1,0:T(8,128)(2,1)S(1)}, u32[]{:S(2)}, u32[]{:S(2)}) collective-permute-start(bf16[528,128]{1,0:T(8,128)(2,1)S(1)} %get-tuple-element.75), channel_id=1, source_target_pairs={{0,4},{2,6},{4,0},{6,2},{8,12},{10,14},{12,8},{14,10},{16,20},{18,... | collective-permute-start | bytes 405512 | tf_op jit(solution)/shard_map/ppermute | solution.py:734
  9.4 8.6 %collective-permute-start.5 = (bf16[528,128]{1,0:T(8,128)(2,1)S(1)}, bf16[528,128]{1,0:T(8,128)(2,1)S(1)}, u32[]{:S(2)}, u32[]{:S(2)}) collective-permute-start(bf16[528,128]{1,0:T(8,128)(2,1)S(1)} %get-tuple-element.76), channel_id=1, source_target_pairs={{0,8},{2,10},{4,12},{6,14},{8,0},{10,2},{12,4},{14,6},{16,24},{18,... | collective-permute-start | bytes 405512 | tf_op jit(solution)/shard_map/ppermute | solution.py:734
  11.0 7.0 %collective-permute-start.6 = (bf16[528,128]{1,0:T(8,128)(2,1)S(1)}, bf16[528,128]{1,0:T(8,128)(2,1)S(1)}, u32[]{:S(2)}, u32[]{:S(2)}) collective-permute-start(bf16[528,128]{1,0:T(8,128)(2,1)S(1)} %get-tuple-element.77), channel_id=1, source_target_pairs={{0,12},{2,14},{4,8},{6,10},{8,4},{10,6},{12,0},{14,2},{16,28},{18,... | collective-permute-start | bytes 405512 | tf_op jit(solution)/shard_map/ppermute | solution.py:734
  11.1 6.9 %collective-permute-start.7 = (bf16[1,64,128]{2,1,0:T(8,128)(2,1)S(1)}, bf16[1,64,128]{2,1,0:T(8,128)(2,1)S(1)}, u32[]{:S(2)}, u32[]{:S(2)}) collective-permute-start(bf16[1,64,128]{2,1,0:T(8,128)(2,1)S(1)} %message.1.first_ref), channel_id=1, source_target_pairs={{0,8},{2,10},{4,12},{6,14},{8,0},{10,2},{12,4},{14,6},{16,24},{18,... | collective-permute-start | bytes 49160 | tf_op jit(solution)/shard_map/ppermute | solution.py:734
  18.2 7.6 %collective-permute-start.9 = (bf16[528,128]{1,0:T(8,128)(2,1)S(1)}, bf16[528,128]{1,0:T(8,128)(2,1)S(1)}, u32[]{:S(2)}, u32[]{:S(2)}) collective-permute-start(bf16[528,128]{1,0:T(8,128)(2,1)S(1)} %group_total.1), channel_id=1, source_target_pairs={{0,24},{2,26},{4,28},{6,30},{8,16},{10,18},{12,20},{14,22},{16,8},... | collective-permute-start | bytes 405512 | tf_op jit(solution)/shard_map/ppermute | solution.py:734
  21.9 3.9 %collective-permute-start.8 = (bf16[2,64,128]{2,1,0:T(8,128)(2,1)S(1)}, bf16[2,64,128]{2,1,0:T(8,128)(2,1)S(1)}, u32[]{:S(2)}, u32[]{:S(2)}) collective-permute-start(bf16[2,64,128]{2,1,0:T(8,128)(2,1)S(1)} %join.2.first_ref), channel_id=1, source_target_pairs={{0,4},{2,6},{4,0},{6,2},{8,12},{10,14},{12,8},{14,10},{16,20},{18,... | collective-permute-start | bytes 98312 | tf_op jit(solution)/shard_map/ppermute | solution.py:734
  25.8 5.4 %collective-permute-start.13 = (bf16[4,64,128]{2,1,0:T(8,128)(2,1)S(1)}, bf16[4,64,128]{2,1,0:T(8,128)(2,1)S(1)}, u32[]{:S(2)}, u32[]{:S(2)}) collective-permute-start(bf16[4,64,128]{2,1,0:T(8,128)(2,1)S(1)} %join.3.near_ref), channel_id=1, source_target_pairs={{0,16},{2,18},{4,20},{6,22},{8,24},{10,26},{12,28},{14,30},{16,0},... | collective-permute-start | bytes 196616 | tf_op jit(solution)/shard_map/ppermute | solution.py:734
  26.3 8.9 %collective-permute-start.10 = (bf16[528,128]{1,0:T(8,128)(2,1)S(1)}, bf16[528,128]{1,0:T(8,128)(2,1)S(1)}, u32[]{:S(2)}, u32[]{:S(2)}) collective-permute-start(bf16[528,128]{1,0:T(8,128)(2,1)S(1)} %get-tuple-element.91), channel_id=1, source_target_pairs={{0,4},{2,6},{4,0},{6,2},{8,12},{10,14},{12,8},{14,10},{16,20},{18,... | collective-permute-start | bytes 405512 | tf_op jit(solution)/shard_map/ppermute | solution.py:734
  27.7 7.5 %collective-permute-start.11 = (bf16[528,128]{1,0:T(8,128)(2,1)S(1)}, bf16[528,128]{1,0:T(8,128)(2,1)S(1)}, u32[]{:S(2)}, u32[]{:S(2)}) collective-permute-start(bf16[528,128]{1,0:T(8,128)(2,1)S(1)} %get-tuple-element.92), channel_id=1, source_target_pairs={{0,8},{2,10},{4,12},{6,14},{8,0},{10,2},{12,4},{14,6},{16,24},{18,... | collective-permute-start | bytes 405512 | tf_op jit(solution)/shard_map/ppermute | solution.py:734
  30.0 5.9 %collective-permute-start.12 = (bf16[528,128]{1,0:T(8,128)(2,1)S(1)}, bf16[528,128]{1,0:T(8,128)(2,1)S(1)}, u32[]{:S(2)}, u32[]{:S(2)}) collective-permute-start(bf16[528,128]{1,0:T(8,128)(2,1)S(1)} %get-tuple-element.93), channel_id=1, source_target_pairs={{0,12},{2,14},{4,8},{6,10},{8,4},{10,6},{12,0},{14,2},{16,28},{18,... | collective-permute-start | bytes 405512 | tf_op jit(solution)/shard_map/ppermute | solution.py:734
  32.6 4.9 %slice-start = ((s8[8388608]{0:T(1024)(128)(4,1)}), s8[4194304]{0:T(1024)(128)(4,1)S(1)}, s32[]{:S(2)}) async-start(s8[8388608]{0:T(1024)(128)(4,1)} %bitcast), calls=%async_computation | async-start | bytes 8388608
  32.6 4.9 %slice-start.1 = ((s8[8388608]{0:T(1024)(128)(4,1)}), s8[4194304]{0:T(1024)(128)(4,1)S(1)}, s32[]{:S(2)}) async-start(s8[8388608]{0:T(1024)(128)(4,1)} %bitcast), calls=%async_computation.1 | async-start | bytes 8388608
  36.9 2.0 %collective-permute-start.14 = (bf16[256,1024]{1,0:T(8,128)(2,1)S(1)}, bf16[256,1024]{1,0:T(8,128)(2,1)S(1)}, u32[]{:S(2)}, u32[]{:S(2)}) collective-permute-start(bf16[256,1024]{1,0:T(8,128)(2,1)S(1)} %get-tuple-element.108), channel_id=1, source_target_pairs={{0,2},{2,0},{4,6},{6,4},{8,10},{10,8},{12,14},{14,12},{16,18},{18,... | collective-permute-start | bytes 1572872 | tf_op jit(solution)/shard_map/ppermute | solution.py:734
  39.3 9.2 %collective-permute-start.16 = (bf16[256,512]{1,0:T(8,128)(2,1)S(1)}, bf16[256,512]{1,0:T(8,128)(2,1)S(1)}, u32[]{:S(2)}, u32[]{:S(2)}) collective-permute-start(bf16[256,512]{1,0:T(8,128)(2,1)S(1)} %project_other.3), channel_id=1, source_target_pairs={{0,1},{1,0},{2,3},{3,2},{4,5},{5,4},{6,7},{7,6},{8,9},{9,8},{10,11... | collective-permute-start | bytes 786440 | tf_op jit(solution)/shard_map/ppermute | solution.py:908
  42.6 10.8 %collective-permute-start.15 = (bf16[256,512]{1,0:T(8,128)(2,1)S(1)}, bf16[256,512]{1,0:T(8,128)(2,1)S(1)}, u32[]{:S(2)}, u32[]{:S(2)}) collective-permute-start(bf16[256,512]{1,0:T(8,128)(2,1)S(1)} %project_other.2), channel_id=1, source_target_pairs={{0,1},{1,0},{2,3},{3,2},{4,5},{5,4},{6,7},{7,6},{8,9},{9,8},{10,11... | collective-permute-start | bytes 786440 | tf_op jit(solution)/shard_map/ppermute | solution.py:908

commit v9 on v8

--- a/solution.py
+++ b/solution.py
@@ -394,7 +394,10 @@
     stabs = shifted_stab(infos, ranks, 4)
     m = functools.reduce(jnp.maximum, stabs)
     weights = [jnp.exp(s - m) for s in stabs]
-    out[0:rows, :] = sum(w * s[0:rows, :].astype(F32) for w, s in zip(weights, states)).astype(BF16)
+    step = math.gcd(rows, 64)
+    for at in range(0, rows, step):
+        span = slice(at, at + step)
+        out[span, :] = sum(w * s[span, :].astype(F32) for w, s in zip(weights, states)).astype(BF16)
     write_info(out, sum(w * i[0] for w, i in zip(weights, infos)), m, sum(i[2] for i in infos))
 
 

time: 54.3 us -> 54.3 us (level)
  no operation moved by 1% of the time
where the time goes in v9:
time: 54.3 us; the launch traced here: 54 us
  starting transfers between devices  18.9 us (35%)
  Pallas kernels  18.3 us (34%)
  waiting for transfers between devices  16.6 us (31%)
    pallas_call x19, Pallas kernels, run(): inner(*(pltpu.with_memory_space_constraint(x, pltpu.HBM) if s in 'hs' els...  18.3 us
    ppermute x15, starting transfers between devices, swap(): return lax.ppermute(x, 'seq', [(i, i ^ off) for i in range(seq_count)])  16.8 us
    ppermute x2, waiting for transfers between devices, on_device(): lax.ppermute(part, 'head', [(i, i ^ off) for i in range(head_count)])  9.41 us
    ppermute x15, waiting for transfers between devices, swap(): return lax.ppermute(x, 'seq', [(i, i ^ off) for i in range(seq_count)])  7.21 us
    ppermute x2, starting transfers between devices, on_device(): lax.ppermute(part, 'head', [(i, i ^ off) for i in range(head_count)])  2.16 us
  transfers between devices with their start and end apart: 17, of which 8 were waited for; matrix products, arithmetic and copies ran while one was open for 0% of the time, Pallas kernels for 27%

profile of v9, /device:TPU:0, one launch (start us, length us, event | category | flops | bytes accessed | tf_op | source)
XLA Modules:
  0.0 54.0 jit_solution(15366522071856526042)
XLA Ops:
  0.0 1.2 %gates.1 = (f32[2,4,256]{2,1,0:T(4,128)S(1)}, bf16[256,512]{1,0:T(8,128)(2,1)S(1)}, bf16[256,1024]{1,0:T(8,128)(2,1)S(1)}) custom-call(f32[4,256]{1,0:T(4,128)} %input_ref.1, f32[4,256]{1,0:T(4,128)} %forget_ref.1, bf16[256,1024]{1,0:T(8,128)(2,1)} %key_ref.2, bf16[256,2048]{1,0:T(8,128)(2,1)} %value_ref.2), custom_call_target="tpu_custom_call" | custom-call | flops 4294967296 | tf_op jit(solution)/shard_map/gates/pallas_call | solution.py:706
  2.3 1.1 %own_part.1 = (bf16[256,512]{1,0:T(8,128)(2,1)S(1)}, bf16[256,1024]{1,0:T(8,128)(2,1)S(1)}, f32[4,512]{1,0:T(4,128)S(1)}) custom-call(bf16[256,1024]{1,0:T(8,128)(2,1)} %key_ref.2, bf16[256,2048]{1,0:T(8,128)(2,1)} %value_ref.2, f32[2,4,1024]{2,1,0:T(4,128)} %taps_ref.3), custom_call_target="tpu_custom_call" | custom-call | flops 4294967296 | tf_op jit(solution)/shard_map/own_part/pallas_call | solution.py:706
  3.7 2.8 %chip_state.1 = (bf16[512,512]{1,0:T(8,128)(2,1)S(1)}, f32[2,8,512]{2,1,0:T(8,128)S(1)}, bf16[2,16,512]{2,1,0:T(8,128)(2,1)S(1)}, f32[2,8,128]{2,1,0:T(8,128)S(1...) custom-call(s32[4]{0:T(128)} %lengths_ref.7, ...), custom_call_target="tpu_custom_call" | custom-call | flops 1073741824 | tf_op jit(solution)/shard_map/chip_state/pallas_call | solution.py:706
  6.4 3.0 %collective-permute-start.4 = (bf16[528,128]{1,0:T(8,128)(2,1)S(1)}, bf16[528,128]{1,0:T(8,128)(2,1)S(1)}, u32[]{:S(2)}, u32[]{:S(2)}) collective-permute-start(bf16[528,128]{1,0:T(8,128)(2,1)S(1)} %get-tuple-element.75), channel_id=1, source_target_pairs={{0,4},{2,6},{4,0},{6,2},{8,12},{10,14},{12,8},{14,10},{16,20},{18,... | collective-permute-start | bytes 405512 | tf_op jit(solution)/shard_map/ppermute | solution.py:737
  9.4 1.6 %collective-permute-start.5 = (bf16[528,128]{1,0:T(8,128)(2,1)S(1)}, bf16[528,128]{1,0:T(8,128)(2,1)S(1)}, u32[]{:S(2)}, u32[]{:S(2)}) collective-permute-start(bf16[528,128]{1,0:T(8,128)(2,1)S(1)} %get-tuple-element.76), channel_id=1, source_target_pairs={{0,8},{2,10},{4,12},{6,14},{8,0},{10,2},{12,4},{14,6},{16,24},{18,... | collective-permute-start | bytes 405512 | tf_op jit(solution)/shard_map/ppermute | solution.py:737
  11.1 2.0 %collective-permute-start.7 = (bf16[1,64,128]{2,1,0:T(8,128)(2,1)S(1)}, bf16[1,64,128]{2,1,0:T(8,128)(2,1)S(1)}, u32[]{:S(2)}, u32[]{:S(2)}) collective-permute-start(bf16[1,64,128]{2,1,0:T(8,128)(2,1)S(1)} %message.1.first_ref), channel_id=1, source_target_pairs={{0,8},{2,10},{4,12},{6,14},{8,0},{10,2},{12,4},{14,6},{16,24},{18,... | collective-permute-start | bytes 49160 | tf_op jit(solution)/shard_map/ppermute | solution.py:737
  13.1 2.7 %query_conv.1 = (bf16[512,512]{1,0:T(8,128)(2,1)S(1)}, f32[4,512]{1,0:T(4,128)S(1)}, bf16[2,16,512]{2,1,0:T(8,128)(2,1)S(1)}, bf16[512,1024]{1,0:T(8,128)(2,1)S(1)}) custom-call(s32[4]{0:T(128)} %lengths_ref.7, bf16[256,1024]{1,0:T(8,128)(2,1)} %query_ref.3, bf16[256,1024]{1,0:T(8,128)(2,1)S(1)} %collective-permute-done.3.query_other, ...), custom_call_target="tpu_custom_call" | custom-call | flops 1073741824 | tf_op jit(solution)/shard_map/query_conv/pallas_call | solution.py:706
  15.8 2.2 %collective-permute-done.7.second_ref = bf16[1,64,128]{2,1,0:T(8,128)(2,1)S(1)} collective-permute-done((bf16[1,64,128]{2,1,0:T(8,128)(2,1)S(1)}, bf16[1,64,128]{2,1,0:T(8,128)(2,1)S(1)}, u32[]{:S(2)}, u32[]{:S(2)}) %collective-permute-start.7) | collective-permute-done | bytes 16416 | tf_op jit(solution)/shard_map/ppermute | solution.py:737
  18.2 3.7 %collective-permute-start.9 = (bf16[528,128]{1,0:T(8,128)(2,1)S(1)}, bf16[528,128]{1,0:T(8,128)(2,1)S(1)}, u32[]{:S(2)}, u32[]{:S(2)}) collective-permute-start(bf16[528,128]{1,0:T(8,128)(2,1)S(1)} %group_total.1), channel_id=1, source_target_pairs={{0,24},{2,26},{4,28},{6,30},{8,16},{10,18},{12,20},{14,22},{16,8},... | collective-permute-start | bytes 405512 | tf_op jit(solution)/shard_map/ppermute | solution.py:737
  21.9 1.3 %collective-permute-start.8 = (bf16[2,64,128]{2,1,0:T(8,128)(2,1)S(1)}, bf16[2,64,128]{2,1,0:T(8,128)(2,1)S(1)}, u32[]{:S(2)}, u32[]{:S(2)}) collective-permute-start(bf16[2,64,128]{2,1,0:T(8,128)(2,1)S(1)} %join.2.first_ref), channel_id=1, source_target_pairs={{0,4},{2,6},{4,0},{6,2},{8,12},{10,14},{12,8},{14,10},{16,20},{18,... | collective-permute-start | bytes 98312 | tf_op jit(solution)/shard_map/ppermute | solution.py:737
  23.1 2.6 %collective-permute-done.8.second_ref = bf16[2,64,128]{2,1,0:T(8,128)(2,1)S(1)} collective-permute-done((bf16[2,64,128]{2,1,0:T(8,128)(2,1)S(1)}, bf16[2,64,128]{2,1,0:T(8,128)(2,1)S(1)}, u32[]{:S(2)}, u32[]{:S(2)}) %collective-permute-start.8) | collective-permute-done | bytes 32800 | tf_op jit(solution)/shard_map/ppermute | solution.py:737
  26.3 1.3 %collective-permute-start.10 = (bf16[528,128]{1,0:T(8,128)(2,1)S(1)}, bf16[528,128]{1,0:T(8,128)(2,1)S(1)}, u32[]{:S(2)}, u32[]{:S(2)}) collective-permute-start(bf16[528,128]{1,0:T(8,128)(2,1)S(1)} %get-tuple-element.91), channel_id=1, source_target_pairs={{0,4},{2,6},{4,0},{6,2},{8,12},{10,14},{12,8},{14,10},{16,20},{18,... | collective-permute-start | bytes 405512 | tf_op jit(solution)/shard_map/ppermute | solution.py:737
  27.6 2.4 %collective-permute-start.11 = (bf16[528,128]{1,0:T(8,128)(2,1)S(1)}, bf16[528,128]{1,0:T(8,128)(2,1)S(1)}, u32[]{:S(2)}, u32[]{:S(2)}) collective-permute-start(bf16[528,128]{1,0:T(8,128)(2,1)S(1)} %get-tuple-element.92), channel_id=1, source_target_pairs={{0,8},{2,10},{4,12},{6,14},{8,0},{10,2},{12,4},{14,6},{16,24},{18,... | collective-permute-start | bytes 405512 | tf_op jit(solution)/shard_map/ppermute | solution.py:737
  30.4 0.8 %collective-permute-done.13.far_ref = bf16[4,64,128]{2,1,0:T(8,128)(2,1)S(1)} collective-permute-done((bf16[4,64,128]{2,1,0:T(8,128)(2,1)S(1)}, bf16[4,64,128]{2,1,0:T(8,128)(2,1)S(1)}, u32[]{:S(2)}, u32[]{:S(2)}) %collective-permute-start.13) | collective-permute-done | bytes 65568 | tf_op jit(solution)/shard_map/ppermute | solution.py:737
  31.2 1.4 %gathered_first.1 = (bf16[256,256]{1,0:T(8,128)(2,1)S(1)}, bf16[256,512]{1,0:T(8,128)(2,1)S(1)}, f32[256,128]{1,0:T(8,128)S(1)}, bf16[2,16,512]{2,1,0:T(8,128)(2,1)S(1)}) custom-call(s32[4]{0:T(128)} %lengths_ref.7, bf16[4,64,128]{2,1,0:T(8,128)(2,1)S(1)} %join.3.near_ref, bf16[4,64,128]{2,1,0:T(8,128)(2,1)S(1)} %collective-permute-done.13.far_ref, ...), custom_call_target="tpu_custom_call" | custom-call | tf_op jit(solution)/shard_map/gathered_first/pallas_call | solution.py:706
  32.6 2.5 %intra.1 = (bf16[512,512]{1,0:T(8,128)(2,1)S(1)}, f32[512,1024]{1,0:T(8,128)S(1)}, f32[3,512,128]{2,1,0:T(8,128)S(1)}) custom-call(s32[4]{0:T(128)} %lengths_ref.7, bf16[512,512]{1,0:T(8,128)(2,1)S(1)} %get-tuple-element.100.query_conv, bf16[512,512]{1,0:T(8,128)(2,1)S(1)} %get-tuple-element.101.key_ref, ...), custom_call_target="tpu_custom_call" | custom-call | flops 4294967296 | tf_op jit(solution)/shard_map/intra/pallas_call | solution.py:706
  35.2 0.8 %collective-permute-done.12.got3 = bf16[528,128]{1,0:T(8,128)(2,1)S(1)} collective-permute-done((bf16[528,128]{1,0:T(8,128)(2,1)S(1)}, bf16[528,128]{1,0:T(8,128)(2,1)S(1)}, u32[]{:S(2)}, u32[]{:S(2)}) %collective-permute-start.12) | collective-permute-done | bytes 135200 | tf_op jit(solution)/shard_map/ppermute | solution.py:737
  35.9 0.9 %head_send.1 = (bf16[256,1024]{1,0:T(8,128)(2,1)S(1)}, bf16[512,512]{1,0:T(8,128)(2,1)S(1)}, bf16[256,256]{1,0:T(8,128)(2,1)S(1)}, f32[8,128]{1,0:T(8,128)S(1)}) custom-call(bf16[528,128]{1,0:T(8,128)(2,1)S(1)} %get-tuple-element.90.own_ref, bf16[528,128]{1,0:T(8,128)(2,1)S(1)} %collective-permute-done.10.got1, ...), custom_call_target="tpu_custom_call" | custom-call | tf_op jit(solution)/shard_map/head_send/pallas_call | solution.py:706
  39.3 1.6 %collective-permute-start.16 = (bf16[256,512]{1,0:T(8,128)(2,1)S(1)}, bf16[256,512]{1,0:T(8,128)(2,1)S(1)}, u32[]{:S(2)}, u32[]{:S(2)}) collective-permute-start(bf16[256,512]{1,0:T(8,128)(2,1)S(1)} %project_other.3), channel_id=1, source_target_pairs={{0,1},{1,0},{2,3},{3,2},{4,5},{5,4},{6,7},{7,6},{8,9},{9,8},{10,11... | collective-permute-start | bytes 786440 | tf_op jit(solution)/shard_map/ppermute | solution.py:911
  40.8 1.2 %project_own.1.own_ref = f32[256,1024]{1,0:T(8,128)S(1)} custom-call(bf16[256,1024]{1,0:T(8,128)(2,1)S(1)} %head_keep.1.keep_ref.head_ref, bf16[256,1024]{1,0:T(8,128)(2,1)S(1)} %collective-permute-done.14.got_ref.head_ref, bf16[2048,2048]{1,0:T(8,128)(2,1)S(1)} %bitcast.1), custom_call_target="tpu_custom_call" | custom-call | flops 4294967296 | tf_op jit(solution)/shard_map/project_own/pallas_call | solution.py:706
  43.1 5.3 %collective-permute-done.16.refs_0_ = bf16[256,512]{1,0:T(8,128)(2,1)S(1)} collective-permute-done((bf16[256,512]{1,0:T(8,128)(2,1)S(1)}, bf16[256,512]{1,0:T(8,128)(2,1)S(1)}, u32[]{:S(2)}, u32[]{:S(2)}) %collective-permute-start.16) | collective-permute-done | bytes 262176 | tf_op jit(solution)/shard_map/ppermute | solution.py:911
  48.5 0.7 %mixed_out.2.refs_1_ = bf16[256,1024]{1,0:T(8,128)(2,1)} custom-call(f32[256,1024]{1,0:T(8,128)S(1)} %project_own.1.own_ref, bf16[256,512]{1,0:T(8,128)(2,1)S(1)} %collective-permute-done.16.refs_0_), custom_call_target="tpu_custom_call" | custom-call | tf_op jit(solution)/shard_map/mixed_out/pallas_call | solution.py:706
  49.2 4.1 %collective-permute-done.15.refs_0_ = bf16[256,512]{1,0:T(8,128)(2,1)S(1)} collective-permute-done((bf16[256,512]{1,0:T(8,128)(2,1)S(1)}, bf16[256,512]{1,0:T(8,128)(2,1)S(1)}, u32[]{:S(2)}, u32[]{:S(2)}) %collective-permute-start.15) | collective-permute-done | bytes 262176 | tf_op jit(solution)/shard_map/ppermute | solution.py:911
  53.3 0.7 %mixed_out.3 = bf16[256,1024]{1,0:T(8,128)(2,1)} custom-call(f32[256,1024]{1,0:T(8,128)S(1)} %project_own.1.own_ref, bf16[256,512]{1,0:T(8,128)(2,1)S(1)} %collective-permute-done.15.refs_0_, bf16[256,1024]{1,0:T(8,128)(2,1)} %mixed_out.2.refs_1_), custom_call_target="tpu_custom_call", output_to_operand_aliasing={{}: (2, {})} | custom-call | tf_op jit(solution)/shard_map/mixed_out/pallas_call | solution.py:706
  (36 shorter events, 5.9 us)
Async XLA Ops:
  0.0 2.3 %copy-start = (bf16[256,1024]{1,0:T(8,128)(2,1)S(1)}, bf16[256,1024]{1,0:T(8,128)(2,1)}, u32[]{:S(2)}) copy-start(bf16[256,1024]{1,0:T(8,128)(2,1)} %query_ref.3) | copy-start | bytes 1572868
  1.2 2.4 %collective-permute-start.1 = (bf16[256,1024]{1,0:T(8,128)(2,1)S(1)}, bf16[256,1024]{1,0:T(8,128)(2,1)S(1)}, u32[]{:S(2)}, u32[]{:S(2)}) collective-permute-start(bf16[256,1024]{1,0:T(8,128)(2,1)S(1)} %get-tuple-element.66), channel_id=1, source_target_pairs={{0,2},{2,0},{4,6},{6,4},{8,10},{10,8},{12,14},{14,12},{16,18},{18,... | collective-permute-start | bytes 1572872 | tf_op jit(solution)/shard_map/ppermute | solution.py:737
  1.7 1.8 %collective-permute-start.2 = (f32[2,4,256]{2,1,0:T(4,128)S(1)}, f32[2,4,256]{2,1,0:T(4,128)S(1)}, u32[]{:S(2)}, u32[]{:S(2)}) collective-permute-start(f32[2,4,256]{2,1,0:T(4,128)S(1)} %get-tuple-element.68.gates_ref), channel_id=1, source_target_pairs={{0,2},{2,0},{4,6},{6,4},{8,10},{10,8},{12,14},{14,12},{16,18},{18,... | collective-permute-start | bytes 24584 | tf_op jit(solution)/shard_map/ppermute | solution.py:737
  1.8 1.8 %collective-permute-start = (bf16[256,512]{1,0:T(8,128)(2,1)S(1)}, bf16[256,512]{1,0:T(8,128)(2,1)S(1)}, u32[]{:S(2)}, u32[]{:S(2)}) collective-permute-start(bf16[256,512]{1,0:T(8,128)(2,1)S(1)} %get-tuple-element.65), channel_id=1, source_target_pairs={{0,2},{2,0},{4,6},{6,4},{8,10},{10,8},{12,14},{14,12},{16,18},{18,... | collective-permute-start | bytes 786440 | tf_op jit(solution)/shard_map/ppermute | solution.py:737
  2.3 8.7 %collective-permute-start.3 = (bf16[256,1024]{1,0:T(8,128)(2,1)S(1)}, bf16[256,1024]{1,0:T(8,128)(2,1)S(1)}, u32[]{:S(2)}, u32[]{:S(2)}) collective-permute-start(bf16[256,1024]{1,0:T(8,128)(2,1)S(1)} %copy-done), channel_id=1, source_target_pairs={{0,2},{2,0},{4,6},{6,4},{8,10},{10,8},{12,14},{14,12},{16,18},{18,... | collective-permute-start | bytes 1572872 | tf_op jit(solution)/shard_map/ppermute | solution.py:737
  6.4 11.6 %collective-permute-start.4 = (bf16[528,128]{1,0:T(8,128)(2,1)S(1)}, bf16[528,128]{1,0:T(8,128)(2,1)S(1)}, u32[]{:S(2)}, u32[]{:S(2)}) collective-permute-start(bf16[528,128]{1,0:T(8,128)(2,1)S(1)} %get-tuple-element.75), channel_id=1, source_target_pairs={{0,4},{2,6},{4,0},{6,2},{8,12},{10,14},{12,8},{14,10},{16,20},{18,... | collective-permute-start | bytes 405512 | tf_op jit(solution)/shard_map/ppermute | solution.py:737
  9.4 8.6 %collective-permute-start.5 = (bf16[528,128]{1,0:T(8,128)(2,1)S(1)}, bf16[528,128]{1,0:T(8,128)(2,1)S(1)}, u32[]{:S(2)}, u32[]{:S(2)}) collective-permute-start(bf16[528,128]{1,0:T(8,128)(2,1)S(1)} %get-tuple-element.76), channel_id=1, source_target_pairs={{0,8},{2,10},{4,12},{6,14},{8,0},{10,2},{12,4},{14,6},{16,24},{18,... | collective-permute-start | bytes 405512 | tf_op jit(solution)/shard_map/ppermute | solution.py:737
  11.0 7.0 %collective-permute-start.6 = (bf16[528,128]{1,0:T(8,128)(2,1)S(1)}, bf16[528,128]{1,0:T(8,128)(2,1)S(1)}, u32[]{:S(2)}, u32[]{:S(2)}) collective-permute-start(bf16[528,128]{1,0:T(8,128)(2,1)S(1)} %get-tuple-element.77), channel_id=1, source_target_pairs={{0,12},{2,14},{4,8},{6,10},{8,4},{10,6},{12,0},{14,2},{16,28},{18,... | collective-permute-start | bytes 405512 | tf_op jit(solution)/shard_map/ppermute | solution.py:737
  11.1 6.9 %collective-permute-start.7 = (bf16[1,64,128]{2,1,0:T(8,128)(2,1)S(1)}, bf16[1,64,128]{2,1,0:T(8,128)(2,1)S(1)}, u32[]{:S(2)}, u32[]{:S(2)}) collective-permute-start(bf16[1,64,128]{2,1,0:T(8,128)(2,1)S(1)} %message.1.first_ref), channel_id=1, source_target_pairs={{0,8},{2,10},{4,12},{6,14},{8,0},{10,2},{12,4},{14,6},{16,24},{18,... | collective-permute-start | bytes 49160 | tf_op jit(solution)/shard_map/ppermute | solution.py:737
  18.2 7.6 %collective-permute-start.9 = (bf16[528,128]{1,0:T(8,128)(2,1)S(1)}, bf16[528,128]{1,0:T(8,128)(2,1)S(1)}, u32[]{:S(2)}, u32[]{:S(2)}) collective-permute-start(bf16[528,128]{1,0:T(8,128)(2,1)S(1)} %group_total.1), channel_id=1, source_target_pairs={{0,24},{2,26},{4,28},{6,30},{8,16},{10,18},{12,20},{14,22},{16,8},... | collective-permute-start | bytes 405512 | tf_op jit(solution)/shard_map/ppermute | solution.py:737
  21.9 3.9 %collective-permute-start.8 = (bf16[2,64,128]{2,1,0:T(8,128)(2,1)S(1)}, bf16[2,64,128]{2,1,0:T(8,128)(2,1)S(1)}, u32[]{:S(2)}, u32[]{:S(2)}) collective-permute-start(bf16[2,64,128]{2,1,0:T(8,128)(2,1)S(1)} %join.2.first_ref), channel_id=1, source_target_pairs={{0,4},{2,6},{4,0},{6,2},{8,12},{10,14},{12,8},{14,10},{16,20},{18,... | collective-permute-start | bytes 98312 | tf_op jit(solution)/shard_map/ppermute | solution.py:737
  25.8 5.4 %collective-permute-start.13 = (bf16[4,64,128]{2,1,0:T(8,128)(2,1)S(1)}, bf16[4,64,128]{2,1,0:T(8,128)(2,1)S(1)}, u32[]{:S(2)}, u32[]{:S(2)}) collective-permute-start(bf16[4,64,128]{2,1,0:T(8,128)(2,1)S(1)} %join.3.near_ref), channel_id=1, source_target_pairs={{0,16},{2,18},{4,20},{6,22},{8,24},{10,26},{12,28},{14,30},{16,0},... | collective-permute-start | bytes 196616 | tf_op jit(solution)/shard_map/ppermute | solution.py:737
  26.3 8.9 %collective-permute-start.10 = (bf16[528,128]{1,0:T(8,128)(2,1)S(1)}, bf16[528,128]{1,0:T(8,128)(2,1)S(1)}, u32[]{:S(2)}, u32[]{:S(2)}) collective-permute-start(bf16[528,128]{1,0:T(8,128)(2,1)S(1)} %get-tuple-element.91), channel_id=1, source_target_pairs={{0,4},{2,6},{4,0},{6,2},{8,12},{10,14},{12,8},{14,10},{16,20},{18,... | collective-permute-start | bytes 405512 | tf_op jit(solution)/shard_map/ppermute | solution.py:737
  27.6 7.5 %collective-permute-start.11 = (bf16[528,128]{1,0:T(8,128)(2,1)S(1)}, bf16[528,128]{1,0:T(8,128)(2,1)S(1)}, u32[]{:S(2)}, u32[]{:S(2)}) collective-permute-start(bf16[528,128]{1,0:T(8,128)(2,1)S(1)} %get-tuple-element.92), channel_id=1, source_target_pairs={{0,8},{2,10},{4,12},{6,14},{8,0},{10,2},{12,4},{14,6},{16,24},{18,... | collective-permute-start | bytes 405512 | tf_op jit(solution)/shard_map/ppermute | solution.py:737
  30.0 5.9 %collective-permute-start.12 = (bf16[528,128]{1,0:T(8,128)(2,1)S(1)}, bf16[528,128]{1,0:T(8,128)(2,1)S(1)}, u32[]{:S(2)}, u32[]{:S(2)}) collective-permute-start(bf16[528,128]{1,0:T(8,128)(2,1)S(1)} %get-tuple-element.93), channel_id=1, source_target_pairs={{0,12},{2,14},{4,8},{6,10},{8,4},{10,6},{12,0},{14,2},{16,28},{18,... | collective-permute-start | bytes 405512 | tf_op jit(solution)/shard_map/ppermute | solution.py:737
  32.6 4.9 %slice-start = ((s8[8388608]{0:T(1024)(128)(4,1)}), s8[4194304]{0:T(1024)(128)(4,1)S(1)}, s32[]{:S(2)}) async-start(s8[8388608]{0:T(1024)(128)(4,1)} %bitcast), calls=%async_computation | async-start | bytes 8388608
  32.6 4.9 %slice-start.1 = ((s8[8388608]{0:T(1024)(128)(4,1)}), s8[4194304]{0:T(1024)(128)(4,1)S(1)}, s32[]{:S(2)}) async-start(s8[8388608]{0:T(1024)(128)(4,1)} %bitcast), calls=%async_computation.1 | async-start | bytes 8388608
  36.8 2.0 %collective-permute-start.14 = (bf16[256,1024]{1,0:T(8,128)(2,1)S(1)}, bf16[256,1024]{1,0:T(8,128)(2,1)S(1)}, u32[]{:S(2)}, u32[]{:S(2)}) collective-permute-start(bf16[256,1024]{1,0:T(8,128)(2,1)S(1)} %get-tuple-element.108), channel_id=1, source_target_pairs={{0,2},{2,0},{4,6},{6,4},{8,10},{10,8},{12,14},{14,12},{16,18},{18,... | collective-permute-start | bytes 1572872 | tf_op jit(solution)/shard_map/ppermute | solution.py:737
  39.3 9.2 %collective-permute-start.16 = (bf16[256,512]{1,0:T(8,128)(2,1)S(1)}, bf16[256,512]{1,0:T(8,128)(2,1)S(1)}, u32[]{:S(2)}, u32[]{:S(2)}) collective-permute-start(bf16[256,512]{1,0:T(8,128)(2,1)S(1)} %project_other.3), channel_id=1, source_target_pairs={{0,1},{1,0},{2,3},{3,2},{4,5},{5,4},{6,7},{7,6},{8,9},{9,8},{10,11... | collective-permute-start | bytes 786440 | tf_op jit(solution)/shard_map/ppermute | solution.py:911
  42.5 10.8 %collective-permute-start.15 = (bf16[256,512]{1,0:T(8,128)(2,1)S(1)}, bf16[256,512]{1,0:T(8,128)(2,1)S(1)}, u32[]{:S(2)}, u32[]{:S(2)}) collective-permute-start(bf16[256,512]{1,0:T(8,128)(2,1)S(1)} %project_other.2), channel_id=1, source_target_pairs={{0,1},{1,0},{2,3},{3,2},{4,5},{5,4},{6,7},{7,6},{8,9},{9,8},{10,11... | collective-permute-start | bytes 786440 | tf_op jit(solution)/shard_map/ppermute | solution.py:911

commit v10 on v8

--- a/solution.py
+++ b/solution.py
@@ -204,7 +204,7 @@
     levels_first[1] = levels[1]
     same = same_request(lengths_ref, offset + iota((length, 128), 0))
     normals[...] = jnp.zeros_like(normals)
-    step = 128
+    step = 256
     key_edge[0] = jnp.where(core == 0, own_keys[0:16, :], key_other[0:16, :])
     key_edge[1] = jnp.where(core == 0, key_other[rows - 16 :, :], own_keys[rows - 16 :, :])
     for i in range(per_core):

time: 54.3 us -> 54.3 us (level)
  no operation moved by 1% of the time
where the time goes in v10:
time: 54.3 us; the launch traced here: 54.1 us
  starting transfers between devices  18.9 us (35%)
  Pallas kernels  18.3 us (34%)
  waiting for transfers between devices  16.6 us (31%)
    pallas_call x19, Pallas kernels, run(): inner(*(pltpu.with_memory_space_constraint(x, pltpu.HBM) if s in 'hs' els...  18.3 us
    ppermute x15, starting transfers between devices, swap(): return lax.ppermute(x, 'seq', [(i, i ^ off) for i in range(seq_count)])  16.8 us
    ppermute x2, waiting for transfers between devices, on_device(): lax.ppermute(part, 'head', [(i, i ^ off) for i in range(head_count)])  9.41 us
    ppermute x15, waiting for transfers between devices, swap(): return lax.ppermute(x, 'seq', [(i, i ^ off) for i in range(seq_count)])  7.2 us
    ppermute x2, starting transfers between devices, on_device(): lax.ppermute(part, 'head', [(i, i ^ off) for i in range(head_count)])  2.16 us
  transfers between devices with their start and end apart: 17, of which 8 were waited for; matrix products, arithmetic and copies ran while one was open for 0% of the time, Pallas kernels for 27%

profile of v10, /device:TPU:0, one launch (start us, length us, event | category | flops | bytes accessed | tf_op | source)
XLA Modules:
  0.0 54.1 jit_solution(3607920799988274554)
XLA Ops:
  0.0 1.2 %gates.1 = (f32[2,4,256]{2,1,0:T(4,128)S(1)}, bf16[256,512]{1,0:T(8,128)(2,1)S(1)}, bf16[256,1024]{1,0:T(8,128)(2,1)S(1)}) custom-call(f32[4,256]{1,0:T(4,128)} %input_ref.1, f32[4,256]{1,0:T(4,128)} %forget_ref.1, bf16[256,1024]{1,0:T(8,128)(2,1)} %key_ref.2, bf16[256,2048]{1,0:T(8,128)(2,1)} %value_ref.2), custom_call_target="tpu_custom_call" | custom-call | flops 4294967296 | tf_op jit(solution)/shard_map/gates/pallas_call | solution.py:703
  2.3 1.1 %own_part.1 = (bf16[256,512]{1,0:T(8,128)(2,1)S(1)}, bf16[256,1024]{1,0:T(8,128)(2,1)S(1)}, f32[4,512]{1,0:T(4,128)S(1)}) custom-call(bf16[256,1024]{1,0:T(8,128)(2,1)} %key_ref.2, bf16[256,2048]{1,0:T(8,128)(2,1)} %value_ref.2, f32[2,4,1024]{2,1,0:T(4,128)} %taps_ref.3), custom_call_target="tpu_custom_call" | custom-call | flops 4294967296 | tf_op jit(solution)/shard_map/own_part/pallas_call | solution.py:703
  3.7 2.8 %chip_state.1 = (bf16[512,512]{1,0:T(8,128)(2,1)S(1)}, f32[2,8,512]{2,1,0:T(8,128)S(1)}, bf16[2,16,512]{2,1,0:T(8,128)(2,1)S(1)}, f32[2,8,128]{2,1,0:T(8,128)S(1...) custom-call(s32[4]{0:T(128)} %lengths_ref.7, ...), custom_call_target="tpu_custom_call" | custom-call | flops 1073741824 | tf_op jit(solution)/shard_map/chip_state/pallas_call | solution.py:703
  6.5 2.9 %collective-permute-start.4 = (bf16[528,128]{1,0:T(8,128)(2,1)S(1)}, bf16[528,128]{1,0:T(8,128)(2,1)S(1)}, u32[]{:S(2)}, u32[]{:S(2)}) collective-permute-start(bf16[528,128]{1,0:T(8,128)(2,1)S(1)} %get-tuple-element.75), channel_id=1, source_target_pairs={{0,4},{2,6},{4,0},{6,2},{8,12},{10,14},{12,8},{14,10},{16,20},{18,... | collective-permute-start | bytes 405512 | tf_op jit(solution)/shard_map/ppermute | solution.py:734
  9.4 1.6 %collective-permute-start.5 = (bf16[528,128]{1,0:T(8,128)(2,1)S(1)}, bf16[528,128]{1,0:T(8,128)(2,1)S(1)}, u32[]{:S(2)}, u32[]{:S(2)}) collective-permute-start(bf16[528,128]{1,0:T(8,128)(2,1)S(1)} %get-tuple-element.76), channel_id=1, source_target_pairs={{0,8},{2,10},{4,12},{6,14},{8,0},{10,2},{12,4},{14,6},{16,24},{18,... | collective-permute-start | bytes 405512 | tf_op jit(solution)/shard_map/ppermute | solution.py:734
  11.1 2.0 %collective-permute-start.7 = (bf16[1,64,128]{2,1,0:T(8,128)(2,1)S(1)}, bf16[1,64,128]{2,1,0:T(8,128)(2,1)S(1)}, u32[]{:S(2)}, u32[]{:S(2)}) collective-permute-start(bf16[1,64,128]{2,1,0:T(8,128)(2,1)S(1)} %message.1.first_ref), channel_id=1, source_target_pairs={{0,8},{2,10},{4,12},{6,14},{8,0},{10,2},{12,4},{14,6},{16,24},{18,... | collective-permute-start | bytes 49160 | tf_op jit(solution)/shard_map/ppermute | solution.py:734
  13.2 2.7 %query_conv.1 = (bf16[512,512]{1,0:T(8,128)(2,1)S(1)}, f32[4,512]{1,0:T(4,128)S(1)}, bf16[2,16,512]{2,1,0:T(8,128)(2,1)S(1)}, bf16[512,1024]{1,0:T(8,128)(2,1)S(1)}) custom-call(s32[4]{0:T(128)} %lengths_ref.7, bf16[256,1024]{1,0:T(8,128)(2,1)} %query_ref.3, bf16[256,1024]{1,0:T(8,128)(2,1)S(1)} %collective-permute-done.3.query_other, ...), custom_call_target="tpu_custom_call" | custom-call | flops 1073741824 | tf_op jit(solution)/shard_map/query_conv/pallas_call | solution.py:703
  15.8 2.2 %collective-permute-done.7.second_ref = bf16[1,64,128]{2,1,0:T(8,128)(2,1)S(1)} collective-permute-done((bf16[1,64,128]{2,1,0:T(8,128)(2,1)S(1)}, bf16[1,64,128]{2,1,0:T(8,128)(2,1)S(1)}, u32[]{:S(2)}, u32[]{:S(2)}) %collective-permute-start.7) | collective-permute-done | bytes 16416 | tf_op jit(solution)/shard_map/ppermute | solution.py:734
  18.3 3.7 %collective-permute-start.9 = (bf16[528,128]{1,0:T(8,128)(2,1)S(1)}, bf16[528,128]{1,0:T(8,128)(2,1)S(1)}, u32[]{:S(2)}, u32[]{:S(2)}) collective-permute-start(bf16[528,128]{1,0:T(8,128)(2,1)S(1)} %group_total.1), channel_id=1, source_target_pairs={{0,24},{2,26},{4,28},{6,30},{8,16},{10,18},{12,20},{14,22},{16,8},... | collective-permute-start | bytes 405512 | tf_op jit(solution)/shard_map/ppermute | solution.py:734
  21.9 1.3 %collective-permute-start.8 = (bf16[2,64,128]{2,1,0:T(8,128)(2,1)S(1)}, bf16[2,64,128]{2,1,0:T(8,128)(2,1)S(1)}, u32[]{:S(2)}, u32[]{:S(2)}) collective-permute-start(bf16[2,64,128]{2,1,0:T(8,128)(2,1)S(1)} %join.2.first_ref), channel_id=1, source_target_pairs={{0,4},{2,6},{4,0},{6,2},{8,12},{10,14},{12,8},{14,10},{16,20},{18,... | collective-permute-start | bytes 98312 | tf_op jit(solution)/shard_map/ppermute | solution.py:734
  23.2 2.6 %collective-permute-done.8.second_ref = bf16[2,64,128]{2,1,0:T(8,128)(2,1)S(1)} collective-permute-done((bf16[2,64,128]{2,1,0:T(8,128)(2,1)S(1)}, bf16[2,64,128]{2,1,0:T(8,128)(2,1)S(1)}, u32[]{:S(2)}, u32[]{:S(2)}) %collective-permute-start.8) | collective-permute-done | bytes 32800 | tf_op jit(solution)/shard_map/ppermute | solution.py:734
  26.3 1.3 %collective-permute-start.10 = (bf16[528,128]{1,0:T(8,128)(2,1)S(1)}, bf16[528,128]{1,0:T(8,128)(2,1)S(1)}, u32[]{:S(2)}, u32[]{:S(2)}) collective-permute-start(bf16[528,128]{1,0:T(8,128)(2,1)S(1)} %get-tuple-element.91), channel_id=1, source_target_pairs={{0,4},{2,6},{4,0},{6,2},{8,12},{10,14},{12,8},{14,10},{16,20},{18,... | collective-permute-start | bytes 405512 | tf_op jit(solution)/shard_map/ppermute | solution.py:734
  27.7 2.4 %collective-permute-start.11 = (bf16[528,128]{1,0:T(8,128)(2,1)S(1)}, bf16[528,128]{1,0:T(8,128)(2,1)S(1)}, u32[]{:S(2)}, u32[]{:S(2)}) collective-permute-start(bf16[528,128]{1,0:T(8,128)(2,1)S(1)} %get-tuple-element.92), channel_id=1, source_target_pairs={{0,8},{2,10},{4,12},{6,14},{8,0},{10,2},{12,4},{14,6},{16,24},{18,... | collective-permute-start | bytes 405512 | tf_op jit(solution)/shard_map/ppermute | solution.py:734
  30.4 0.8 %collective-permute-done.13.far_ref = bf16[4,64,128]{2,1,0:T(8,128)(2,1)S(1)} collective-permute-done((bf16[4,64,128]{2,1,0:T(8,128)(2,1)S(1)}, bf16[4,64,128]{2,1,0:T(8,128)(2,1)S(1)}, u32[]{:S(2)}, u32[]{:S(2)}) %collective-permute-start.13) | collective-permute-done | bytes 65568 | tf_op jit(solution)/shard_map/ppermute | solution.py:734
  31.3 1.4 %gathered_first.1 = (bf16[256,256]{1,0:T(8,128)(2,1)S(1)}, bf16[256,512]{1,0:T(8,128)(2,1)S(1)}, f32[256,128]{1,0:T(8,128)S(1)}, bf16[2,16,512]{2,1,0:T(8,128)(2,1)S(1)}) custom-call(s32[4]{0:T(128)} %lengths_ref.7, bf16[4,64,128]{2,1,0:T(8,128)(2,1)S(1)} %join.3.near_ref, bf16[4,64,128]{2,1,0:T(8,128)(2,1)S(1)} %collective-permute-done.13.far_ref, ...), custom_call_target="tpu_custom_call" | custom-call | tf_op jit(solution)/shard_map/gathered_first/pallas_call | solution.py:703
  32.7 2.5 %intra.1 = (bf16[512,512]{1,0:T(8,128)(2,1)S(1)}, f32[512,1024]{1,0:T(8,128)S(1)}, f32[3,512,128]{2,1,0:T(8,128)S(1)}) custom-call(s32[4]{0:T(128)} %lengths_ref.7, bf16[512,512]{1,0:T(8,128)(2,1)S(1)} %get-tuple-element.100.query_conv, bf16[512,512]{1,0:T(8,128)(2,1)S(1)} %get-tuple-element.101.key_ref, ...), custom_call_target="tpu_custom_call" | custom-call | flops 4294967296 | tf_op jit(solution)/shard_map/intra/pallas_call | solution.py:703
  35.2 0.8 %collective-permute-done.12.got3 = bf16[528,128]{1,0:T(8,128)(2,1)S(1)} collective-permute-done((bf16[528,128]{1,0:T(8,128)(2,1)S(1)}, bf16[528,128]{1,0:T(8,128)(2,1)S(1)}, u32[]{:S(2)}, u32[]{:S(2)}) %collective-permute-start.12) | collective-permute-done | bytes 135200 | tf_op jit(solution)/shard_map/ppermute | solution.py:734
  36.0 0.9 %head_send.1 = (bf16[256,1024]{1,0:T(8,128)(2,1)S(1)}, bf16[512,512]{1,0:T(8,128)(2,1)S(1)}, bf16[256,256]{1,0:T(8,128)(2,1)S(1)}, f32[8,128]{1,0:T(8,128)S(1)}) custom-call(bf16[528,128]{1,0:T(8,128)(2,1)S(1)} %get-tuple-element.90.own_ref, bf16[528,128]{1,0:T(8,128)(2,1)S(1)} %collective-permute-done.10.got1, ...), custom_call_target="tpu_custom_call" | custom-call | tf_op jit(solution)/shard_map/head_send/pallas_call | solution.py:703
  39.3 1.5 %collective-permute-start.16 = (bf16[256,512]{1,0:T(8,128)(2,1)S(1)}, bf16[256,512]{1,0:T(8,128)(2,1)S(1)}, u32[]{:S(2)}, u32[]{:S(2)}) collective-permute-start(bf16[256,512]{1,0:T(8,128)(2,1)S(1)} %project_other.3), channel_id=1, source_target_pairs={{0,1},{1,0},{2,3},{3,2},{4,5},{5,4},{6,7},{7,6},{8,9},{9,8},{10,11... | collective-permute-start | bytes 786440 | tf_op jit(solution)/shard_map/ppermute | solution.py:908
  40.9 1.2 %project_own.1.own_ref = f32[256,1024]{1,0:T(8,128)S(1)} custom-call(bf16[256,1024]{1,0:T(8,128)(2,1)S(1)} %head_keep.1.keep_ref.head_ref, bf16[256,1024]{1,0:T(8,128)(2,1)S(1)} %collective-permute-done.14.got_ref.head_ref, bf16[2048,2048]{1,0:T(8,128)(2,1)S(1)} %bitcast.1), custom_call_target="tpu_custom_call" | custom-call | flops 4294967296 | tf_op jit(solution)/shard_map/project_own/pallas_call | solution.py:703
  43.2 5.3 %collective-permute-done.16.refs_0_ = bf16[256,512]{1,0:T(8,128)(2,1)S(1)} collective-permute-done((bf16[256,512]{1,0:T(8,128)(2,1)S(1)}, bf16[256,512]{1,0:T(8,128)(2,1)S(1)}, u32[]{:S(2)}, u32[]{:S(2)}) %collective-permute-start.16) | collective-permute-done | bytes 262176 | tf_op jit(solution)/shard_map/ppermute | solution.py:908
  48.6 0.7 %mixed_out.2.refs_1_ = bf16[256,1024]{1,0:T(8,128)(2,1)} custom-call(f32[256,1024]{1,0:T(8,128)S(1)} %project_own.1.own_ref, bf16[256,512]{1,0:T(8,128)(2,1)S(1)} %collective-permute-done.16.refs_0_), custom_call_target="tpu_custom_call" | custom-call | tf_op jit(solution)/shard_map/mixed_out/pallas_call | solution.py:703
  49.3 4.1 %collective-permute-done.15.refs_0_ = bf16[256,512]{1,0:T(8,128)(2,1)S(1)} collective-permute-done((bf16[256,512]{1,0:T(8,128)(2,1)S(1)}, bf16[256,512]{1,0:T(8,128)(2,1)S(1)}, u32[]{:S(2)}, u32[]{:S(2)}) %collective-permute-start.15) | collective-permute-done | bytes 262176 | tf_op jit(solution)/shard_map/ppermute | solution.py:908
  53.4 0.7 %mixed_out.3 = bf16[256,1024]{1,0:T(8,128)(2,1)} custom-call(f32[256,1024]{1,0:T(8,128)S(1)} %project_own.1.own_ref, bf16[256,512]{1,0:T(8,128)(2,1)S(1)} %collective-permute-done.15.refs_0_, bf16[256,1024]{1,0:T(8,128)(2,1)} %mixed_out.2.refs_1_), custom_call_target="tpu_custom_call", output_to_operand_aliasing={{}: (2, {})} | custom-call | tf_op jit(solution)/shard_map/mixed_out/pallas_call | solution.py:703
  (36 shorter events, 5.9 us)
Async XLA Ops:
  0.0 2.3 %copy-start = (bf16[256,1024]{1,0:T(8,128)(2,1)S(1)}, bf16[256,1024]{1,0:T(8,128)(2,1)}, u32[]{:S(2)}) copy-start(bf16[256,1024]{1,0:T(8,128)(2,1)} %query_ref.3) | copy-start | bytes 1572868
  1.2 2.4 %collective-permute-start.1 = (bf16[256,1024]{1,0:T(8,128)(2,1)S(1)}, bf16[256,1024]{1,0:T(8,128)(2,1)S(1)}, u32[]{:S(2)}, u32[]{:S(2)}) collective-permute-start(bf16[256,1024]{1,0:T(8,128)(2,1)S(1)} %get-tuple-element.66), channel_id=1, source_target_pairs={{0,2},{2,0},{4,6},{6,4},{8,10},{10,8},{12,14},{14,12},{16,18},{18,... | collective-permute-start | bytes 1572872 | tf_op jit(solution)/shard_map/ppermute | solution.py:734
  1.7 1.8 %collective-permute-start.2 = (f32[2,4,256]{2,1,0:T(4,128)S(1)}, f32[2,4,256]{2,1,0:T(4,128)S(1)}, u32[]{:S(2)}, u32[]{:S(2)}) collective-permute-start(f32[2,4,256]{2,1,0:T(4,128)S(1)} %get-tuple-element.68.gates_ref), channel_id=1, source_target_pairs={{0,2},{2,0},{4,6},{6,4},{8,10},{10,8},{12,14},{14,12},{16,18},{18,... | collective-permute-start | bytes 24584 | tf_op jit(solution)/shard_map/ppermute | solution.py:734
  1.8 1.8 %collective-permute-start = (bf16[256,512]{1,0:T(8,128)(2,1)S(1)}, bf16[256,512]{1,0:T(8,128)(2,1)S(1)}, u32[]{:S(2)}, u32[]{:S(2)}) collective-permute-start(bf16[256,512]{1,0:T(8,128)(2,1)S(1)} %get-tuple-element.65), channel_id=1, source_target_pairs={{0,2},{2,0},{4,6},{6,4},{8,10},{10,8},{12,14},{14,12},{16,18},{18,... | collective-permute-start | bytes 786440 | tf_op jit(solution)/shard_map/ppermute | solution.py:734
  2.3 8.8 %collective-permute-start.3 = (bf16[256,1024]{1,0:T(8,128)(2,1)S(1)}, bf16[256,1024]{1,0:T(8,128)(2,1)S(1)}, u32[]{:S(2)}, u32[]{:S(2)}) collective-permute-start(bf16[256,1024]{1,0:T(8,128)(2,1)S(1)} %copy-done), channel_id=1, source_target_pairs={{0,2},{2,0},{4,6},{6,4},{8,10},{10,8},{12,14},{14,12},{16,18},{18,... | collective-permute-start | bytes 1572872 | tf_op jit(solution)/shard_map/ppermute | solution.py:734
  6.5 11.5 %collective-permute-start.4 = (bf16[528,128]{1,0:T(8,128)(2,1)S(1)}, bf16[528,128]{1,0:T(8,128)(2,1)S(1)}, u32[]{:S(2)}, u32[]{:S(2)}) collective-permute-start(bf16[528,128]{1,0:T(8,128)(2,1)S(1)} %get-tuple-element.75), channel_id=1, source_target_pairs={{0,4},{2,6},{4,0},{6,2},{8,12},{10,14},{12,8},{14,10},{16,20},{18,... | collective-permute-start | bytes 405512 | tf_op jit(solution)/shard_map/ppermute | solution.py:734
  9.4 8.6 %collective-permute-start.5 = (bf16[528,128]{1,0:T(8,128)(2,1)S(1)}, bf16[528,128]{1,0:T(8,128)(2,1)S(1)}, u32[]{:S(2)}, u32[]{:S(2)}) collective-permute-start(bf16[528,128]{1,0:T(8,128)(2,1)S(1)} %get-tuple-element.76), channel_id=1, source_target_pairs={{0,8},{2,10},{4,12},{6,14},{8,0},{10,2},{12,4},{14,6},{16,24},{18,... | collective-permute-start | bytes 405512 | tf_op jit(solution)/shard_map/ppermute | solution.py:734
  11.0 7.0 %collective-permute-start.6 = (bf16[528,128]{1,0:T(8,128)(2,1)S(1)}, bf16[528,128]{1,0:T(8,128)(2,1)S(1)}, u32[]{:S(2)}, u32[]{:S(2)}) collective-permute-start(bf16[528,128]{1,0:T(8,128)(2,1)S(1)} %get-tuple-element.77), channel_id=1, source_target_pairs={{0,12},{2,14},{4,8},{6,10},{8,4},{10,6},{12,0},{14,2},{16,28},{18,... | collective-permute-start | bytes 405512 | tf_op jit(solution)/shard_map/ppermute | solution.py:734
  11.1 6.9 %collective-permute-start.7 = (bf16[1,64,128]{2,1,0:T(8,128)(2,1)S(1)}, bf16[1,64,128]{2,1,0:T(8,128)(2,1)S(1)}, u32[]{:S(2)}, u32[]{:S(2)}) collective-permute-start(bf16[1,64,128]{2,1,0:T(8,128)(2,1)S(1)} %message.1.first_ref), channel_id=1, source_target_pairs={{0,8},{2,10},{4,12},{6,14},{8,0},{10,2},{12,4},{14,6},{16,24},{18,... | collective-permute-start | bytes 49160 | tf_op jit(solution)/shard_map/ppermute | solution.py:734
  18.3 7.6 %collective-permute-start.9 = (bf16[528,128]{1,0:T(8,128)(2,1)S(1)}, bf16[528,128]{1,0:T(8,128)(2,1)S(1)}, u32[]{:S(2)}, u32[]{:S(2)}) collective-permute-start(bf16[528,128]{1,0:T(8,128)(2,1)S(1)} %group_total.1), channel_id=1, source_target_pairs={{0,24},{2,26},{4,28},{6,30},{8,16},{10,18},{12,20},{14,22},{16,8},... | collective-permute-start | bytes 405512 | tf_op jit(solution)/shard_map/ppermute | solution.py:734
  21.9 3.9 %collective-permute-start.8 = (bf16[2,64,128]{2,1,0:T(8,128)(2,1)S(1)}, bf16[2,64,128]{2,1,0:T(8,128)(2,1)S(1)}, u32[]{:S(2)}, u32[]{:S(2)}) collective-permute-start(bf16[2,64,128]{2,1,0:T(8,128)(2,1)S(1)} %join.2.first_ref), channel_id=1, source_target_pairs={{0,4},{2,6},{4,0},{6,2},{8,12},{10,14},{12,8},{14,10},{16,20},{18,... | collective-permute-start | bytes 98312 | tf_op jit(solution)/shard_map/ppermute | solution.py:734
  25.9 5.4 %collective-permute-start.13 = (bf16[4,64,128]{2,1,0:T(8,128)(2,1)S(1)}, bf16[4,64,128]{2,1,0:T(8,128)(2,1)S(1)}, u32[]{:S(2)}, u32[]{:S(2)}) collective-permute-start(bf16[4,64,128]{2,1,0:T(8,128)(2,1)S(1)} %join.3.near_ref), channel_id=1, source_target_pairs={{0,16},{2,18},{4,20},{6,22},{8,24},{10,26},{12,28},{14,30},{16,0},... | collective-permute-start | bytes 196616 | tf_op jit(solution)/shard_map/ppermute | solution.py:734
  26.3 8.9 %collective-permute-start.10 = (bf16[528,128]{1,0:T(8,128)(2,1)S(1)}, bf16[528,128]{1,0:T(8,128)(2,1)S(1)}, u32[]{:S(2)}, u32[]{:S(2)}) collective-permute-start(bf16[528,128]{1,0:T(8,128)(2,1)S(1)} %get-tuple-element.91), channel_id=1, source_target_pairs={{0,4},{2,6},{4,0},{6,2},{8,12},{10,14},{12,8},{14,10},{16,20},{18,... | collective-permute-start | bytes 405512 | tf_op jit(solution)/shard_map/ppermute | solution.py:734
  27.7 7.6 %collective-permute-start.11 = (bf16[528,128]{1,0:T(8,128)(2,1)S(1)}, bf16[528,128]{1,0:T(8,128)(2,1)S(1)}, u32[]{:S(2)}, u32[]{:S(2)}) collective-permute-start(bf16[528,128]{1,0:T(8,128)(2,1)S(1)} %get-tuple-element.92), channel_id=1, source_target_pairs={{0,8},{2,10},{4,12},{6,14},{8,0},{10,2},{12,4},{14,6},{16,24},{18,... | collective-permute-start | bytes 405512 | tf_op jit(solution)/shard_map/ppermute | solution.py:734
  30.1 5.9 %collective-permute-start.12 = (bf16[528,128]{1,0:T(8,128)(2,1)S(1)}, bf16[528,128]{1,0:T(8,128)(2,1)S(1)}, u32[]{:S(2)}, u32[]{:S(2)}) collective-permute-start(bf16[528,128]{1,0:T(8,128)(2,1)S(1)} %get-tuple-element.93), channel_id=1, source_target_pairs={{0,12},{2,14},{4,8},{6,10},{8,4},{10,6},{12,0},{14,2},{16,28},{18,... | collective-permute-start | bytes 405512 | tf_op jit(solution)/shard_map/ppermute | solution.py:734
  32.6 4.9 %slice-start = ((s8[8388608]{0:T(1024)(128)(4,1)}), s8[4194304]{0:T(1024)(128)(4,1)S(1)}, s32[]{:S(2)}) async-start(s8[8388608]{0:T(1024)(128)(4,1)} %bitcast), calls=%async_computation | async-start | bytes 8388608
  32.7 4.9 %slice-start.1 = ((s8[8388608]{0:T(1024)(128)(4,1)}), s8[4194304]{0:T(1024)(128)(4,1)S(1)}, s32[]{:S(2)}) async-start(s8[8388608]{0:T(1024)(128)(4,1)} %bitcast), calls=%async_computation.1 | async-start | bytes 8388608
  36.9 2.0 %collective-permute-start.14 = (bf16[256,1024]{1,0:T(8,128)(2,1)S(1)}, bf16[256,1024]{1,0:T(8,128)(2,1)S(1)}, u32[]{:S(2)}, u32[]{:S(2)}) collective-permute-start(bf16[256,1024]{1,0:T(8,128)(2,1)S(1)} %get-tuple-element.108), channel_id=1, source_target_pairs={{0,2},{2,0},{4,6},{6,4},{8,10},{10,8},{12,14},{14,12},{16,18},{18,... | collective-permute-start | bytes 1572872 | tf_op jit(solution)/shard_map/ppermute | solution.py:734
  39.3 9.2 %collective-permute-start.16 = (bf16[256,512]{1,0:T(8,128)(2,1)S(1)}, bf16[256,512]{1,0:T(8,128)(2,1)S(1)}, u32[]{:S(2)}, u32[]{:S(2)}) collective-permute-start(bf16[256,512]{1,0:T(8,128)(2,1)S(1)} %project_other.3), channel_id=1, source_target_pairs={{0,1},{1,0},{2,3},{3,2},{4,5},{5,4},{6,7},{7,6},{8,9},{9,8},{10,11... | collective-permute-start | bytes 786440 | tf_op jit(solution)/shard_map/ppermute | solution.py:908
  42.6 10.8 %collective-permute-start.15 = (bf16[256,512]{1,0:T(8,128)(2,1)S(1)}, bf16[256,512]{1,0:T(8,128)(2,1)S(1)}, u32[]{:S(2)}, u32[]{:S(2)}) collective-permute-start(bf16[256,512]{1,0:T(8,128)(2,1)S(1)} %project_other.2), channel_id=1, source_target_pairs={{0,1},{1,0},{2,3},{3,2},{4,5},{5,4},{6,7},{7,6},{8,9},{9,8},{10,11... | collective-permute-start | bytes 786440 | tf_op jit(solution)/shard_map/ppermute | solution.py:908
